TPU v7x, 128 devices: a whole 4x4x4 slice. The times are simulated.
128 devices in a mesh: tm: 4 (over y_hi, core), ha: 4 (over x), wa: 8 (over y_lo, z).
Axes of the slice: x: 4, y: 4 (y_hi: 2, y_lo: 2; y = y_hi * 2 + y_lo), z: 4, core: 2. Of those that a mesh axis runs over, the one named last changes fastest.
Arguments:
- queries: bfloat16 [1, 4, 64, 128, 1536], P(None, 'tm', 'ha', 'wa'), may hold values from -6 to 6
- tile_keys: bfloat16 [1, 4, 64, 128, 1536], P(None, 'tm', 'ha', 'wa'), may hold values from -6 to 6
- values: bfloat16 [1, 4, 64, 128, 1536], P(None, 'tm', 'ha', 'wa'), may hold values from -6 to 6
- probes: bfloat16 [1, 4, 64, 128, 1536], P(None, 'tm', 'ha', 'wa'), may hold values from -6 to 6
- anchors: bfloat16 [1, 4, 64, 128, 1536], P(None, 'tm', 'ha', 'wa'), may hold values from -6 to 6
- upstream: bfloat16 [1, 4, 64, 128, 1536], P(None, 'tm', 'ha', 'wa'), may hold values from -6 to 6
Outputs:
- query_grad: bfloat16 [1, 4, 64, 128, 1536], P(None, 'tm', 'ha', 'wa')
- key_grad: bfloat16 [1, 4, 64, 128, 1536], P(None, 'tm', 'ha', 'wa')
- value_grad: bfloat16 [1, 4, 64, 128, 1536], P(None, 'tm', 'ha', 'wa')
- probe_grad: bfloat16 [1, 4, 64, 128, 1536], P(None, 'tm', 'ha', 'wa')
- anchor_grad: bfloat16 [1, 4, 64, 128, 1536], P(None, 'tm', 'ha', 'wa')
All inputs are finite; a program needn't handle non-finite values.
Results may differ from a plain program's by a relative error of at most 0.025.
Values may be sent and summed in bfloat16 or wider, within the bound.
No kernel may reach another device: no remote copies, remote signals or barrier semaphores. Data moves between devices by JAX's collectives and lax.ppermute only.
A program may use at most 192 MiB of HBM per device.

v0:
```python
import jax
import jax.numpy as jnp
from jax import lax
from jax.sharding import PartitionSpec as P

HEADS = 12
HEAD_DIM = 128


NEG_FILL = -1e30


def padded(cells, sides, width):
    for axis, dim in sides:
        count = lax.axis_size(axis)
        ends = count - 1
        head = lax.slice_in_dim(cells, 0, width, axis=dim)
        tail = lax.slice_in_dim(cells, cells.shape[dim] - width, cells.shape[dim], axis=dim)
        cells = jnp.concatenate(
            [
                lax.ppermute(tail, axis, [(i, (i + 1) % count) for i in range(ends)]),
                cells,
                lax.ppermute(head, axis, [((i + 1) % count, i) for i in range(ends)]),
            ],
            axis=dim,
        )
    return cells


def split_heads(block):
    return block.reshape(block.shape[:-1] + (block.shape[-1] // HEAD_DIM, HEAD_DIM))


def merge_heads(block):
    return block.reshape(block.shape[:-2] + (block.shape[-2] * block.shape[-1],))


def region_valid(tile_size):
    places = jnp.arange(3 * tile_size, dtype=jnp.int32) // tile_size - 1
    row_place = places + lax.axis_index("ha")
    col_place = places + lax.axis_index("wa")
    row_ok = (row_place >= 0) & (row_place < lax.axis_size("ha"))
    col_ok = (col_place >= 0) & (col_place < lax.axis_size("wa"))
    return row_ok[:, None] & col_ok[None, :]


def attend_forward(query_heads, key_heads, value_heads, valid_keys, score_scale):
    scores = (
        jnp.einsum("bhqd,bhkd->bhqk", query_heads, key_heads, preferred_element_type=jnp.float32)
        * score_scale
    )
    scores = jnp.where(valid_keys, scores, NEG_FILL)
    row_max = jnp.max(scores, axis=-1, keepdims=True)
    log_total = row_max + jnp.log(jnp.sum(jnp.exp(scores - row_max), axis=-1, keepdims=True))
    weights = jnp.exp(scores - log_total)
    weights_low = weights.astype(jnp.bfloat16)
    mixed_block = jnp.einsum(
        "bhqk,bhkd->bhqd", weights_low, value_heads, preferred_element_type=jnp.float32
    )
    return (mixed_block.astype(jnp.bfloat16), weights, weights_low)


def attend_backward(
    query_heads, key_heads, value_heads, weights, weights_low, grad_heads, mixed_heads, score_scale
):
    weight_grads = jnp.einsum(
        "bhqd,bhkd->bhqk", grad_heads, value_heads, preferred_element_type=jnp.float32
    )
    row_term = jnp.sum(
        grad_heads.astype(jnp.float32) * mixed_heads.astype(jnp.float32), axis=-1, keepdims=True
    )
    score_grads = (weights * (weight_grads - row_term)).astype(jnp.bfloat16)
    query_block = (
        jnp.einsum("bhqk,bhkd->bhqd", score_grads, key_heads, preferred_element_type=jnp.float32)
        * score_scale
    ).astype(jnp.bfloat16)
    key_terms = (
        jnp.einsum("bhqk,bhqd->bhkd", score_grads, query_heads, preferred_element_type=jnp.float32)
        * score_scale
    ).astype(jnp.bfloat16)
    value_terms = jnp.einsum(
        "bhqk,bhqd->bhkd", weights_low, grad_heads, preferred_element_type=jnp.float32
    ).astype(jnp.bfloat16)
    return (query_block, key_terms, value_terms)


def temporal_grads(probe_part, anchor_part, mixed_part, upstream_part, score_scale):
    probe_heads = split_heads(probe_part)
    anchor_heads = split_heads(anchor_part)
    mixed_heads = split_heads(mixed_part)
    upstream_heads = split_heads(upstream_part)
    scores = (
        jnp.einsum(
            "bfxyhd,bgxyhd->bxyhfg", probe_heads, anchor_heads, preferred_element_type=jnp.float32
        )
        * score_scale
    )
    row_max = jnp.max(scores, axis=-1, keepdims=True)
    shifted = jnp.exp(scores - row_max)
    weights = shifted / jnp.sum(shifted, axis=-1, keepdims=True)
    mixed_terms = jnp.einsum(
        "bxyhfg,bfxyhd->bgxyhd",
        weights.astype(jnp.bfloat16),
        upstream_heads,
        preferred_element_type=jnp.float32,
    )
    weight_grads = jnp.einsum(
        "bfxyhd,bgxyhd->bxyhfg", upstream_heads, mixed_heads, preferred_element_type=jnp.float32
    )
    row_dot = jnp.sum(weights * weight_grads, axis=-1, keepdims=True)
    score_grads = (weights * (weight_grads - row_dot)).astype(jnp.bfloat16)
    probe_grad = (
        jnp.einsum(
            "bxyhfg,bgxyhd->bfxyhd", score_grads, anchor_heads, preferred_element_type=jnp.float32
        )
        * score_scale
    ).astype(jnp.bfloat16)
    anchor_terms = (
        jnp.einsum(
            "bxyhfg,bfxyhd->bgxyhd", score_grads, probe_heads, preferred_element_type=jnp.float32
        )
        * score_scale
    )
    return (merge_heads(probe_grad), merge_heads(anchor_terms), merge_heads(mixed_terms))


def return_partials(partials, tile_size):
    sides = jnp.concatenate((partials[:, :, :tile_size], partials[:, :, 2 * tile_size :]), axis=2)
    arrived = padded(sides, (("wa", 2),), tile_size)
    from_left = arrived[:, :, :tile_size]
    from_right = arrived[:, :, 3 * tile_size :]
    upward = jnp.concatenate(
        (
            partials[:, :tile_size, tile_size : 2 * tile_size],
            from_left[:, :tile_size],
            from_right[:, :tile_size],
        ),
        axis=0,
    )
    downward = jnp.concatenate(
        (
            partials[:, 2 * tile_size :, tile_size : 2 * tile_size],
            from_left[:, 2 * tile_size :],
            from_right[:, 2 * tile_size :],
        ),
        axis=0,
    )
    vertical = jnp.concatenate((upward, downward), axis=1)
    arrived_rows = padded(vertical, (("ha", 1),), tile_size)
    count = partials.shape[0]
    above_rows = arrived_rows[:, :tile_size]
    below_rows = arrived_rows[:, 3 * tile_size :]
    from_above = (
        above_rows.astype(jnp.float32).reshape((3, count) + above_rows.shape[1:]).sum(axis=0)
    )
    from_below = (
        below_rows.astype(jnp.float32).reshape((3, count) + below_rows.shape[1:]).sum(axis=0)
    )
    summed = partials[:, tile_size : 2 * tile_size, tile_size : 2 * tile_size].astype(jnp.float32)
    summed = (
        summed
        + from_left[:, tile_size : 2 * tile_size].astype(jnp.float32)
        + from_right[:, tile_size : 2 * tile_size].astype(jnp.float32)
    )
    return summed + from_above + from_below


def shards(queries, tile_keys, values, probes, anchors, upstream):
    videos = queries.shape[0]
    tile_size = queries.shape[2]
    tokens = tile_size * tile_size
    feature_width = queries.shape[-1]
    score_scale = HEAD_DIM ** (-0.5)
    head_block = 4
    starts = list(range(0, HEADS, head_block))
    query_heads = queries[:, 0].reshape(videos, tokens, HEADS, HEAD_DIM).transpose(0, 2, 1, 3)
    stacked = jnp.concatenate((tile_keys[:, 0], values[:, 0]), axis=0)
    nearby = padded(stacked, (("ha", 1), ("wa", 2)), tile_size)
    near_heads = nearby.reshape(2 * videos, 9 * tokens, HEADS, HEAD_DIM).transpose(0, 2, 1, 3)
    key_heads = near_heads[:videos]
    value_heads = near_heads[videos:]
    valid_keys = region_valid(tile_size).reshape(-1)
    mixed_blocks = []
    weight_blocks = []
    low_blocks = []
    for block_start in starts:
        block_end = block_start + head_block
        mixed_block, weights, weights_low = attend_forward(
            query_heads[:, block_start:block_end],
            key_heads[:, block_start:block_end],
            value_heads[:, block_start:block_end],
            valid_keys,
            score_scale,
        )
        mixed_blocks.append(mixed_block)
        weight_blocks.append(weights)
        low_blocks.append(weights_low)
    mixed_heads = jnp.concatenate(mixed_blocks, axis=1)
    mixed_grid = mixed_heads.transpose(0, 2, 1, 3).reshape(
        videos, 1, tile_size, tile_size, feature_width
    )
    arrived = (
        lax.all_to_all(probes, "tm", split_axis=4, concat_axis=1, tiled=True),
        lax.all_to_all(anchors, "tm", split_axis=4, concat_axis=1, tiled=True),
        lax.all_to_all(mixed_grid, "tm", split_axis=4, concat_axis=1, tiled=True),
        lax.all_to_all(upstream, "tm", split_axis=4, concat_axis=1, tiled=True),
    )
    probe_part, anchor_terms, mixed_terms = temporal_grads(
        arrived[0], arrived[1], arrived[2], arrived[3], score_scale
    )
    returned = (
        lax.all_to_all(probe_part, "tm", split_axis=1, concat_axis=4, tiled=True),
        lax.all_to_all(
            anchor_terms.astype(jnp.bfloat16), "tm", split_axis=1, concat_axis=4, tiled=True
        ),
        lax.all_to_all(
            mixed_terms.astype(jnp.bfloat16), "tm", split_axis=1, concat_axis=4, tiled=True
        ),
    )
    probe_out = returned[0]
    anchor_out = returned[1]
    mixed_grad = returned[2]
    grad_heads = mixed_grad[:, 0].reshape(videos, tokens, HEADS, HEAD_DIM).transpose(0, 2, 1, 3)
    query_blocks = []
    key_blocks = []
    value_blocks = []
    for block_number, block_start in enumerate(starts):
        block_end = block_start + head_block
        query_block, key_block, value_block = attend_backward(
            query_heads[:, block_start:block_end],
            key_heads[:, block_start:block_end],
            value_heads[:, block_start:block_end],
            weight_blocks[block_number],
            low_blocks[block_number],
            grad_heads[:, block_start:block_end],
            mixed_heads[:, block_start:block_end],
            score_scale,
        )
        query_blocks.append(query_block)
        key_blocks.append(key_block)
        value_blocks.append(value_block)
    term_heads = jnp.concatenate(
        (jnp.concatenate(key_blocks, axis=1), jnp.concatenate(value_blocks, axis=1)), axis=0
    )
    partials = term_heads.transpose(0, 2, 1, 3).reshape(
        2 * videos, 3 * tile_size, 3 * tile_size, feature_width
    )
    summed = return_partials(partials, tile_size)
    key_grad = summed[:videos].astype(jnp.bfloat16)
    value_grad = summed[videos:].astype(jnp.bfloat16)
    query_grad = (
        jnp.concatenate(query_blocks, axis=1)
        .transpose(0, 2, 1, 3)
        .reshape(videos, 1, tile_size, tile_size, feature_width)
    )
    return (query_grad, key_grad[:, None], value_grad[:, None], probe_out, anchor_out)


def solution(mesh):
    return jax.shard_map(
        shards,
        mesh=mesh,
        in_specs=(
            P(None, "tm", "ha", "wa", None),
            P(None, "tm", "ha", "wa", None),
            P(None, "tm", "ha", "wa", None),
            P(None, "tm", "ha", "wa", None),
            P(None, "tm", "ha", "wa", None),
            P(None, "tm", "ha", "wa", None),
        ),
        out_specs=(
            P(None, "tm", "ha", "wa", None),
            P(None, "tm", "ha", "wa", None),
            P(None, "tm", "ha", "wa", None),
            P(None, "tm", "ha", "wa", None),
            P(None, "tm", "ha", "wa", None),
        ),
        check_vma=False,
    )
```

profile of v0, /device:TPU:8, one launch (start us, length us, event | category | flops | bytes accessed | tf_op | source)
XLA Modules:
  0.0 695.8 jit_solution(9721131183915048291)
XLA Ops:
  8.2 32.1 %collective-permute-done.1 = bf16[2,16,16,1536]{3,2,1,0:T(8,128)(2,1)S(1)} collective-permute-done((bf16[2,16,16,1536]{3,2,1,0:T(8,128)(2,1)S(1)}, bf16[2,16,16,1536]{3,2,1,0:T(8,128)(2,1)S(1)}, u32[]{:S(2)}, u32[]{:S(2)}) %collective-permute-start.1) | collective-permute-done | bytes 1572896 | tf_op jit(solution)/shard_map/ppermute | solution.py:23
  46.0 5.8 collective-permute-start.3
  53.8 6.5 copy.82
  60.3 8.6 %reshape.431 = bf16[4,2,49152]{2,1,0:T(2,128)(2,1)} reshape(bf16[1536,1,1,16,16]{4,3,2,1,0:T(8,128)(2,1)} %bitcast.314) | data formatting | bytes 1572864
  72.7 6.5 copy.84
  79.2 8.5 %reshape.429 = bf16[4,2,49152]{2,1,0:T(2,128)(2,1)} reshape(bf16[1536,1,1,16,16]{4,3,2,1,0:T(8,128)(2,1)} %bitcast.315) | data formatting | bytes 1572864
  87.7 75.6 %all-to-all-done = bf16[4,2,49152]{2,1,0:T(2,128)(2,1)S(1)} async-done(((bf16[4,2,49152]{2,1,0:T(2,128)(2,1)}), bf16[4,2,49152]{2,1,0:T(2,128)(2,1)S(1)}, u32[]{:S(2)}, u32[]{:S(2)}) %all-to-all-start) | async-done | bytes 786464 | tf_op jit(solution)/shard_map/all_to_all | solution.py:203
  166.9 7.6 %copy.88 = bf16[1,1,16,16,1536]{3,2,1,0,4:T(8,128)(2,1)} copy(bf16[1,1,16,16,1536]{4,3,2,1,0:T(8,128)(2,1)} %param.11) | data formatting | bytes 1572864 | tf_op args[5]
  174.5 8.5 %reshape.427 = bf16[4,2,49152]{2,1,0:T(2,128)(2,1)} reshape(bf16[1536,1,1,16,16]{4,3,2,1,0:T(8,128)(2,1)} %bitcast.316) | data formatting | bytes 1572864
  187.9 5.7 reshape.432
  193.6 6.8 copy.83
  201.6 5.7 reshape.430
  207.3 6.8 copy.85
  215.2 6.6 reshape.428
  221.9 6.8 copy.89
  250.7 8.3 %all-to-all-done.3 = bf16[1,4,16,16,384]{4,3,2,0,1:T(8,128)(2,1)} async-done(((bf16[1,4,16,16,384]{4,3,2,0,1:T(8,128)(2,1)}), bf16[1,4,16,16,384]{4,3,2,0,1:T(8,128)(2,1)}, u32[]{:S(2)}, u32[]{:S(2)}) %all-to-all-start.3) | async-done | bytes 786464 | tf_op jit(solution)/shard_map/all_to_all | solution.py:216
  266.3 12.5 %pad_maximum_fusion = bf16[2,48,48,1536]{3,2,1,0:T(8,128)(2,1)} fusion(bf16[2,48,16,1536]{3,2,1,0:T(8,128)(2,1)} %collective-permute-done.3, bf16[2,16,16,1536]{3,2,1,0:T(8,128)(2,1)S(1)} %collective-permute-done.1, bf16[1,16,16,1536]{3,2,1,0:T(8,128)(2,1)S(1)} %bitcast.326, bf16[1,16,16,1536]{3,2,1,0:T(8,128)(2,1)S(1)} %bitcast.329, ...), kind=kLoop, calls=%fused_computation.1 | loop fusion | flops 84934656 | bytes 28311552 | tf_op jit(solution)/shard_map/concatenate | solution.py:19
  278.9 26.1 %reshape.397 = bf16[2,2304,12,128]{3,2,1,0:T(8,128)(2,1)} reshape(bf16[2,48,48,1536]{3,2,1,0:T(8,128)(2,1)} %pad_maximum_fusion) | data formatting | bytes 28311552 | tf_op jit(solution)/shard_map/reshape | solution.py:179
  305.0 11.1 %copy.171 = bf16[2,2304,12,128]{3,1,2,0:T(8,128)(2,1)S(1)} copy(bf16[2,2304,12,128]{3,2,1,0:T(8,128)(2,1)} %reshape.397) | data formatting | bytes 28311552 | tf_op jit(solution)/shard_map/reshape | solution.py:179
  352.7 8.6 %multiply_convert_fusion = bf16[4,256,2304]{1,2,0:T(8,128)(2,1)} fusion(f32[4,2304,256]{2,1,0:T(8,128)} %copy-done, f32[4,256]{1,0:T(4,128)S(1)} %get-tuple-element.7, f32[4,256]{1,0:T(4,128)S(1)} %log_add_fusion, bf16[2,12,2304,128]{3,2,1,0:T(8,128)(2,1)} %bitcast.303, bf16[1,12,256,128]{3,2,1,0:T(8,128)(2,1)} %bitcast.318), kind=kOutput, calls=%fused_computation.24 | convolution fusion | flops 613416960 | bytes 16785408 | tf_op jit(solution)/shard_map/bhqd,bhkd->bhqk/dot_general | solution.py:66
  383.5 6.0 maximum_bitcast_fusion
  389.5 41.7 %copy.111 = bf16[2,2304,12,128]{3,2,1,0:T(8,128)(2,1)} copy(bf16[2,2304,12,128]{3,1,2,0:T(8,128)(2,1)S(1)} %maximum_bitcast_fusion) | data formatting | bytes 28311552 | tf_op jit(solution)/shard_map/transpose | solution.py:245
  431.1 26.1 %reshape.414 = bf16[2,48,48,1536]{3,2,1,0:T(8,128)(2,1)} reshape(bf16[2,2304,12,128]{3,2,1,0:T(8,128)(2,1)} %copy.111) | data formatting | bytes 28311552 | tf_op jit(solution)/shard_map/reshape | solution.py:245
  463.8 8.3 %collective-permute-start.5 = (bf16[2,48,16,1536]{3,2,1,0:T(8,128)(2,1)S(1)}, bf16[2,48,16,1536]{3,2,1,0:T(8,128)(2,1)S(1)}, u32[]{:S(2)}, u32[]{:S(2)}) collective-permute-start(bf16[2,48,16,1536]{3,2,1,0:T(8,128)(2,1)S(1)} %get-tuple-element.11), channel_id=1, source_target_pairs={{1,0},{2,1},{3,2},{4,3},{5,4},{6,5},{7,6},{9,8},{10,9},{11,10},{12... | collective-permute-start | bytes 14155784 | tf_op jit(solution)/shard_map/ppermute | solution.py:23
  474.2 97.6 %collective-permute-done.4 = bf16[2,48,16,1536]{3,2,1,0:T(8,128)(2,1)S(1)} collective-permute-done((bf16[2,48,16,1536]{3,2,1,0:T(8,128)(2,1)S(1)}, bf16[2,48,16,1536]{3,2,1,0:T(8,128)(2,1)S(1)}, u32[]{:S(2)}, u32[]{:S(2)}) %collective-permute-start.4) | collective-permute-done | bytes 4718624 | tf_op jit(solution)/shard_map/ppermute | solution.py:21
  581.1 7.5 %collective-permute-start.6 = (bf16[6,16,16,1536]{3,2,1,0:T(8,128)(2,1)}, bf16[6,16,16,1536]{3,2,1,0:T(8,128)(2,1)}, u32[]{:S(2)}, u32[]{:S(2)}) collective-permute-start(bf16[6,16,16,1536]{3,2,1,0:T(8,128)(2,1)} %pad_maximum_fusion.2), channel_id=1, source_target_pairs={{0,8},{8,16},{16,24},{1,9},{9,17},{17,25},{2,10},{10,18},{18,26},{... | collective-permute-start | bytes 14155784 | tf_op jit(solution)/shard_map/ppermute | solution.py:21
  589.1 5.9 reshape.426
  594.9 8.5 %reshape.433 = bf16[4,2,49152]{2,1,0:T(2,128)(2,1)} reshape(bf16[1536,1,1,16,16]{4,3,2,1,0:T(8,128)(2,1)} %bitcast.312) | data formatting | bytes 1572864
  612.5 7.6 %all-to-all-done.4 = bf16[4,2,49152]{2,1,0:T(2,128)(2,1)S(1)} async-done(((bf16[4,2,49152]{2,1,0:T(2,128)(2,1)}), bf16[4,2,49152]{2,1,0:T(2,128)(2,1)S(1)}, u32[]{:S(2)}, u32[]{:S(2)}) %all-to-all-start.4) | async-done | bytes 786464 | tf_op jit(solution)/shard_map/all_to_all | solution.py:205
  620.1 5.6 reshape.434
  625.7 7.0 %copy.114 = bf16[1,1,16,16,4,384]{5,3,2,4,1,0:T(8,128)(2,1)S(1)} copy(bf16[1,1,16,16,4,384]{3,2,5,4,1,0:T(8,128)(2,1)} %bitcast.313) | data formatting | bytes 1572864 | tf_op jit(solution)/shard_map/all_to_all | solution.py:205
  676.9 6.2 collective-permute-done.7
  (139 shorter events, 201.7 us)
Async XLA Ops:
  2.2 51.6 %copy-start.21 = (bf16[1,1,16,16,1536]{4,3,2,1,0:T(8,128)(2,1)S(1)}, bf16[1,1,16,16,1536]{4,3,2,1,0:T(8,128)(2,1)}, u32[]{:S(2)}) copy-start(bf16[1,1,16,16,1536]{4,3,2,1,0:T(8,128)(2,1)} %param.9) | copy-start | bytes 2359300
  2.2 38.2 %collective-permute-start.1 = (bf16[2,16,16,1536]{3,2,1,0:T(8,128)(2,1)S(1)}, bf16[2,16,16,1536]{3,2,1,0:T(8,128)(2,1)S(1)}, u32[]{:S(2)}, u32[]{:S(2)}) collective-permute-start(bf16[2,16,16,1536]{3,2,1,0:T(8,128)(2,1)S(1)} %pad_maximum_fusion.4), channel_id=1, source_target_pairs={{8,0},{16,8},{24,16},{9,1},{17,9},{25,17},{10,2},{18,10},{26,18},{... | collective-permute-start | bytes 4718600 | tf_op jit(solution)/shard_map/ppermute | solution.py:23
  3.6 37.9 %collective-permute-start = (bf16[2,16,16,1536]{3,2,1,0:T(8,128)(2,1)S(1)}, bf16[2,16,16,1536]{3,2,1,0:T(8,128)(2,1)S(1)}, u32[]{:S(2)}, u32[]{:S(2)}) collective-permute-start(bf16[2,16,16,1536]{3,2,1,0:T(8,128)(2,1)S(1)} %pad_maximum_fusion.4), channel_id=1, source_target_pairs={{0,8},{8,16},{16,24},{1,9},{9,17},{17,25},{2,10},{10,18},{18,26},{... | collective-permute-start | bytes 4718600 | tf_op jit(solution)/shard_map/ppermute | solution.py:21
  41.5 4.5 copy-start.9
  46.0 220.3 %collective-permute-start.3 = (bf16[2,48,16,1536]{3,2,1,0:T(8,128)(2,1)}, bf16[2,48,16,1536]{3,2,1,0:T(8,128)(2,1)}, u32[]{:S(2)}, u32[]{:S(2)}) collective-permute-start(bf16[2,48,16,1536]{3,2,1,0:T(8,128)(2,1)} %pad_maximum_fusion.1), channel_id=1, source_target_pairs={{1,0},{2,1},{3,2},{4,3},{5,4},{6,5},{7,6},{9,8},{10,9},{11,10},{12... | collective-permute-start | bytes 14155784 | tf_op jit(solution)/shard_map/ppermute | solution.py:23
  51.8 214.5 %collective-permute-start.2 = (bf16[2,48,16,1536]{3,2,1,0:T(8,128)(2,1)}, bf16[2,48,16,1536]{3,2,1,0:T(8,128)(2,1)}, u32[]{:S(2)}, u32[]{:S(2)}) collective-permute-start(bf16[2,48,16,1536]{3,2,1,0:T(8,128)(2,1)} %pad_maximum_fusion.1), channel_id=1, source_target_pairs={{0,1},{1,2},{2,3},{3,4},{4,5},{5,6},{6,7},{8,9},{9,10},{10,11},{11... | collective-permute-start | bytes 14155784 | tf_op jit(solution)/shard_map/ppermute | solution.py:21
  60.3 12.4 %copy-start.22 = (bf16[1,1,16,16,1536]{4,3,2,1,0:T(8,128)(2,1)S(1)}, bf16[1,1,16,16,1536]{4,3,2,1,0:T(8,128)(2,1)}, u32[]{:S(2)}) copy-start(bf16[1,1,16,16,1536]{4,3,2,1,0:T(8,128)(2,1)} %param.10) | copy-start | bytes 2359300
  68.9 94.5 %all-to-all-start = ((bf16[4,2,49152]{2,1,0:T(2,128)(2,1)}), bf16[4,2,49152]{2,1,0:T(2,128)(2,1)S(1)}, u32[]{:S(2)}, u32[]{:S(2)}) async-start(bf16[4,2,49152]{2,1,0:T(2,128)(2,1)} %reshape.431), calls=%async_computation | async-start | bytes 1572864 | tf_op jit(solution)/shard_map/all_to_all | solution.py:203
  163.4 19.6 %all-to-all-start.1 = ((bf16[4,2,49152]{2,1,0:T(2,128)(2,1)}), bf16[4,2,49152]{2,1,0:T(2,128)(2,1)S(1)}, u32[]{:S(2)}, u32[]{:S(2)}) async-start(bf16[4,2,49152]{2,1,0:T(2,128)(2,1)} %reshape.429), calls=%async_computation.1 | async-start | bytes 1572864 | tf_op jit(solution)/shard_map/all_to_all | solution.py:204
  183.0 32.2 %all-to-all-start.2 = ((bf16[4,2,49152]{2,1,0:T(2,128)(2,1)}), bf16[4,2,49152]{2,1,0:T(2,128)(2,1)}, u32[]{:S(2)}, u32[]{:S(2)}) async-start(bf16[4,2,49152]{2,1,0:T(2,128)(2,1)} %reshape.427), calls=%async_computation.2 | async-start | bytes 1572864 | tf_op jit(solution)/shard_map/all_to_all | solution.py:206
  240.9 18.1 %all-to-all-start.3 = ((bf16[1,4,16,16,384]{4,3,2,0,1:T(8,128)(2,1)}), bf16[1,4,16,16,384]{4,3,2,0,1:T(8,128)(2,1)}, u32[]{:S(2)}, u32[]{:S(2)}) async-start(bf16[1,4,16,16,384]{4,3,2,0,1:T(8,128)(2,1)} %bitcast.334), calls=%async_computation.3 | async-start | bytes 1572864 | tf_op jit(solution)/shard_map/all_to_all | solution.py:216
  245.7 20.6 %copy-start.7 = (bf16[1,1,16,16,1536]{4,3,2,1,0:T(8,128)(2,1)S(1)}, bf16[1,1,16,16,1536]{4,3,2,1,0:T(8,128)(2,1)}, u32[]{:S(2)}) copy-start(bf16[1,1,16,16,1536]{4,3,2,1,0:T(8,128)(2,1)} %param.8) | copy-start | bytes 2359300
  245.7 20.6 %copy-start.8 = (bf16[1,1,16,16,1536]{4,3,2,1,0:T(8,128)(2,1)S(1)}, bf16[1,1,16,16,1536]{4,3,2,1,0:T(8,128)(2,1)}, u32[]{:S(2)}) copy-start(bf16[1,1,16,16,1536]{4,3,2,1,0:T(8,128)(2,1)} %param.7) | copy-start | bytes 2359300
  305.0 11.2 %copy-start.23 = (bf16[1,256,12,128]{3,1,2,0:T(8,128)(2,1)S(1)}, bf16[1,256,12,128]{3,1,2,0:T(8,128)(2,1)}, u32[]{:S(2)}) copy-start(bf16[1,256,12,128]{3,1,2,0:T(8,128)(2,1)} %copy.173) | copy-start | bytes 2359300
  316.1 5.1 copy-start.1
  321.2 7.0 %copy-start = (f32[4,2304,256]{2,1,0:T(8,128)}, f32[4,2304,256]{2,1,0:T(8,128)S(1)}, u32[]{:S(2)}) copy-start(f32[4,2304,256]{2,1,0:T(8,128)S(1)} %get-tuple-element.25) | copy-start | bytes 28311556
  352.7 8.6 %copy-start.6 = (bf16[1,256,12,128]{3,1,2,0:T(8,128)(2,1)S(1)}, bf16[1,256,12,128]{3,1,2,0:T(8,128)(2,1)}, u32[]{:S(2)}) copy-start(bf16[1,256,12,128]{3,1,2,0:T(8,128)(2,1)} %copy.172) | copy-start | bytes 2359300
  378.6 10.9 %copy-start.12 = (bf16[4,256,2304]{1,2,0:T(8,128)(2,1)}, bf16[4,256,2304]{1,2,0:T(8,128)(2,1)S(1)}, u32[]{:S(2)}) copy-start(bf16[4,256,2304]{1,2,0:T(8,128)(2,1)S(1)} %multiply_convert_fusion.2) | copy-start | bytes 14155780
  378.6 4.8 copy-start.4
  461.8 109.9 %collective-permute-start.4 = (bf16[2,48,16,1536]{3,2,1,0:T(8,128)(2,1)S(1)}, bf16[2,48,16,1536]{3,2,1,0:T(8,128)(2,1)S(1)}, u32[]{:S(2)}, u32[]{:S(2)}) collective-permute-start(bf16[2,48,16,1536]{3,2,1,0:T(8,128)(2,1)S(1)} %get-tuple-element.10), channel_id=1, source_target_pairs={{0,1},{1,2},{2,3},{3,4},{4,5},{5,6},{6,7},{8,9},{9,10},{10,11},{11... | collective-permute-start | bytes 14155784 | tf_op jit(solution)/shard_map/ppermute | solution.py:21
  463.8 110.1 %collective-permute-start.5 = (bf16[2,48,16,1536]{3,2,1,0:T(8,128)(2,1)S(1)}, bf16[2,48,16,1536]{3,2,1,0:T(8,128)(2,1)S(1)}, u32[]{:S(2)}, u32[]{:S(2)}) collective-permute-start(bf16[2,48,16,1536]{3,2,1,0:T(8,128)(2,1)S(1)} %get-tuple-element.11), channel_id=1, source_target_pairs={{1,0},{2,1},{3,2},{4,3},{5,4},{6,5},{7,6},{9,8},{10,9},{11,10},{12... | collective-permute-start | bytes 14155784 | tf_op jit(solution)/shard_map/ppermute | solution.py:23
  577.4 105.7 %collective-permute-start.7 = (bf16[6,16,16,1536]{3,2,1,0:T(8,128)(2,1)}, bf16[6,16,16,1536]{3,2,1,0:T(8,128)(2,1)}, u32[]{:S(2)}, u32[]{:S(2)}) collective-permute-start(bf16[6,16,16,1536]{3,2,1,0:T(8,128)(2,1)} %pad_maximum_fusion.3), channel_id=1, source_target_pairs={{8,0},{16,8},{24,16},{9,1},{17,9},{25,17},{10,2},{18,10},{26,18},{... | collective-permute-start | bytes 14155784 | tf_op jit(solution)/shard_map/ppermute | solution.py:23
  578.7 10.0 %copy-start.14 = (bf16[1,4,256,128]{3,2,1,0:T(8,128)(2,1)S(1)}, bf16[1,4,256,128]{3,2,1,0:T(8,128)(2,1)}, u32[]{:S(2)}) copy-start(bf16[1,4,256,128]{3,2,1,0:T(8,128)(2,1)} %fusion.63) | copy-start | bytes 786436
  578.7 9.9 %copy-start.20 = (bf16[1,4,256,128]{3,2,1,0:T(8,128)(2,1)S(1)}, bf16[1,4,256,128]{3,2,1,0:T(8,128)(2,1)}, u32[]{:S(2)}) copy-start(bf16[1,4,256,128]{3,2,1,0:T(8,128)(2,1)} %get-tuple-element.26) | copy-start | bytes 786436
  581.1 105.7 %collective-permute-start.6 = (bf16[6,16,16,1536]{3,2,1,0:T(8,128)(2,1)}, bf16[6,16,16,1536]{3,2,1,0:T(8,128)(2,1)}, u32[]{:S(2)}, u32[]{:S(2)}) collective-permute-start(bf16[6,16,16,1536]{3,2,1,0:T(8,128)(2,1)} %pad_maximum_fusion.2), channel_id=1, source_target_pairs={{0,8},{8,16},{16,24},{1,9},{9,17},{17,25},{2,10},{10,18},{18,26},{... | collective-permute-start | bytes 14155784 | tf_op jit(solution)/shard_map/ppermute | solution.py:21
  603.4 16.6 %all-to-all-start.4 = ((bf16[4,2,49152]{2,1,0:T(2,128)(2,1)}), bf16[4,2,49152]{2,1,0:T(2,128)(2,1)S(1)}, u32[]{:S(2)}, u32[]{:S(2)}) async-start(bf16[4,2,49152]{2,1,0:T(2,128)(2,1)} %reshape.433), calls=%async_computation.4 | async-start | bytes 1572864 | tf_op jit(solution)/shard_map/all_to_all | solution.py:205
  625.7 8.1 %copy-start.16 = (f32[16,16,3,4,4]{3,4,2,1,0:T(4,128)S(1)}, f32[16,16,3,4,4]{3,4,2,1,0:T(4,128)}, u32[]{:S(2)}) copy-start(f32[16,16,3,4,4]{3,4,2,1,0:T(4,128)} %copy-done.15) | copy-start | bytes 147460
  625.7 8.1 %copy-start.19 = (bf16[4,16,16,3,128]{4,3,2,1,0:T(4,128)(2,1)S(1)}, bf16[4,16,16,3,128]{4,3,2,1,0:T(4,128)(2,1)}, u32[]{:S(2)}) copy-start(bf16[4,16,16,3,128]{4,3,2,1,0:T(4,128)(2,1)} %reshape.402) | copy-start | bytes 2359300
  642.2 8.6 %copy-start.17 = (bf16[4,16,16,3,128]{4,3,2,1,0:T(4,128)(2,1)S(1)}, bf16[4,16,16,3,128]{4,3,2,1,0:T(4,128)(2,1)}, u32[]{:S(2)}) copy-start(bf16[4,16,16,3,128]{4,3,2,1,0:T(4,128)(2,1)} %reshape.400) | copy-start | bytes 2359300
  642.2 16.9 %all-to-all-start.5 = ((bf16[1,4,16,16,384]{4,3,2,0,1:T(8,128)(2,1)}), bf16[1,4,16,16,384]{4,3,2,0,1:T(8,128)(2,1)S(1)}, u32[]{:S(2)}, u32[]{:S(2)}) async-start(bf16[1,4,16,16,384]{4,3,2,0,1:T(8,128)(2,1)} %bitcast.57), calls=%async_computation.5 | async-start | bytes 1572864 | tf_op jit(solution)/shard_map/all_to_all | solution.py:212
  659.1 8.5 %copy-start.25 = (bf16[1,4,256,128]{3,2,1,0:T(8,128)(2,1)S(1)}, bf16[1,4,256,128]{3,2,1,0:T(8,128)(2,1)}, u32[]{:S(2)}) copy-start(bf16[1,4,256,128]{3,2,1,0:T(8,128)(2,1)} %fusion.58) | copy-start | bytes 786436
  659.1 16.8 %all-to-all-start.6 = ((bf16[1,4,16,16,384]{4,3,2,0,1:T(8,128)(2,1)}), bf16[1,4,16,16,384]{4,3,2,0,1:T(8,128)(2,1)S(1)}, u32[]{:S(2)}, u32[]{:S(2)}) async-start(bf16[1,4,16,16,384]{4,3,2,0,1:T(8,128)(2,1)} %bitcast.63), calls=%async_computation.6 | async-start | bytes 1572864 | tf_op jit(solution)/shard_map/all_to_all | solution.py:213
  (9 other events, 27.7 us)
where the time goes:
time: 709 us; the launch traced here: 696 us
  local copies, waits for them, and re-layouts  262 us (37%)
  waiting for transfers between devices  239 us (34%)
  matrix products  87.1 us (12%)
  starting transfers between devices  60.8 us (9%)
  other arithmetic  45.8 us (6%)
    ppermute x4, waiting for transfers between devices, padded(): lax.ppermute(tail, axis, [(i, (i + 1) % count) for i in range(ends)])  98.7 us
    unnamed x63, local copies, waits for them, and re-layouts  88.2 us
    all_to_all x1, waiting for transfers between devices, shards(): lax.all_to_all(probes, 'tm', split_axis=4, concat_axis=1, tiled=True)  75.6 us
    transpose x1, local copies, waits for them, and re-layouts, shards(): term_heads.transpose(0, 2, 1, 3)  41.7 us
    ppermute x4, waiting for transfers between devices, padded(): lax.ppermute(head, axis, [((i + 1) % count, i) for i in range(ends)])  38.3 us
    reshape x2, local copies, waits for them, and re-layouts, shards(): nearby.reshape(2 * videos, 9 * tokens, HEADS, HEAD_DIM)  37.2 us
    reshape x1, local copies, waits for them, and re-layouts, shards(): term_heads.transpose(0, 2, 1, 3)  26.1 us
    dot_general x3, matrix products, attend_backward(): jnp.einsum('bhqd,bhkd->bhqk', grad_heads, value_heads, preferred_element_...  18.1 us
  transfers between devices with their start and end apart: 15, of which 9 were waited for; matrix products, arithmetic and copies ran while one was open for 26% of the time, Pallas kernels for 0%

commit v1 on v0

v1 whole, which is shorter than its diff:
```python
import functools

import jax
import jax.numpy as jnp
from jax import lax
from jax.experimental import pallas as pl
from jax.experimental.pallas import tpu as pltpu
from jax.sharding import PartitionSpec as P

HEADS = 12
HEAD_DIM = 128
PARTS = 4
GROUP = HEADS // PARTS
ROWS = 4
BIG = 1e30
SCALE = HEAD_DIM ** (-0.5)
LOG2E = 1.4426950408889634
BASE2 = SCALE * LOG2E

NT = (((1,), (1,)), ((), ()))
NN = (((1,), (0,)), ((), ()))
TN = (((0,), (0,)), ((), ()))


def dot(a, b, dims):
    return lax.dot_general(a, b, dims, preferred_element_type=jnp.float32)


def params():
    return pltpu.CompilerParams(vmem_limit_bytes=56 * 1024 * 1024)


def cost(flops, bytes_accessed, transcendentals=0):
    return pl.CostEstimate(
        flops=flops, bytes_accessed=bytes_accessed, transcendentals=transcendentals
    )


def pack(arrays):
    count = len(arrays)
    tokens = arrays[0].shape[0]

    def kernel(*refs):
        out = refs[-1]
        for a in range(count):
            for h in range(GROUP):
                out[0, h, a] = refs[a][:, h * HEAD_DIM : (h + 1) * HEAD_DIM]

    total = count * tokens * HEADS * HEAD_DIM
    return pl.pallas_call(
        kernel,
        grid=(PARTS,),
        in_specs=[pl.BlockSpec((tokens, GROUP * HEAD_DIM), lambda i: (0, i))] * count,
        out_specs=pl.BlockSpec((1, GROUP, count, tokens, HEAD_DIM), lambda i: (i, 0, 0, 0, 0)),
        out_shape=jax.ShapeDtypeStruct(
            (PARTS, GROUP, count, tokens, HEAD_DIM), arrays[0].dtype
        ),
        cost_estimate=cost(0, 4 * total),
        compiler_params=params(),
    )(*arrays)


def unpack(block):
    count, tokens = block.shape[2:4]

    def kernel(block_ref, *outs):
        for a in range(count):
            for h in range(GROUP):
                outs[a][:, h * HEAD_DIM : (h + 1) * HEAD_DIM] = block_ref[0, h, a]

    total = count * tokens * HEADS * HEAD_DIM
    return pl.pallas_call(
        kernel,
        grid=(PARTS,),
        in_specs=[
            pl.BlockSpec((1, GROUP, count, tokens, HEAD_DIM), lambda i: (i, 0, 0, 0, 0))
        ],
        out_specs=[pl.BlockSpec((tokens, GROUP * HEAD_DIM), lambda i: (0, i))] * count,
        out_shape=[jax.ShapeDtypeStruct((tokens, HEADS * HEAD_DIM), block.dtype)] * count,
        cost_estimate=cost(0, 4 * total),
        compiler_params=params(),
    )(block)


def near_rows(row):
    return range(max(row - 1, 0), min(row + 2, ROWS))


def forward_kernel(bad_ref, q_ref, kl_ref, kc_ref, kr_ref, o_ref, lse_ref):
    bads = (bad_ref[0], jnp.float32(0.0), bad_ref[1])
    sides = (kl_ref, kc_ref, kr_ref)
    for b in range(ROWS):
        query = q_ref[b, 0, 0]
        scores = []
        for side in range(3):
            for u in near_rows(b):
                scores.append((side, u, dot(sides[side][u, 0, 0], query, NT)))
        top = None
        for side in range(3):
            local = None
            for at, _, s in scores:
                if at == side:
                    one = jnp.max(s, axis=0, keepdims=True)
                    local = one if local is None else jnp.maximum(local, one)
            local = local - bads[side]
            top = local if top is None else jnp.maximum(top, local)
        top = top * BASE2
        total = None
        mixed = None
        for side, u, s in scores:
            p = jnp.exp2(s * BASE2 - (top + bads[side]))
            one = jnp.sum(p, axis=0, keepdims=True)
            total = one if total is None else total + one
            term = dot(sides[side][u, 0, 1], p.astype(jnp.bfloat16), TN)
            mixed = term if mixed is None else mixed + term
        mixed = mixed * (1.0 / total)
        o_ref[b, 0, 0] = mixed.T.astype(jnp.bfloat16)
        lse_ref[0, b] = top + jnp.log2(total)


def column_spec(count, tokens):
    return pl.BlockSpec((ROWS, 1, count, tokens, HEAD_DIM), lambda h: (0, h, 0, 0, 0))


def attend_forward(bad, q, kv_left, kv, kv_right):
    tokens = q.shape[3]
    group = q.shape[1]
    pairs = 3 * 10 * group
    return pl.pallas_call(
        forward_kernel,
        grid=(group,),
        in_specs=[pl.BlockSpec(memory_space=pltpu.SMEM), column_spec(1, tokens)]
        + [column_spec(2, tokens)] * 3,
        out_specs=[
            column_spec(1, tokens),
            pl.BlockSpec((1, ROWS, 1, tokens), lambda h: (h, 0, 0, 0)),
        ],
        out_shape=[
            jax.ShapeDtypeStruct(q.shape, jnp.bfloat16),
            jax.ShapeDtypeStruct((group, ROWS, 1, tokens), jnp.float32),
        ],
        cost_estimate=cost(
            4 * pairs * tokens * tokens * HEAD_DIM, 8 * q.size * 2, pairs * tokens * tokens
        ),
        compiler_params=params(),
    )(bad, q, kv_left, kv, kv_right)


def backward_kernel(
    bad_ref,
    q_ref,
    kl_ref,
    kc_ref,
    kr_ref,
    do_ref,
    o_ref,
    lse_ref,
    dq_ref,
    dl_ref,
    dc_ref,
    dr_ref,
    dqt_ref,
    row_ref,
):
    bads = (bad_ref[0], jnp.float32(0.0), bad_ref[1])
    sides = (kl_ref, kc_ref, kr_ref)
    outs = (dl_ref, dc_ref, dr_ref)
    for b in range(ROWS):
        product = do_ref[b, 0, 0].astype(jnp.float32) * o_ref[b, 0, 0].astype(jnp.float32)
        row_ref[b] = jnp.sum(product.T, axis=0, keepdims=True)
    seen = set()
    for side in (0, 2, 1):
        for u in range(ROWS):
            key = sides[side][u, 0, 0]
            value = sides[side][u, 0, 1]
            dk = None
            dv = None
            for b in near_rows(u):
                query = q_ref[b, 0, 0]
                grad = do_ref[b, 0, 0]
                s = dot(key, query, NT)
                p = jnp.exp2(s * BASE2 - (lse_ref[0, b] + bads[side]))
                e = dot(value, grad, NT)
                g = (p * (e - row_ref[b])).astype(jnp.bfloat16)
                tv = dot(p.astype(jnp.bfloat16), grad, NN)
                tk = dot(g, query, NN)
                tq = dot(key, g, TN)
                dv = tv if dv is None else dv + tv
                dk = tk if dk is None else dk + tk
                if b in seen:
                    dqt_ref[b] += tq
                else:
                    seen.add(b)
                    dqt_ref[b] = tq
            outs[side][u, 0, 0] = (dk * SCALE).astype(outs[side].dtype)
            outs[side][u, 0, 1] = dv.astype(outs[side].dtype)
    for b in range(ROWS):
        dq_ref[b, 0, 0] = (dqt_ref[b] * SCALE).T.astype(jnp.bfloat16)


def attend_backward(bad, q, kv_left, kv, kv_right, grad, mixed, lse):
    tokens = q.shape[3]
    group = q.shape[1]
    pairs = 3 * 10 * group
    return pl.pallas_call(
        backward_kernel,
        grid=(group,),
        in_specs=[pl.BlockSpec(memory_space=pltpu.SMEM), column_spec(1, tokens)]
        + [column_spec(2, tokens)] * 3
        + [column_spec(1, tokens)] * 2
        + [pl.BlockSpec((1, ROWS, 1, tokens), lambda h: (h, 0, 0, 0))],
        out_specs=[column_spec(1, tokens)] + [column_spec(2, tokens)] * 3,
        out_shape=[
            jax.ShapeDtypeStruct(q.shape, jnp.bfloat16),
            jax.ShapeDtypeStruct(kv.shape, jnp.bfloat16),
            jax.ShapeDtypeStruct(kv.shape, jnp.float32),
            jax.ShapeDtypeStruct(kv.shape, jnp.bfloat16),
        ],
        scratch_shapes=[
            pltpu.VMEM((ROWS, HEAD_DIM, tokens), jnp.float32),
            pltpu.VMEM((ROWS, 1, tokens), jnp.float32),
        ],
        cost_estimate=cost(
            10 * pairs * tokens * tokens * HEAD_DIM, 20 * q.size * 2, pairs * tokens * tokens
        ),
        compiler_params=params(),
    )(bad, q, kv_left, kv, kv_right, grad, mixed, lse)


def lane_dots(a, b, ones):
    product = a * b
    high = product.astype(jnp.bfloat16)
    low = (product - high.astype(jnp.float32)).astype(jnp.bfloat16)
    return dot(high, ones, NN) + dot(low, ones, NN)


def temporal_weights(probes, anchors, ones):
    weights = []
    for f in range(PARTS):
        scores = [lane_dots(probes[f], anchors[g], ones) * SCALE for g in range(PARTS)]
        top = functools.reduce(jnp.maximum, scores)
        shifted = [jnp.exp(s - top) for s in scores]
        inverse = 1.0 / functools.reduce(jnp.add, shifted)
        weights.append([s * inverse for s in shifted])
    return weights


def rounded(x):
    return x.astype(jnp.bfloat16).astype(jnp.float32)


def temporal_forward_kernel(pau_ref, out_ref):
    ones = jnp.ones((HEAD_DIM, HEAD_DIM), jnp.bfloat16)
    parts = [[pau_ref[f, 0, t].astype(jnp.float32) for f in range(PARTS)] for t in range(3)]
    weights = temporal_weights(parts[0], parts[1], ones)
    for g in range(PARTS):
        terms = [rounded(weights[f][g]) * parts[2][f] for f in range(PARTS)]
        out_ref[g, 0, 0] = functools.reduce(jnp.add, terms).astype(jnp.bfloat16)


def temporal_backward_kernel(pau_ref, mixed_ref, out_ref):
    ones = jnp.ones((HEAD_DIM, HEAD_DIM), jnp.bfloat16)
    parts = [[pau_ref[f, 0, t].astype(jnp.float32) for f in range(PARTS)] for t in range(3)]
    mixed = [mixed_ref[g, 0, 0].astype(jnp.float32) for g in range(PARTS)]
    weights = temporal_weights(parts[0], parts[1], ones)
    anchor_grads = [None] * PARTS
    for f in range(PARTS):
        grads = [lane_dots(parts[2][f], mixed[g], ones) for g in range(PARTS)]
        row = functools.reduce(jnp.add, [w * c for w, c in zip(weights[f], grads)])
        scores = [rounded(w * (c - row)) for w, c in zip(weights[f], grads)]
        probe = functools.reduce(jnp.add, [s * parts[1][g] for g, s in enumerate(scores)])
        out_ref[f, 0, 0] = (probe * SCALE).astype(jnp.bfloat16)
        for g in range(PARTS):
            term = scores[g] * parts[0][f]
            anchor_grads[g] = term if f == 0 else anchor_grads[g] + term
    for g in range(PARTS):
        out_ref[g, 0, 1] = (anchor_grads[g] * SCALE).astype(jnp.bfloat16)


def temporal_call(kernel, arrays, count_out):
    _, group, _, tokens, _ = arrays[0].shape
    rows = 64
    pairs = 16 * group * tokens

    def spec(count):
        return pl.BlockSpec(
            (PARTS, 1, count, rows, HEAD_DIM), lambda h, i: (0, h, 0, i, 0)
        )

    return pl.pallas_call(
        kernel,
        grid=(group, tokens // rows),
        in_specs=[spec(a.shape[2]) for a in arrays],
        out_specs=spec(count_out),
        out_shape=jax.ShapeDtypeStruct(
            (PARTS, group, count_out, tokens, HEAD_DIM), jnp.bfloat16
        ),
        cost_estimate=cost(
            pairs * 4 * HEAD_DIM * HEAD_DIM,
            2 * sum(a.size for a in arrays),
            pairs * HEAD_DIM,
        ),
        compiler_params=params(),
    )(*arrays)


def swap(x, axis):
    return lax.all_to_all(x, axis, split_axis=0, concat_axis=0, tiled=True)


def shift_right(x):
    count = lax.axis_size("wa")
    return lax.ppermute(x, "wa", [(i, i + 1) for i in range(count - 1)])


def shift_left(x):
    count = lax.axis_size("wa")
    return lax.ppermute(x, "wa", [(i + 1, i) for i in range(count - 1)])


def shards(queries, tile_keys, values, probes, anchors, upstream):
    shape = queries.shape
    tokens = shape[2] * shape[3]

    def flat(x):
        return x.reshape(tokens, shape[-1])

    place = lax.axis_index("wa")
    bad = jnp.stack([place == 0, place == lax.axis_size("wa") - 1]).astype(jnp.float32) * BIG

    kv = swap(pack([flat(tile_keys), flat(values)]), "ha")
    pau = swap(pack([flat(probes), flat(anchors), flat(upstream)]), "tm")
    q = swap(pack([flat(queries)]), "ha")
    kv_left = shift_right(kv)
    kv_right = shift_left(kv)
    grad = swap(swap(temporal_call(temporal_forward_kernel, [pau], 1), "tm"), "ha")
    mixed, lse = attend_forward(bad, q, kv_left, kv, kv_right)
    mixed_back = swap(swap(mixed, "ha"), "tm")
    dq, to_left, own, to_right = attend_backward(
        bad, q, kv_left, kv, kv_right, grad, mixed, lse
    )
    times = swap(temporal_call(temporal_backward_kernel, [pau, mixed_back], 2), "tm")
    query_grad = unpack(swap(dq, "ha"))[0]
    summed = (
        own
        + shift_right(to_right).astype(jnp.float32)
        + shift_left(to_left).astype(jnp.float32)
    ).astype(jnp.bfloat16)
    key_grad, value_grad = unpack(swap(summed, "ha"))
    probe_grad, anchor_grad = unpack(times)
    outs = (query_grad, key_grad, value_grad, probe_grad, anchor_grad)
    return tuple(x.reshape(shape) for x in outs)


def solution(mesh):
    spec = P(None, "tm", "ha", "wa", None)
    return jax.shard_map(
        shards,
        mesh=mesh,
        in_specs=(spec,) * 6,
        out_specs=(spec,) * 5,
        check_vma=False,
    )
```

time: 709 us -> 266 us (0.38); the launches traced: 696 us -> 264 us
  local copies, waits for them, and re-layouts: 262 us -> 4.46 us
  waiting for transfers between devices: 239 us -> 80.4 us
  matrix products: 87.1 us -> 0 us
  Pallas kernels: 0 us -> 84.3 us
  blocking collectives: 0 us -> 42.9 us
  other arithmetic: 45.8 us -> 4.82 us
  starting transfers between devices: 60.8 us -> 46.6 us
    ppermute x8 -> x4, waiting for transfers between devices: 137 us -> 14.1 us  [the longest x2 12.5 us: shift_right(): return lax.ppermute(x, 'wa', [(i, i + 1) for i in range(count - 1)])]
    pallas_call x0 -> x10, Pallas kernels: none -> 84.3 us  [the longest x1 27.3 us: attend_backward(): pl.pallas_call(backward_kernel, grid=(group,), in_specs=[pl.BlockSpec(mem...]
    unnamed x63 -> x16, local copies, waits for them, and re-layouts: 88.2 us -> 4.46 us
    dot_general x22 -> x0, matrix products: 81.8 us -> none  [the longest x3 18.1 us: attend_backward(): jnp.einsum('bhqd,bhkd->bhqk', grad_heads, value_heads, preferred_element_...]
    reshape x7 -> x0, local copies, waits for them, and re-layouts: 72.3 us -> none  [the longest x2 37.2 us: shards(): nearby.reshape(2 * videos, 9 * tokens, HEADS, HEAD_DIM)]
    all_to_all x0 -> x2, blocking collectives: none -> 42.9 us  [swap(): return lax.all_to_all(x, axis, split_axis=0, concat_axis=0, tiled=True)]
    transpose x2 -> x0, local copies, waits for them, and re-layouts: 42.2 us -> none  [the longest x1 41.7 us: shards(): term_heads.transpose(0, 2, 1, 3)]
    all_to_all x7 -> x8, waiting for transfers between devices: 102 us -> 66.3 us  [swap(): return lax.all_to_all(x, axis, split_axis=0, concat_axis=0, tiled=True)]
  transfers between devices with their start and end apart: 15 -> 12, of which waited for: 9 -> 8; matrix products, arithmetic and copies ran while one was open for 26% -> 2% of each run, Pallas kernels for 0% -> 29%
where the time goes in v1:
time: 266 us; the launch traced here: 264 us
  Pallas kernels  84.3 us (32%)
  waiting for transfers between devices  80.4 us (30%)
  starting transfers between devices  46.6 us (18%)
  blocking collectives  42.9 us (16%)
  other arithmetic  4.82 us (2%)
  local copies, waits for them, and re-layouts  4.46 us (2%)
    all_to_all x8, waiting for transfers between devices, swap(): return lax.all_to_all(x, axis, split_axis=0, concat_axis=0, tiled=True)  66.3 us
    all_to_all x2, blocking collectives, swap(): return lax.all_to_all(x, axis, split_axis=0, concat_axis=0, tiled=True)  42.9 us
    all_to_all x8, starting transfers between devices, swap(): return lax.all_to_all(x, axis, split_axis=0, concat_axis=0, tiled=True)  29.5 us
    pallas_call x1, Pallas kernels, attend_backward(): pl.pallas_call(backward_kernel, grid=(group,), in_specs=[pl.BlockSpec(mem...  27.3 us
    pallas_call x2, Pallas kernels, temporal_call(): pl.pallas_call(kernel, grid=(group, tokens // rows), in_specs=[spec(a.sha...  21.9 us
    pallas_call x1, Pallas kernels, attend_forward(): pl.pallas_call(forward_kernel, grid=(group,), in_specs=[pl.BlockSpec(memo...  13.4 us
    ppermute x2, starting transfers between devices, shift_left(): return lax.ppermute(x, 'wa', [(i + 1, i) for i in range(count - 1)])  13.3 us
    ppermute x2, waiting for transfers between devices, shift_right(): return lax.ppermute(x, 'wa', [(i, i + 1) for i in range(count - 1)])  12.5 us
  transfers between devices with their start and end apart: 12, of which 8 were waited for; matrix products, arithmetic and copies ran while one was open for 2% of the time, Pallas kernels for 29%

profile of v1, /device:TPU:8, one launch (start us, length us, event | category | flops | bytes accessed | tf_op | source)
XLA Modules:
  0.0 264.3 jit_solution(13499791840491545115)
XLA Ops:
  0.6 3.7 %shard_map.102 = bf16[4,3,2,256,128]{4,3,2,1,0:T(8,128)(2,1)} custom-call(bf16[256,1536]{1,0:T(8,128)(2,1)} %bitcast.18, bf16[256,1536]{1,0:T(8,128)(2,1)} %bitcast.19), custom_call_target="tpu_custom_call" | custom-call | bytes 3145728 | tf_op jit(solution)/shard_map/pallas_call | solution.py:50
  4.4 4.3 %all-to-all-start.1 = ((bf16[4,3,2,256,128]{4,3,2,1,0:T(8,128)(2,1)}), bf16[4,3,2,256,128]{4,3,2,1,0:T(8,128)(2,1)S(1)}, u32[]{:S(2)}, u32[]{:S(2)}) async-start(bf16[4,3,2,256,128]{4,3,2,1,0:T(8,128)(2,1)} %shard_map.102), calls=%async_computation.1 | async-start | bytes 3145728 | tf_op jit(solution)/shard_map/all_to_all | solution.py:308
  8.6 4.1 %shard_map.103 = bf16[4,3,3,256,128]{4,3,2,1,0:T(8,128)(2,1)} custom-call(bf16[256,1536]{1,0:T(8,128)(2,1)} %bitcast.13, bf16[256,1536]{1,0:T(8,128)(2,1)} %bitcast.14, bf16[256,1536]{1,0:T(8,128)(2,1)} %bitcast.15), custom_call_target="tpu_custom_call" | custom-call | bytes 4718592 | tf_op jit(solution)/shard_map/pallas_call | solution.py:50
  12.7 16.6 %all-to-all-done.1.kc_ref = bf16[4,3,2,256,128]{4,3,2,1,0:T(8,128)(2,1)S(1)} async-done(((bf16[4,3,2,256,128]{4,3,2,1,0:T(8,128)(2,1)}), bf16[4,3,2,256,128]{4,3,2,1,0:T(8,128)(2,1)S(1)}, u32[]{:S(2)}, u32[]{:S(2)}) %all-to-all-start.1) | async-done | bytes 1572896 | tf_op jit(solution)/shard_map/all_to_all | solution.py:308
  30.5 3.6 %all-to-all-start.2 = ((bf16[4,3,3,256,128]{4,3,2,1,0:T(8,128)(2,1)}), bf16[4,3,3,256,128]{4,3,2,1,0:T(8,128)(2,1)S(1)}, u32[]{:S(2)}, u32[]{:S(2)}) async-start(bf16[4,3,3,256,128]{4,3,2,1,0:T(8,128)(2,1)} %shard_map.103), calls=%async_computation.2 | async-start | bytes 4718592 | tf_op jit(solution)/shard_map/all_to_all | solution.py:308
  34.2 6.6 %collective-permute-start.1 = (bf16[4,3,2,256,128]{4,3,2,1,0:T(8,128)(2,1)}, bf16[4,3,2,256,128]{4,3,2,1,0:T(8,128)(2,1)}, u32[]{:S(2)}, u32[]{:S(2)}) collective-permute-start(bf16[4,3,2,256,128]{4,3,2,1,0:T(8,128)(2,1)} %copy-done.5), channel_id=1, source_target_pairs={{1,0},{2,1},{3,2},{4,3},{5,4},{6,5},{7,6},{9,8},{10,9},{11,10},{12... | collective-permute-start | bytes 4718600 | tf_op jit(solution)/shard_map/ppermute | solution.py:318
  40.8 1.9 collective-permute-start
  42.8 3.3 %shard_map.101 = bf16[4,3,1,256,128]{4,3,2,1,0:T(8,128)(2,1)} custom-call(bf16[256,1536]{1,0:T(8,128)(2,1)} %bitcast.16), custom_call_target="tpu_custom_call" | custom-call | bytes 1572864 | tf_op jit(solution)/shard_map/pallas_call | solution.py:50
  46.1 18.6 %all-to-all-done.2.pau_ref = bf16[4,3,3,256,128]{4,3,2,1,0:T(8,128)(2,1)S(1)} async-done(((bf16[4,3,3,256,128]{4,3,2,1,0:T(8,128)(2,1)}), bf16[4,3,3,256,128]{4,3,2,1,0:T(8,128)(2,1)S(1)}, u32[]{:S(2)}, u32[]{:S(2)}) %all-to-all-start.2) | async-done | bytes 2359328 | tf_op jit(solution)/shard_map/all_to_all | solution.py:308
  64.6 3.5 %all-to-all-start = ((bf16[4,3,1,256,128]{4,3,2,1,0:T(8,128)(2,1)}), bf16[4,3,1,256,128]{4,3,2,1,0:T(8,128)(2,1)S(1)}, u32[]{:S(2)}, u32[]{:S(2)}) async-start(bf16[4,3,1,256,128]{4,3,2,1,0:T(8,128)(2,1)} %shard_map.101), calls=%async_computation | async-start | bytes 1572864 | tf_op jit(solution)/shard_map/all_to_all | solution.py:308
  68.1 9.9 %shard_map.104 = bf16[4,3,1,256,128]{4,3,2,1,0:T(8,128)(2,1)} custom-call(bf16[4,3,3,256,128]{4,3,2,1,0:T(8,128)(2,1)} %copy-done), custom_call_target="tpu_custom_call" | custom-call | flops 805306368 | bytes 2359296 | tf_op jit(solution)/shard_map/pallas_call | solution.py:290
  78.0 1.9 all-to-all-done.q_ref
  80.0 26.4 %all_to_all.50 = bf16[4,3,1,256,128]{4,3,2,1,0:T(8,128)(2,1)} all-to-all(bf16[4,3,1,256,128]{4,3,2,1,0:T(8,128)(2,1)} %shard_map.104), channel_id=1, replica_groups=mesh['tm'=4,'ha'=4,'wa'=8] {'tm'}, dimensions={0} | all-to-all | bytes 1572864 | tf_op jit(solution)/shard_map/all_to_all | solution.py:308
  106.4 3.5 %all-to-all-start.4 = ((bf16[4,3,1,256,128]{4,3,2,1,0:T(8,128)(2,1)}), bf16[4,3,1,256,128]{4,3,2,1,0:T(8,128)(2,1)S(1)}, u32[]{:S(2)}, u32[]{:S(2)}) async-start(bf16[4,3,1,256,128]{4,3,2,1,0:T(8,128)(2,1)} %all_to_all.50), calls=%async_computation.4 | async-start | bytes 1572864 | tf_op jit(solution)/shard_map/all_to_all | solution.py:308
  110.6 13.4 %shard_map.105 = (bf16[4,3,1,256,128]{4,3,2,1,0:T(8,128)(2,1)}, f32[3,4,1,256]{3,2,1,0:T(1,128)}) custom-call(f32[2]{0:T(128)} %add_select_fusion.bad_ref, bf16[4,3,1,256,128]{4,3,2,1,0:T(8,128)(2,1)} %copy-done.6, bf16[4,3,2,256,128]{4,3,2,1,0:T(8,128)(2,1)} %collective-permute-done.kl_ref, bf16[4,3,2,256,128]{4,3,2,1,0:T(8,128)(2,1)} %copy-done.5, ...), custom_call_target="tpu_custom_call" | custom-call | flops 3019898880 | bytes 6291456 | tf_op jit(solution)/shard_map/pallas_call | solution.py:129
  124.0 16.5 %all_to_all.51 = bf16[4,3,1,256,128]{4,3,2,1,0:T(8,128)(2,1)} all-to-all(bf16[4,3,1,256,128]{4,3,2,1,0:T(8,128)(2,1)} %get-tuple-element.15.o_ref), channel_id=1, replica_groups=mesh['tm'=4,'ha'=4,'wa'=8] {'ha'}, dimensions={0} | all-to-all | bytes 1572864 | tf_op jit(solution)/shard_map/all_to_all | solution.py:308
  140.5 3.7 %all-to-all-start.8 = ((bf16[4,3,1,256,128]{4,3,2,1,0:T(8,128)(2,1)}), bf16[4,3,1,256,128]{4,3,2,1,0:T(8,128)(2,1)S(1)}, u32[]{:S(2)}, u32[]{:S(2)}) async-start(bf16[4,3,1,256,128]{4,3,2,1,0:T(8,128)(2,1)} %all_to_all.51), calls=%async_computation.8 | async-start | bytes 1572864 | tf_op jit(solution)/shard_map/all_to_all | solution.py:308
  144.2 27.3 %shard_map.106 = (bf16[4,3,1,256,128]{4,3,2,1,0:T(8,128)(2,1)}, bf16[4,3,2,256,128]{4,3,2,1,0:T(8,128)(2,1)}, f32[4,3,2,256,128]{4,3,2,1,0:T(8,128)}, bf16[4,3,2,256,128]{4,3,2,1,0:T(8,128)(2,1)}) custom-call(f32[2]{0:T(128)} %add_select_fusion.bad_ref, bf16[4,3,1,256,128]{4,3,2,1,0:T(8,128)(2,1)} %copy-done.6, ...), custom_call_target="tpu_custom_call" | custom-call | flops 7549747200 | bytes 15728640 | tf_op jit(solution)/shard_map/pallas_call | solution.py:205
  171.5 1.9 collective-permute-start.2
  173.4 6.7 %collective-permute-start.3 = (bf16[4,3,2,256,128]{4,3,2,1,0:T(8,128)(2,1)}, bf16[4,3,2,256,128]{4,3,2,1,0:T(8,128)(2,1)}, u32[]{:S(2)}, u32[]{:S(2)}) collective-permute-start(bf16[4,3,2,256,128]{4,3,2,1,0:T(8,128)(2,1)} %get-tuple-element.20), channel_id=1, source_target_pairs={{1,0},{2,1},{3,2},{4,3},{5,4},{6,5},{7,6},{9,8},{10,9},{11,10},{12... | collective-permute-start | bytes 4718600 | tf_op jit(solution)/shard_map/ppermute | solution.py:318
  180.1 3.5 %all-to-all-start.5 = ((bf16[4,3,1,256,128]{4,3,2,1,0:T(8,128)(2,1)}), bf16[4,3,1,256,128]{4,3,2,1,0:T(8,128)(2,1)S(1)}, u32[]{:S(2)}, u32[]{:S(2)}) async-start(bf16[4,3,1,256,128]{4,3,2,1,0:T(8,128)(2,1)} %get-tuple-element.17), calls=%async_computation.5 | async-start | bytes 1572864 | tf_op jit(solution)/shard_map/all_to_all | solution.py:308
  183.6 12.0 %shard_map.109 = bf16[4,3,2,256,128]{4,3,2,1,0:T(8,128)(2,1)} custom-call(bf16[4,3,3,256,128]{4,3,2,1,0:T(8,128)(2,1)} %copy-done, bf16[4,3,1,256,128]{4,3,2,1,0:T(8,128)(2,1)} %copy-done.3), custom_call_target="tpu_custom_call" | custom-call | flops 805306368 | bytes 3145728 | tf_op jit(solution)/shard_map/pallas_call | solution.py:290
  197.2 3.8 %all-to-all-start.9 = ((bf16[4,3,2,256,128]{4,3,2,1,0:T(8,128)(2,1)}), bf16[4,3,2,256,128]{4,3,2,1,0:T(8,128)(2,1)S(1)}, u32[]{:S(2)}, u32[]{:S(2)}) async-start(bf16[4,3,2,256,128]{4,3,2,1,0:T(8,128)(2,1)} %shard_map.109), calls=%async_computation.9 | async-start | bytes 3145728 | tf_op jit(solution)/shard_map/all_to_all | solution.py:308
  201.0 12.5 %collective-permute-done.2 = bf16[4,3,2,256,128]{4,3,2,1,0:T(8,128)(2,1)S(1)} collective-permute-done((bf16[4,3,2,256,128]{4,3,2,1,0:T(8,128)(2,1)}, bf16[4,3,2,256,128]{4,3,2,1,0:T(8,128)(2,1)S(1)}, u32[]{:S(2)}, u32[]{:S(2)}) %collective-permute-start.2) | collective-permute-done | bytes 1572896 | tf_op jit(solution)/shard_map/ppermute | solution.py:313
  213.5 1.6 collective-permute-done.3
  215.1 4.2 %add_convert_fusion = bf16[4,3,2,256,128]{4,3,2,1,0:T(8,128)(2,1)} fusion(bf16[4,3,2,256,128]{4,3,2,1,0:T(8,128)(2,1)} %collective-permute-done.3, f32[4,3,2,256,128]{4,3,2,1,0:T(8,128)} %get-tuple-element.18, bf16[4,3,2,256,128]{4,3,2,1,0:T(8,128)(2,1)S(1)} %collective-permute-done.2), kind=kLoop, calls=%fused_computation | loop fusion | flops 3932160 | bytes 7864320 | tf_op jit(solution)/shard_map/convert_element_type | solution.py:348
  219.3 15.0 %all-to-all-done.9.block_ref = bf16[4,3,2,256,128]{4,3,2,1,0:T(8,128)(2,1)S(1)} async-done(((bf16[4,3,2,256,128]{4,3,2,1,0:T(8,128)(2,1)}), bf16[4,3,2,256,128]{4,3,2,1,0:T(8,128)(2,1)S(1)}, u32[]{:S(2)}, u32[]{:S(2)}) %all-to-all-start.9) | async-done | bytes 1572896 | tf_op jit(solution)/shard_map/all_to_all | solution.py:308
  235.4 3.6 %all-to-all-start.6 = ((bf16[4,3,2,256,128]{4,3,2,1,0:T(8,128)(2,1)}), bf16[4,3,2,256,128]{4,3,2,1,0:T(8,128)(2,1)S(1)}, u32[]{:S(2)}, u32[]{:S(2)}) async-start(bf16[4,3,2,256,128]{4,3,2,1,0:T(8,128)(2,1)} %add_convert_fusion), calls=%async_computation.6 | async-start | bytes 3145728 | tf_op jit(solution)/shard_map/all_to_all | solution.py:308
  239.0 3.3 %shard_map.107 = bf16[256,1536]{1,0:T(8,128)(2,1)} custom-call(bf16[4,3,1,256,128]{4,3,2,1,0:T(8,128)(2,1)} %copy-done.4), custom_call_target="tpu_custom_call" | custom-call | bytes 1572864 | tf_op jit(solution)/shard_map/pallas_call | solution.py:72
  242.3 3.6 %shard_map.110 = (bf16[256,1536]{1,0:T(8,128)(2,1)}, bf16[256,1536]{1,0:T(8,128)(2,1)}) custom-call(bf16[4,3,2,256,128]{4,3,2,1,0:T(8,128)(2,1)} %copy-done.1), custom_call_target="tpu_custom_call" | custom-call | bytes 3145728 | tf_op jit(solution)/shard_map/pallas_call | solution.py:72
  246.0 13.5 %all-to-all-done.6.block_ref = bf16[4,3,2,256,128]{4,3,2,1,0:T(8,128)(2,1)S(1)} async-done(((bf16[4,3,2,256,128]{4,3,2,1,0:T(8,128)(2,1)}), bf16[4,3,2,256,128]{4,3,2,1,0:T(8,128)(2,1)S(1)}, u32[]{:S(2)}, u32[]{:S(2)}) %all-to-all-start.6) | async-done | bytes 1572896 | tf_op jit(solution)/shard_map/all_to_all | solution.py:308
  260.6 3.6 %shard_map.108 = (bf16[256,1536]{1,0:T(8,128)(2,1)}, bf16[256,1536]{1,0:T(8,128)(2,1)}) custom-call(bf16[4,3,2,256,128]{4,3,2,1,0:T(8,128)(2,1)} %copy-done.2), custom_call_target="tpu_custom_call" | custom-call | bytes 3145728 | tf_op jit(solution)/shard_map/pallas_call | solution.py:72
  (22 shorter events, 5.8 us)
Async XLA Ops:
  4.4 25.0 %all-to-all-start.1 = ((bf16[4,3,2,256,128]{4,3,2,1,0:T(8,128)(2,1)}), bf16[4,3,2,256,128]{4,3,2,1,0:T(8,128)(2,1)S(1)}, u32[]{:S(2)}, u32[]{:S(2)}) async-start(bf16[4,3,2,256,128]{4,3,2,1,0:T(8,128)(2,1)} %shard_map.102), calls=%async_computation.1 | async-start | bytes 3145728 | tf_op jit(solution)/shard_map/all_to_all | solution.py:308
  29.4 1.2 copy-start.5
  30.5 34.1 %all-to-all-start.2 = ((bf16[4,3,3,256,128]{4,3,2,1,0:T(8,128)(2,1)}), bf16[4,3,3,256,128]{4,3,2,1,0:T(8,128)(2,1)S(1)}, u32[]{:S(2)}, u32[]{:S(2)}) async-start(bf16[4,3,3,256,128]{4,3,2,1,0:T(8,128)(2,1)} %shard_map.103), calls=%async_computation.2 | async-start | bytes 4718592 | tf_op jit(solution)/shard_map/all_to_all | solution.py:308
  34.2 76.4 %collective-permute-start.1 = (bf16[4,3,2,256,128]{4,3,2,1,0:T(8,128)(2,1)}, bf16[4,3,2,256,128]{4,3,2,1,0:T(8,128)(2,1)}, u32[]{:S(2)}, u32[]{:S(2)}) collective-permute-start(bf16[4,3,2,256,128]{4,3,2,1,0:T(8,128)(2,1)} %copy-done.5), channel_id=1, source_target_pairs={{1,0},{2,1},{3,2},{4,3},{5,4},{6,5},{7,6},{9,8},{10,9},{11,10},{12... | collective-permute-start | bytes 4718600 | tf_op jit(solution)/shard_map/ppermute | solution.py:318
  40.8 69.7 %collective-permute-start = (bf16[4,3,2,256,128]{4,3,2,1,0:T(8,128)(2,1)}, bf16[4,3,2,256,128]{4,3,2,1,0:T(8,128)(2,1)}, u32[]{:S(2)}, u32[]{:S(2)}) collective-permute-start(bf16[4,3,2,256,128]{4,3,2,1,0:T(8,128)(2,1)} %copy-done.5), channel_id=1, source_target_pairs={{0,1},{1,2},{2,3},{3,4},{4,5},{5,6},{6,7},{8,9},{9,10},{10,11},{11... | collective-permute-start | bytes 4718600 | tf_op jit(solution)/shard_map/ppermute | solution.py:313
  64.6 3.5 %copy-start = (bf16[4,3,3,256,128]{4,3,2,1,0:T(8,128)(2,1)}, bf16[4,3,3,256,128]{4,3,2,1,0:T(8,128)(2,1)S(1)}, u32[]{:S(2)}) copy-start(bf16[4,3,3,256,128]{4,3,2,1,0:T(8,128)(2,1)S(1)} %all-to-all-done.2.pau_ref) | copy-start | bytes 7077892
  64.6 15.4 %all-to-all-start = ((bf16[4,3,1,256,128]{4,3,2,1,0:T(8,128)(2,1)}), bf16[4,3,1,256,128]{4,3,2,1,0:T(8,128)(2,1)S(1)}, u32[]{:S(2)}, u32[]{:S(2)}) async-start(bf16[4,3,1,256,128]{4,3,2,1,0:T(8,128)(2,1)} %shard_map.101), calls=%async_computation | async-start | bytes 1572864 | tf_op jit(solution)/shard_map/all_to_all | solution.py:308
  80.0 26.4 %copy-start.6 = (bf16[4,3,1,256,128]{4,3,2,1,0:T(8,128)(2,1)}, bf16[4,3,1,256,128]{4,3,2,1,0:T(8,128)(2,1)S(1)}, u32[]{:S(2)}) copy-start(bf16[4,3,1,256,128]{4,3,2,1,0:T(8,128)(2,1)S(1)} %all-to-all-done.q_ref) | copy-start | bytes 2359300
  106.4 17.6 %all-to-all-start.4 = ((bf16[4,3,1,256,128]{4,3,2,1,0:T(8,128)(2,1)}), bf16[4,3,1,256,128]{4,3,2,1,0:T(8,128)(2,1)S(1)}, u32[]{:S(2)}, u32[]{:S(2)}) async-start(bf16[4,3,1,256,128]{4,3,2,1,0:T(8,128)(2,1)} %all_to_all.50), calls=%async_computation.4 | async-start | bytes 1572864 | tf_op jit(solution)/shard_map/all_to_all | solution.py:308
  123.9 16.5 %copy-start.7 = (bf16[4,3,1,256,128]{4,3,2,1,0:T(8,128)(2,1)}, bf16[4,3,1,256,128]{4,3,2,1,0:T(8,128)(2,1)S(1)}, u32[]{:S(2)}) copy-start(bf16[4,3,1,256,128]{4,3,2,1,0:T(8,128)(2,1)S(1)} %all-to-all-done.4.do_ref) | copy-start | bytes 2359300
  140.5 39.6 %all-to-all-start.8 = ((bf16[4,3,1,256,128]{4,3,2,1,0:T(8,128)(2,1)}), bf16[4,3,1,256,128]{4,3,2,1,0:T(8,128)(2,1)S(1)}, u32[]{:S(2)}, u32[]{:S(2)}) async-start(bf16[4,3,1,256,128]{4,3,2,1,0:T(8,128)(2,1)} %all_to_all.51), calls=%async_computation.8 | async-start | bytes 1572864 | tf_op jit(solution)/shard_map/all_to_all | solution.py:308
  171.5 42.0 %collective-permute-start.2 = (bf16[4,3,2,256,128]{4,3,2,1,0:T(8,128)(2,1)}, bf16[4,3,2,256,128]{4,3,2,1,0:T(8,128)(2,1)S(1)}, u32[]{:S(2)}, u32[]{:S(2)}) collective-permute-start(bf16[4,3,2,256,128]{4,3,2,1,0:T(8,128)(2,1)} %get-tuple-element.19), channel_id=1, source_target_pairs={{0,1},{1,2},{2,3},{3,4},{4,5},{5,6},{6,7},{8,9},{9,10},{10,11},{11... | collective-permute-start | bytes 4718600 | tf_op jit(solution)/shard_map/ppermute | solution.py:313
  173.4 41.7 %collective-permute-start.3 = (bf16[4,3,2,256,128]{4,3,2,1,0:T(8,128)(2,1)}, bf16[4,3,2,256,128]{4,3,2,1,0:T(8,128)(2,1)}, u32[]{:S(2)}, u32[]{:S(2)}) collective-permute-start(bf16[4,3,2,256,128]{4,3,2,1,0:T(8,128)(2,1)} %get-tuple-element.20), channel_id=1, source_target_pairs={{1,0},{2,1},{3,2},{4,3},{5,4},{6,5},{7,6},{9,8},{10,9},{11,10},{12... | collective-permute-start | bytes 4718600 | tf_op jit(solution)/shard_map/ppermute | solution.py:318
  180.1 3.5 %copy-start.3 = (bf16[4,3,1,256,128]{4,3,2,1,0:T(8,128)(2,1)}, bf16[4,3,1,256,128]{4,3,2,1,0:T(8,128)(2,1)S(1)}, u32[]{:S(2)}) copy-start(bf16[4,3,1,256,128]{4,3,2,1,0:T(8,128)(2,1)S(1)} %all-to-all-done.8.mixed_ref) | copy-start | bytes 2359300
  180.1 16.2 %all-to-all-start.5 = ((bf16[4,3,1,256,128]{4,3,2,1,0:T(8,128)(2,1)}), bf16[4,3,1,256,128]{4,3,2,1,0:T(8,128)(2,1)S(1)}, u32[]{:S(2)}, u32[]{:S(2)}) async-start(bf16[4,3,1,256,128]{4,3,2,1,0:T(8,128)(2,1)} %get-tuple-element.17), calls=%async_computation.5 | async-start | bytes 1572864 | tf_op jit(solution)/shard_map/all_to_all | solution.py:308
  196.3 0.9 copy-start.4
  197.2 37.0 %all-to-all-start.9 = ((bf16[4,3,2,256,128]{4,3,2,1,0:T(8,128)(2,1)}), bf16[4,3,2,256,128]{4,3,2,1,0:T(8,128)(2,1)S(1)}, u32[]{:S(2)}, u32[]{:S(2)}) async-start(bf16[4,3,2,256,128]{4,3,2,1,0:T(8,128)(2,1)} %shard_map.109), calls=%async_computation.9 | async-start | bytes 3145728 | tf_op jit(solution)/shard_map/all_to_all | solution.py:308
  234.2 1.2 copy-start.1
  235.4 24.0 %all-to-all-start.6 = ((bf16[4,3,2,256,128]{4,3,2,1,0:T(8,128)(2,1)}), bf16[4,3,2,256,128]{4,3,2,1,0:T(8,128)(2,1)S(1)}, u32[]{:S(2)}, u32[]{:S(2)}) async-start(bf16[4,3,2,256,128]{4,3,2,1,0:T(8,128)(2,1)} %add_convert_fusion), calls=%async_computation.6 | async-start | bytes 3145728 | tf_op jit(solution)/shard_map/all_to_all | solution.py:308
  259.4 1.2 copy-start.2

commit v2 on v1

v2 whole, which is shorter than its diff:
```python
import functools

import jax
import jax.numpy as jnp
from jax import lax
from jax.experimental import pallas as pl
from jax.experimental.pallas import tpu as pltpu
from jax.sharding import PartitionSpec as P

HEADS = 12
HEAD_DIM = 128
PARTS = 4
GROUP = HEADS // PARTS
ROWS = 4
BIG = 1e30
SCALE = HEAD_DIM ** (-0.5)
LOG2E = 1.4426950408889634
BASE2 = SCALE * LOG2E

NT = (((1,), (1,)), ((), ()))
NN = (((1,), (0,)), ((), ()))
TN = (((0,), (0,)), ((), ()))


def dot(a, b, dims):
    return lax.dot_general(a, b, dims, preferred_element_type=jnp.float32)


def params():
    return pltpu.CompilerParams(vmem_limit_bytes=56 * 1024 * 1024)


def cost(microseconds):
    return pl.CostEstimate(
        flops=int(microseconds * 1e9), bytes_accessed=1024, transcendentals=0
    )


def move(inputs, out_shapes, plan, axis=None, after=(), told=0.1):
    first = len(inputs) + len(after)

    def kernel(*refs):
        ins = refs[: len(inputs)]
        outs = refs[first:]
        me = 0 if axis is None else lax.axis_index(axis)
        for i, at, o, to in plan(me):
            outs[o][to] = ins[i][at]

    return pl.pallas_call(
        kernel,
        in_specs=[pl.BlockSpec(memory_space=pltpu.VMEM)] * len(inputs)
        + [pl.BlockSpec(memory_space=pl.ANY)] * len(after),
        out_specs=[pl.BlockSpec(memory_space=pltpu.VMEM)] * len(out_shapes),
        out_shape=out_shapes,
        cost_estimate=cost(told),
        compiler_params=params(),
    )(*inputs, *after)


def columns(group, head):
    start = (group * GROUP + head) * HEAD_DIM
    if not isinstance(start, int):
        start = pl.multiple_of(start, HEAD_DIM)
    return (slice(None), pl.ds(start, HEAD_DIM))


def bf16(*shape):
    return jax.ShapeDtypeStruct(shape, jnp.bfloat16)


def pack(arrays, after=()):
    tokens = arrays[0].shape[0]
    cells = [(a, d, h) for d in range(PARTS) for h in range(GROUP) for a in range(len(arrays))]
    return move(
        arrays,
        [bf16(PARTS, GROUP, len(arrays), tokens, HEAD_DIM)],
        lambda me: [(a, columns(d, h), 0, (d, h, a)) for a, d, h in cells],
        after=after,
    )[0]


def pack_partners(arrays):
    tokens = arrays[0].shape[0]
    cells = [(a, s, h) for s in range(PARTS) for h in range(GROUP) for a in range(len(arrays))]
    return move(
        arrays,
        [bf16(GROUP, len(arrays), tokens, HEAD_DIM)] * PARTS,
        lambda me: [(a, columns(me ^ s, h), s, (h, a)) for a, s, h in cells],
        "tm",
    )


def unpack_partners(chunks):
    _, count, tokens, _ = chunks[0].shape
    cells = [(a, s, h) for s in range(PARTS) for h in range(GROUP) for a in range(count)]
    return move(
        chunks,
        [bf16(tokens, HEADS * HEAD_DIM)] * count,
        lambda me: [(s, (h, a), a, columns(me ^ s, h)) for a, s, h in cells],
        "tm",
        told=100,
    )


def join_partners(chunks):
    return move(
        chunks,
        [bf16(PARTS, *chunks[0].shape)],
        lambda me: [(s, (slice(None),), 0, (me ^ s,)) for s in range(PARTS)],
        "tm",
    )[0]


def split_partners(block):
    return move(
        [block],
        [bf16(*block.shape[1:])] * PARTS,
        lambda me: [(0, (me ^ s,), s, (slice(None),)) for s in range(PARTS)],
        "tm",
    )


def unpack_heads(blocks):
    count, tokens = blocks[0].shape[2:4]
    cells = [(a, d, h) for h in range(GROUP) for d in range(PARTS) for a in range(count)]
    return move(
        blocks,
        [bf16(tokens, HEADS * HEAD_DIM)] * count,
        lambda me: [(h, (d, 0, a), a, columns(d, h)) for a, d, h in cells],
    )


def trade(chunks):
    out = [chunks[0]]
    for s in range(1, PARTS):
        out.append(lax.ppermute(chunks[s], "tm", [(i, i ^ s) for i in range(PARTS)]))
    return out


def near_rows(row):
    return range(max(row - 1, 0), min(row + 2, ROWS))


def forward_kernel(bad_ref, q_ref, kl_ref, kc_ref, kr_ref, o_ref, lse_ref):
    bads = (bad_ref[0], jnp.float32(0.0), bad_ref[1])
    sides = (kl_ref, kc_ref, kr_ref)
    for b in range(ROWS):
        query = q_ref[b, 0, 0]
        scores = []
        for side in range(3):
            for u in near_rows(b):
                scores.append((side, u, dot(sides[side][u, 0, 0], query, NT)))
        top = None
        for side in range(3):
            local = None
            for at, _, s in scores:
                if at == side:
                    one = jnp.max(s, axis=0, keepdims=True)
                    local = one if local is None else jnp.maximum(local, one)
            local = local - bads[side]
            top = local if top is None else jnp.maximum(top, local)
        top = top * BASE2
        total = None
        mixed = None
        for side, u, s in scores:
            p = jnp.exp2(s * BASE2 - (top + bads[side]))
            one = jnp.sum(p, axis=0, keepdims=True)
            total = one if total is None else total + one
            term = dot(sides[side][u, 0, 1], p.astype(jnp.bfloat16), TN)
            mixed = term if mixed is None else mixed + term
        mixed = mixed * (1.0 / total)
        o_ref[b, 0, 0] = mixed.T.astype(jnp.bfloat16)
        lse_ref[0, b] = top + jnp.log2(total)


def column_spec(count, tokens):
    return pl.BlockSpec((ROWS, 1, count, tokens, HEAD_DIM), lambda h: (0, h, 0, 0, 0))


def attend_forward(bad, q, kv_left, kv, kv_right):
    tokens = q.shape[3]
    group = q.shape[1]
    return pl.pallas_call(
        forward_kernel,
        grid=(group,),
        in_specs=[pl.BlockSpec(memory_space=pltpu.SMEM), column_spec(1, tokens)]
        + [column_spec(2, tokens)] * 3,
        out_specs=[
            column_spec(1, tokens),
            pl.BlockSpec((1, ROWS, 1, tokens), lambda h: (h, 0, 0, 0)),
        ],
        out_shape=[
            jax.ShapeDtypeStruct(q.shape, jnp.bfloat16),
            jax.ShapeDtypeStruct((group, ROWS, 1, tokens), jnp.float32),
        ],
        cost_estimate=cost(100),
        compiler_params=params(),
    )(bad, q, kv_left, kv, kv_right)


def backward_kernel(
    bad_ref,
    q_ref,
    kl_ref,
    kc_ref,
    kr_ref,
    do_ref,
    o_ref,
    lse_ref,
    _,
    dq_ref,
    dl_ref,
    dc_ref,
    dr_ref,
    dqt_ref,
    row_ref,
):
    bads = (bad_ref[0], jnp.float32(0.0), bad_ref[1])
    sides = (kl_ref, kc_ref, kr_ref)
    outs = (dl_ref, dc_ref, dr_ref)
    for b in range(ROWS):
        product = do_ref[b, 0, 0].astype(jnp.float32) * o_ref[b, 0, 0].astype(jnp.float32)
        row_ref[b] = jnp.sum(product.T, axis=0, keepdims=True)
    seen = set()
    for side in (0, 2, 1):
        for u in range(ROWS):
            key = sides[side][u, 0, 0]
            value = sides[side][u, 0, 1]
            dk = None
            dv = None
            for b in near_rows(u):
                query = q_ref[b, 0, 0]
                grad = do_ref[b, 0, 0]
                s = dot(key, query, NT)
                p = jnp.exp2(s * BASE2 - (lse_ref[0, b] + bads[side]))
                e = dot(value, grad, NT)
                g = (p * (e - row_ref[b])).astype(jnp.bfloat16)
                tv = dot(p.astype(jnp.bfloat16), grad, NN)
                tk = dot(g, query, NN)
                tq = dot(key, g, TN)
                dv = tv if dv is None else dv + tv
                dk = tk if dk is None else dk + tk
                if b in seen:
                    dqt_ref[b] += tq
                else:
                    seen.add(b)
                    dqt_ref[b] = tq
            outs[side][u, 0, 0] = (dk * SCALE).astype(outs[side].dtype)
            outs[side][u, 0, 1] = dv.astype(outs[side].dtype)
    for b in range(ROWS):
        dq_ref[b, 0, 0] = (dqt_ref[b] * SCALE).T.astype(jnp.bfloat16)


def head_spec(head, count, tokens):
    return pl.BlockSpec((ROWS, 1, count, tokens, HEAD_DIM), lambda i: (0, head, 0, 0, 0))


def attend_backward(head, bad, q, kv_left, kv, kv_right, grad, mixed, lse, after):
    tokens = q.shape[3]
    return pl.pallas_call(
        backward_kernel,
        grid=(1,),
        in_specs=[pl.BlockSpec(memory_space=pltpu.SMEM), head_spec(head, 1, tokens)]
        + [head_spec(head, 2, tokens)] * 3
        + [head_spec(head, 1, tokens)] * 2
        + [pl.BlockSpec((1, ROWS, 1, tokens), lambda i: (head, 0, 0, 0))]
        + [pl.BlockSpec(memory_space=pl.ANY)],
        out_specs=[head_spec(0, 1, tokens)] + [head_spec(0, 2, tokens)] * 3,
        out_shape=[bf16(ROWS, 1, 1, tokens, HEAD_DIM)]
        + [bf16(ROWS, 1, 2, tokens, HEAD_DIM)] * 3,
        scratch_shapes=[
            pltpu.VMEM((ROWS, HEAD_DIM, tokens), jnp.float32),
            pltpu.VMEM((ROWS, 1, tokens), jnp.float32),
        ],
        cost_estimate=cost(100),
        compiler_params=params(),
    )(bad, q, kv_left, kv, kv_right, grad, mixed, lse, after)


def total_kernel(dq_ref, own_ref, a_ref, b_ref, _, out_ref):
    out_ref[0, 0, 0] = dq_ref[0, 0, 0]
    for t in range(2):
        total = own_ref[0, 0, t].astype(jnp.float32) + a_ref[0, 0, t].astype(jnp.float32)
        out_ref[0, 0, 1 + t] = (total + b_ref[0, 0, t].astype(jnp.float32)).astype(jnp.bfloat16)


def totals(dq, own, a, b, after):
    tokens = dq.shape[3]

    def spec(count):
        return pl.BlockSpec((1, 1, count, tokens, HEAD_DIM), lambda i: (i, 0, 0, 0, 0))

    return pl.pallas_call(
        total_kernel,
        grid=(ROWS,),
        in_specs=[spec(1), spec(2), spec(2), spec(2), pl.BlockSpec(memory_space=pl.ANY)],
        out_specs=spec(3),
        out_shape=bf16(ROWS, 1, 3, tokens, HEAD_DIM),
        cost_estimate=cost(0.1),
        compiler_params=params(),
    )(dq, own, a, b, after)


def lane_sums(products):
    rows = products[0].shape[0]
    product = jnp.concatenate(products, axis=0)
    high = product.astype(jnp.bfloat16)
    low = (product - high.astype(jnp.float32)).astype(jnp.bfloat16)
    ones = jnp.ones((2 * HEAD_DIM, HEAD_DIM), jnp.bfloat16)
    sums = dot(jnp.concatenate([high, low], axis=1), ones, NN)
    return [sums[i * rows : (i + 1) * rows] for i in range(len(products))]


def temporal_weights(probes, anchors):
    scores = lane_sums([p * a for p in probes for a in anchors])
    weights = []
    for f in range(PARTS):
        row = [s * SCALE for s in scores[f * PARTS : (f + 1) * PARTS]]
        top = functools.reduce(jnp.maximum, row)
        shifted = [jnp.exp(s - top) for s in row]
        inverse = 1.0 / functools.reduce(jnp.add, shifted)
        weights.append([s * inverse for s in shifted])
    return weights


def rounded(x):
    return x.astype(jnp.bfloat16).astype(jnp.float32)


def temporal_forward_kernel(*refs):
    ins, outs = refs[:PARTS], refs[PARTS:]
    parts = [[ref[0, t].astype(jnp.float32) for ref in ins] for t in range(3)]
    weights = temporal_weights(parts[0], parts[1])
    for g in range(PARTS):
        terms = [rounded(weights[f][g]) * parts[2][f] for f in range(PARTS)]
        outs[g][0, 0] = functools.reduce(jnp.add, terms).astype(jnp.bfloat16)


def temporal_backward_kernel(*refs):
    ins, mixed_refs, outs = refs[:PARTS], refs[PARTS : 2 * PARTS], refs[-PARTS:]
    parts = [[ref[0, t].astype(jnp.float32) for ref in ins] for t in range(3)]
    mixed = [ref[0, 0].astype(jnp.float32) for ref in mixed_refs]
    weights = temporal_weights(parts[0], parts[1])
    sums = lane_sums([u * m for u in parts[2] for m in mixed])
    anchor_grads = [None] * PARTS
    for f in range(PARTS):
        grads = sums[f * PARTS : (f + 1) * PARTS]
        row = functools.reduce(jnp.add, [w * c for w, c in zip(weights[f], grads)])
        scores = [rounded(w * (c - row)) for w, c in zip(weights[f], grads)]
        probe = functools.reduce(jnp.add, [s * parts[1][g] for g, s in enumerate(scores)])
        outs[f][0, 0] = (probe * SCALE).astype(jnp.bfloat16)
        for g in range(PARTS):
            term = scores[g] * parts[0][f]
            anchor_grads[g] = term if f == 0 else anchor_grads[g] + term
    for g in range(PARTS):
        outs[g][0, 1] = (anchor_grads[g] * SCALE).astype(jnp.bfloat16)


def temporal_call(kernel, arrays, count_out, told, after=()):
    group, _, tokens, _ = arrays[0].shape
    rows = 128

    def spec(count):
        return pl.BlockSpec((1, count, rows, HEAD_DIM), lambda h, i: (h, 0, i, 0))

    return pl.pallas_call(
        kernel,
        grid=(group, tokens // rows),
        in_specs=[spec(a.shape[1]) for a in arrays]
        + [pl.BlockSpec(memory_space=pl.ANY)] * len(after),
        out_specs=[spec(count_out)] * PARTS,
        out_shape=[bf16(group, count_out, tokens, HEAD_DIM)] * PARTS,
        cost_estimate=cost(told),
        compiler_params=params(),
    )(*arrays, *after)


def swap(x, axis):
    return lax.all_to_all(x, axis, split_axis=0, concat_axis=0, tiled=True)


def shift_right(x):
    count = lax.axis_size("wa")
    return lax.ppermute(x, "wa", [(i, i + 1) for i in range(count - 1)])


def shift_left(x):
    count = lax.axis_size("wa")
    return lax.ppermute(x, "wa", [(i + 1, i) for i in range(count - 1)])


def shards(queries, tile_keys, values, probes, anchors, upstream):
    shape = queries.shape
    tokens = shape[2] * shape[3]

    def flat(x):
        return x.reshape(tokens, shape[-1])

    place = lax.axis_index("wa")
    bad = jnp.stack([place == 0, place == lax.axis_size("wa") - 1]).astype(jnp.float32) * BIG

    pau_sent = pack_partners([flat(probes), flat(anchors), flat(upstream)])
    pau = trade(pau_sent)
    kv = swap(pack([flat(tile_keys), flat(values)], [pau_sent[1]]), "ha")
    kv_left = shift_right(kv)
    kv_right = shift_left(kv)
    q = swap(pack([flat(queries)], [kv]), "ha")
    grad_parts = trade(temporal_call(temporal_forward_kernel, pau, 1, 100))
    grad = swap(join_partners(grad_parts), "ha")
    mixed, lse = attend_forward(bad, q, kv_left, kv, kv_right)
    mixed_sent = split_partners(swap(mixed, "ha"))
    mixed_parts = trade(mixed_sent)
    def backward(head, after):
        dq, to_left, own, to_right = attend_backward(
            head, bad, q, kv_left, kv, kv_right, grad, mixed, lse, after
        )
        return dq, own, shift_right(to_right), shift_left(to_left)

    zero = backward(0, q)
    one = backward(1, mixed_sent[0])
    summed = [totals(*zero, one[0])]
    times_sent = temporal_call(
        temporal_backward_kernel, pau + mixed_parts, 2, 100, [summed[0]]
    )
    probe_grad, anchor_grad = unpack_partners(trade(times_sent))
    two = backward(2, times_sent[0])
    summed += [totals(*one, two[0]), totals(*two, probe_grad)]
    summed = [swap(x, "ha") for x in summed]
    query_grad, key_grad, value_grad = unpack_heads(summed)
    outs = (query_grad, key_grad, value_grad, probe_grad, anchor_grad)
    return tuple(x.reshape(shape) for x in outs)


def solution(mesh):
    spec = P(None, "tm", "ha", "wa", None)
    return jax.shard_map(
        shards,
        mesh=mesh,
        in_specs=(spec,) * 6,
        out_specs=(spec,) * 5,
        check_vma=False,
    )
```

time: 266 us -> 240 us (0.902)
  waiting for transfers between devices: 80.4 us -> 48.9 us
  starting transfers between devices: 46.6 us -> 74.7 us
  blocking collectives: 42.9 us -> 15.6 us
  Pallas kernels: 84.3 us -> 89.8 us
  other arithmetic: 4.82 us -> 0.58 us
  local copies, waits for them, and re-layouts: 4.46 us -> 7.67 us
    all_to_all x8 -> x6, waiting for transfers between devices: 66.3 us -> 20.3 us  [swap(): return lax.all_to_all(x, axis, split_axis=0, concat_axis=0, tiled=True)]
    ppermute x0 -> x12, waiting for transfers between devices: none -> 28.6 us  [trade(): lax.ppermute(chunks[s], 'tm', [(i, i ^ s) for i in range(PARTS)])]
    all_to_all x2 -> x1, blocking collectives: 42.9 us -> 15.6 us  [swap(): return lax.all_to_all(x, axis, split_axis=0, concat_axis=0, tiled=True)]
    ppermute x0 -> x12, starting transfers between devices: none -> 14.1 us  [trade(): lax.ppermute(chunks[s], 'tm', [(i, i ^ s) for i in range(PARTS)])]
    ppermute x2 -> x4, starting transfers between devices: 13.3 us -> 26.2 us  [shift_left(): return lax.ppermute(x, 'wa', [(i + 1, i) for i in range(count - 1)])]
    ppermute x2 -> x4, waiting for transfers between devices: 12.5 us -> 0.01 us  [shift_right(): return lax.ppermute(x, 'wa', [(i, i + 1) for i in range(count - 1)])]
    pallas_call x7 -> x13, Pallas kernels: 49 us -> 61.2 us  [the longest x3 31.6 us: attend_backward(): pl.pallas_call(backward_kernel, grid=(1,), in_specs=[pl.BlockSpec(memory_...]
    pallas_call x2, Pallas kernels: 21.9 us -> 15.2 us  [temporal_call(): pl.pallas_call(kernel, grid=(group, tokens // rows), in_specs=[spec(a.sha...]
  transfers between devices with their start and end apart: 12 -> 26, of which waited for: 8 -> 3; matrix products, arithmetic and copies ran while one was open for 2% -> 0% of each run, Pallas kernels for 29% -> 34%
where the time goes in v2:
time: 240 us; the launch traced here: 238 us
  Pallas kernels  89.8 us (37%)
  starting transfers between devices  74.7 us (31%)
  waiting for transfers between devices  48.9 us (20%)
  blocking collectives  15.6 us (6%)
  local copies, waits for them, and re-layouts  7.67 us (3%)
    pallas_call x3, Pallas kernels, attend_backward(): pl.pallas_call(backward_kernel, grid=(1,), in_specs=[pl.BlockSpec(memory_...  31.6 us
    ppermute x12, waiting for transfers between devices, trade(): lax.ppermute(chunks[s], 'tm', [(i, i ^ s) for i in range(PARTS)])  28.6 us
    all_to_all x6, starting transfers between devices, swap(): return lax.all_to_all(x, axis, split_axis=0, concat_axis=0, tiled=True)  26.7 us
    ppermute x4, starting transfers between devices, shift_left(): return lax.ppermute(x, 'wa', [(i + 1, i) for i in range(count - 1)])  26.2 us
    all_to_all x6, waiting for transfers between devices, swap(): return lax.all_to_all(x, axis, split_axis=0, concat_axis=0, tiled=True)  20.3 us
    pallas_call x7, Pallas kernels, move(): pl.pallas_call(kernel, in_specs=[pl.BlockSpec(memory_space=pltpu.VMEM)] *...  18.8 us
    all_to_all x1, blocking collectives, swap(): return lax.all_to_all(x, axis, split_axis=0, concat_axis=0, tiled=True)  15.6 us
    pallas_call x2, Pallas kernels, temporal_call(): pl.pallas_call(kernel, grid=(group, tokens // rows), in_specs=[spec(a.sha...  15.2 us
  transfers between devices with their start and end apart: 26, of which 3 were waited for; matrix products, arithmetic and copies ran while one was open for 0% of the time, Pallas kernels for 34%

profile of v2, /device:TPU:8, one launch (start us, length us, event | category | flops | bytes accessed | tf_op | source)
XLA Modules:
  0.0 238.1 jit_solution(17122135703856477337)
XLA Ops:
  0.6 3.4 %shard_map.101 = (bf16[3,3,256,128]{3,2,1,0:T(8,128)(2,1)}, bf16[3,3,256,128]{3,2,1,0:T(8,128)(2,1)}, bf16[3,3,256,128]{3,2,1,0:T(8,128)(2,1)}, bf16[3,3,256,128]{3,2,1,0:T(8,128)(2,1)}) custom-call(bf16[256,1536]{1,0:T(8,128)(2,1)} %bitcast.15, bf16[256,1536]{1,0:T(8,128)(2,1)} %bitcast.16, bf16[256,1536]{1,0:T(8,128)(2,1)} %bitcast.17), custom_call_target="tpu_custom_call" | custom-call | flops 100000000 | bytes 1024 | tf_op jit(solution)/shard_map/pallas_call | solution.py:49
  4.0 2.8 %shard_map.102 = bf16[4,3,2,256,128]{4,3,2,1,0:T(8,128)(2,1)} custom-call(bf16[256,1536]{1,0:T(8,128)(2,1)} %bitcast.13, bf16[256,1536]{1,0:T(8,128)(2,1)} %bitcast.14, bf16[3,3,256,128]{3,2,1,0:T(8,128)(2,1)} %get-tuple-element.40.refs_2_), custom_call_target="tpu_custom_call" | custom-call | flops 100000000 | bytes 1024 | tf_op jit(solution)/shard_map/pallas_call | solution.py:49
  6.9 4.4 %all-to-all-start = ((bf16[4,3,2,256,128]{4,3,2,1,0:T(8,128)(2,1)}), bf16[4,3,2,256,128]{4,3,2,1,0:T(8,128)(2,1)S(1)}, u32[]{:S(2)}, u32[]{:S(2)}) async-start(bf16[4,3,2,256,128]{4,3,2,1,0:T(8,128)(2,1)} %shard_map.102), calls=%async_computation | async-start | bytes 3145728 | tf_op jit(solution)/shard_map/all_to_all | solution.py:379
  11.3 2.3 collective-permute-start.3
  15.0 17.1 %all-to-all-done.refs_1_.kc_ref = bf16[4,3,2,256,128]{4,3,2,1,0:T(8,128)(2,1)S(1)} async-done(((bf16[4,3,2,256,128]{4,3,2,1,0:T(8,128)(2,1)}), bf16[4,3,2,256,128]{4,3,2,1,0:T(8,128)(2,1)S(1)}, u32[]{:S(2)}, u32[]{:S(2)}) %all-to-all-start) | async-done | bytes 1572896 | tf_op jit(solution)/shard_map/all_to_all | solution.py:379
  35.4 3.6 %all-to-all-start.1 = ((bf16[4,3,1,256,128]{4,3,2,1,0:T(8,128)(2,1)}), bf16[4,3,1,256,128]{4,3,2,1,0:T(8,128)(2,1)S(1)}, u32[]{:S(2)}, u32[]{:S(2)}) async-start(bf16[4,3,1,256,128]{4,3,2,1,0:T(8,128)(2,1)} %shard_map.103), calls=%async_computation.1 | async-start | bytes 1572864 | tf_op jit(solution)/shard_map/all_to_all | solution.py:379
  39.0 5.8 %collective-permute-start.1 = (bf16[4,3,2,256,128]{4,3,2,1,0:T(8,128)(2,1)S(1)}, bf16[4,3,2,256,128]{4,3,2,1,0:T(8,128)(2,1)}, u32[]{:S(2)}, u32[]{:S(2)}) collective-permute-start(bf16[4,3,2,256,128]{4,3,2,1,0:T(8,128)(2,1)S(1)} %copy-done.1), channel_id=1, source_target_pairs={{1,0},{2,1},{3,2},{4,3},{5,4},{6,5},{7,6},{9,8},{10,9},{11,10},{12... | collective-permute-start | bytes 4718600 | tf_op jit(solution)/shard_map/ppermute | solution.py:389
  47.6 6.5 %shard_map.104 = (bf16[3,1,256,128]{3,2,1,0:T(8,128)(2,1)}, bf16[3,1,256,128]{3,2,1,0:T(8,128)(2,1)}, bf16[3,1,256,128]{3,2,1,0:T(8,128)(2,1)}, bf16[3,1,256,128]{3,2,1,0:T(8,128)(2,1)}) custom-call(bf16[3,3,256,128]{3,2,1,0:T(8,128)(2,1)} %get-tuple-element.41.refs_0_, bf16[3,3,256,128]{3,2,1,0:T(8,128)(2,1)} %collective-permute-done.2.refs_1_, ...), custom_call_target="tpu_custom_call" | custom-call | flops 99999997952 | bytes 1024 | tf_op jit(solution)/shard_map/pallas_call | solution.py:366
  54.1 2.7 %collective-permute-start.6 = (bf16[3,1,256,128]{3,2,1,0:T(8,128)(2,1)}, bf16[3,1,256,128]{3,2,1,0:T(8,128)(2,1)S(1)}, u32[]{:S(2)}, u32[]{:S(2)}) collective-permute-start(bf16[3,1,256,128]{3,2,1,0:T(8,128)(2,1)} %get-tuple-element.46), channel_id=1, source_target_pairs={{0,64},{32,96},{64,0},{96,32},{1,65},{33,97},{65,1},{97,33},{2,66}... | collective-permute-start | bytes 589832 | tf_op jit(solution)/shard_map/ppermute | solution.py:136
  58.1 28.6 %collective-permute-done.6.refs_2_ = bf16[3,1,256,128]{3,2,1,0:T(8,128)(2,1)S(1)} collective-permute-done((bf16[3,1,256,128]{3,2,1,0:T(8,128)(2,1)}, bf16[3,1,256,128]{3,2,1,0:T(8,128)(2,1)S(1)}, u32[]{:S(2)}, u32[]{:S(2)}) %collective-permute-start.6) | collective-permute-done | bytes 196640 | tf_op jit(solution)/shard_map/ppermute | solution.py:136
  87.4 2.2 shard_map.105
  89.6 4.5 %all-to-all-start.2 = ((bf16[4,3,1,256,128]{4,3,2,1,0:T(8,128)(2,1)}), bf16[4,3,1,256,128]{4,3,2,1,0:T(8,128)(2,1)S(1)}, u32[]{:S(2)}, u32[]{:S(2)}) async-start(bf16[4,3,1,256,128]{4,3,2,1,0:T(8,128)(2,1)} %shard_map.105), calls=%async_computation.2 | async-start | bytes 1572864 | tf_op jit(solution)/shard_map/all_to_all | solution.py:379
  94.0 13.4 %shard_map.106 = (bf16[4,3,1,256,128]{4,3,2,1,0:T(8,128)(2,1)}, f32[3,4,1,256]{3,2,1,0:T(1,128)}) custom-call(f32[2]{0:T(128)} %add_select_fusion.bad_ref, bf16[4,3,1,256,128]{4,3,2,1,0:T(8,128)(2,1)} %copy-done.4, bf16[4,3,2,256,128]{4,3,2,1,0:T(8,128)(2,1)} %collective-permute-done.kl_ref, bf16[4,3,2,256,128]{4,3,2,1,0:T(8,128)(2,1)} %copy-done, ...), custom_call_target="tpu_custom_call" | custom-call | flops 99999997952 | bytes 1024 | tf_op jit(solution)/shard_map/pallas_call | solution.py:183
  107.5 4.8 %all-to-all-start.3 = ((bf16[4,3,1,256,128]{4,3,2,1,0:T(8,128)(2,1)}), bf16[4,3,1,256,128]{4,3,2,1,0:T(8,128)(2,1)S(1)}, u32[]{:S(2)}, u32[]{:S(2)}) async-start(bf16[4,3,1,256,128]{4,3,2,1,0:T(8,128)(2,1)} %get-tuple-element.48.o_ref), calls=%async_computation.3 | async-start | bytes 1572864 | tf_op jit(solution)/shard_map/all_to_all | solution.py:379
  112.3 10.5 %shard_map.107 = (bf16[4,1,1,256,128]{4,3,2,1,0:T(8,128)(2,1)}, bf16[4,1,2,256,128]{4,3,2,1,0:T(8,128)(2,1)}, bf16[4,1,2,256,128]{4,3,2,1,0:T(8,128)(2,1)}, bf16[4,1,2,256,128]{4,3,2,1,0:T(8,128)(2,1)}) custom-call(f32[2]{0:T(128)} %add_select_fusion.bad_ref, bf16[4,3,1,256,128]{4,3,2,1,0:T(8,128)(2,1)} %copy-done.4, ...), custom_call_target="tpu_custom_call" | custom-call | flops 99999997952 | bytes 1024 | tf_op jit(solution)/shard_map/pallas_call | solution.py:260
  124.7 8.3 %collective-permute-start.9 = (bf16[4,1,2,256,128]{4,3,2,1,0:T(8,128)(2,1)}, bf16[4,1,2,256,128]{4,3,2,1,0:T(8,128)(2,1)S(1)}, u32[]{:S(2)}, u32[]{:S(2)}) collective-permute-start(bf16[4,1,2,256,128]{4,3,2,1,0:T(8,128)(2,1)} %get-tuple-element.53), channel_id=1, source_target_pairs={{1,0},{2,1},{3,2},{4,3},{5,4},{6,5},{7,6},{9,8},{10,9},{11,10},{12... | collective-permute-start | bytes 1572872 | tf_op jit(solution)/shard_map/ppermute | solution.py:389
  137.0 2.5 %collective-permute-start.14 = (bf16[3,1,256,128]{3,2,1,0:T(8,128)(2,1)}, bf16[3,1,256,128]{3,2,1,0:T(8,128)(2,1)S(1)}, u32[]{:S(2)}, u32[]{:S(2)}) collective-permute-start(bf16[3,1,256,128]{3,2,1,0:T(8,128)(2,1)} %get-tuple-element.61), channel_id=1, source_target_pairs={{0,96},{32,64},{64,32},{96,0},{1,97},{33,65},{65,33},{97,1},{2,98}... | collective-permute-start | bytes 589832 | tf_op jit(solution)/shard_map/ppermute | solution.py:136
  139.6 10.5 %shard_map.109 = (bf16[4,1,1,256,128]{4,3,2,1,0:T(8,128)(2,1)}, bf16[4,1,2,256,128]{4,3,2,1,0:T(8,128)(2,1)}, bf16[4,1,2,256,128]{4,3,2,1,0:T(8,128)(2,1)}, bf16[4,1,2,256,128]{4,3,2,1,0:T(8,128)(2,1)}) custom-call(f32[2]{0:T(128)} %add_select_fusion.bad_ref, bf16[4,3,1,256,128]{4,3,2,1,0:T(8,128)(2,1)} %copy-done.4, ...), custom_call_target="tpu_custom_call" | custom-call | flops 99999997952 | bytes 1024 | tf_op jit(solution)/shard_map/pallas_call | solution.py:260
  152.1 6.0 %collective-permute-start.11 = (bf16[4,1,2,256,128]{4,3,2,1,0:T(8,128)(2,1)}, bf16[4,1,2,256,128]{4,3,2,1,0:T(8,128)(2,1)}, u32[]{:S(2)}, u32[]{:S(2)}) collective-permute-start(bf16[4,1,2,256,128]{4,3,2,1,0:T(8,128)(2,1)} %get-tuple-element.58), channel_id=1, source_target_pairs={{1,0},{2,1},{3,2},{4,3},{5,4},{6,5},{7,6},{9,8},{10,9},{11,10},{12... | collective-permute-start | bytes 1572872 | tf_op jit(solution)/shard_map/ppermute | solution.py:389
  158.1 3.6 %shard_map.110.refs_8_ = bf16[4,1,3,256,128]{4,3,2,1,0:T(8,128)(2,1)} custom-call(bf16[4,1,1,256,128]{4,3,2,1,0:T(8,128)(2,1)} %get-tuple-element.50.dq_ref, bf16[4,1,2,256,128]{4,3,2,1,0:T(8,128)(2,1)} %get-tuple-element.51.own_ref, bf16[4,1,2,256,128]{4,3,2,1,0:T(8,128)(2,1)} %copy-done.8, bf16[4,1,2,256,128]{4,3,2,1,0:T(8,128)(2,1)} %copy-done.9, ...), custom_call_target="tpu_custom_call" | custom-call | flops 100000000 | bytes 1024 | tf_op jit(solution)/shard_map/pallas_call | solution.py:293
  161.7 4.6 %all-to-all-start.4 = ((bf16[4,1,3,256,128]{4,3,2,1,0:T(8,128)(2,1)}), bf16[4,1,3,256,128]{4,3,2,1,0:T(8,128)(2,1)}, u32[]{:S(2)}, u32[]{:S(2)}) async-start(bf16[4,1,3,256,128]{4,3,2,1,0:T(8,128)(2,1)} %shard_map.110.refs_8_), calls=%async_computation.4 | async-start | bytes 1572864 | tf_op jit(solution)/shard_map/all_to_all | solution.py:379
  167.8 8.7 %shard_map.111 = (bf16[3,2,256,128]{3,2,1,0:T(8,128)(2,1)}, bf16[3,2,256,128]{3,2,1,0:T(8,128)(2,1)}, bf16[3,2,256,128]{3,2,1,0:T(8,128)(2,1)}, bf16[3,2,256,128]{3,2,1,0:T(8,128)(2,1)}) custom-call(bf16[3,3,256,128]{3,2,1,0:T(8,128)(2,1)} %get-tuple-element.41.refs_0_, bf16[3,3,256,128]{3,2,1,0:T(8,128)(2,1)} %collective-permute-done.2.refs_1_, ...), custom_call_target="tpu_custom_call" | custom-call | flops 99999997952 | bytes 1024 | tf_op jit(solution)/shard_map/pallas_call | solution.py:366
  177.8 2.2 collective-permute-start.19
  180.0 10.5 %shard_map.112 = (bf16[4,1,1,256,128]{4,3,2,1,0:T(8,128)(2,1)}, bf16[4,1,2,256,128]{4,3,2,1,0:T(8,128)(2,1)}, bf16[4,1,2,256,128]{4,3,2,1,0:T(8,128)(2,1)}, bf16[4,1,2,256,128]{4,3,2,1,0:T(8,128)(2,1)}) custom-call(f32[2]{0:T(128)} %add_select_fusion.bad_ref, bf16[4,3,1,256,128]{4,3,2,1,0:T(8,128)(2,1)} %copy-done.4, ...), custom_call_target="tpu_custom_call" | custom-call | flops 99999997952 | bytes 1024 | tf_op jit(solution)/shard_map/pallas_call | solution.py:260
  192.4 6.0 %collective-permute-start.16 = (bf16[4,1,2,256,128]{4,3,2,1,0:T(8,128)(2,1)}, bf16[4,1,2,256,128]{4,3,2,1,0:T(8,128)(2,1)S(1)}, u32[]{:S(2)}, u32[]{:S(2)}) collective-permute-start(bf16[4,1,2,256,128]{4,3,2,1,0:T(8,128)(2,1)} %get-tuple-element.66), channel_id=1, source_target_pairs={{1,0},{2,1},{3,2},{4,3},{5,4},{6,5},{7,6},{9,8},{10,9},{11,10},{12... | collective-permute-start | bytes 1572872 | tf_op jit(solution)/shard_map/ppermute | solution.py:389
  198.5 3.6 %shard_map.113 = bf16[4,1,3,256,128]{4,3,2,1,0:T(8,128)(2,1)} custom-call(bf16[4,1,1,256,128]{4,3,2,1,0:T(8,128)(2,1)} %get-tuple-element.55._.dq_ref, bf16[4,1,2,256,128]{4,3,2,1,0:T(8,128)(2,1)} %get-tuple-element.56.own_ref, bf16[4,1,2,256,128]{4,3,2,1,0:T(8,128)(2,1)} %collective-permute-done.10.a_ref, ...), custom_call_target="tpu_custom_call" | custom-call | flops 100000000 | bytes 1024 | tf_op jit(solution)/shard_map/pallas_call | solution.py:293
  202.1 4.8 %all-to-all-start.5 = ((bf16[4,1,3,256,128]{4,3,2,1,0:T(8,128)(2,1)}), bf16[4,1,3,256,128]{4,3,2,1,0:T(8,128)(2,1)S(1)}, u32[]{:S(2)}, u32[]{:S(2)}) async-start(bf16[4,1,3,256,128]{4,3,2,1,0:T(8,128)(2,1)} %shard_map.113), calls=%async_computation.5 | async-start | bytes 1572864 | tf_op jit(solution)/shard_map/all_to_all | solution.py:379
  208.6 2.8 %shard_map.114 = (bf16[256,1536]{1,0:T(8,128)(2,1)}, bf16[256,1536]{1,0:T(8,128)(2,1)}) custom-call(bf16[3,2,256,128]{3,2,1,0:T(8,128)(2,1)} %get-tuple-element.62._.refs_0_, bf16[3,2,256,128]{3,2,1,0:T(8,128)(2,1)} %copy-done.15, bf16[3,2,256,128]{3,2,1,0:T(8,128)(2,1)} %copy-done.16, bf16[3,2,256,128]{3,2,1,0:T(8,128)(2,1)} %copy-done.17), custom_call_target="tpu_custom_call" | custom-call | flops 99999997952 | bytes 1024 | tf_op jit(solution)/shard_map/pallas_call | solution.py:49
  212.3 3.6 %shard_map.115 = bf16[4,1,3,256,128]{4,3,2,1,0:T(8,128)(2,1)} custom-call(bf16[4,1,1,256,128]{4,3,2,1,0:T(8,128)(2,1)} %get-tuple-element.63._.dq_ref, bf16[4,1,2,256,128]{4,3,2,1,0:T(8,128)(2,1)} %get-tuple-element.64.own_ref, bf16[4,1,2,256,128]{4,3,2,1,0:T(8,128)(2,1)} %copy-done.7, bf16[4,1,2,256,128]{4,3,2,1,0:T(8,128)(2,1)} %copy-done.10, ...), custom_call_target="tpu_custom_call" | custom-call | flops 100000000 | bytes 1024 | tf_op jit(solution)/shard_map/pallas_call | solution.py:293
  215.9 3.2 %all-to-all-done.5.refs_1_ = bf16[4,1,3,256,128]{4,3,2,1,0:T(8,128)(2,1)S(1)} async-done(((bf16[4,1,3,256,128]{4,3,2,1,0:T(8,128)(2,1)}), bf16[4,1,3,256,128]{4,3,2,1,0:T(8,128)(2,1)S(1)}, u32[]{:S(2)}, u32[]{:S(2)}) %all-to-all-start.5) | async-done | bytes 786464 | tf_op jit(solution)/shard_map/all_to_all | solution.py:379
  219.1 15.6 %all_to_all.35.refs_2_ = bf16[4,1,3,256,128]{4,3,2,1,0:T(8,128)(2,1)} all-to-all(bf16[4,1,3,256,128]{4,3,2,1,0:T(8,128)(2,1)} %shard_map.115), channel_id=1, replica_groups=mesh['tm'=4,'ha'=4,'wa'=8] {'ha'}, dimensions={0} | all-to-all | bytes 1572864 | tf_op jit(solution)/shard_map/all_to_all | solution.py:379
  234.7 3.4 %shard_map.116 = (bf16[256,1536]{1,0:T(8,128)(2,1)}, bf16[256,1536]{1,0:T(8,128)(2,1)}, bf16[256,1536]{1,0:T(8,128)(2,1)}) custom-call(bf16[4,1,3,256,128]{4,3,2,1,0:T(8,128)(2,1)} %all-to-all-done.4.refs_0_, bf16[4,1,3,256,128]{4,3,2,1,0:T(8,128)(2,1)} %copy-done.3, bf16[4,1,3,256,128]{4,3,2,1,0:T(8,128)(2,1)} %all_to_all.35.refs_2_), custom_call_target="tpu_custom_call" | custom-call | flops 100000000 | bytes 1024 | tf_op jit(solution)/shard_map/pallas_call | solution.py:49
  (80 shorter events, 24.6 us)
Async XLA Ops:
  6.9 6.8 %copy-start.6 = (bf16[3,3,256,128]{3,2,1,0:T(8,128)(2,1)S(1)}, bf16[3,3,256,128]{3,2,1,0:T(8,128)(2,1)}, u32[]{:S(2)}) copy-start(bf16[3,3,256,128]{3,2,1,0:T(8,128)(2,1)} %get-tuple-element.40.refs_2_) | copy-start | bytes 1769476
  6.9 25.1 %all-to-all-start = ((bf16[4,3,2,256,128]{4,3,2,1,0:T(8,128)(2,1)}), bf16[4,3,2,256,128]{4,3,2,1,0:T(8,128)(2,1)S(1)}, u32[]{:S(2)}, u32[]{:S(2)}) async-start(bf16[4,3,2,256,128]{4,3,2,1,0:T(8,128)(2,1)} %shard_map.102), calls=%async_computation | async-start | bytes 3145728 | tf_op jit(solution)/shard_map/all_to_all | solution.py:379
  11.3 35.5 %collective-permute-start.3 = (bf16[3,3,256,128]{3,2,1,0:T(8,128)(2,1)}, bf16[3,3,256,128]{3,2,1,0:T(8,128)(2,1)S(1)}, u32[]{:S(2)}, u32[]{:S(2)}) collective-permute-start(bf16[3,3,256,128]{3,2,1,0:T(8,128)(2,1)} %get-tuple-element.42), channel_id=1, source_target_pairs={{0,64},{32,96},{64,0},{96,32},{1,65},{33,97},{65,1},{97,33},{2,66}... | collective-permute-start | bytes 1769480 | tf_op jit(solution)/shard_map/ppermute | solution.py:136
  13.6 33.2 %collective-permute-start.4 = (bf16[3,3,256,128]{3,2,1,0:T(8,128)(2,1)}, bf16[3,3,256,128]{3,2,1,0:T(8,128)(2,1)}, u32[]{:S(2)}, u32[]{:S(2)}) collective-permute-start(bf16[3,3,256,128]{3,2,1,0:T(8,128)(2,1)} %get-tuple-element.43), channel_id=1, source_target_pairs={{0,96},{32,64},{64,32},{96,0},{1,97},{33,65},{65,33},{97,1},{2,98}... | collective-permute-start | bytes 1769480 | tf_op jit(solution)/shard_map/ppermute | solution.py:136
  13.7 33.1 %collective-permute-start.2 = (bf16[3,3,256,128]{3,2,1,0:T(8,128)(2,1)S(1)}, bf16[3,3,256,128]{3,2,1,0:T(8,128)(2,1)}, u32[]{:S(2)}, u32[]{:S(2)}) collective-permute-start(bf16[3,3,256,128]{3,2,1,0:T(8,128)(2,1)S(1)} %copy-done.6), channel_id=1, source_target_pairs={{0,32},{32,0},{64,96},{96,64},{1,33},{33,1},{65,97},{97,65},{2,34}... | collective-permute-start | bytes 1769480 | tf_op jit(solution)/shard_map/ppermute | solution.py:136
  35.4 54.2 %all-to-all-start.1 = ((bf16[4,3,1,256,128]{4,3,2,1,0:T(8,128)(2,1)}), bf16[4,3,1,256,128]{4,3,2,1,0:T(8,128)(2,1)S(1)}, u32[]{:S(2)}, u32[]{:S(2)}) async-start(bf16[4,3,1,256,128]{4,3,2,1,0:T(8,128)(2,1)} %shard_map.103), calls=%async_computation.1 | async-start | bytes 1572864 | tf_op jit(solution)/shard_map/all_to_all | solution.py:379
  39.0 55.0 %collective-permute-start.1 = (bf16[4,3,2,256,128]{4,3,2,1,0:T(8,128)(2,1)S(1)}, bf16[4,3,2,256,128]{4,3,2,1,0:T(8,128)(2,1)}, u32[]{:S(2)}, u32[]{:S(2)}) collective-permute-start(bf16[4,3,2,256,128]{4,3,2,1,0:T(8,128)(2,1)S(1)} %copy-done.1), channel_id=1, source_target_pairs={{1,0},{2,1},{3,2},{4,3},{5,4},{6,5},{7,6},{9,8},{10,9},{11,10},{12... | collective-permute-start | bytes 4718600 | tf_op jit(solution)/shard_map/ppermute | solution.py:389
  44.8 49.2 %collective-permute-start = (bf16[4,3,2,256,128]{4,3,2,1,0:T(8,128)(2,1)S(1)}, bf16[4,3,2,256,128]{4,3,2,1,0:T(8,128)(2,1)}, u32[]{:S(2)}, u32[]{:S(2)}) collective-permute-start(bf16[4,3,2,256,128]{4,3,2,1,0:T(8,128)(2,1)S(1)} %copy-done.1), channel_id=1, source_target_pairs={{0,1},{1,2},{2,3},{3,4},{4,5},{5,6},{6,7},{8,9},{9,10},{10,11},{11... | collective-permute-start | bytes 4718600 | tf_op jit(solution)/shard_map/ppermute | solution.py:384
  54.1 4.0 %collective-permute-start.5 = (bf16[3,1,256,128]{3,2,1,0:T(8,128)(2,1)}, bf16[3,1,256,128]{3,2,1,0:T(8,128)(2,1)S(1)}, u32[]{:S(2)}, u32[]{:S(2)}) collective-permute-start(bf16[3,1,256,128]{3,2,1,0:T(8,128)(2,1)} %get-tuple-element.45), channel_id=1, source_target_pairs={{0,32},{32,0},{64,96},{96,64},{1,33},{33,1},{65,97},{97,65},{2,34}... | collective-permute-start | bytes 589832 | tf_op jit(solution)/shard_map/ppermute | solution.py:136
  54.1 32.5 %collective-permute-start.6 = (bf16[3,1,256,128]{3,2,1,0:T(8,128)(2,1)}, bf16[3,1,256,128]{3,2,1,0:T(8,128)(2,1)S(1)}, u32[]{:S(2)}, u32[]{:S(2)}) collective-permute-start(bf16[3,1,256,128]{3,2,1,0:T(8,128)(2,1)} %get-tuple-element.46), channel_id=1, source_target_pairs={{0,64},{32,96},{64,0},{96,32},{1,65},{33,97},{65,1},{97,33},{2,66}... | collective-permute-start | bytes 589832 | tf_op jit(solution)/shard_map/ppermute | solution.py:136
  56.8 29.8 %collective-permute-start.7 = (bf16[3,1,256,128]{3,2,1,0:T(8,128)(2,1)}, bf16[3,1,256,128]{3,2,1,0:T(8,128)(2,1)S(1)}, u32[]{:S(2)}, u32[]{:S(2)}) collective-permute-start(bf16[3,1,256,128]{3,2,1,0:T(8,128)(2,1)} %get-tuple-element.47), channel_id=1, source_target_pairs={{0,96},{32,64},{64,32},{96,0},{1,97},{33,65},{65,33},{97,1},{2,98}... | collective-permute-start | bytes 589832 | tf_op jit(solution)/shard_map/ppermute | solution.py:136
  58.1 28.6 %copy-start.11 = (bf16[3,1,256,128]{3,2,1,0:T(8,128)(2,1)}, bf16[3,1,256,128]{3,2,1,0:T(8,128)(2,1)S(1)}, u32[]{:S(2)}) copy-start(bf16[3,1,256,128]{3,2,1,0:T(8,128)(2,1)S(1)} %collective-permute-done.5.refs_1_) | copy-start | bytes 589828
  89.6 17.9 %all-to-all-start.2 = ((bf16[4,3,1,256,128]{4,3,2,1,0:T(8,128)(2,1)}), bf16[4,3,1,256,128]{4,3,2,1,0:T(8,128)(2,1)S(1)}, u32[]{:S(2)}, u32[]{:S(2)}) async-start(bf16[4,3,1,256,128]{4,3,2,1,0:T(8,128)(2,1)} %shard_map.105), calls=%async_computation.2 | async-start | bytes 1572864 | tf_op jit(solution)/shard_map/all_to_all | solution.py:379
  107.4 4.8 %copy-start.5 = (bf16[4,3,1,256,128]{4,3,2,1,0:T(8,128)(2,1)}, bf16[4,3,1,256,128]{4,3,2,1,0:T(8,128)(2,1)S(1)}, u32[]{:S(2)}) copy-start(bf16[4,3,1,256,128]{4,3,2,1,0:T(8,128)(2,1)S(1)} %all-to-all-done.2.do_ref) | copy-start | bytes 2359300
  107.5 25.5 %all-to-all-start.3 = ((bf16[4,3,1,256,128]{4,3,2,1,0:T(8,128)(2,1)}), bf16[4,3,1,256,128]{4,3,2,1,0:T(8,128)(2,1)S(1)}, u32[]{:S(2)}, u32[]{:S(2)}) async-start(bf16[4,3,1,256,128]{4,3,2,1,0:T(8,128)(2,1)} %get-tuple-element.48.o_ref), calls=%async_computation.3 | async-start | bytes 1572864 | tf_op jit(solution)/shard_map/all_to_all | solution.py:379
  122.8 27.3 %collective-permute-start.8 = (bf16[4,1,2,256,128]{4,3,2,1,0:T(8,128)(2,1)}, bf16[4,1,2,256,128]{4,3,2,1,0:T(8,128)(2,1)S(1)}, u32[]{:S(2)}, u32[]{:S(2)}) collective-permute-start(bf16[4,1,2,256,128]{4,3,2,1,0:T(8,128)(2,1)} %get-tuple-element.52), channel_id=1, source_target_pairs={{0,1},{1,2},{2,3},{3,4},{4,5},{5,6},{6,7},{8,9},{9,10},{10,11},{11... | collective-permute-start | bytes 1572872 | tf_op jit(solution)/shard_map/ppermute | solution.py:384
  124.7 27.3 %collective-permute-start.9 = (bf16[4,1,2,256,128]{4,3,2,1,0:T(8,128)(2,1)}, bf16[4,1,2,256,128]{4,3,2,1,0:T(8,128)(2,1)S(1)}, u32[]{:S(2)}, u32[]{:S(2)}) collective-permute-start(bf16[4,1,2,256,128]{4,3,2,1,0:T(8,128)(2,1)} %get-tuple-element.53), channel_id=1, source_target_pairs={{1,0},{2,1},{3,2},{4,3},{5,4},{6,5},{7,6},{9,8},{10,9},{11,10},{12... | collective-permute-start | bytes 1572872 | tf_op jit(solution)/shard_map/ppermute | solution.py:389
  136.0 30.3 %collective-permute-start.12 = (bf16[3,1,256,128]{3,2,1,0:T(8,128)(2,1)}, bf16[3,1,256,128]{3,2,1,0:T(8,128)(2,1)S(1)}, u32[]{:S(2)}, u32[]{:S(2)}) collective-permute-start(bf16[3,1,256,128]{3,2,1,0:T(8,128)(2,1)} %get-tuple-element.59), channel_id=1, source_target_pairs={{0,32},{32,0},{64,96},{96,64},{1,33},{33,1},{65,97},{97,65},{2,34}... | collective-permute-start | bytes 589832 | tf_op jit(solution)/shard_map/ppermute | solution.py:136
  136.7 29.6 %collective-permute-start.13 = (bf16[3,1,256,128]{3,2,1,0:T(8,128)(2,1)}, bf16[3,1,256,128]{3,2,1,0:T(8,128)(2,1)S(1)}, u32[]{:S(2)}, u32[]{:S(2)}) collective-permute-start(bf16[3,1,256,128]{3,2,1,0:T(8,128)(2,1)} %get-tuple-element.60), channel_id=1, source_target_pairs={{0,64},{32,96},{64,0},{96,32},{1,65},{33,97},{65,1},{97,33},{2,66}... | collective-permute-start | bytes 589832 | tf_op jit(solution)/shard_map/ppermute | solution.py:136
  137.0 29.3 %collective-permute-start.14 = (bf16[3,1,256,128]{3,2,1,0:T(8,128)(2,1)}, bf16[3,1,256,128]{3,2,1,0:T(8,128)(2,1)S(1)}, u32[]{:S(2)}, u32[]{:S(2)}) collective-permute-start(bf16[3,1,256,128]{3,2,1,0:T(8,128)(2,1)} %get-tuple-element.61), channel_id=1, source_target_pairs={{0,96},{32,64},{64,32},{96,0},{1,97},{33,65},{65,33},{97,1},{2,98}... | collective-permute-start | bytes 589832 | tf_op jit(solution)/shard_map/ppermute | solution.py:136
  150.1 8.0 %copy-start.8 = (bf16[4,1,2,256,128]{4,3,2,1,0:T(8,128)(2,1)}, bf16[4,1,2,256,128]{4,3,2,1,0:T(8,128)(2,1)S(1)}, u32[]{:S(2)}) copy-start(bf16[4,1,2,256,128]{4,3,2,1,0:T(8,128)(2,1)S(1)} %collective-permute-done.8.a_ref) | copy-start | bytes 1572868
  150.1 40.4 %collective-permute-start.10 = (bf16[4,1,2,256,128]{4,3,2,1,0:T(8,128)(2,1)}, bf16[4,1,2,256,128]{4,3,2,1,0:T(8,128)(2,1)}, u32[]{:S(2)}, u32[]{:S(2)}) collective-permute-start(bf16[4,1,2,256,128]{4,3,2,1,0:T(8,128)(2,1)} %get-tuple-element.57), channel_id=1, source_target_pairs={{0,1},{1,2},{2,3},{3,4},{4,5},{5,6},{6,7},{8,9},{9,10},{10,11},{11... | collective-permute-start | bytes 1572872 | tf_op jit(solution)/shard_map/ppermute | solution.py:384
  152.1 6.1 %copy-start.9 = (bf16[4,1,2,256,128]{4,3,2,1,0:T(8,128)(2,1)}, bf16[4,1,2,256,128]{4,3,2,1,0:T(8,128)(2,1)S(1)}, u32[]{:S(2)}) copy-start(bf16[4,1,2,256,128]{4,3,2,1,0:T(8,128)(2,1)S(1)} %collective-permute-done.9.b_ref) | copy-start | bytes 1572868
  152.1 40.4 %collective-permute-start.11 = (bf16[4,1,2,256,128]{4,3,2,1,0:T(8,128)(2,1)}, bf16[4,1,2,256,128]{4,3,2,1,0:T(8,128)(2,1)}, u32[]{:S(2)}, u32[]{:S(2)}) collective-permute-start(bf16[4,1,2,256,128]{4,3,2,1,0:T(8,128)(2,1)} %get-tuple-element.58), channel_id=1, source_target_pairs={{1,0},{2,1},{3,2},{4,3},{5,4},{6,5},{7,6},{9,8},{10,9},{11,10},{12... | collective-permute-start | bytes 1572872 | tf_op jit(solution)/shard_map/ppermute | solution.py:389
  161.7 40.4 %all-to-all-start.4 = ((bf16[4,1,3,256,128]{4,3,2,1,0:T(8,128)(2,1)}), bf16[4,1,3,256,128]{4,3,2,1,0:T(8,128)(2,1)}, u32[]{:S(2)}, u32[]{:S(2)}) async-start(bf16[4,1,3,256,128]{4,3,2,1,0:T(8,128)(2,1)} %shard_map.110.refs_8_), calls=%async_computation.4 | async-start | bytes 1572864 | tf_op jit(solution)/shard_map/all_to_all | solution.py:379
  176.5 30.4 %collective-permute-start.17 = (bf16[3,2,256,128]{3,2,1,0:T(8,128)(2,1)}, bf16[3,2,256,128]{3,2,1,0:T(8,128)(2,1)S(1)}, u32[]{:S(2)}, u32[]{:S(2)}) collective-permute-start(bf16[3,2,256,128]{3,2,1,0:T(8,128)(2,1)} %get-tuple-element.67), channel_id=1, source_target_pairs={{0,32},{32,0},{64,96},{96,64},{1,33},{33,1},{65,97},{97,65},{2,34}... | collective-permute-start | bytes 1179656 | tf_op jit(solution)/shard_map/ppermute | solution.py:136
  176.6 30.3 %collective-permute-start.18 = (bf16[3,2,256,128]{3,2,1,0:T(8,128)(2,1)}, bf16[3,2,256,128]{3,2,1,0:T(8,128)(2,1)S(1)}, u32[]{:S(2)}, u32[]{:S(2)}) collective-permute-start(bf16[3,2,256,128]{3,2,1,0:T(8,128)(2,1)} %get-tuple-element.68), channel_id=1, source_target_pairs={{0,64},{32,96},{64,0},{96,32},{1,65},{33,97},{65,1},{97,33},{2,66}... | collective-permute-start | bytes 1179656 | tf_op jit(solution)/shard_map/ppermute | solution.py:136
  177.8 29.2 %collective-permute-start.19 = (bf16[3,2,256,128]{3,2,1,0:T(8,128)(2,1)}, bf16[3,2,256,128]{3,2,1,0:T(8,128)(2,1)S(1)}, u32[]{:S(2)}, u32[]{:S(2)}) collective-permute-start(bf16[3,2,256,128]{3,2,1,0:T(8,128)(2,1)} %get-tuple-element.69), channel_id=1, source_target_pairs={{0,96},{32,64},{64,32},{96,0},{1,97},{33,65},{65,33},{97,1},{2,98}... | collective-permute-start | bytes 1179656 | tf_op jit(solution)/shard_map/ppermute | solution.py:136
  190.5 20.8 %collective-permute-start.15 = (bf16[4,1,2,256,128]{4,3,2,1,0:T(8,128)(2,1)}, bf16[4,1,2,256,128]{4,3,2,1,0:T(8,128)(2,1)S(1)}, u32[]{:S(2)}, u32[]{:S(2)}) collective-permute-start(bf16[4,1,2,256,128]{4,3,2,1,0:T(8,128)(2,1)} %get-tuple-element.65), channel_id=1, source_target_pairs={{0,1},{1,2},{2,3},{3,4},{4,5},{5,6},{6,7},{8,9},{9,10},{10,11},{11... | collective-permute-start | bytes 1572872 | tf_op jit(solution)/shard_map/ppermute | solution.py:384
  192.4 18.9 %collective-permute-start.16 = (bf16[4,1,2,256,128]{4,3,2,1,0:T(8,128)(2,1)}, bf16[4,1,2,256,128]{4,3,2,1,0:T(8,128)(2,1)S(1)}, u32[]{:S(2)}, u32[]{:S(2)}) collective-permute-start(bf16[4,1,2,256,128]{4,3,2,1,0:T(8,128)(2,1)} %get-tuple-element.66), channel_id=1, source_target_pairs={{1,0},{2,1},{3,2},{4,3},{5,4},{6,5},{7,6},{9,8},{10,9},{11,10},{12... | collective-permute-start | bytes 1572872 | tf_op jit(solution)/shard_map/ppermute | solution.py:389
  202.1 17.0 %all-to-all-start.5 = ((bf16[4,1,3,256,128]{4,3,2,1,0:T(8,128)(2,1)}), bf16[4,1,3,256,128]{4,3,2,1,0:T(8,128)(2,1)S(1)}, u32[]{:S(2)}, u32[]{:S(2)}) async-start(bf16[4,1,3,256,128]{4,3,2,1,0:T(8,128)(2,1)} %shard_map.113), calls=%async_computation.5 | async-start | bytes 1572864 | tf_op jit(solution)/shard_map/all_to_all | solution.py:379
  219.1 15.6 %copy-start.3 = (bf16[4,1,3,256,128]{4,3,2,1,0:T(8,128)(2,1)}, bf16[4,1,3,256,128]{4,3,2,1,0:T(8,128)(2,1)S(1)}, u32[]{:S(2)}) copy-start(bf16[4,1,3,256,128]{4,3,2,1,0:T(8,128)(2,1)S(1)} %all-to-all-done.5.refs_1_) | copy-start | bytes 2359300
  (15 other events, 18.7 us)

commit v3 on v2

--- a/solution.py
+++ b/solution.py
@@ -27,7 +27,7 @@
 
 
 def params():
-    return pltpu.CompilerParams(vmem_limit_bytes=56 * 1024 * 1024)
+    return pltpu.CompilerParams(vmem_limit_bytes=63 * 1024 * 1024)
 
 
 def cost(microseconds):
@@ -79,7 +79,7 @@
     )[0]
 
 
-def pack_partners(arrays):
+def pack_partners(arrays, after=()):
     tokens = arrays[0].shape[0]
     cells = [(a, s, h) for s in range(PARTS) for h in range(GROUP) for a in range(len(arrays))]
     return move(
@@ -87,10 +87,11 @@
         [bf16(GROUP, len(arrays), tokens, HEAD_DIM)] * PARTS,
         lambda me: [(a, columns(me ^ s, h), s, (h, a)) for a, s, h in cells],
         "tm",
-    )
-
-
-def unpack_partners(chunks):
+        after,
+    )
+
+
+def unpack_partners(chunks, after):
     _, count, tokens, _ = chunks[0].shape
     cells = [(a, s, h) for s in range(PARTS) for h in range(GROUP) for a in range(count)]
     return move(
@@ -98,6 +99,7 @@
         [bf16(tokens, HEADS * HEAD_DIM)] * count,
         lambda me: [(s, (h, a), a, columns(me ^ s, h)) for a, s, h in cells],
         "tm",
+        after,
         told=100,
     )
 
@@ -122,11 +124,14 @@
 
 def unpack_heads(blocks):
     count, tokens = blocks[0].shape[2:4]
+    heads = [(n, i) for n, block in enumerate(blocks) for i in range(block.shape[1])]
     cells = [(a, d, h) for h in range(GROUP) for d in range(PARTS) for a in range(count)]
     return move(
         blocks,
         [bf16(tokens, HEADS * HEAD_DIM)] * count,
-        lambda me: [(h, (d, 0, a), a, columns(d, h)) for a, d, h in cells],
+        lambda me: [
+            (heads[h][0], (d, heads[h][1], a), a, columns(d, h)) for a, d, h in cells
+        ],
     )
 
 
@@ -141,7 +146,7 @@
     return range(max(row - 1, 0), min(row + 2, ROWS))
 
 
-def forward_kernel(bad_ref, q_ref, kl_ref, kc_ref, kr_ref, o_ref, lse_ref):
+def forward_kernel(bad_ref, q_ref, kl_ref, kc_ref, kr_ref, _, o_ref, lse_ref):
     bads = (bad_ref[0], jnp.float32(0.0), bad_ref[1])
     sides = (kl_ref, kc_ref, kr_ref)
     for b in range(ROWS):
@@ -177,14 +182,15 @@
     return pl.BlockSpec((ROWS, 1, count, tokens, HEAD_DIM), lambda h: (0, h, 0, 0, 0))
 
 
-def attend_forward(bad, q, kv_left, kv, kv_right):
+def attend_forward(bad, q, kv_left, kv, kv_right, after):
     tokens = q.shape[3]
     group = q.shape[1]
     return pl.pallas_call(
         forward_kernel,
         grid=(group,),
         in_specs=[pl.BlockSpec(memory_space=pltpu.SMEM), column_spec(1, tokens)]
-        + [column_spec(2, tokens)] * 3,
+        + [column_spec(2, tokens)] * 3
+        + [pl.BlockSpec(memory_space=pl.ANY)],
         out_specs=[
             column_spec(1, tokens),
             pl.BlockSpec((1, ROWS, 1, tokens), lambda h: (h, 0, 0, 0)),
@@ -195,7 +201,7 @@
         ],
         cost_estimate=cost(100),
         compiler_params=params(),
-    )(bad, q, kv_left, kv, kv_right)
+    )(bad, q, kv_left, kv, kv_right, after)
 
 
 def backward_kernel(
@@ -207,14 +213,9 @@
     do_ref,
     o_ref,
     lse_ref,
-    _,
-    dq_ref,
-    dl_ref,
-    dc_ref,
-    dr_ref,
-    dqt_ref,
-    row_ref,
+    *rest,
 ):
+    dq_ref, dl_ref, dc_ref, dr_ref, dqt_ref, row_ref = rest[-6:]
     bads = (bad_ref[0], jnp.float32(0.0), bad_ref[1])
     sides = (kl_ref, kc_ref, kr_ref)
     outs = (dl_ref, dc_ref, dr_ref)
@@ -251,51 +252,50 @@
         dq_ref[b, 0, 0] = (dqt_ref[b] * SCALE).T.astype(jnp.bfloat16)
 
 
-def head_spec(head, count, tokens):
-    return pl.BlockSpec((ROWS, 1, count, tokens, HEAD_DIM), lambda i: (0, head, 0, 0, 0))
-
-
-def attend_backward(head, bad, q, kv_left, kv, kv_right, grad, mixed, lse, after):
+def heads_spec(first, count, tokens):
+    return pl.BlockSpec((ROWS, 1, count, tokens, HEAD_DIM), lambda i: (0, first + i, 0, 0, 0))
+
+
+def attend_backward(first, heads, bad, q, kv_left, kv, kv_right, grad, mixed, lse, after):
     tokens = q.shape[3]
     return pl.pallas_call(
         backward_kernel,
-        grid=(1,),
-        in_specs=[pl.BlockSpec(memory_space=pltpu.SMEM), head_spec(head, 1, tokens)]
-        + [head_spec(head, 2, tokens)] * 3
-        + [head_spec(head, 1, tokens)] * 2
-        + [pl.BlockSpec((1, ROWS, 1, tokens), lambda i: (head, 0, 0, 0))]
-        + [pl.BlockSpec(memory_space=pl.ANY)],
-        out_specs=[head_spec(0, 1, tokens)] + [head_spec(0, 2, tokens)] * 3,
-        out_shape=[bf16(ROWS, 1, 1, tokens, HEAD_DIM)]
-        + [bf16(ROWS, 1, 2, tokens, HEAD_DIM)] * 3,
+        grid=(heads,),
+        in_specs=[pl.BlockSpec(memory_space=pltpu.SMEM), heads_spec(first, 1, tokens)]
+        + [heads_spec(first, 2, tokens)] * 3
+        + [heads_spec(first, 1, tokens)] * 2
+        + [pl.BlockSpec((1, ROWS, 1, tokens), lambda i: (first + i, 0, 0, 0))]
+        + [pl.BlockSpec(memory_space=pl.ANY)] * len(after),
+        out_specs=[heads_spec(0, 1, tokens)] + [heads_spec(0, 2, tokens)] * 3,
+        out_shape=[bf16(ROWS, heads, 1, tokens, HEAD_DIM)]
+        + [bf16(ROWS, heads, 2, tokens, HEAD_DIM)] * 3,
         scratch_shapes=[
             pltpu.VMEM((ROWS, HEAD_DIM, tokens), jnp.float32),
             pltpu.VMEM((ROWS, 1, tokens), jnp.float32),
         ],
         cost_estimate=cost(100),
         compiler_params=params(),
-    )(bad, q, kv_left, kv, kv_right, grad, mixed, lse, after)
+    )(bad, q, kv_left, kv, kv_right, grad, mixed, lse, *after)
 
 
 def total_kernel(dq_ref, own_ref, a_ref, b_ref, _, out_ref):
-    out_ref[0, 0, 0] = dq_ref[0, 0, 0]
-    for t in range(2):
-        total = own_ref[0, 0, t].astype(jnp.float32) + a_ref[0, 0, t].astype(jnp.float32)
-        out_ref[0, 0, 1 + t] = (total + b_ref[0, 0, t].astype(jnp.float32)).astype(jnp.bfloat16)
+    for h in range(out_ref.shape[1]):
+        for r in range(ROWS):
+            out_ref[r, h, 0] = dq_ref[r, h, 0]
+            for t in range(2):
+                total = own_ref[r, h, t].astype(jnp.float32) + a_ref[r, h, t].astype(jnp.float32)
+                total = total + b_ref[r, h, t].astype(jnp.float32)
+                out_ref[r, h, 1 + t] = total.astype(jnp.bfloat16)
 
 
 def totals(dq, own, a, b, after):
-    tokens = dq.shape[3]
-
-    def spec(count):
-        return pl.BlockSpec((1, 1, count, tokens, HEAD_DIM), lambda i: (i, 0, 0, 0, 0))
-
+    heads, tokens = dq.shape[1], dq.shape[3]
+    vmem = pl.BlockSpec(memory_space=pltpu.VMEM)
     return pl.pallas_call(
         total_kernel,
-        grid=(ROWS,),
-        in_specs=[spec(1), spec(2), spec(2), spec(2), pl.BlockSpec(memory_space=pl.ANY)],
-        out_specs=spec(3),
-        out_shape=bf16(ROWS, 1, 3, tokens, HEAD_DIM),
+        in_specs=[vmem] * 4 + [pl.BlockSpec(memory_space=pl.ANY)],
+        out_specs=vmem,
+        out_shape=bf16(ROWS, heads, 3, tokens, HEAD_DIM),
         cost_estimate=cost(0.1),
         compiler_params=params(),
     )(dq, own, a, b, after)
@@ -399,33 +399,34 @@
     place = lax.axis_index("wa")
     bad = jnp.stack([place == 0, place == lax.axis_size("wa") - 1]).astype(jnp.float32) * BIG
 
-    pau_sent = pack_partners([flat(probes), flat(anchors), flat(upstream)])
-    pau = trade(pau_sent)
-    kv = swap(pack([flat(tile_keys), flat(values)], [pau_sent[1]]), "ha")
+    kv_sent = pack([flat(tile_keys), flat(values)])
+    kv = swap(kv_sent, "ha")
+    pau = trade(pack_partners([flat(probes), flat(anchors), flat(upstream)], [kv_sent]))
     kv_left = shift_right(kv)
     kv_right = shift_left(kv)
-    q = swap(pack([flat(queries)], [kv]), "ha")
-    grad_parts = trade(temporal_call(temporal_forward_kernel, pau, 1, 100))
-    grad = swap(join_partners(grad_parts), "ha")
-    mixed, lse = attend_forward(bad, q, kv_left, kv, kv_right)
+    forward_sent = temporal_call(temporal_forward_kernel, pau, 1, 100)
+    q = swap(pack([flat(queries)], forward_sent[:1]), "ha")
+    grad_sent = join_partners(trade(forward_sent))
+    grad = swap(grad_sent, "ha")
+    mixed, lse = attend_forward(bad, q, kv_left, kv, kv_right, grad_sent)
     mixed_sent = split_partners(swap(mixed, "ha"))
     mixed_parts = trade(mixed_sent)
-    def backward(head, after):
+    def backward(first, heads, after):
         dq, to_left, own, to_right = attend_backward(
-            head, bad, q, kv_left, kv, kv_right, grad, mixed, lse, after
+            first, heads, bad, q, kv_left, kv, kv_right, grad, mixed, lse, after
         )
         return dq, own, shift_right(to_right), shift_left(to_left)
 
-    zero = backward(0, q)
-    one = backward(1, mixed_sent[0])
-    summed = [totals(*zero, one[0])]
+    early = GROUP - 1
+    one = backward(0, early, [])
+    two = backward(early, 1, [mixed_sent[0], one[0]])
+    summed = [totals(*one, two[0])]
     times_sent = temporal_call(
-        temporal_backward_kernel, pau + mixed_parts, 2, 100, [summed[0]]
-    )
-    probe_grad, anchor_grad = unpack_partners(trade(times_sent))
-    two = backward(2, times_sent[0])
-    summed += [totals(*one, two[0]), totals(*two, probe_grad)]
-    summed = [swap(x, "ha") for x in summed]
+        temporal_backward_kernel, pau + mixed_parts, 2, 100, summed
+    )
+    summed = [swap(summed[0], "ha")]
+    summed.append(swap(totals(*two, summed[0]), "ha"))
+    probe_grad, anchor_grad = unpack_partners(trade(times_sent), [])
     query_grad, key_grad, value_grad = unpack_heads(summed)
     outs = (query_grad, key_grad, value_grad, probe_grad, anchor_grad)
     return tuple(x.reshape(shape) for x in outs)

time: 240 us -> 214 us (0.89)
  blocking collectives: 15.6 us -> 0 us
  waiting for transfers between devices: 48.9 us -> 61.1 us
  starting transfers between devices: 74.7 us -> 64.2 us
  Pallas kernels: 89.8 us -> 83 us
  local copies, waits for them, and re-layouts: 7.67 us -> 2.51 us
    all_to_all x1 -> x0, blocking collectives: 15.6 us -> none  [swap(): return lax.all_to_all(x, axis, split_axis=0, concat_axis=0, tiled=True)]
    ppermute x4 -> x3, starting transfers between devices: 26.2 us -> 17.9 us  [shift_left(): return lax.ppermute(x, 'wa', [(i + 1, i) for i in range(count - 1)])]
    ppermute x12, waiting for transfers between devices: 28.6 us -> 36.7 us  [trade(): lax.ppermute(chunks[s], 'tm', [(i, i ^ s) for i in range(PARTS)])]
    pallas_call x6 -> x4, Pallas kernels: 42.4 us -> 35.6 us  [the longest x2 29.6 us: attend_backward(): pl.pallas_call(backward_kernel, grid=(heads,), in_specs=[pl.BlockSpec(mem...]
    ppermute x4 -> x3, waiting for transfers between devices: 0.01 us -> 5.61 us  [shift_right(): return lax.ppermute(x, 'wa', [(i, i + 1) for i in range(count - 1)])]
    unnamed x42 -> x22, local copies, waits for them, and re-layouts: 7.67 us -> 2.51 us
    ppermute x4 -> x3, starting transfers between devices: 7.67 us -> 5.74 us  [shift_right(): return lax.ppermute(x, 'wa', [(i, i + 1) for i in range(count - 1)])]
  transfers between devices with their start and end apart: 26 -> 24, of which waited for: 3 -> 9; matrix products, arithmetic and copies ran while one was open for 0% -> 0% of each run, Pallas kernels for 34% -> 36%
where the time goes in v3:
time: 214 us; the launch traced here: 212 us
  Pallas kernels  83 us (39%)
  starting transfers between devices  64.2 us (30%)
  waiting for transfers between devices  61.1 us (29%)
  local copies, waits for them, and re-layouts  2.51 us (1%)
    ppermute x12, waiting for transfers between devices, trade(): lax.ppermute(chunks[s], 'tm', [(i, i ^ s) for i in range(PARTS)])  36.7 us
    pallas_call x2, Pallas kernels, attend_backward(): pl.pallas_call(backward_kernel, grid=(heads,), in_specs=[pl.BlockSpec(mem...  29.6 us
    all_to_all x6, starting transfers between devices, swap(): return lax.all_to_all(x, axis, split_axis=0, concat_axis=0, tiled=True)  27.1 us
    pallas_call x7, Pallas kernels, move(): pl.pallas_call(kernel, in_specs=[pl.BlockSpec(memory_space=pltpu.VMEM)] *...  18.8 us
    all_to_all x6, waiting for transfers between devices, swap(): return lax.all_to_all(x, axis, split_axis=0, concat_axis=0, tiled=True)  18.7 us
    ppermute x3, starting transfers between devices, shift_left(): return lax.ppermute(x, 'wa', [(i + 1, i) for i in range(count - 1)])  17.9 us
    pallas_call x2, Pallas kernels, temporal_call(): pl.pallas_call(kernel, grid=(group, tokens // rows), in_specs=[spec(a.sha...  15.2 us
    ppermute x12, starting transfers between devices, trade(): lax.ppermute(chunks[s], 'tm', [(i, i ^ s) for i in range(PARTS)])  13.5 us
  transfers between devices with their start and end apart: 24, of which 9 were waited for; matrix products, arithmetic and copies ran while one was open for 0% of the time, Pallas kernels for 36%

profile of v3, /device:TPU:8, one launch (start us, length us, event | category | flops | bytes accessed | tf_op | source)
XLA Modules:
  0.0 212.2 jit_solution(984814832426551212)
XLA Ops:
  0.6 2.8 %shard_map.101.refs_3_ = bf16[4,3,2,256,128]{4,3,2,1,0:T(8,128)(2,1)} custom-call(bf16[256,1536]{1,0:T(8,128)(2,1)} %bitcast.14, bf16[256,1536]{1,0:T(8,128)(2,1)} %bitcast.15), custom_call_target="tpu_custom_call" | custom-call | flops 100000000 | bytes 1024 | tf_op jit(solution)/shard_map/pallas_call | solution.py:49
  3.4 4.3 %all-to-all-start.1 = ((bf16[4,3,2,256,128]{4,3,2,1,0:T(8,128)(2,1)}), bf16[4,3,2,256,128]{4,3,2,1,0:T(8,128)(2,1)}, u32[]{:S(2)}, u32[]{:S(2)}) async-start(bf16[4,3,2,256,128]{4,3,2,1,0:T(8,128)(2,1)} %shard_map.101.refs_3_), calls=%async_computation.1 | async-start | bytes 3145728 | tf_op jit(solution)/shard_map/all_to_all | solution.py:379
  7.8 3.4 %shard_map.102 = (bf16[3,3,256,128]{3,2,1,0:T(8,128)(2,1)}, bf16[3,3,256,128]{3,2,1,0:T(8,128)(2,1)}, bf16[3,3,256,128]{3,2,1,0:T(8,128)(2,1)}, bf16[3,3,256,128]{3,2,1,0:T(8,128)(2,1)}) custom-call(bf16[256,1536]{1,0:T(8,128)(2,1)} %bitcast.16, bf16[256,1536]{1,0:T(8,128)(2,1)} %bitcast.17, bf16[256,1536]{1,0:T(8,128)(2,1)} %bitcast.18, ...), custom_call_target="tpu_custom_call" | custom-call | flops 100000000 | bytes 1024 | tf_op jit(solution)/shard_map/pallas_call | solution.py:49
  11.2 2.3 %collective-permute-start.1 = (bf16[3,3,256,128]{3,2,1,0:T(8,128)(2,1)}, bf16[3,3,256,128]{3,2,1,0:T(8,128)(2,1)}, u32[]{:S(2)}, u32[]{:S(2)}) collective-permute-start(bf16[3,3,256,128]{3,2,1,0:T(8,128)(2,1)} %get-tuple-element.38), channel_id=1, source_target_pairs={{0,64},{32,96},{64,0},{96,32},{1,65},{33,97},{65,1},{97,33},{2,66}... | collective-permute-start | bytes 1769480 | tf_op jit(solution)/shard_map/ppermute | solution.py:141
  14.6 14.3 %all-to-all-done.1.kc_ref = bf16[4,3,2,256,128]{4,3,2,1,0:T(8,128)(2,1)} async-done(((bf16[4,3,2,256,128]{4,3,2,1,0:T(8,128)(2,1)}), bf16[4,3,2,256,128]{4,3,2,1,0:T(8,128)(2,1)}, u32[]{:S(2)}, u32[]{:S(2)}) %all-to-all-start.1) | async-done | bytes 1572896 | tf_op jit(solution)/shard_map/all_to_all | solution.py:379
  28.8 5.8 %collective-permute-start.4 = (bf16[4,3,2,256,128]{4,3,2,1,0:T(8,128)(2,1)}, bf16[4,3,2,256,128]{4,3,2,1,0:T(8,128)(2,1)}, u32[]{:S(2)}, u32[]{:S(2)}) collective-permute-start(bf16[4,3,2,256,128]{4,3,2,1,0:T(8,128)(2,1)} %all-to-all-done.1.kc_ref), channel_id=1, source_target_pairs={{1,0},{2,1},{3,2},{4,3},{5,4},{6,5},{7,6},{9,8},{10,9},{11,10},{12... | collective-permute-start | bytes 4718600 | tf_op jit(solution)/shard_map/ppermute | solution.py:389
  36.6 4.4 %collective-permute-done.2.refs_3_ = bf16[3,3,256,128]{3,2,1,0:T(8,128)(2,1)} collective-permute-done((bf16[3,3,256,128]{3,2,1,0:T(8,128)(2,1)}, bf16[3,3,256,128]{3,2,1,0:T(8,128)(2,1)}, u32[]{:S(2)}, u32[]{:S(2)}) %collective-permute-start.2) | collective-permute-done | bytes 589856 | tf_op jit(solution)/shard_map/ppermute | solution.py:141
  41.0 6.5 %shard_map.103 = (bf16[3,1,256,128]{3,2,1,0:T(8,128)(2,1)}, bf16[3,1,256,128]{3,2,1,0:T(8,128)(2,1)}, bf16[3,1,256,128]{3,2,1,0:T(8,128)(2,1)}, bf16[3,1,256,128]{3,2,1,0:T(8,128)(2,1)}) custom-call(bf16[3,3,256,128]{3,2,1,0:T(8,128)(2,1)} %get-tuple-element.36.refs_0_, bf16[3,3,256,128]{3,2,1,0:T(8,128)(2,1)} %copy-done.5, ...), custom_call_target="tpu_custom_call" | custom-call | flops 99999997952 | bytes 1024 | tf_op jit(solution)/shard_map/pallas_call | solution.py:366
  49.6 4.9 %all-to-all-start = ((bf16[4,3,1,256,128]{4,3,2,1,0:T(8,128)(2,1)}), bf16[4,3,1,256,128]{4,3,2,1,0:T(8,128)(2,1)S(1)}, u32[]{:S(2)}, u32[]{:S(2)}) async-start(bf16[4,3,1,256,128]{4,3,2,1,0:T(8,128)(2,1)} %shard_map.104), calls=%async_computation | async-start | bytes 1572864 | tf_op jit(solution)/shard_map/all_to_all | solution.py:379
  54.8 2.3 %collective-permute-start.6 = (bf16[3,1,256,128]{3,2,1,0:T(8,128)(2,1)S(1)}, bf16[3,1,256,128]{3,2,1,0:T(8,128)(2,1)}, u32[]{:S(2)}, u32[]{:S(2)}) collective-permute-start(bf16[3,1,256,128]{3,2,1,0:T(8,128)(2,1)S(1)} %copy-done.9), channel_id=1, source_target_pairs={{0,64},{32,96},{64,0},{96,32},{1,65},{33,97},{65,1},{97,33},{2,66}... | collective-permute-start | bytes 589832 | tf_op jit(solution)/shard_map/ppermute | solution.py:141
  58.5 21.2 %collective-permute-done.6.refs_2_ = bf16[3,1,256,128]{3,2,1,0:T(8,128)(2,1)} collective-permute-done((bf16[3,1,256,128]{3,2,1,0:T(8,128)(2,1)S(1)}, bf16[3,1,256,128]{3,2,1,0:T(8,128)(2,1)}, u32[]{:S(2)}, u32[]{:S(2)}) %collective-permute-start.6) | collective-permute-done | bytes 196640 | tf_op jit(solution)/shard_map/ppermute | solution.py:141
  79.7 3.4 %collective-permute-done.7.refs_3_ = bf16[3,1,256,128]{3,2,1,0:T(8,128)(2,1)} collective-permute-done((bf16[3,1,256,128]{3,2,1,0:T(8,128)(2,1)S(1)}, bf16[3,1,256,128]{3,2,1,0:T(8,128)(2,1)}, u32[]{:S(2)}, u32[]{:S(2)}) %collective-permute-start.7) | collective-permute-done | bytes 196640 | tf_op jit(solution)/shard_map/ppermute | solution.py:141
  83.1 2.2 %shard_map.105._ = bf16[4,3,1,256,128]{4,3,2,1,0:T(8,128)(2,1)} custom-call(bf16[3,1,256,128]{3,2,1,0:T(8,128)(2,1)} %get-tuple-element.40.refs_1_.refs_0_, bf16[3,1,256,128]{3,2,1,0:T(8,128)(2,1)} %copy-done.4, bf16[3,1,256,128]{3,2,1,0:T(8,128)(2,1)} %collective-permute-done.6.refs_2_, bf16[3,1,256,128]{3,2,1,0:T(8,128)(2,1)} %collective-permute-done.7.refs_3_), custom_call_target="tpu_custom_call" | custom-call | flops 100000000 | bytes 1024 | tf_op jit(solution)/shard_map/pallas_call | solution.py:49
  85.3 4.7 %all-to-all-start.2 = ((bf16[4,3,1,256,128]{4,3,2,1,0:T(8,128)(2,1)}), bf16[4,3,1,256,128]{4,3,2,1,0:T(8,128)(2,1)}, u32[]{:S(2)}, u32[]{:S(2)}) async-start(bf16[4,3,1,256,128]{4,3,2,1,0:T(8,128)(2,1)} %shard_map.105._), calls=%async_computation.2 | async-start | bytes 1572864 | tf_op jit(solution)/shard_map/all_to_all | solution.py:379
  90.1 13.4 %shard_map.106 = (bf16[4,3,1,256,128]{4,3,2,1,0:T(8,128)(2,1)}, f32[3,4,1,256]{3,2,1,0:T(1,128)}) custom-call(f32[2]{0:T(128)} %add_select_fusion.bad_ref, bf16[4,3,1,256,128]{4,3,2,1,0:T(8,128)(2,1)} %copy-done.2, bf16[4,3,2,256,128]{4,3,2,1,0:T(8,128)(2,1)} %collective-permute-done.3.kl_ref, bf16[4,3,2,256,128]{4,3,2,1,0:T(8,128)(2,1)} %all-to-all-done.1.kc_ref, ...), custom_call_target="tpu_custom_call" | custom-call | flops 99999997952 | bytes 1024 | tf_op jit(solution)/shard_map/pallas_call | solution.py:188
  103.5 4.8 %all-to-all-start.3 = ((bf16[4,3,1,256,128]{4,3,2,1,0:T(8,128)(2,1)}), bf16[4,3,1,256,128]{4,3,2,1,0:T(8,128)(2,1)S(1)}, u32[]{:S(2)}, u32[]{:S(2)}) async-start(bf16[4,3,1,256,128]{4,3,2,1,0:T(8,128)(2,1)} %get-tuple-element.44.o_ref), calls=%async_computation.3 | async-start | bytes 1572864 | tf_op jit(solution)/shard_map/all_to_all | solution.py:379
  108.3 19.0 %shard_map.107 = (bf16[4,2,1,256,128]{4,3,2,1,0:T(8,128)(2,1)}, bf16[4,2,2,256,128]{4,3,2,1,0:T(8,128)(2,1)}, bf16[4,2,2,256,128]{4,3,2,1,0:T(8,128)(2,1)}, bf16[4,2,2,256,128]{4,3,2,1,0:T(8,128)(2,1)}) custom-call(f32[2]{0:T(128)} %add_select_fusion.bad_ref, bf16[4,3,1,256,128]{4,3,2,1,0:T(8,128)(2,1)} %copy-done.2, ...), custom_call_target="tpu_custom_call" | custom-call | flops 99999997952 | bytes 1024 | tf_op jit(solution)/shard_map/pallas_call | solution.py:261
  129.2 6.0 %collective-permute-start.9 = (bf16[4,2,2,256,128]{4,3,2,1,0:T(8,128)(2,1)}, bf16[4,2,2,256,128]{4,3,2,1,0:T(8,128)(2,1)}, u32[]{:S(2)}, u32[]{:S(2)}) collective-permute-start(bf16[4,2,2,256,128]{4,3,2,1,0:T(8,128)(2,1)} %get-tuple-element.49), channel_id=1, source_target_pairs={{1,0},{2,1},{3,2},{4,3},{5,4},{6,5},{7,6},{9,8},{10,9},{11,10},{12... | collective-permute-start | bytes 3145736 | tf_op jit(solution)/shard_map/ppermute | solution.py:389
  138.2 2.4 %collective-permute-start.13 = (bf16[3,1,256,128]{3,2,1,0:T(8,128)(2,1)}, bf16[3,1,256,128]{3,2,1,0:T(8,128)(2,1)S(1)}, u32[]{:S(2)}, u32[]{:S(2)}) collective-permute-start(bf16[3,1,256,128]{3,2,1,0:T(8,128)(2,1)} %get-tuple-element.59), channel_id=1, source_target_pairs={{0,64},{32,96},{64,0},{96,32},{1,65},{33,97},{65,1},{97,33},{2,66}... | collective-permute-start | bytes 589832 | tf_op jit(solution)/shard_map/ppermute | solution.py:141
  141.6 10.5 %shard_map.109 = (bf16[4,1,1,256,128]{4,3,2,1,0:T(8,128)(2,1)}, bf16[4,1,2,256,128]{4,3,2,1,0:T(8,128)(2,1)}, bf16[4,1,2,256,128]{4,3,2,1,0:T(8,128)(2,1)}, bf16[4,1,2,256,128]{4,3,2,1,0:T(8,128)(2,1)}) custom-call(f32[2]{0:T(128)} %add_select_fusion.bad_ref, bf16[4,3,1,256,128]{4,3,2,1,0:T(8,128)(2,1)} %copy-done.2, ...), custom_call_target="tpu_custom_call" | custom-call | flops 99999997952 | bytes 1024 | tf_op jit(solution)/shard_map/pallas_call | solution.py:261
  152.1 5.6 %collective-permute-done.8.a_ref = bf16[4,2,2,256,128]{4,3,2,1,0:T(8,128)(2,1)} collective-permute-done((bf16[4,2,2,256,128]{4,3,2,1,0:T(8,128)(2,1)}, bf16[4,2,2,256,128]{4,3,2,1,0:T(8,128)(2,1)}, u32[]{:S(2)}, u32[]{:S(2)}) %collective-permute-start.8) | collective-permute-done | bytes 1048608 | tf_op jit(solution)/shard_map/ppermute | solution.py:384
  159.6 6.0 %collective-permute-start.11 = (bf16[4,1,2,256,128]{4,3,2,1,0:T(8,128)(2,1)}, bf16[4,1,2,256,128]{4,3,2,1,0:T(8,128)(2,1)}, u32[]{:S(2)}, u32[]{:S(2)}) collective-permute-start(bf16[4,1,2,256,128]{4,3,2,1,0:T(8,128)(2,1)} %get-tuple-element.54), channel_id=1, source_target_pairs={{1,0},{2,1},{3,2},{4,3},{5,4},{6,5},{7,6},{9,8},{10,9},{11,10},{12... | collective-permute-start | bytes 1572872 | tf_op jit(solution)/shard_map/ppermute | solution.py:389
  165.7 3.5 %shard_map.110.refs_8_ = bf16[4,2,3,256,128]{4,3,2,1,0:T(8,128)(2,1)} custom-call(bf16[4,2,1,256,128]{4,3,2,1,0:T(8,128)(2,1)} %get-tuple-element.46.rest_1_.dq_ref, bf16[4,2,2,256,128]{4,3,2,1,0:T(8,128)(2,1)} %get-tuple-element.47.own_ref, bf16[4,2,2,256,128]{4,3,2,1,0:T(8,128)(2,1)} %collective-permute-done.8.a_ref, ...), custom_call_target="tpu_custom_call" | custom-call | flops 100000000 | bytes 1024 | tf_op jit(solution)/shard_map/pallas_call | solution.py:294
  169.2 4.8 %all-to-all-start.4 = ((bf16[4,2,3,256,128]{4,3,2,1,0:T(8,128)(2,1)}), bf16[4,2,3,256,128]{4,3,2,1,0:T(8,128)(2,1)}, u32[]{:S(2)}, u32[]{:S(2)}) async-start(bf16[4,2,3,256,128]{4,3,2,1,0:T(8,128)(2,1)} %shard_map.110.refs_8_), calls=%async_computation.4 | async-start | bytes 3145728 | tf_op jit(solution)/shard_map/all_to_all | solution.py:379
  174.8 8.7 %shard_map.113 = (bf16[3,2,256,128]{3,2,1,0:T(8,128)(2,1)}, bf16[3,2,256,128]{3,2,1,0:T(8,128)(2,1)}, bf16[3,2,256,128]{3,2,1,0:T(8,128)(2,1)}, bf16[3,2,256,128]{3,2,1,0:T(8,128)(2,1)}) custom-call(bf16[3,3,256,128]{3,2,1,0:T(8,128)(2,1)} %get-tuple-element.36.refs_0_, bf16[3,3,256,128]{3,2,1,0:T(8,128)(2,1)} %copy-done.5, ...), custom_call_target="tpu_custom_call" | custom-call | flops 99999997952 | bytes 1024 | tf_op jit(solution)/shard_map/pallas_call | solution.py:366
  183.6 2.5 %collective-permute-start.16 = (bf16[3,2,256,128]{3,2,1,0:T(8,128)(2,1)}, bf16[3,2,256,128]{3,2,1,0:T(8,128)(2,1)}, u32[]{:S(2)}, u32[]{:S(2)}) collective-permute-start(bf16[3,2,256,128]{3,2,1,0:T(8,128)(2,1)} %get-tuple-element.63), channel_id=1, source_target_pairs={{0,64},{32,96},{64,0},{96,32},{1,65},{33,97},{65,1},{97,33},{2,66}... | collective-permute-start | bytes 1179656 | tf_op jit(solution)/shard_map/ppermute | solution.py:141
  187.0 4.2 %all-to-all-done.4._.refs_0_ = bf16[4,2,3,256,128]{4,3,2,1,0:T(8,128)(2,1)} async-done(((bf16[4,2,3,256,128]{4,3,2,1,0:T(8,128)(2,1)}), bf16[4,2,3,256,128]{4,3,2,1,0:T(8,128)(2,1)}, u32[]{:S(2)}, u32[]{:S(2)}) %all-to-all-start.4) | async-done | bytes 1572896 | tf_op jit(solution)/shard_map/all_to_all | solution.py:379
  191.2 2.5 %shard_map.111 = bf16[4,1,3,256,128]{4,3,2,1,0:T(8,128)(2,1)} custom-call(bf16[4,1,1,256,128]{4,3,2,1,0:T(8,128)(2,1)} %get-tuple-element.51._.dq_ref, bf16[4,1,2,256,128]{4,3,2,1,0:T(8,128)(2,1)} %get-tuple-element.52.own_ref, bf16[4,1,2,256,128]{4,3,2,1,0:T(8,128)(2,1)} %copy-done.3, bf16[4,1,2,256,128]{4,3,2,1,0:T(8,128)(2,1)} %collective-permute-done.11.b_ref, ...), custom_call_target="tpu_custom_call" | custom-call | flops 100000000 | bytes 1024 | tf_op jit(solution)/shard_map/pallas_call | solution.py:294
  193.7 3.5 %all-to-all-start.5 = ((bf16[4,1,3,256,128]{4,3,2,1,0:T(8,128)(2,1)}), bf16[4,1,3,256,128]{4,3,2,1,0:T(8,128)(2,1)S(1)}, u32[]{:S(2)}, u32[]{:S(2)}) async-start(bf16[4,1,3,256,128]{4,3,2,1,0:T(8,128)(2,1)} %shard_map.111), calls=%async_computation.5 | async-start | bytes 1572864 | tf_op jit(solution)/shard_map/all_to_all | solution.py:379
  197.4 7.5 %collective-permute-done.17.refs_3_ = bf16[3,2,256,128]{3,2,1,0:T(8,128)(2,1)} collective-permute-done((bf16[3,2,256,128]{3,2,1,0:T(8,128)(2,1)}, bf16[3,2,256,128]{3,2,1,0:T(8,128)(2,1)}, u32[]{:S(2)}, u32[]{:S(2)}) %collective-permute-start.17) | collective-permute-done | bytes 393248 | tf_op jit(solution)/shard_map/ppermute | solution.py:141
  204.9 2.8 %shard_map.114 = (bf16[256,1536]{1,0:T(8,128)(2,1)}, bf16[256,1536]{1,0:T(8,128)(2,1)}) custom-call(bf16[3,2,256,128]{3,2,1,0:T(8,128)(2,1)} %get-tuple-element.61.refs_0_, bf16[3,2,256,128]{3,2,1,0:T(8,128)(2,1)} %collective-permute-done.15.refs_1_, bf16[3,2,256,128]{3,2,1,0:T(8,128)(2,1)} %collective-permute-done.16.refs_2_, ...), custom_call_target="tpu_custom_call" | custom-call | flops 99999997952 | bytes 1024 | tf_op jit(solution)/shard_map/pallas_call | solution.py:49
  208.8 3.4 %shard_map.112 = (bf16[256,1536]{1,0:T(8,128)(2,1)}, bf16[256,1536]{1,0:T(8,128)(2,1)}, bf16[256,1536]{1,0:T(8,128)(2,1)}) custom-call(bf16[4,2,3,256,128]{4,3,2,1,0:T(8,128)(2,1)} %all-to-all-done.4._.refs_0_, bf16[4,1,3,256,128]{4,3,2,1,0:T(8,128)(2,1)} %copy-done.1), custom_call_target="tpu_custom_call" | custom-call | flops 100000000 | bytes 1024 | tf_op jit(solution)/shard_map/pallas_call | solution.py:49
  (53 shorter events, 17.6 us)
Async XLA Ops:
  3.4 25.4 %all-to-all-start.1 = ((bf16[4,3,2,256,128]{4,3,2,1,0:T(8,128)(2,1)}), bf16[4,3,2,256,128]{4,3,2,1,0:T(8,128)(2,1)}, u32[]{:S(2)}, u32[]{:S(2)}) async-start(bf16[4,3,2,256,128]{4,3,2,1,0:T(8,128)(2,1)} %shard_map.101.refs_3_), calls=%async_computation.1 | async-start | bytes 3145728 | tf_op jit(solution)/shard_map/all_to_all | solution.py:379
  11.2 25.4 %collective-permute-start = (bf16[3,3,256,128]{3,2,1,0:T(8,128)(2,1)}, bf16[3,3,256,128]{3,2,1,0:T(8,128)(2,1)S(1)}, u32[]{:S(2)}, u32[]{:S(2)}) collective-permute-start(bf16[3,3,256,128]{3,2,1,0:T(8,128)(2,1)} %get-tuple-element.37), channel_id=1, source_target_pairs={{0,32},{32,0},{64,96},{96,64},{1,33},{33,1},{65,97},{97,65},{2,34}... | collective-permute-start | bytes 1769480 | tf_op jit(solution)/shard_map/ppermute | solution.py:141
  11.2 25.4 %collective-permute-start.1 = (bf16[3,3,256,128]{3,2,1,0:T(8,128)(2,1)}, bf16[3,3,256,128]{3,2,1,0:T(8,128)(2,1)}, u32[]{:S(2)}, u32[]{:S(2)}) collective-permute-start(bf16[3,3,256,128]{3,2,1,0:T(8,128)(2,1)} %get-tuple-element.38), channel_id=1, source_target_pairs={{0,64},{32,96},{64,0},{96,32},{1,65},{33,97},{65,1},{97,33},{2,66}... | collective-permute-start | bytes 1769480 | tf_op jit(solution)/shard_map/ppermute | solution.py:141
  13.5 27.5 %collective-permute-start.2 = (bf16[3,3,256,128]{3,2,1,0:T(8,128)(2,1)}, bf16[3,3,256,128]{3,2,1,0:T(8,128)(2,1)}, u32[]{:S(2)}, u32[]{:S(2)}) collective-permute-start(bf16[3,3,256,128]{3,2,1,0:T(8,128)(2,1)} %get-tuple-element.39), channel_id=1, source_target_pairs={{0,96},{32,64},{64,32},{96,0},{1,97},{33,65},{65,33},{97,1},{2,98}... | collective-permute-start | bytes 1769480 | tf_op jit(solution)/shard_map/ppermute | solution.py:141
  28.8 61.2 %collective-permute-start.4 = (bf16[4,3,2,256,128]{4,3,2,1,0:T(8,128)(2,1)}, bf16[4,3,2,256,128]{4,3,2,1,0:T(8,128)(2,1)}, u32[]{:S(2)}, u32[]{:S(2)}) collective-permute-start(bf16[4,3,2,256,128]{4,3,2,1,0:T(8,128)(2,1)} %all-to-all-done.1.kc_ref), channel_id=1, source_target_pairs={{1,0},{2,1},{3,2},{4,3},{5,4},{6,5},{7,6},{9,8},{10,9},{11,10},{12... | collective-permute-start | bytes 4718600 | tf_op jit(solution)/shard_map/ppermute | solution.py:389
  34.6 55.4 %collective-permute-start.3 = (bf16[4,3,2,256,128]{4,3,2,1,0:T(8,128)(2,1)}, bf16[4,3,2,256,128]{4,3,2,1,0:T(8,128)(2,1)}, u32[]{:S(2)}, u32[]{:S(2)}) collective-permute-start(bf16[4,3,2,256,128]{4,3,2,1,0:T(8,128)(2,1)} %all-to-all-done.1.kc_ref), channel_id=1, source_target_pairs={{0,1},{1,2},{2,3},{3,4},{4,5},{5,6},{6,7},{8,9},{9,10},{10,11},{11... | collective-permute-start | bytes 4718600 | tf_op jit(solution)/shard_map/ppermute | solution.py:384
  36.6 4.4 %copy-start.5 = (bf16[3,3,256,128]{3,2,1,0:T(8,128)(2,1)}, bf16[3,3,256,128]{3,2,1,0:T(8,128)(2,1)S(1)}, u32[]{:S(2)}) copy-start(bf16[3,3,256,128]{3,2,1,0:T(8,128)(2,1)S(1)} %collective-permute-done.refs_1_) | copy-start | bytes 1769476
  49.6 4.9 %copy-start.10 = (bf16[3,1,256,128]{3,2,1,0:T(8,128)(2,1)S(1)}, bf16[3,1,256,128]{3,2,1,0:T(8,128)(2,1)}, u32[]{:S(2)}) copy-start(bf16[3,1,256,128]{3,2,1,0:T(8,128)(2,1)} %get-tuple-element.41) | copy-start | bytes 589828
  49.6 5.2 %copy-start.9 = (bf16[3,1,256,128]{3,2,1,0:T(8,128)(2,1)S(1)}, bf16[3,1,256,128]{3,2,1,0:T(8,128)(2,1)}, u32[]{:S(2)}) copy-start(bf16[3,1,256,128]{3,2,1,0:T(8,128)(2,1)} %get-tuple-element.42) | copy-start | bytes 589828
  49.6 7.5 %copy-start.8 = (bf16[3,1,256,128]{3,2,1,0:T(8,128)(2,1)S(1)}, bf16[3,1,256,128]{3,2,1,0:T(8,128)(2,1)}, u32[]{:S(2)}) copy-start(bf16[3,1,256,128]{3,2,1,0:T(8,128)(2,1)} %get-tuple-element.43) | copy-start | bytes 589828
  49.6 35.7 %all-to-all-start = ((bf16[4,3,1,256,128]{4,3,2,1,0:T(8,128)(2,1)}), bf16[4,3,1,256,128]{4,3,2,1,0:T(8,128)(2,1)S(1)}, u32[]{:S(2)}, u32[]{:S(2)}) async-start(bf16[4,3,1,256,128]{4,3,2,1,0:T(8,128)(2,1)} %shard_map.104), calls=%async_computation | async-start | bytes 1572864 | tf_op jit(solution)/shard_map/all_to_all | solution.py:379
  54.5 4.0 %collective-permute-start.5 = (bf16[3,1,256,128]{3,2,1,0:T(8,128)(2,1)S(1)}, bf16[3,1,256,128]{3,2,1,0:T(8,128)(2,1)S(1)}, u32[]{:S(2)}, u32[]{:S(2)}) collective-permute-start(bf16[3,1,256,128]{3,2,1,0:T(8,128)(2,1)S(1)} %copy-done.10), channel_id=1, source_target_pairs={{0,32},{32,0},{64,96},{96,64},{1,33},{33,1},{65,97},{97,65},{2,34}... | collective-permute-start | bytes 589832 | tf_op jit(solution)/shard_map/ppermute | solution.py:141
  54.8 24.9 %collective-permute-start.6 = (bf16[3,1,256,128]{3,2,1,0:T(8,128)(2,1)S(1)}, bf16[3,1,256,128]{3,2,1,0:T(8,128)(2,1)}, u32[]{:S(2)}, u32[]{:S(2)}) collective-permute-start(bf16[3,1,256,128]{3,2,1,0:T(8,128)(2,1)S(1)} %copy-done.9), channel_id=1, source_target_pairs={{0,64},{32,96},{64,0},{96,32},{1,65},{33,97},{65,1},{97,33},{2,66}... | collective-permute-start | bytes 589832 | tf_op jit(solution)/shard_map/ppermute | solution.py:141
  57.1 26.0 %collective-permute-start.7 = (bf16[3,1,256,128]{3,2,1,0:T(8,128)(2,1)S(1)}, bf16[3,1,256,128]{3,2,1,0:T(8,128)(2,1)}, u32[]{:S(2)}, u32[]{:S(2)}) collective-permute-start(bf16[3,1,256,128]{3,2,1,0:T(8,128)(2,1)S(1)} %copy-done.8), channel_id=1, source_target_pairs={{0,96},{32,64},{64,32},{96,0},{1,97},{33,65},{65,33},{97,1},{2,98}... | collective-permute-start | bytes 589832 | tf_op jit(solution)/shard_map/ppermute | solution.py:141
  58.5 24.7 %copy-start.4 = (bf16[3,1,256,128]{3,2,1,0:T(8,128)(2,1)}, bf16[3,1,256,128]{3,2,1,0:T(8,128)(2,1)S(1)}, u32[]{:S(2)}) copy-start(bf16[3,1,256,128]{3,2,1,0:T(8,128)(2,1)S(1)} %collective-permute-done.5.refs_1_) | copy-start | bytes 589828
  85.3 4.8 %copy-start.2 = (bf16[4,3,1,256,128]{4,3,2,1,0:T(8,128)(2,1)}, bf16[4,3,1,256,128]{4,3,2,1,0:T(8,128)(2,1)S(1)}, u32[]{:S(2)}) copy-start(bf16[4,3,1,256,128]{4,3,2,1,0:T(8,128)(2,1)S(1)} %all-to-all-done.q_ref) | copy-start | bytes 2359300
  85.3 18.2 %all-to-all-start.2 = ((bf16[4,3,1,256,128]{4,3,2,1,0:T(8,128)(2,1)}), bf16[4,3,1,256,128]{4,3,2,1,0:T(8,128)(2,1)}, u32[]{:S(2)}, u32[]{:S(2)}) async-start(bf16[4,3,1,256,128]{4,3,2,1,0:T(8,128)(2,1)} %shard_map.105._), calls=%async_computation.2 | async-start | bytes 1572864 | tf_op jit(solution)/shard_map/all_to_all | solution.py:379
  103.5 31.8 %all-to-all-start.3 = ((bf16[4,3,1,256,128]{4,3,2,1,0:T(8,128)(2,1)}), bf16[4,3,1,256,128]{4,3,2,1,0:T(8,128)(2,1)S(1)}, u32[]{:S(2)}, u32[]{:S(2)}) async-start(bf16[4,3,1,256,128]{4,3,2,1,0:T(8,128)(2,1)} %get-tuple-element.44.o_ref), calls=%async_computation.3 | async-start | bytes 1572864 | tf_op jit(solution)/shard_map/all_to_all | solution.py:379
  127.3 30.4 %collective-permute-start.8 = (bf16[4,2,2,256,128]{4,3,2,1,0:T(8,128)(2,1)}, bf16[4,2,2,256,128]{4,3,2,1,0:T(8,128)(2,1)}, u32[]{:S(2)}, u32[]{:S(2)}) collective-permute-start(bf16[4,2,2,256,128]{4,3,2,1,0:T(8,128)(2,1)} %get-tuple-element.48), channel_id=1, source_target_pairs={{0,1},{1,2},{2,3},{3,4},{4,5},{5,6},{6,7},{8,9},{9,10},{10,11},{11... | collective-permute-start | bytes 3145736 | tf_op jit(solution)/shard_map/ppermute | solution.py:384
  129.2 30.4 %collective-permute-start.9 = (bf16[4,2,2,256,128]{4,3,2,1,0:T(8,128)(2,1)}, bf16[4,2,2,256,128]{4,3,2,1,0:T(8,128)(2,1)}, u32[]{:S(2)}, u32[]{:S(2)}) collective-permute-start(bf16[4,2,2,256,128]{4,3,2,1,0:T(8,128)(2,1)} %get-tuple-element.49), channel_id=1, source_target_pairs={{1,0},{2,1},{3,2},{4,3},{5,4},{6,5},{7,6},{9,8},{10,9},{11,10},{12... | collective-permute-start | bytes 3145736 | tf_op jit(solution)/shard_map/ppermute | solution.py:389
  138.2 35.8 %collective-permute-start.12 = (bf16[3,1,256,128]{3,2,1,0:T(8,128)(2,1)}, bf16[3,1,256,128]{3,2,1,0:T(8,128)(2,1)S(1)}, u32[]{:S(2)}, u32[]{:S(2)}) collective-permute-start(bf16[3,1,256,128]{3,2,1,0:T(8,128)(2,1)} %get-tuple-element.58), channel_id=1, source_target_pairs={{0,32},{32,0},{64,96},{96,64},{1,33},{33,1},{65,97},{97,65},{2,34}... | collective-permute-start | bytes 589832 | tf_op jit(solution)/shard_map/ppermute | solution.py:141
  138.2 35.8 %collective-permute-start.13 = (bf16[3,1,256,128]{3,2,1,0:T(8,128)(2,1)}, bf16[3,1,256,128]{3,2,1,0:T(8,128)(2,1)S(1)}, u32[]{:S(2)}, u32[]{:S(2)}) collective-permute-start(bf16[3,1,256,128]{3,2,1,0:T(8,128)(2,1)} %get-tuple-element.59), channel_id=1, source_target_pairs={{0,64},{32,96},{64,0},{96,32},{1,65},{33,97},{65,1},{97,33},{2,66}... | collective-permute-start | bytes 589832 | tf_op jit(solution)/shard_map/ppermute | solution.py:141
  140.6 33.4 %collective-permute-start.14 = (bf16[3,1,256,128]{3,2,1,0:T(8,128)(2,1)}, bf16[3,1,256,128]{3,2,1,0:T(8,128)(2,1)}, u32[]{:S(2)}, u32[]{:S(2)}) collective-permute-start(bf16[3,1,256,128]{3,2,1,0:T(8,128)(2,1)} %get-tuple-element.60), channel_id=1, source_target_pairs={{0,96},{32,64},{64,32},{96,0},{1,97},{33,65},{65,33},{97,1},{2,98}... | collective-permute-start | bytes 589832 | tf_op jit(solution)/shard_map/ppermute | solution.py:141
  157.7 29.3 %collective-permute-start.10 = (bf16[4,1,2,256,128]{4,3,2,1,0:T(8,128)(2,1)}, bf16[4,1,2,256,128]{4,3,2,1,0:T(8,128)(2,1)S(1)}, u32[]{:S(2)}, u32[]{:S(2)}) collective-permute-start(bf16[4,1,2,256,128]{4,3,2,1,0:T(8,128)(2,1)} %get-tuple-element.53), channel_id=1, source_target_pairs={{0,1},{1,2},{2,3},{3,4},{4,5},{5,6},{6,7},{8,9},{9,10},{10,11},{11... | collective-permute-start | bytes 1572872 | tf_op jit(solution)/shard_map/ppermute | solution.py:384
  159.6 27.3 %collective-permute-start.11 = (bf16[4,1,2,256,128]{4,3,2,1,0:T(8,128)(2,1)}, bf16[4,1,2,256,128]{4,3,2,1,0:T(8,128)(2,1)}, u32[]{:S(2)}, u32[]{:S(2)}) collective-permute-start(bf16[4,1,2,256,128]{4,3,2,1,0:T(8,128)(2,1)} %get-tuple-element.54), channel_id=1, source_target_pairs={{1,0},{2,1},{3,2},{4,3},{5,4},{6,5},{7,6},{9,8},{10,9},{11,10},{12... | collective-permute-start | bytes 1572872 | tf_op jit(solution)/shard_map/ppermute | solution.py:389
  169.2 22.0 %all-to-all-start.4 = ((bf16[4,2,3,256,128]{4,3,2,1,0:T(8,128)(2,1)}), bf16[4,2,3,256,128]{4,3,2,1,0:T(8,128)(2,1)}, u32[]{:S(2)}, u32[]{:S(2)}) async-start(bf16[4,2,3,256,128]{4,3,2,1,0:T(8,128)(2,1)} %shard_map.110.refs_8_), calls=%async_computation.4 | async-start | bytes 3145728 | tf_op jit(solution)/shard_map/all_to_all | solution.py:379
  183.5 13.7 %collective-permute-start.15 = (bf16[3,2,256,128]{3,2,1,0:T(8,128)(2,1)}, bf16[3,2,256,128]{3,2,1,0:T(8,128)(2,1)}, u32[]{:S(2)}, u32[]{:S(2)}) collective-permute-start(bf16[3,2,256,128]{3,2,1,0:T(8,128)(2,1)} %get-tuple-element.62), channel_id=1, source_target_pairs={{0,32},{32,0},{64,96},{96,64},{1,33},{33,1},{65,97},{97,65},{2,34}... | collective-permute-start | bytes 1179656 | tf_op jit(solution)/shard_map/ppermute | solution.py:141
  183.6 13.8 %collective-permute-start.16 = (bf16[3,2,256,128]{3,2,1,0:T(8,128)(2,1)}, bf16[3,2,256,128]{3,2,1,0:T(8,128)(2,1)}, u32[]{:S(2)}, u32[]{:S(2)}) collective-permute-start(bf16[3,2,256,128]{3,2,1,0:T(8,128)(2,1)} %get-tuple-element.63), channel_id=1, source_target_pairs={{0,64},{32,96},{64,0},{96,32},{1,65},{33,97},{65,1},{97,33},{2,66}... | collective-permute-start | bytes 1179656 | tf_op jit(solution)/shard_map/ppermute | solution.py:141
  186.1 18.8 %collective-permute-start.17 = (bf16[3,2,256,128]{3,2,1,0:T(8,128)(2,1)}, bf16[3,2,256,128]{3,2,1,0:T(8,128)(2,1)}, u32[]{:S(2)}, u32[]{:S(2)}) collective-permute-start(bf16[3,2,256,128]{3,2,1,0:T(8,128)(2,1)} %get-tuple-element.64), channel_id=1, source_target_pairs={{0,96},{32,64},{64,32},{96,0},{1,97},{33,65},{65,33},{97,1},{2,98}... | collective-permute-start | bytes 1179656 | tf_op jit(solution)/shard_map/ppermute | solution.py:141
  187.0 4.2 %copy-start.3 = (bf16[4,1,2,256,128]{4,3,2,1,0:T(8,128)(2,1)}, bf16[4,1,2,256,128]{4,3,2,1,0:T(8,128)(2,1)S(1)}, u32[]{:S(2)}) copy-start(bf16[4,1,2,256,128]{4,3,2,1,0:T(8,128)(2,1)S(1)} %collective-permute-done.10.a_ref) | copy-start | bytes 1572868
  193.7 14.2 %all-to-all-start.5 = ((bf16[4,1,3,256,128]{4,3,2,1,0:T(8,128)(2,1)}), bf16[4,1,3,256,128]{4,3,2,1,0:T(8,128)(2,1)S(1)}, u32[]{:S(2)}, u32[]{:S(2)}) async-start(bf16[4,1,3,256,128]{4,3,2,1,0:T(8,128)(2,1)} %shard_map.111), calls=%async_computation.5 | async-start | bytes 1572864 | tf_op jit(solution)/shard_map/all_to_all | solution.py:379
  207.9 0.9 copy-start.1
  (3 other events, 2.3 us)

commit v4 on v3

--- a/solution.py
+++ b/solution.py
@@ -68,7 +68,7 @@
     return jax.ShapeDtypeStruct(shape, jnp.bfloat16)
 
 
-def pack(arrays, after=()):
+def pack(arrays, after=(), told=0.1):
     tokens = arrays[0].shape[0]
     cells = [(a, d, h) for d in range(PARTS) for h in range(GROUP) for a in range(len(arrays))]
     return move(
@@ -76,6 +76,7 @@
         [bf16(PARTS, GROUP, len(arrays), tokens, HEAD_DIM)],
         lambda me: [(a, columns(d, h), 0, (d, h, a)) for a, d, h in cells],
         after=after,
+        told=told,
     )[0]
 
 
@@ -143,46 +144,46 @@
 
 
 def near_rows(row):
-    return range(max(row - 1, 0), min(row + 2, ROWS))
-
-
-def forward_kernel(bad_ref, q_ref, kl_ref, kc_ref, kr_ref, _, o_ref, lse_ref):
-    bads = (bad_ref[0], jnp.float32(0.0), bad_ref[1])
-    sides = (kl_ref, kc_ref, kr_ref)
+    return max(row - 1, 0), min(row + 2, ROWS)
+
+
+def tiles(ref, rows, tensor):
+    low, high = rows
+    block = ref[low:high, 0, tensor]
+    return block.reshape((high - low) * block.shape[1], HEAD_DIM)
+
+
+def forward_kernel(bad_ref, q_ref, other_ref, own_ref, partner_ref, _, o_ref, lse_ref, vt_ref):
+    bad = bad_ref[0]
+    sides = (other_ref, own_ref, partner_ref)
+    tokens = q_ref.shape[3]
+    for side in range(3):
+        vt_ref[side] = tiles(sides[side], (0, ROWS), 1).T
     for b in range(ROWS):
         query = q_ref[b, 0, 0]
-        scores = []
-        for side in range(3):
-            for u in near_rows(b):
-                scores.append((side, u, dot(sides[side][u, 0, 0], query, NT)))
-        top = None
-        for side in range(3):
-            local = None
-            for at, _, s in scores:
-                if at == side:
-                    one = jnp.max(s, axis=0, keepdims=True)
-                    local = one if local is None else jnp.maximum(local, one)
-            local = local - bads[side]
-            top = local if top is None else jnp.maximum(top, local)
-        top = top * BASE2
+        rows = near_rows(b)
+        span = slice(rows[0] * tokens, rows[1] * tokens)
+        scores = [dot(tiles(ref, rows, 0), query, NT) for ref in sides]
+        tops = [jnp.max(s, axis=0, keepdims=True) for s in scores]
+        top = functools.reduce(jnp.maximum, [tops[0] - bad] + tops[1:]) * BASE2
         total = None
         mixed = None
-        for side, u, s in scores:
-            p = jnp.exp2(s * BASE2 - (top + bads[side]))
+        for side, s in enumerate(scores):
+            p = jnp.exp2(s * BASE2 - (top + bad if side == 0 else top))
             one = jnp.sum(p, axis=0, keepdims=True)
             total = one if total is None else total + one
-            term = dot(sides[side][u, 0, 1], p.astype(jnp.bfloat16), TN)
+            term = dot(vt_ref[side, :, span], p.astype(jnp.bfloat16), NN)
             mixed = term if mixed is None else mixed + term
         mixed = mixed * (1.0 / total)
         o_ref[b, 0, 0] = mixed.T.astype(jnp.bfloat16)
-        lse_ref[0, b] = top + jnp.log2(total)
+        lse_ref[0, :, b * tokens : (b + 1) * tokens] = top + jnp.log2(total)
 
 
 def column_spec(count, tokens):
     return pl.BlockSpec((ROWS, 1, count, tokens, HEAD_DIM), lambda h: (0, h, 0, 0, 0))
 
 
-def attend_forward(bad, q, kv_left, kv, kv_right, after):
+def attend_forward(bad, q, kv_other, kv, kv_partner, after):
     tokens = q.shape[3]
     group = q.shape[1]
     return pl.pallas_call(
@@ -193,70 +194,58 @@
         + [pl.BlockSpec(memory_space=pl.ANY)],
         out_specs=[
             column_spec(1, tokens),
-            pl.BlockSpec((1, ROWS, 1, tokens), lambda h: (h, 0, 0, 0)),
+            pl.BlockSpec((1, 1, ROWS * tokens), lambda h: (h, 0, 0)),
         ],
         out_shape=[
             jax.ShapeDtypeStruct(q.shape, jnp.bfloat16),
-            jax.ShapeDtypeStruct((group, ROWS, 1, tokens), jnp.float32),
+            jax.ShapeDtypeStruct((group, 1, ROWS * tokens), jnp.float32),
         ],
+        scratch_shapes=[pltpu.VMEM((3, HEAD_DIM, ROWS * tokens), jnp.bfloat16)],
         cost_estimate=cost(100),
         compiler_params=params(),
-    )(bad, q, kv_left, kv, kv_right, after)
+    )(bad, q, kv_other, kv, kv_partner, after)
 
 
 def backward_kernel(
-    bad_ref,
-    q_ref,
-    kl_ref,
-    kc_ref,
-    kr_ref,
-    do_ref,
-    o_ref,
-    lse_ref,
-    *rest,
+    bad_ref, q_ref, other_ref, own_ref, partner_ref, do_ref, o_ref, lse_ref, *rest
 ):
-    dq_ref, dl_ref, dc_ref, dr_ref, dqt_ref, row_ref = rest[-6:]
-    bads = (bad_ref[0], jnp.float32(0.0), bad_ref[1])
-    sides = (kl_ref, kc_ref, kr_ref)
-    outs = (dl_ref, dc_ref, dr_ref)
+    dq_ref, d_other_ref, d_own_ref, d_partner_ref, dqt_ref, row_ref = rest[-6:]
+    bad = bad_ref[0]
+    sides = (other_ref, own_ref, partner_ref)
+    outs = (d_other_ref, d_own_ref, d_partner_ref)
+    tokens = q_ref.shape[3]
     for b in range(ROWS):
         product = do_ref[b, 0, 0].astype(jnp.float32) * o_ref[b, 0, 0].astype(jnp.float32)
-        row_ref[b] = jnp.sum(product.T, axis=0, keepdims=True)
-    seen = set()
-    for side in (0, 2, 1):
+        row_ref[:, b * tokens : (b + 1) * tokens] = jnp.sum(product.T, axis=0, keepdims=True)
+    dqt_ref[...] = jnp.zeros_like(dqt_ref)
+    for side in range(3):
         for u in range(ROWS):
+            rows = near_rows(u)
+            span = slice(rows[0] * tokens, rows[1] * tokens)
             key = sides[side][u, 0, 0]
-            value = sides[side][u, 0, 1]
-            dk = None
-            dv = None
-            for b in near_rows(u):
-                query = q_ref[b, 0, 0]
-                grad = do_ref[b, 0, 0]
-                s = dot(key, query, NT)
-                p = jnp.exp2(s * BASE2 - (lse_ref[0, b] + bads[side]))
-                e = dot(value, grad, NT)
-                g = (p * (e - row_ref[b])).astype(jnp.bfloat16)
-                tv = dot(p.astype(jnp.bfloat16), grad, NN)
-                tk = dot(g, query, NN)
-                tq = dot(key, g, TN)
-                dv = tv if dv is None else dv + tv
-                dk = tk if dk is None else dk + tk
-                if b in seen:
-                    dqt_ref[b] += tq
-                else:
-                    seen.add(b)
-                    dqt_ref[b] = tq
-            outs[side][u, 0, 0] = (dk * SCALE).astype(outs[side].dtype)
+            query = tiles(q_ref, rows, 0)
+            grad = tiles(do_ref, rows, 0)
+            lse = lse_ref[0, :, span]
+            if side == 0:
+                lse = lse + bad
+            p = jnp.exp2(dot(key, query, NT) * BASE2 - lse)
+            e = dot(sides[side][u, 0, 1], grad, NT)
+            g = (p * (e - row_ref[:, span])).astype(jnp.bfloat16)
+            dk = dot(g, query, NN) * SCALE
+            dv = dot(p.astype(jnp.bfloat16), grad, NN)
+            dqt_ref[:, span] += dot(key, g, TN)
+            outs[side][u, 0, 0] = dk.astype(outs[side].dtype)
             outs[side][u, 0, 1] = dv.astype(outs[side].dtype)
     for b in range(ROWS):
-        dq_ref[b, 0, 0] = (dqt_ref[b] * SCALE).T.astype(jnp.bfloat16)
+        dq = dqt_ref[:, b * tokens : (b + 1) * tokens] * SCALE
+        dq_ref[b, 0, 0] = dq.T.astype(jnp.bfloat16)
 
 
 def heads_spec(first, count, tokens):
     return pl.BlockSpec((ROWS, 1, count, tokens, HEAD_DIM), lambda i: (0, first + i, 0, 0, 0))
 
 
-def attend_backward(first, heads, bad, q, kv_left, kv, kv_right, grad, mixed, lse, after):
+def attend_backward(first, heads, bad, q, kv_other, kv, kv_partner, grad, mixed, lse, after):
     tokens = q.shape[3]
     return pl.pallas_call(
         backward_kernel,
@@ -264,18 +253,18 @@
         in_specs=[pl.BlockSpec(memory_space=pltpu.SMEM), heads_spec(first, 1, tokens)]
         + [heads_spec(first, 2, tokens)] * 3
         + [heads_spec(first, 1, tokens)] * 2
-        + [pl.BlockSpec((1, ROWS, 1, tokens), lambda i: (first + i, 0, 0, 0))]
+        + [pl.BlockSpec((1, 1, ROWS * tokens), lambda i: (first + i, 0, 0))]
         + [pl.BlockSpec(memory_space=pl.ANY)] * len(after),
         out_specs=[heads_spec(0, 1, tokens)] + [heads_spec(0, 2, tokens)] * 3,
         out_shape=[bf16(ROWS, heads, 1, tokens, HEAD_DIM)]
         + [bf16(ROWS, heads, 2, tokens, HEAD_DIM)] * 3,
         scratch_shapes=[
-            pltpu.VMEM((ROWS, HEAD_DIM, tokens), jnp.float32),
-            pltpu.VMEM((ROWS, 1, tokens), jnp.float32),
+            pltpu.VMEM((HEAD_DIM, ROWS * tokens), jnp.float32),
+            pltpu.VMEM((1, ROWS * tokens), jnp.float32),
         ],
         cost_estimate=cost(100),
         compiler_params=params(),
-    )(bad, q, kv_left, kv, kv_right, grad, mixed, lse, *after)
+    )(bad, q, kv_other, kv, kv_partner, grad, mixed, lse, *after)
 
 
 def total_kernel(dq_ref, own_ref, a_ref, b_ref, _, out_ref):
@@ -328,7 +317,7 @@
 
 
 def temporal_forward_kernel(*refs):
-    ins, outs = refs[:PARTS], refs[PARTS:]
+    ins, outs = refs[:PARTS], refs[-PARTS:]
     parts = [[ref[0, t].astype(jnp.float32) for ref in ins] for t in range(3)]
     weights = temporal_weights(parts[0], parts[1])
     for g in range(PARTS):
@@ -379,14 +368,14 @@
     return lax.all_to_all(x, axis, split_axis=0, concat_axis=0, tiled=True)
 
 
-def shift_right(x):
-    count = lax.axis_size("wa")
-    return lax.ppermute(x, "wa", [(i, i + 1) for i in range(count - 1)])
-
-
-def shift_left(x):
-    count = lax.axis_size("wa")
-    return lax.ppermute(x, "wa", [(i + 1, i) for i in range(count - 1)])
+def trade_partner(x):
+    return lax.ppermute(x, "wa", [(i, i ^ 1) for i in range(lax.axis_size("wa"))])
+
+
+def trade_other(x):
+    firsts = range(1, lax.axis_size("wa") - 1, 2)
+    pairs = [(i, i + 1) for i in firsts] + [(i + 1, i) for i in firsts]
+    return lax.ppermute(x, "wa", pairs)
 
 
 def shards(queries, tile_keys, values, probes, anchors, upstream):
@@ -397,25 +386,28 @@
         return x.reshape(tokens, shape[-1])
 
     place = lax.axis_index("wa")
-    bad = jnp.stack([place == 0, place == lax.axis_size("wa") - 1]).astype(jnp.float32) * BIG
+    no_other = (place == 0) | (place == lax.axis_size("wa") - 1)
+    bad = no_other.astype(jnp.float32).reshape(1) * BIG
 
     kv_sent = pack([flat(tile_keys), flat(values)])
     kv = swap(kv_sent, "ha")
-    pau = trade(pack_partners([flat(probes), flat(anchors), flat(upstream)], [kv_sent]))
-    kv_left = shift_right(kv)
-    kv_right = shift_left(kv)
-    forward_sent = temporal_call(temporal_forward_kernel, pau, 1, 100)
-    q = swap(pack([flat(queries)], forward_sent[:1]), "ha")
-    grad_sent = join_partners(trade(forward_sent))
+    kv_other = trade_other(kv)
+    kv_partner = trade_partner(kv)
+    pau_sent = pack_partners([flat(probes), flat(anchors), flat(upstream)], [kv_sent])
+    pau = trade(pau_sent)
+    q_sent = pack([flat(queries)], pau_sent[:1])
+    q = swap(q_sent, "ha")
+    grad_parts = trade(temporal_call(temporal_forward_kernel, pau, 1, 100, [kv, q_sent]))
+    grad_sent = join_partners(grad_parts)
     grad = swap(grad_sent, "ha")
-    mixed, lse = attend_forward(bad, q, kv_left, kv, kv_right, grad_sent)
+    mixed, lse = attend_forward(bad, q, kv_other, kv, kv_partner, grad_sent)
     mixed_sent = split_partners(swap(mixed, "ha"))
     mixed_parts = trade(mixed_sent)
     def backward(first, heads, after):
-        dq, to_left, own, to_right = attend_backward(
-            first, heads, bad, q, kv_left, kv, kv_right, grad, mixed, lse, after
+        dq, to_other, own, to_partner = attend_backward(
+            first, heads, bad, q, kv_other, kv, kv_partner, grad, mixed, lse, after
         )
-        return dq, own, shift_right(to_right), shift_left(to_left)
+        return dq, own, trade_other(to_other), trade_partner(to_partner)
 
     early = GROUP - 1
     one = backward(0, early, [])

time: 214 us -> 207 us (0.967)
  Pallas kernels: 83 us -> 74.5 us
  waiting for transfers between devices: 61.1 us -> 68.3 us
  starting transfers between devices: 64.2 us -> 58.2 us
    pallas_call x2, Pallas kernels: 29.6 us -> 21.8 us  [attend_backward(): pl.pallas_call(backward_kernel, grid=(heads,), in_specs=[pl.BlockSpec(mem...]
    ppermute x6, waiting for transfers between devices: 5.62 us -> 10.1 us  [the longest x3 10 us: trade_other(): return lax.ppermute(x, 'wa', pairs)]
    ppermute x6, starting transfers between devices: 23.6 us -> 19.6 us  [the longest x3 17.5 us: trade_other(): return lax.ppermute(x, 'wa', pairs)]
    ppermute x12, waiting for transfers between devices: 36.7 us -> 40.7 us  [trade(): lax.ppermute(chunks[s], 'tm', [(i, i ^ s) for i in range(PARTS)])]
    all_to_all x6, starting transfers between devices: 27.1 us -> 24.8 us  [swap(): return lax.all_to_all(x, axis, split_axis=0, concat_axis=0, tiled=True)]
  transfers between devices with their start and end apart: 24 -> 24, of which waited for: 9 -> 10; matrix products, arithmetic and copies ran while one was open for 0% -> 0% of each run, Pallas kernels for 36% -> 33%
where the time goes in v4:
time: 207 us; the launch traced here: 204 us
  Pallas kernels  74.5 us (36%)
  waiting for transfers between devices  68.3 us (33%)
  starting transfers between devices  58.2 us (28%)
  local copies, waits for them, and re-layouts  2.49 us (1%)
    ppermute x12, waiting for transfers between devices, trade(): lax.ppermute(chunks[s], 'tm', [(i, i ^ s) for i in range(PARTS)])  40.7 us
    all_to_all x6, starting transfers between devices, swap(): return lax.all_to_all(x, axis, split_axis=0, concat_axis=0, tiled=True)  24.8 us
    pallas_call x2, Pallas kernels, attend_backward(): pl.pallas_call(backward_kernel, grid=(heads,), in_specs=[pl.BlockSpec(mem...  21.8 us
    pallas_call x7, Pallas kernels, move(): pl.pallas_call(kernel, in_specs=[pl.BlockSpec(memory_space=pltpu.VMEM)] *...  18.8 us
    all_to_all x6, waiting for transfers between devices, swap(): return lax.all_to_all(x, axis, split_axis=0, concat_axis=0, tiled=True)  17.6 us
    ppermute x3, starting transfers between devices, trade_other(): return lax.ppermute(x, 'wa', pairs)  17.5 us
    pallas_call x2, Pallas kernels, temporal_call(): pl.pallas_call(kernel, grid=(group, tokens // rows), in_specs=[spec(a.sha...  15.1 us
    ppermute x12, starting transfers between devices, trade(): lax.ppermute(chunks[s], 'tm', [(i, i ^ s) for i in range(PARTS)])  13.8 us
  transfers between devices with their start and end apart: 24, of which 10 were waited for; matrix products, arithmetic and copies ran while one was open for 0% of the time, Pallas kernels for 33%

profile of v4, /device:TPU:8, one launch (start us, length us, event | category | flops | bytes accessed | tf_op | source)
XLA Modules:
  0.0 204.3 jit_solution(16187059978964339395)
XLA Ops:
  0.6 2.8 %shard_map.101.refs_3_ = bf16[4,3,2,256,128]{4,3,2,1,0:T(8,128)(2,1)} custom-call(bf16[256,1536]{1,0:T(8,128)(2,1)} %bitcast.13, bf16[256,1536]{1,0:T(8,128)(2,1)} %bitcast.14), custom_call_target="tpu_custom_call" | custom-call | flops 100000000 | bytes 1024 | tf_op jit(solution)/shard_map/pallas_call | solution.py:49
  3.4 4.3 %all-to-all-start.1 = ((bf16[4,3,2,256,128]{4,3,2,1,0:T(8,128)(2,1)}), bf16[4,3,2,256,128]{4,3,2,1,0:T(8,128)(2,1)}, u32[]{:S(2)}, u32[]{:S(2)}) async-start(bf16[4,3,2,256,128]{4,3,2,1,0:T(8,128)(2,1)} %shard_map.101.refs_3_), calls=%async_computation.1 | async-start | bytes 3145728 | tf_op jit(solution)/shard_map/all_to_all | solution.py:368
  7.8 3.4 %shard_map.102 = (bf16[3,3,256,128]{3,2,1,0:T(8,128)(2,1)}, bf16[3,3,256,128]{3,2,1,0:T(8,128)(2,1)}, bf16[3,3,256,128]{3,2,1,0:T(8,128)(2,1)}, bf16[3,3,256,128]{3,2,1,0:T(8,128)(2,1)}) custom-call(bf16[256,1536]{1,0:T(8,128)(2,1)} %bitcast.15, bf16[256,1536]{1,0:T(8,128)(2,1)} %bitcast.16, bf16[256,1536]{1,0:T(8,128)(2,1)} %bitcast.17, ...), custom_call_target="tpu_custom_call" | custom-call | flops 100000000 | bytes 1024 | tf_op jit(solution)/shard_map/pallas_call | solution.py:49
  11.2 2.3 %collective-permute-start.3 = (bf16[3,3,256,128]{3,2,1,0:T(8,128)(2,1)}, bf16[3,3,256,128]{3,2,1,0:T(8,128)(2,1)}, u32[]{:S(2)}, u32[]{:S(2)}) collective-permute-start(bf16[3,3,256,128]{3,2,1,0:T(8,128)(2,1)} %get-tuple-element.38), channel_id=1, source_target_pairs={{0,64},{32,96},{64,0},{96,32},{1,65},{33,97},{65,1},{97,33},{2,66}... | collective-permute-start | bytes 1769480 | tf_op jit(solution)/shard_map/ppermute | solution.py:142
  14.6 2.1 %shard_map.103.refs_5_ = bf16[4,3,1,256,128]{4,3,2,1,0:T(8,128)(2,1)} custom-call(bf16[256,1536]{1,0:T(8,128)(2,1)} %bitcast.12, bf16[3,3,256,128]{3,2,1,0:T(8,128)(2,1)} %get-tuple-element.36.refs_1_.refs_0_), custom_call_target="tpu_custom_call" | custom-call | flops 100000000 | bytes 1024 | tf_op jit(solution)/shard_map/pallas_call | solution.py:49
  16.7 12.1 %all-to-all-done.1.refs_4_.own_ref = bf16[4,3,2,256,128]{4,3,2,1,0:T(8,128)(2,1)} async-done(((bf16[4,3,2,256,128]{4,3,2,1,0:T(8,128)(2,1)}), bf16[4,3,2,256,128]{4,3,2,1,0:T(8,128)(2,1)}, u32[]{:S(2)}, u32[]{:S(2)}) %all-to-all-start.1) | async-done | bytes 1572896 | tf_op jit(solution)/shard_map/all_to_all | solution.py:368
  28.8 3.5 %all-to-all-start = ((bf16[4,3,1,256,128]{4,3,2,1,0:T(8,128)(2,1)}), bf16[4,3,1,256,128]{4,3,2,1,0:T(8,128)(2,1)S(1)}, u32[]{:S(2)}, u32[]{:S(2)}) async-start(bf16[4,3,1,256,128]{4,3,2,1,0:T(8,128)(2,1)} %shard_map.103.refs_5_), calls=%async_computation | async-start | bytes 1572864 | tf_op jit(solution)/shard_map/all_to_all | solution.py:368
  34.3 4.3 %collective-permute-start = (bf16[4,3,2,256,128]{4,3,2,1,0:T(8,128)(2,1)}, bf16[4,3,2,256,128]{4,3,2,1,0:T(8,128)(2,1)}, u32[]{:S(2)}, u32[]{:S(2)}) collective-permute-start(bf16[4,3,2,256,128]{4,3,2,1,0:T(8,128)(2,1)} %all-to-all-done.1.refs_4_.own_ref), channel_id=1, source_target_pairs={{1,2},{3,4},{5,6},{2,1},{4,3},{6,5},{9,10},{11,12},{13,14},{10,9},... | collective-permute-start | bytes 4718600 | tf_op jit(solution)/shard_map/ppermute | solution.py:378
  38.7 2.3 %collective-permute-done.4.refs_3_ = bf16[3,3,256,128]{3,2,1,0:T(8,128)(2,1)} collective-permute-done((bf16[3,3,256,128]{3,2,1,0:T(8,128)(2,1)}, bf16[3,3,256,128]{3,2,1,0:T(8,128)(2,1)}, u32[]{:S(2)}, u32[]{:S(2)}) %collective-permute-start.4) | collective-permute-done | bytes 589856 | tf_op jit(solution)/shard_map/ppermute | solution.py:142
  41.0 6.5 %shard_map.104 = (bf16[3,1,256,128]{3,2,1,0:T(8,128)(2,1)}, bf16[3,1,256,128]{3,2,1,0:T(8,128)(2,1)}, bf16[3,1,256,128]{3,2,1,0:T(8,128)(2,1)}, bf16[3,1,256,128]{3,2,1,0:T(8,128)(2,1)}) custom-call(bf16[3,3,256,128]{3,2,1,0:T(8,128)(2,1)} %get-tuple-element.36.refs_1_.refs_0_, bf16[3,3,256,128]{3,2,1,0:T(8,128)(2,1)} %collective-permute-done.2.refs_1_, ...), custom_call_target="tpu_custom_call" | custom-call | flops 99999997952 | bytes 1024 | tf_op jit(solution)/shard_map/pallas_call | solution.py:355
  48.1 2.3 %collective-permute-start.6 = (bf16[3,1,256,128]{3,2,1,0:T(8,128)(2,1)}, bf16[3,1,256,128]{3,2,1,0:T(8,128)(2,1)}, u32[]{:S(2)}, u32[]{:S(2)}) collective-permute-start(bf16[3,1,256,128]{3,2,1,0:T(8,128)(2,1)} %get-tuple-element.42), channel_id=1, source_target_pairs={{0,64},{32,96},{64,0},{96,32},{1,65},{33,97},{65,1},{97,33},{2,66}... | collective-permute-start | bytes 589832 | tf_op jit(solution)/shard_map/ppermute | solution.py:142
  51.1 30.0 %collective-permute-done.6.refs_2_ = bf16[3,1,256,128]{3,2,1,0:T(8,128)(2,1)} collective-permute-done((bf16[3,1,256,128]{3,2,1,0:T(8,128)(2,1)}, bf16[3,1,256,128]{3,2,1,0:T(8,128)(2,1)}, u32[]{:S(2)}, u32[]{:S(2)}) %collective-permute-start.6) | collective-permute-done | bytes 196640 | tf_op jit(solution)/shard_map/ppermute | solution.py:142
  81.9 2.2 %shard_map.105._ = bf16[4,3,1,256,128]{4,3,2,1,0:T(8,128)(2,1)} custom-call(bf16[3,1,256,128]{3,2,1,0:T(8,128)(2,1)} %get-tuple-element.40.refs_0_, bf16[3,1,256,128]{3,2,1,0:T(8,128)(2,1)} %copy-done.4, bf16[3,1,256,128]{3,2,1,0:T(8,128)(2,1)} %collective-permute-done.6.refs_2_, bf16[3,1,256,128]{3,2,1,0:T(8,128)(2,1)} %collective-permute-done.7.refs_3_), custom_call_target="tpu_custom_call" | custom-call | flops 100000000 | bytes 1024 | tf_op jit(solution)/shard_map/pallas_call | solution.py:49
  84.0 4.8 %all-to-all-start.2 = ((bf16[4,3,1,256,128]{4,3,2,1,0:T(8,128)(2,1)}), bf16[4,3,1,256,128]{4,3,2,1,0:T(8,128)(2,1)}, u32[]{:S(2)}, u32[]{:S(2)}) async-start(bf16[4,3,1,256,128]{4,3,2,1,0:T(8,128)(2,1)} %shard_map.105._), calls=%async_computation.2 | async-start | bytes 1572864 | tf_op jit(solution)/shard_map/all_to_all | solution.py:368
  88.8 12.7 %shard_map.106 = (bf16[4,3,1,256,128]{4,3,2,1,0:T(8,128)(2,1)}, f32[3,1,1024]{2,1,0:T(1,128)}) custom-call(f32[1]{0:T(128)} %bitcast.bad_ref, bf16[4,3,1,256,128]{4,3,2,1,0:T(8,128)(2,1)} %copy-done.2, bf16[4,3,2,256,128]{4,3,2,1,0:T(8,128)(2,1)} %collective-permute-done.other_ref, bf16[4,3,2,256,128]{4,3,2,1,0:T(8,128)(2,1)} %all-to-all-done.1.refs_4_.own_ref, ...), custom_call_target="tpu_custom_call" | custom-call | flops 99999997952 | bytes 1024 | tf_op jit(solution)/shard_map/pallas_call | solution.py:189
  102.4 3.9 %all-to-all-start.3 = ((bf16[4,3,1,256,128]{4,3,2,1,0:T(8,128)(2,1)}), bf16[4,3,1,256,128]{4,3,2,1,0:T(8,128)(2,1)S(1)}, u32[]{:S(2)}, u32[]{:S(2)}) async-start(bf16[4,3,1,256,128]{4,3,2,1,0:T(8,128)(2,1)} %get-tuple-element.44.o_ref), calls=%async_computation.3 | async-start | bytes 1572864 | tf_op jit(solution)/shard_map/all_to_all | solution.py:368
  106.3 13.9 %shard_map.107 = (bf16[4,2,1,256,128]{4,3,2,1,0:T(8,128)(2,1)}, bf16[4,2,2,256,128]{4,3,2,1,0:T(8,128)(2,1)}, bf16[4,2,2,256,128]{4,3,2,1,0:T(8,128)(2,1)}, bf16[4,2,2,256,128]{4,3,2,1,0:T(8,128)(2,1)}) custom-call(f32[1]{0:T(128)} %bitcast.bad_ref, bf16[4,3,1,256,128]{4,3,2,1,0:T(8,128)(2,1)} %copy-done.2, ...), custom_call_target="tpu_custom_call" | custom-call | flops 99999997952 | bytes 1024 | tf_op jit(solution)/shard_map/pallas_call | solution.py:250
  120.2 7.1 %collective-permute-start.8 = (bf16[4,2,2,256,128]{4,3,2,1,0:T(8,128)(2,1)}, bf16[4,2,2,256,128]{4,3,2,1,0:T(8,128)(2,1)}, u32[]{:S(2)}, u32[]{:S(2)}) collective-permute-start(bf16[4,2,2,256,128]{4,3,2,1,0:T(8,128)(2,1)} %get-tuple-element.48), channel_id=1, source_target_pairs={{1,2},{3,4},{5,6},{2,1},{4,3},{6,5},{9,10},{11,12},{13,14},{10,9},... | collective-permute-start | bytes 3145736 | tf_op jit(solution)/shard_map/ppermute | solution.py:378
  130.4 2.6 %collective-permute-start.13 = (bf16[3,1,256,128]{3,2,1,0:T(8,128)(2,1)}, bf16[3,1,256,128]{3,2,1,0:T(8,128)(2,1)S(1)}, u32[]{:S(2)}, u32[]{:S(2)}) collective-permute-start(bf16[3,1,256,128]{3,2,1,0:T(8,128)(2,1)} %get-tuple-element.59), channel_id=1, source_target_pairs={{0,64},{32,96},{64,0},{96,32},{1,65},{33,97},{65,1},{97,33},{2,66}... | collective-permute-start | bytes 589832 | tf_op jit(solution)/shard_map/ppermute | solution.py:142
  133.8 7.9 %shard_map.109 = (bf16[4,1,1,256,128]{4,3,2,1,0:T(8,128)(2,1)}, bf16[4,1,2,256,128]{4,3,2,1,0:T(8,128)(2,1)}, bf16[4,1,2,256,128]{4,3,2,1,0:T(8,128)(2,1)}, bf16[4,1,2,256,128]{4,3,2,1,0:T(8,128)(2,1)}) custom-call(f32[1]{0:T(128)} %bitcast.bad_ref, bf16[4,3,1,256,128]{4,3,2,1,0:T(8,128)(2,1)} %copy-done.2, ...), custom_call_target="tpu_custom_call" | custom-call | flops 99999997952 | bytes 1024 | tf_op jit(solution)/shard_map/pallas_call | solution.py:250
  141.7 10.0 %collective-permute-done.8.a_ref = bf16[4,2,2,256,128]{4,3,2,1,0:T(8,128)(2,1)} collective-permute-done((bf16[4,2,2,256,128]{4,3,2,1,0:T(8,128)(2,1)}, bf16[4,2,2,256,128]{4,3,2,1,0:T(8,128)(2,1)}, u32[]{:S(2)}, u32[]{:S(2)}) %collective-permute-start.8) | collective-permute-done | bytes 1048608 | tf_op jit(solution)/shard_map/ppermute | solution.py:378
  151.7 6.0 %collective-permute-start.10 = (bf16[4,1,2,256,128]{4,3,2,1,0:T(8,128)(2,1)}, bf16[4,1,2,256,128]{4,3,2,1,0:T(8,128)(2,1)S(1)}, u32[]{:S(2)}, u32[]{:S(2)}) collective-permute-start(bf16[4,1,2,256,128]{4,3,2,1,0:T(8,128)(2,1)} %get-tuple-element.53), channel_id=1, source_target_pairs={{1,2},{3,4},{5,6},{2,1},{4,3},{6,5},{9,10},{11,12},{13,14},{10,9},... | collective-permute-start | bytes 1572872 | tf_op jit(solution)/shard_map/ppermute | solution.py:378
  157.8 3.6 %shard_map.110.refs_8_ = bf16[4,2,3,256,128]{4,3,2,1,0:T(8,128)(2,1)} custom-call(bf16[4,2,1,256,128]{4,3,2,1,0:T(8,128)(2,1)} %get-tuple-element.46.rest_1_.dq_ref, bf16[4,2,2,256,128]{4,3,2,1,0:T(8,128)(2,1)} %get-tuple-element.47.own_ref, bf16[4,2,2,256,128]{4,3,2,1,0:T(8,128)(2,1)} %collective-permute-done.8.a_ref, ...), custom_call_target="tpu_custom_call" | custom-call | flops 100000000 | bytes 1024 | tf_op jit(solution)/shard_map/pallas_call | solution.py:283
  161.4 4.8 %all-to-all-start.4 = ((bf16[4,2,3,256,128]{4,3,2,1,0:T(8,128)(2,1)}), bf16[4,2,3,256,128]{4,3,2,1,0:T(8,128)(2,1)}, u32[]{:S(2)}, u32[]{:S(2)}) async-start(bf16[4,2,3,256,128]{4,3,2,1,0:T(8,128)(2,1)} %shard_map.110.refs_8_), calls=%async_computation.4 | async-start | bytes 3145728 | tf_op jit(solution)/shard_map/all_to_all | solution.py:368
  167.0 8.7 %shard_map.113 = (bf16[3,2,256,128]{3,2,1,0:T(8,128)(2,1)}, bf16[3,2,256,128]{3,2,1,0:T(8,128)(2,1)}, bf16[3,2,256,128]{3,2,1,0:T(8,128)(2,1)}, bf16[3,2,256,128]{3,2,1,0:T(8,128)(2,1)}) custom-call(bf16[3,3,256,128]{3,2,1,0:T(8,128)(2,1)} %get-tuple-element.36.refs_1_.refs_0_, bf16[3,3,256,128]{3,2,1,0:T(8,128)(2,1)} %collective-permute-done.2.refs_1_, ...), custom_call_target="tpu_custom_call" | custom-call | flops 99999997952 | bytes 1024 | tf_op jit(solution)/shard_map/pallas_call | solution.py:355
  175.7 2.7 %collective-permute-start.16 = (bf16[3,2,256,128]{3,2,1,0:T(8,128)(2,1)}, bf16[3,2,256,128]{3,2,1,0:T(8,128)(2,1)}, u32[]{:S(2)}, u32[]{:S(2)}) collective-permute-start(bf16[3,2,256,128]{3,2,1,0:T(8,128)(2,1)} %get-tuple-element.63), channel_id=1, source_target_pairs={{0,64},{32,96},{64,0},{96,32},{1,65},{33,97},{65,1},{97,33},{2,66}... | collective-permute-start | bytes 1179656 | tf_op jit(solution)/shard_map/ppermute | solution.py:142
  179.1 4.4 %all-to-all-done.4._.refs_0_ = bf16[4,2,3,256,128]{4,3,2,1,0:T(8,128)(2,1)} async-done(((bf16[4,2,3,256,128]{4,3,2,1,0:T(8,128)(2,1)}), bf16[4,2,3,256,128]{4,3,2,1,0:T(8,128)(2,1)}, u32[]{:S(2)}, u32[]{:S(2)}) %all-to-all-start.4) | async-done | bytes 1572896 | tf_op jit(solution)/shard_map/all_to_all | solution.py:368
  183.5 2.5 %shard_map.111 = bf16[4,1,3,256,128]{4,3,2,1,0:T(8,128)(2,1)} custom-call(bf16[4,1,1,256,128]{4,3,2,1,0:T(8,128)(2,1)} %get-tuple-element.51._.dq_ref, bf16[4,1,2,256,128]{4,3,2,1,0:T(8,128)(2,1)} %get-tuple-element.52.own_ref, bf16[4,1,2,256,128]{4,3,2,1,0:T(8,128)(2,1)} %copy-done.3, bf16[4,1,2,256,128]{4,3,2,1,0:T(8,128)(2,1)} %collective-permute-done.11.b_ref, ...), custom_call_target="tpu_custom_call" | custom-call | flops 100000000 | bytes 1024 | tf_op jit(solution)/shard_map/pallas_call | solution.py:283
  186.0 3.5 %all-to-all-start.5 = ((bf16[4,1,3,256,128]{4,3,2,1,0:T(8,128)(2,1)}), bf16[4,1,3,256,128]{4,3,2,1,0:T(8,128)(2,1)S(1)}, u32[]{:S(2)}, u32[]{:S(2)}) async-start(bf16[4,1,3,256,128]{4,3,2,1,0:T(8,128)(2,1)} %shard_map.111), calls=%async_computation.5 | async-start | bytes 1572864 | tf_op jit(solution)/shard_map/all_to_all | solution.py:368
  189.6 7.5 %collective-permute-done.17.refs_3_ = bf16[3,2,256,128]{3,2,1,0:T(8,128)(2,1)} collective-permute-done((bf16[3,2,256,128]{3,2,1,0:T(8,128)(2,1)}, bf16[3,2,256,128]{3,2,1,0:T(8,128)(2,1)}, u32[]{:S(2)}, u32[]{:S(2)}) %collective-permute-start.17) | collective-permute-done | bytes 393248 | tf_op jit(solution)/shard_map/ppermute | solution.py:142
  197.0 2.8 %shard_map.114 = (bf16[256,1536]{1,0:T(8,128)(2,1)}, bf16[256,1536]{1,0:T(8,128)(2,1)}) custom-call(bf16[3,2,256,128]{3,2,1,0:T(8,128)(2,1)} %get-tuple-element.61.refs_0_, bf16[3,2,256,128]{3,2,1,0:T(8,128)(2,1)} %collective-permute-done.15.refs_1_, bf16[3,2,256,128]{3,2,1,0:T(8,128)(2,1)} %collective-permute-done.16.refs_2_, ...), custom_call_target="tpu_custom_call" | custom-call | flops 99999997952 | bytes 1024 | tf_op jit(solution)/shard_map/pallas_call | solution.py:49
  200.9 3.4 %shard_map.112 = (bf16[256,1536]{1,0:T(8,128)(2,1)}, bf16[256,1536]{1,0:T(8,128)(2,1)}, bf16[256,1536]{1,0:T(8,128)(2,1)}) custom-call(bf16[4,2,3,256,128]{4,3,2,1,0:T(8,128)(2,1)} %all-to-all-done.4._.refs_0_, bf16[4,1,3,256,128]{4,3,2,1,0:T(8,128)(2,1)} %copy-done.1), custom_call_target="tpu_custom_call" | custom-call | flops 100000000 | bytes 1024 | tf_op jit(solution)/shard_map/pallas_call | solution.py:49
  (44 shorter events, 12.7 us)
Async XLA Ops:
  3.4 25.4 %all-to-all-start.1 = ((bf16[4,3,2,256,128]{4,3,2,1,0:T(8,128)(2,1)}), bf16[4,3,2,256,128]{4,3,2,1,0:T(8,128)(2,1)}, u32[]{:S(2)}, u32[]{:S(2)}) async-start(bf16[4,3,2,256,128]{4,3,2,1,0:T(8,128)(2,1)} %shard_map.101.refs_3_), calls=%async_computation.1 | async-start | bytes 3145728 | tf_op jit(solution)/shard_map/all_to_all | solution.py:368
  11.2 27.4 %collective-permute-start.2 = (bf16[3,3,256,128]{3,2,1,0:T(8,128)(2,1)}, bf16[3,3,256,128]{3,2,1,0:T(8,128)(2,1)}, u32[]{:S(2)}, u32[]{:S(2)}) collective-permute-start(bf16[3,3,256,128]{3,2,1,0:T(8,128)(2,1)} %get-tuple-element.37), channel_id=1, source_target_pairs={{0,32},{32,0},{64,96},{96,64},{1,33},{33,1},{65,97},{97,65},{2,34}... | collective-permute-start | bytes 1769480 | tf_op jit(solution)/shard_map/ppermute | solution.py:142
  11.2 27.5 %collective-permute-start.3 = (bf16[3,3,256,128]{3,2,1,0:T(8,128)(2,1)}, bf16[3,3,256,128]{3,2,1,0:T(8,128)(2,1)}, u32[]{:S(2)}, u32[]{:S(2)}) collective-permute-start(bf16[3,3,256,128]{3,2,1,0:T(8,128)(2,1)} %get-tuple-element.38), channel_id=1, source_target_pairs={{0,64},{32,96},{64,0},{96,32},{1,65},{33,97},{65,1},{97,33},{2,66}... | collective-permute-start | bytes 1769480 | tf_op jit(solution)/shard_map/ppermute | solution.py:142
  13.5 27.5 %collective-permute-start.4 = (bf16[3,3,256,128]{3,2,1,0:T(8,128)(2,1)}, bf16[3,3,256,128]{3,2,1,0:T(8,128)(2,1)}, u32[]{:S(2)}, u32[]{:S(2)}) collective-permute-start(bf16[3,3,256,128]{3,2,1,0:T(8,128)(2,1)} %get-tuple-element.39), channel_id=1, source_target_pairs={{0,96},{32,64},{64,32},{96,0},{1,97},{33,65},{65,33},{97,1},{2,98}... | collective-permute-start | bytes 1769480 | tf_op jit(solution)/shard_map/ppermute | solution.py:142
  28.8 55.2 %all-to-all-start = ((bf16[4,3,1,256,128]{4,3,2,1,0:T(8,128)(2,1)}), bf16[4,3,1,256,128]{4,3,2,1,0:T(8,128)(2,1)S(1)}, u32[]{:S(2)}, u32[]{:S(2)}) async-start(bf16[4,3,1,256,128]{4,3,2,1,0:T(8,128)(2,1)} %shard_map.103.refs_5_), calls=%async_computation | async-start | bytes 1572864 | tf_op jit(solution)/shard_map/all_to_all | solution.py:368
  32.3 56.5 %collective-permute-start.1 = (bf16[4,3,2,256,128]{4,3,2,1,0:T(8,128)(2,1)}, bf16[4,3,2,256,128]{4,3,2,1,0:T(8,128)(2,1)}, u32[]{:S(2)}, u32[]{:S(2)}) collective-permute-start(bf16[4,3,2,256,128]{4,3,2,1,0:T(8,128)(2,1)} %all-to-all-done.1.refs_4_.own_ref), channel_id=1, source_target_pairs={{0,1},{1,0},{2,3},{3,2},{4,5},{5,4},{6,7},{7,6},{8,9},{9,8},{10,11... | collective-permute-start | bytes 4718600 | tf_op jit(solution)/shard_map/ppermute | solution.py:372
  34.3 54.5 %collective-permute-start = (bf16[4,3,2,256,128]{4,3,2,1,0:T(8,128)(2,1)}, bf16[4,3,2,256,128]{4,3,2,1,0:T(8,128)(2,1)}, u32[]{:S(2)}, u32[]{:S(2)}) collective-permute-start(bf16[4,3,2,256,128]{4,3,2,1,0:T(8,128)(2,1)} %all-to-all-done.1.refs_4_.own_ref), channel_id=1, source_target_pairs={{1,2},{3,4},{5,6},{2,1},{4,3},{6,5},{9,10},{11,12},{13,14},{10,9},... | collective-permute-start | bytes 4718600 | tf_op jit(solution)/shard_map/ppermute | solution.py:378
  47.5 3.6 %collective-permute-start.5 = (bf16[3,1,256,128]{3,2,1,0:T(8,128)(2,1)}, bf16[3,1,256,128]{3,2,1,0:T(8,128)(2,1)S(1)}, u32[]{:S(2)}, u32[]{:S(2)}) collective-permute-start(bf16[3,1,256,128]{3,2,1,0:T(8,128)(2,1)} %get-tuple-element.41), channel_id=1, source_target_pairs={{0,32},{32,0},{64,96},{96,64},{1,33},{33,1},{65,97},{97,65},{2,34}... | collective-permute-start | bytes 589832 | tf_op jit(solution)/shard_map/ppermute | solution.py:142
  48.1 32.9 %collective-permute-start.6 = (bf16[3,1,256,128]{3,2,1,0:T(8,128)(2,1)}, bf16[3,1,256,128]{3,2,1,0:T(8,128)(2,1)}, u32[]{:S(2)}, u32[]{:S(2)}) collective-permute-start(bf16[3,1,256,128]{3,2,1,0:T(8,128)(2,1)} %get-tuple-element.42), channel_id=1, source_target_pairs={{0,64},{32,96},{64,0},{96,32},{1,65},{33,97},{65,1},{97,33},{2,66}... | collective-permute-start | bytes 589832 | tf_op jit(solution)/shard_map/ppermute | solution.py:142
  50.4 31.4 %collective-permute-start.7 = (bf16[3,1,256,128]{3,2,1,0:T(8,128)(2,1)}, bf16[3,1,256,128]{3,2,1,0:T(8,128)(2,1)}, u32[]{:S(2)}, u32[]{:S(2)}) collective-permute-start(bf16[3,1,256,128]{3,2,1,0:T(8,128)(2,1)} %get-tuple-element.43), channel_id=1, source_target_pairs={{0,96},{32,64},{64,32},{96,0},{1,97},{33,65},{65,33},{97,1},{2,98}... | collective-permute-start | bytes 589832 | tf_op jit(solution)/shard_map/ppermute | solution.py:142
  51.1 30.8 %copy-start.4 = (bf16[3,1,256,128]{3,2,1,0:T(8,128)(2,1)}, bf16[3,1,256,128]{3,2,1,0:T(8,128)(2,1)S(1)}, u32[]{:S(2)}) copy-start(bf16[3,1,256,128]{3,2,1,0:T(8,128)(2,1)S(1)} %collective-permute-done.5.refs_1_) | copy-start | bytes 589828
  84.0 4.8 %copy-start.2 = (bf16[4,3,1,256,128]{4,3,2,1,0:T(8,128)(2,1)}, bf16[4,3,1,256,128]{4,3,2,1,0:T(8,128)(2,1)S(1)}, u32[]{:S(2)}) copy-start(bf16[4,3,1,256,128]{4,3,2,1,0:T(8,128)(2,1)S(1)} %all-to-all-done.q_ref) | copy-start | bytes 2359300
  84.0 18.3 %all-to-all-start.2 = ((bf16[4,3,1,256,128]{4,3,2,1,0:T(8,128)(2,1)}), bf16[4,3,1,256,128]{4,3,2,1,0:T(8,128)(2,1)}, u32[]{:S(2)}, u32[]{:S(2)}) async-start(bf16[4,3,1,256,128]{4,3,2,1,0:T(8,128)(2,1)} %shard_map.105._), calls=%async_computation.2 | async-start | bytes 1572864 | tf_op jit(solution)/shard_map/all_to_all | solution.py:368
  102.4 25.1 %all-to-all-start.3 = ((bf16[4,3,1,256,128]{4,3,2,1,0:T(8,128)(2,1)}), bf16[4,3,1,256,128]{4,3,2,1,0:T(8,128)(2,1)S(1)}, u32[]{:S(2)}, u32[]{:S(2)}) async-start(bf16[4,3,1,256,128]{4,3,2,1,0:T(8,128)(2,1)} %get-tuple-element.44.o_ref), calls=%async_computation.3 | async-start | bytes 1572864 | tf_op jit(solution)/shard_map/all_to_all | solution.py:368
  120.2 31.5 %collective-permute-start.8 = (bf16[4,2,2,256,128]{4,3,2,1,0:T(8,128)(2,1)}, bf16[4,2,2,256,128]{4,3,2,1,0:T(8,128)(2,1)}, u32[]{:S(2)}, u32[]{:S(2)}) collective-permute-start(bf16[4,2,2,256,128]{4,3,2,1,0:T(8,128)(2,1)} %get-tuple-element.48), channel_id=1, source_target_pairs={{1,2},{3,4},{5,6},{2,1},{4,3},{6,5},{9,10},{11,12},{13,14},{10,9},... | collective-permute-start | bytes 3145736 | tf_op jit(solution)/shard_map/ppermute | solution.py:378
  127.3 30.4 %collective-permute-start.9 = (bf16[4,2,2,256,128]{4,3,2,1,0:T(8,128)(2,1)}, bf16[4,2,2,256,128]{4,3,2,1,0:T(8,128)(2,1)}, u32[]{:S(2)}, u32[]{:S(2)}) collective-permute-start(bf16[4,2,2,256,128]{4,3,2,1,0:T(8,128)(2,1)} %get-tuple-element.49), channel_id=1, source_target_pairs={{0,1},{1,0},{2,3},{3,2},{4,5},{5,4},{6,7},{7,6},{8,9},{9,8},{10,11... | collective-permute-start | bytes 3145736 | tf_op jit(solution)/shard_map/ppermute | solution.py:372
  127.4 0.9 copy-start
  130.4 35.8 %collective-permute-start.12 = (bf16[3,1,256,128]{3,2,1,0:T(8,128)(2,1)}, bf16[3,1,256,128]{3,2,1,0:T(8,128)(2,1)S(1)}, u32[]{:S(2)}, u32[]{:S(2)}) collective-permute-start(bf16[3,1,256,128]{3,2,1,0:T(8,128)(2,1)} %get-tuple-element.58), channel_id=1, source_target_pairs={{0,32},{32,0},{64,96},{96,64},{1,33},{33,1},{65,97},{97,65},{2,34}... | collective-permute-start | bytes 589832 | tf_op jit(solution)/shard_map/ppermute | solution.py:142
  130.4 35.8 %collective-permute-start.13 = (bf16[3,1,256,128]{3,2,1,0:T(8,128)(2,1)}, bf16[3,1,256,128]{3,2,1,0:T(8,128)(2,1)S(1)}, u32[]{:S(2)}, u32[]{:S(2)}) collective-permute-start(bf16[3,1,256,128]{3,2,1,0:T(8,128)(2,1)} %get-tuple-element.59), channel_id=1, source_target_pairs={{0,64},{32,96},{64,0},{96,32},{1,65},{33,97},{65,1},{97,33},{2,66}... | collective-permute-start | bytes 589832 | tf_op jit(solution)/shard_map/ppermute | solution.py:142
  133.0 33.3 %collective-permute-start.14 = (bf16[3,1,256,128]{3,2,1,0:T(8,128)(2,1)}, bf16[3,1,256,128]{3,2,1,0:T(8,128)(2,1)}, u32[]{:S(2)}, u32[]{:S(2)}) collective-permute-start(bf16[3,1,256,128]{3,2,1,0:T(8,128)(2,1)} %get-tuple-element.60), channel_id=1, source_target_pairs={{0,96},{32,64},{64,32},{96,0},{1,97},{33,65},{65,33},{97,1},{2,98}... | collective-permute-start | bytes 589832 | tf_op jit(solution)/shard_map/ppermute | solution.py:142
  151.7 27.4 %collective-permute-start.10 = (bf16[4,1,2,256,128]{4,3,2,1,0:T(8,128)(2,1)}, bf16[4,1,2,256,128]{4,3,2,1,0:T(8,128)(2,1)S(1)}, u32[]{:S(2)}, u32[]{:S(2)}) collective-permute-start(bf16[4,1,2,256,128]{4,3,2,1,0:T(8,128)(2,1)} %get-tuple-element.53), channel_id=1, source_target_pairs={{1,2},{3,4},{5,6},{2,1},{4,3},{6,5},{9,10},{11,12},{13,14},{10,9},... | collective-permute-start | bytes 1572872 | tf_op jit(solution)/shard_map/ppermute | solution.py:378
  157.8 21.4 %collective-permute-start.11 = (bf16[4,1,2,256,128]{4,3,2,1,0:T(8,128)(2,1)}, bf16[4,1,2,256,128]{4,3,2,1,0:T(8,128)(2,1)}, u32[]{:S(2)}, u32[]{:S(2)}) collective-permute-start(bf16[4,1,2,256,128]{4,3,2,1,0:T(8,128)(2,1)} %get-tuple-element.54), channel_id=1, source_target_pairs={{0,1},{1,0},{2,3},{3,2},{4,5},{5,4},{6,7},{7,6},{8,9},{9,8},{10,11... | collective-permute-start | bytes 1572872 | tf_op jit(solution)/shard_map/ppermute | solution.py:372
  161.4 22.0 %all-to-all-start.4 = ((bf16[4,2,3,256,128]{4,3,2,1,0:T(8,128)(2,1)}), bf16[4,2,3,256,128]{4,3,2,1,0:T(8,128)(2,1)}, u32[]{:S(2)}, u32[]{:S(2)}) async-start(bf16[4,2,3,256,128]{4,3,2,1,0:T(8,128)(2,1)} %shard_map.110.refs_8_), calls=%async_computation.4 | async-start | bytes 3145728 | tf_op jit(solution)/shard_map/all_to_all | solution.py:368
  166.2 0.7 copy-start.5
  166.2 0.7 copy-start.6
  175.6 13.8 %collective-permute-start.15 = (bf16[3,2,256,128]{3,2,1,0:T(8,128)(2,1)}, bf16[3,2,256,128]{3,2,1,0:T(8,128)(2,1)}, u32[]{:S(2)}, u32[]{:S(2)}) collective-permute-start(bf16[3,2,256,128]{3,2,1,0:T(8,128)(2,1)} %get-tuple-element.62), channel_id=1, source_target_pairs={{0,32},{32,0},{64,96},{96,64},{1,33},{33,1},{65,97},{97,65},{2,34}... | collective-permute-start | bytes 1179656 | tf_op jit(solution)/shard_map/ppermute | solution.py:142
  175.7 13.8 %collective-permute-start.16 = (bf16[3,2,256,128]{3,2,1,0:T(8,128)(2,1)}, bf16[3,2,256,128]{3,2,1,0:T(8,128)(2,1)}, u32[]{:S(2)}, u32[]{:S(2)}) collective-permute-start(bf16[3,2,256,128]{3,2,1,0:T(8,128)(2,1)} %get-tuple-element.63), channel_id=1, source_target_pairs={{0,64},{32,96},{64,0},{96,32},{1,65},{33,97},{65,1},{97,33},{2,66}... | collective-permute-start | bytes 1179656 | tf_op jit(solution)/shard_map/ppermute | solution.py:142
  178.4 18.6 %collective-permute-start.17 = (bf16[3,2,256,128]{3,2,1,0:T(8,128)(2,1)}, bf16[3,2,256,128]{3,2,1,0:T(8,128)(2,1)}, u32[]{:S(2)}, u32[]{:S(2)}) collective-permute-start(bf16[3,2,256,128]{3,2,1,0:T(8,128)(2,1)} %get-tuple-element.64), channel_id=1, source_target_pairs={{0,96},{32,64},{64,32},{96,0},{1,97},{33,65},{65,33},{97,1},{2,98}... | collective-permute-start | bytes 1179656 | tf_op jit(solution)/shard_map/ppermute | solution.py:142
  179.1 4.4 %copy-start.3 = (bf16[4,1,2,256,128]{4,3,2,1,0:T(8,128)(2,1)}, bf16[4,1,2,256,128]{4,3,2,1,0:T(8,128)(2,1)S(1)}, u32[]{:S(2)}) copy-start(bf16[4,1,2,256,128]{4,3,2,1,0:T(8,128)(2,1)S(1)} %collective-permute-done.10.a_ref) | copy-start | bytes 1572868
  186.0 14.0 %all-to-all-start.5 = ((bf16[4,1,3,256,128]{4,3,2,1,0:T(8,128)(2,1)}), bf16[4,1,3,256,128]{4,3,2,1,0:T(8,128)(2,1)S(1)}, u32[]{:S(2)}, u32[]{:S(2)}) async-start(bf16[4,1,3,256,128]{4,3,2,1,0:T(8,128)(2,1)} %shard_map.111), calls=%async_computation.5 | async-start | bytes 1572864 | tf_op jit(solution)/shard_map/all_to_all | solution.py:368
  200.0 0.9 copy-start.1

commit v5 on v4

--- a/solution.py
+++ b/solution.py
@@ -123,15 +123,17 @@
     )
 
 
-def unpack_heads(blocks):
-    count, tokens = blocks[0].shape[2:4]
-    heads = [(n, i) for n, block in enumerate(blocks) for i in range(block.shape[1])]
-    cells = [(a, d, h) for h in range(GROUP) for d in range(PARTS) for a in range(count)]
-    return move(
-        blocks,
-        [bf16(tokens, HEADS * HEAD_DIM)] * count,
+def unpack_heads(early, late):
+    tokens = early.shape[2]
+    places = [[(0, 0), (0, 1), (0, 2)]]
+    for h in range(GROUP - 1):
+        places.append([(0, 3 + h), (1, 2 * h), (1, 2 * h + 1)])
+    cells = [(a, d, h) for h in range(GROUP) for d in range(PARTS) for a in range(3)]
+    return move(
+        [early, late],
+        [bf16(tokens, HEADS * HEAD_DIM)] * 3,
         lambda me: [
-            (heads[h][0], (d, heads[h][1], a), a, columns(d, h)) for a, d, h in cells
+            (places[h][a][0], (d, places[h][a][1]), a, columns(d, h)) for a, d, h in cells
         ],
     )
 
@@ -267,27 +269,40 @@
     )(bad, q, kv_other, kv, kv_partner, grad, mixed, lse, *after)
 
 
-def total_kernel(dq_ref, own_ref, a_ref, b_ref, _, out_ref):
-    for h in range(out_ref.shape[1]):
-        for r in range(ROWS):
-            out_ref[r, h, 0] = dq_ref[r, h, 0]
+def add_terms(refs, row, head, tensor):
+    terms = [ref[row, head, tensor].astype(jnp.float32) for ref in refs]
+    return functools.reduce(jnp.add, terms).astype(jnp.bfloat16)
+
+
+def early_kernel(dq_ref, *refs):
+    terms, late_ref, out_ref = refs[:3], refs[3], refs[-1]
+    for r in range(ROWS):
+        out_ref[r, 0] = dq_ref[r, 0, 0]
+        for t in range(2):
+            out_ref[r, 1 + t] = add_terms(terms, r, 0, t)
+        for h in range(late_ref.shape[1]):
+            out_ref[r, 3 + h] = late_ref[r, h, 0]
+
+
+def late_kernel(*refs):
+    terms, out_ref = refs[:3], refs[-1]
+    for r in range(ROWS):
+        for h in range(terms[0].shape[1]):
             for t in range(2):
-                total = own_ref[r, h, t].astype(jnp.float32) + a_ref[r, h, t].astype(jnp.float32)
-                total = total + b_ref[r, h, t].astype(jnp.float32)
-                out_ref[r, h, 1 + t] = total.astype(jnp.bfloat16)
-
-
-def totals(dq, own, a, b, after):
-    heads, tokens = dq.shape[1], dq.shape[3]
+                out_ref[r, 2 * h + t] = add_terms(terms, r, h, t)
+
+
+def totals(kernel, slots, arrays, after=(), told=0.1):
+    tokens = arrays[0].shape[3]
     vmem = pl.BlockSpec(memory_space=pltpu.VMEM)
     return pl.pallas_call(
-        total_kernel,
-        in_specs=[vmem] * 4 + [pl.BlockSpec(memory_space=pl.ANY)],
+        kernel,
+        in_specs=[vmem] * len(arrays) + [pl.BlockSpec(memory_space=pl.ANY)] * len(after),
         out_specs=vmem,
-        out_shape=bf16(ROWS, heads, 3, tokens, HEAD_DIM),
-        cost_estimate=cost(0.1),
+        out_shape=bf16(ROWS, slots, tokens, HEAD_DIM),
+        cost_estimate=cost(told),
         compiler_params=params(),
-    )(dq, own, a, b, after)
+    )(*arrays, *after)
 
 
 def lane_sums(products):
@@ -397,7 +412,7 @@
     pau = trade(pau_sent)
     q_sent = pack([flat(queries)], pau_sent[:1])
     q = swap(q_sent, "ha")
-    grad_parts = trade(temporal_call(temporal_forward_kernel, pau, 1, 100, [kv, q_sent]))
+    grad_parts = trade(temporal_call(temporal_forward_kernel, pau, 1, 10, [kv, q_sent]))
     grad_sent = join_partners(grad_parts)
     grad = swap(grad_sent, "ha")
     mixed, lse = attend_forward(bad, q, kv_other, kv, kv_partner, grad_sent)
@@ -409,17 +424,16 @@
         )
         return dq, own, trade_other(to_other), trade_partner(to_partner)
 
-    early = GROUP - 1
-    one = backward(0, early, [])
-    two = backward(early, 1, [mixed_sent[0], one[0]])
-    summed = [totals(*one, two[0])]
+    one = backward(0, 1, [])
+    two = backward(1, GROUP - 1, [mixed_sent[0], one[0]])
+    early = totals(early_kernel, GROUP + 2, (*one, two[0]), told=0.1)
     times_sent = temporal_call(
-        temporal_backward_kernel, pau + mixed_parts, 2, 100, summed
-    )
-    summed = [swap(summed[0], "ha")]
-    summed.append(swap(totals(*two, summed[0]), "ha"))
+        temporal_backward_kernel, pau + mixed_parts, 2, 5, [early]
+    )
+    early = swap(early, "ha")
+    late = swap(totals(late_kernel, 2 * (GROUP - 1), two[1:], [early]), "ha")
     probe_grad, anchor_grad = unpack_partners(trade(times_sent), [])
-    query_grad, key_grad, value_grad = unpack_heads(summed)
+    query_grad, key_grad, value_grad = unpack_heads(early, late)
     outs = (query_grad, key_grad, value_grad, probe_grad, anchor_grad)
     return tuple(x.reshape(shape) for x in outs)
 

time: 207 us -> 199 us (0.961)
  waiting for transfers between devices: 68.3 us -> 63.1 us
    ppermute x3, waiting for transfers between devices: 10 us -> 0.45 us  [trade_other(): return lax.ppermute(x, 'wa', pairs)]
    all_to_all x6, waiting for transfers between devices: 17.6 us -> 22.2 us  [swap(): return lax.all_to_all(x, axis, split_axis=0, concat_axis=0, tiled=True)]
    ppermute x3, starting transfers between devices: 17.5 us -> 14.2 us  [trade_other(): return lax.ppermute(x, 'wa', pairs)]
  transfers between devices with their start and end apart: 24 -> 24, of which waited for: 10 -> 10; matrix products, arithmetic and copies ran while one was open for 0% -> 0% of each run, Pallas kernels for 33% -> 35%
where the time goes in v5:
time: 199 us; the launch traced here: 198 us
  Pallas kernels  74.6 us (37%)
  waiting for transfers between devices  63.1 us (32%)
  starting transfers between devices  56.8 us (29%)
  local copies, waits for them, and re-layouts  2.33 us (1%)
    ppermute x12, waiting for transfers between devices, trade(): lax.ppermute(chunks[s], 'tm', [(i, i ^ s) for i in range(PARTS)])  40.5 us
    all_to_all x6, starting transfers between devices, swap(): return lax.all_to_all(x, axis, split_axis=0, concat_axis=0, tiled=True)  26.8 us
    all_to_all x6, waiting for transfers between devices, swap(): return lax.all_to_all(x, axis, split_axis=0, concat_axis=0, tiled=True)  22.2 us
    pallas_call x2, Pallas kernels, attend_backward(): pl.pallas_call(backward_kernel, grid=(heads,), in_specs=[pl.BlockSpec(mem...  21.9 us
    pallas_call x7, Pallas kernels, move(): pl.pallas_call(kernel, in_specs=[pl.BlockSpec(memory_space=pltpu.VMEM)] *...  18.8 us
    pallas_call x2, Pallas kernels, temporal_call(): pl.pallas_call(kernel, grid=(group, tokens // rows), in_specs=[spec(a.sha...  15.2 us
    ppermute x3, starting transfers between devices, trade_other(): return lax.ppermute(x, 'wa', pairs)  14.2 us
    ppermute x12, starting transfers between devices, trade(): lax.ppermute(chunks[s], 'tm', [(i, i ^ s) for i in range(PARTS)])  13.8 us
  transfers between devices with their start and end apart: 24, of which 10 were waited for; matrix products, arithmetic and copies ran while one was open for 0% of the time, Pallas kernels for 35%

profile of v5, /device:TPU:8, one launch (start us, length us, event | category | flops | bytes accessed | tf_op | source)
XLA Modules:
  0.0 197.7 jit_solution(6110782252268824111)
XLA Ops:
  0.6 2.8 %shard_map.101.refs_3_ = bf16[4,3,2,256,128]{4,3,2,1,0:T(8,128)(2,1)} custom-call(bf16[256,1536]{1,0:T(8,128)(2,1)} %bitcast.13, bf16[256,1536]{1,0:T(8,128)(2,1)} %bitcast.14), custom_call_target="tpu_custom_call" | custom-call | flops 100000000 | bytes 1024 | tf_op jit(solution)/shard_map/pallas_call | solution.py:49
  3.5 4.3 %all-to-all-start.1 = ((bf16[4,3,2,256,128]{4,3,2,1,0:T(8,128)(2,1)}), bf16[4,3,2,256,128]{4,3,2,1,0:T(8,128)(2,1)}, u32[]{:S(2)}, u32[]{:S(2)}) async-start(bf16[4,3,2,256,128]{4,3,2,1,0:T(8,128)(2,1)} %shard_map.101.refs_3_), calls=%async_computation.1 | async-start | bytes 3145728 | tf_op jit(solution)/shard_map/all_to_all | solution.py:383
  7.8 3.4 %shard_map.102 = (bf16[3,3,256,128]{3,2,1,0:T(8,128)(2,1)}, bf16[3,3,256,128]{3,2,1,0:T(8,128)(2,1)}, bf16[3,3,256,128]{3,2,1,0:T(8,128)(2,1)}, bf16[3,3,256,128]{3,2,1,0:T(8,128)(2,1)}) custom-call(bf16[256,1536]{1,0:T(8,128)(2,1)} %bitcast.15, bf16[256,1536]{1,0:T(8,128)(2,1)} %bitcast.16, bf16[256,1536]{1,0:T(8,128)(2,1)} %bitcast.17, ...), custom_call_target="tpu_custom_call" | custom-call | flops 100000000 | bytes 1024 | tf_op jit(solution)/shard_map/pallas_call | solution.py:49
  11.2 2.3 %collective-permute-start.3 = (bf16[3,3,256,128]{3,2,1,0:T(8,128)(2,1)}, bf16[3,3,256,128]{3,2,1,0:T(8,128)(2,1)}, u32[]{:S(2)}, u32[]{:S(2)}) collective-permute-start(bf16[3,3,256,128]{3,2,1,0:T(8,128)(2,1)} %get-tuple-element.38), channel_id=1, source_target_pairs={{0,64},{32,96},{64,0},{96,32},{1,65},{33,97},{65,1},{97,33},{2,66}... | collective-permute-start | bytes 1769480 | tf_op jit(solution)/shard_map/ppermute | solution.py:144
  14.6 14.3 %all-to-all-done.1.refs_4_.own_ref = bf16[4,3,2,256,128]{4,3,2,1,0:T(8,128)(2,1)} async-done(((bf16[4,3,2,256,128]{4,3,2,1,0:T(8,128)(2,1)}), bf16[4,3,2,256,128]{4,3,2,1,0:T(8,128)(2,1)}, u32[]{:S(2)}, u32[]{:S(2)}) %all-to-all-start.1) | async-done | bytes 1572896 | tf_op jit(solution)/shard_map/all_to_all | solution.py:383
  30.8 4.3 %collective-permute-start = (bf16[4,3,2,256,128]{4,3,2,1,0:T(8,128)(2,1)}, bf16[4,3,2,256,128]{4,3,2,1,0:T(8,128)(2,1)}, u32[]{:S(2)}, u32[]{:S(2)}) collective-permute-start(bf16[4,3,2,256,128]{4,3,2,1,0:T(8,128)(2,1)} %all-to-all-done.1.refs_4_.own_ref), channel_id=1, source_target_pairs={{1,2},{3,4},{5,6},{2,1},{4,3},{6,5},{9,10},{11,12},{13,14},{10,9},... | collective-permute-start | bytes 4718600 | tf_op jit(solution)/shard_map/ppermute | solution.py:393
  35.1 2.1 %shard_map.103.refs_5_ = bf16[4,3,1,256,128]{4,3,2,1,0:T(8,128)(2,1)} custom-call(bf16[256,1536]{1,0:T(8,128)(2,1)} %bitcast.12, bf16[3,3,256,128]{3,2,1,0:T(8,128)(2,1)} %get-tuple-element.36.refs_1_.refs_0_), custom_call_target="tpu_custom_call" | custom-call | flops 100000000 | bytes 1024 | tf_op jit(solution)/shard_map/pallas_call | solution.py:49
  37.2 3.5 %all-to-all-start = ((bf16[4,3,1,256,128]{4,3,2,1,0:T(8,128)(2,1)}), bf16[4,3,1,256,128]{4,3,2,1,0:T(8,128)(2,1)S(1)}, u32[]{:S(2)}, u32[]{:S(2)}) async-start(bf16[4,3,1,256,128]{4,3,2,1,0:T(8,128)(2,1)} %shard_map.103.refs_5_), calls=%async_computation | async-start | bytes 1572864 | tf_op jit(solution)/shard_map/all_to_all | solution.py:383
  41.0 6.5 %shard_map.104 = (bf16[3,1,256,128]{3,2,1,0:T(8,128)(2,1)}, bf16[3,1,256,128]{3,2,1,0:T(8,128)(2,1)}, bf16[3,1,256,128]{3,2,1,0:T(8,128)(2,1)}, bf16[3,1,256,128]{3,2,1,0:T(8,128)(2,1)}) custom-call(bf16[3,3,256,128]{3,2,1,0:T(8,128)(2,1)} %get-tuple-element.36.refs_1_.refs_0_, bf16[3,3,256,128]{3,2,1,0:T(8,128)(2,1)} %collective-permute-done.2.refs_1_, ...), custom_call_target="tpu_custom_call" | custom-call | flops 10000000000 | bytes 1024 | tf_op jit(solution)/shard_map/pallas_call | solution.py:370
  48.2 2.3 %collective-permute-start.6 = (bf16[3,1,256,128]{3,2,1,0:T(8,128)(2,1)}, bf16[3,1,256,128]{3,2,1,0:T(8,128)(2,1)}, u32[]{:S(2)}, u32[]{:S(2)}) collective-permute-start(bf16[3,1,256,128]{3,2,1,0:T(8,128)(2,1)} %get-tuple-element.42), channel_id=1, source_target_pairs={{0,64},{32,96},{64,0},{96,32},{1,65},{33,97},{65,1},{97,33},{2,66}... | collective-permute-start | bytes 589832 | tf_op jit(solution)/shard_map/ppermute | solution.py:144
  51.1 28.6 %collective-permute-done.6.refs_2_ = bf16[3,1,256,128]{3,2,1,0:T(8,128)(2,1)} collective-permute-done((bf16[3,1,256,128]{3,2,1,0:T(8,128)(2,1)}, bf16[3,1,256,128]{3,2,1,0:T(8,128)(2,1)}, u32[]{:S(2)}, u32[]{:S(2)}) %collective-permute-start.6) | collective-permute-done | bytes 196640 | tf_op jit(solution)/shard_map/ppermute | solution.py:144
  79.7 3.4 %collective-permute-done.7.refs_3_ = bf16[3,1,256,128]{3,2,1,0:T(8,128)(2,1)} collective-permute-done((bf16[3,1,256,128]{3,2,1,0:T(8,128)(2,1)}, bf16[3,1,256,128]{3,2,1,0:T(8,128)(2,1)}, u32[]{:S(2)}, u32[]{:S(2)}) %collective-permute-start.7) | collective-permute-done | bytes 196640 | tf_op jit(solution)/shard_map/ppermute | solution.py:144
  83.2 2.2 %shard_map.105._ = bf16[4,3,1,256,128]{4,3,2,1,0:T(8,128)(2,1)} custom-call(bf16[3,1,256,128]{3,2,1,0:T(8,128)(2,1)} %get-tuple-element.40.refs_0_, bf16[3,1,256,128]{3,2,1,0:T(8,128)(2,1)} %copy-done.2, bf16[3,1,256,128]{3,2,1,0:T(8,128)(2,1)} %collective-permute-done.6.refs_2_, bf16[3,1,256,128]{3,2,1,0:T(8,128)(2,1)} %collective-permute-done.7.refs_3_), custom_call_target="tpu_custom_call" | custom-call | flops 100000000 | bytes 1024 | tf_op jit(solution)/shard_map/pallas_call | solution.py:49
  85.3 4.7 %all-to-all-start.2 = ((bf16[4,3,1,256,128]{4,3,2,1,0:T(8,128)(2,1)}), bf16[4,3,1,256,128]{4,3,2,1,0:T(8,128)(2,1)}, u32[]{:S(2)}, u32[]{:S(2)}) async-start(bf16[4,3,1,256,128]{4,3,2,1,0:T(8,128)(2,1)} %shard_map.105._), calls=%async_computation.2 | async-start | bytes 1572864 | tf_op jit(solution)/shard_map/all_to_all | solution.py:383
  90.1 12.7 %shard_map.106 = (bf16[4,3,1,256,128]{4,3,2,1,0:T(8,128)(2,1)}, f32[3,1,1024]{2,1,0:T(1,128)}) custom-call(f32[1]{0:T(128)} %bitcast.bad_ref, bf16[4,3,1,256,128]{4,3,2,1,0:T(8,128)(2,1)} %copy-done.1, bf16[4,3,2,256,128]{4,3,2,1,0:T(8,128)(2,1)} %collective-permute-done.other_ref, bf16[4,3,2,256,128]{4,3,2,1,0:T(8,128)(2,1)} %all-to-all-done.1.refs_4_.own_ref, ...), custom_call_target="tpu_custom_call" | custom-call | flops 99999997952 | bytes 1024 | tf_op jit(solution)/shard_map/pallas_call | solution.py:191
  102.9 4.7 %all-to-all-start.3 = ((bf16[4,3,1,256,128]{4,3,2,1,0:T(8,128)(2,1)}), bf16[4,3,1,256,128]{4,3,2,1,0:T(8,128)(2,1)S(1)}, u32[]{:S(2)}, u32[]{:S(2)}) async-start(bf16[4,3,1,256,128]{4,3,2,1,0:T(8,128)(2,1)} %get-tuple-element.44.o_ref), calls=%async_computation.3 | async-start | bytes 1572864 | tf_op jit(solution)/shard_map/all_to_all | solution.py:383
  107.6 8.0 %shard_map.107 = (bf16[4,1,1,256,128]{4,3,2,1,0:T(8,128)(2,1)}, bf16[4,1,2,256,128]{4,3,2,1,0:T(8,128)(2,1)}, bf16[4,1,2,256,128]{4,3,2,1,0:T(8,128)(2,1)}, bf16[4,1,2,256,128]{4,3,2,1,0:T(8,128)(2,1)}) custom-call(f32[1]{0:T(128)} %bitcast.bad_ref, bf16[4,3,1,256,128]{4,3,2,1,0:T(8,128)(2,1)} %copy-done.1, ...), custom_call_target="tpu_custom_call" | custom-call | flops 99999997952 | bytes 1024 | tf_op jit(solution)/shard_map/pallas_call | solution.py:252
  115.5 5.8 %collective-permute-start.8 = (bf16[4,1,2,256,128]{4,3,2,1,0:T(8,128)(2,1)}, bf16[4,1,2,256,128]{4,3,2,1,0:T(8,128)(2,1)}, u32[]{:S(2)}, u32[]{:S(2)}) collective-permute-start(bf16[4,1,2,256,128]{4,3,2,1,0:T(8,128)(2,1)} %get-tuple-element.48), channel_id=1, source_target_pairs={{1,2},{3,4},{5,6},{2,1},{4,3},{6,5},{9,10},{11,12},{13,14},{10,9},... | collective-permute-start | bytes 1572872 | tf_op jit(solution)/shard_map/ppermute | solution.py:393
  124.4 2.6 %collective-permute-start.13 = (bf16[3,1,256,128]{3,2,1,0:T(8,128)(2,1)}, bf16[3,1,256,128]{3,2,1,0:T(8,128)(2,1)S(1)}, u32[]{:S(2)}, u32[]{:S(2)}) collective-permute-start(bf16[3,1,256,128]{3,2,1,0:T(8,128)(2,1)} %get-tuple-element.59), channel_id=1, source_target_pairs={{0,64},{32,96},{64,0},{96,32},{1,65},{33,97},{65,1},{97,33},{2,66}... | collective-permute-start | bytes 589832 | tf_op jit(solution)/shard_map/ppermute | solution.py:144
  127.8 14.0 %shard_map.109 = (bf16[4,2,1,256,128]{4,3,2,1,0:T(8,128)(2,1)}, bf16[4,2,2,256,128]{4,3,2,1,0:T(8,128)(2,1)}, bf16[4,2,2,256,128]{4,3,2,1,0:T(8,128)(2,1)}, bf16[4,2,2,256,128]{4,3,2,1,0:T(8,128)(2,1)}) custom-call(f32[1]{0:T(128)} %bitcast.bad_ref, bf16[4,3,1,256,128]{4,3,2,1,0:T(8,128)(2,1)} %copy-done.1, ...), custom_call_target="tpu_custom_call" | custom-call | flops 99999997952 | bytes 1024 | tf_op jit(solution)/shard_map/pallas_call | solution.py:252
  141.8 4.0 %collective-permute-start.10 = (bf16[4,2,2,256,128]{4,3,2,1,0:T(8,128)(2,1)}, bf16[4,2,2,256,128]{4,3,2,1,0:T(8,128)(2,1)}, u32[]{:S(2)}, u32[]{:S(2)}) collective-permute-start(bf16[4,2,2,256,128]{4,3,2,1,0:T(8,128)(2,1)} %get-tuple-element.53), channel_id=1, source_target_pairs={{1,2},{3,4},{5,6},{2,1},{4,3},{6,5},{9,10},{11,12},{13,14},{10,9},... | collective-permute-start | bytes 3145736 | tf_op jit(solution)/shard_map/ppermute | solution.py:393
  145.9 2.9 %shard_map.110.refs_8_ = bf16[4,5,256,128]{3,2,1,0:T(8,128)(2,1)} custom-call(bf16[4,1,1,256,128]{4,3,2,1,0:T(8,128)(2,1)} %get-tuple-element.46.rest_1_.dq_ref, bf16[4,1,2,256,128]{4,3,2,1,0:T(8,128)(2,1)} %get-tuple-element.47.refs_0_, bf16[4,1,2,256,128]{4,3,2,1,0:T(8,128)(2,1)} %collective-permute-done.8.refs_1_, ...), custom_call_target="tpu_custom_call" | custom-call | flops 100000000 | bytes 1024 | tf_op jit(solution)/shard_map/pallas_call | solution.py:298
  148.8 4.7 %all-to-all-start.4 = ((bf16[4,5,256,128]{3,2,1,0:T(8,128)(2,1)}), bf16[4,5,256,128]{3,2,1,0:T(8,128)(2,1)}, u32[]{:S(2)}, u32[]{:S(2)}) async-start(bf16[4,5,256,128]{3,2,1,0:T(8,128)(2,1)} %shard_map.110.refs_8_), calls=%async_computation.4 | async-start | bytes 2621440 | tf_op jit(solution)/shard_map/all_to_all | solution.py:383
  154.9 8.7 %shard_map.113 = (bf16[3,2,256,128]{3,2,1,0:T(8,128)(2,1)}, bf16[3,2,256,128]{3,2,1,0:T(8,128)(2,1)}, bf16[3,2,256,128]{3,2,1,0:T(8,128)(2,1)}, bf16[3,2,256,128]{3,2,1,0:T(8,128)(2,1)}) custom-call(bf16[3,3,256,128]{3,2,1,0:T(8,128)(2,1)} %get-tuple-element.36.refs_1_.refs_0_, bf16[3,3,256,128]{3,2,1,0:T(8,128)(2,1)} %collective-permute-done.2.refs_1_, ...), custom_call_target="tpu_custom_call" | custom-call | flops 5000000000 | bytes 1024 | tf_op jit(solution)/shard_map/pallas_call | solution.py:370
  163.7 2.7 %collective-permute-start.16 = (bf16[3,2,256,128]{3,2,1,0:T(8,128)(2,1)}, bf16[3,2,256,128]{3,2,1,0:T(8,128)(2,1)S(1)}, u32[]{:S(2)}, u32[]{:S(2)}) collective-permute-start(bf16[3,2,256,128]{3,2,1,0:T(8,128)(2,1)} %get-tuple-element.63), channel_id=1, source_target_pairs={{0,64},{32,96},{64,0},{96,32},{1,65},{33,97},{65,1},{97,33},{2,66}... | collective-permute-start | bytes 1179656 | tf_op jit(solution)/shard_map/ppermute | solution.py:144
  167.1 4.6 %all-to-all-done.4.refs_3_.refs_0_ = bf16[4,5,256,128]{3,2,1,0:T(8,128)(2,1)} async-done(((bf16[4,5,256,128]{3,2,1,0:T(8,128)(2,1)}), bf16[4,5,256,128]{3,2,1,0:T(8,128)(2,1)}, u32[]{:S(2)}, u32[]{:S(2)}) %all-to-all-start.4) | async-done | bytes 1310752 | tf_op jit(solution)/shard_map/all_to_all | solution.py:383
  172.1 3.2 %shard_map.111 = bf16[4,4,256,128]{3,2,1,0:T(8,128)(2,1)} custom-call(bf16[4,2,2,256,128]{4,3,2,1,0:T(8,128)(2,1)} %get-tuple-element.52.refs_0_, bf16[4,2,2,256,128]{4,3,2,1,0:T(8,128)(2,1)} %collective-permute-done.10.refs_1_, bf16[4,2,2,256,128]{4,3,2,1,0:T(8,128)(2,1)} %collective-permute-done.11.refs_2_, ...), custom_call_target="tpu_custom_call" | custom-call | flops 100000000 | bytes 1024 | tf_op jit(solution)/shard_map/pallas_call | solution.py:298
  175.3 4.8 %all-to-all-start.5 = ((bf16[4,4,256,128]{3,2,1,0:T(8,128)(2,1)}), bf16[4,4,256,128]{3,2,1,0:T(8,128)(2,1)}, u32[]{:S(2)}, u32[]{:S(2)}) async-start(bf16[4,4,256,128]{3,2,1,0:T(8,128)(2,1)} %shard_map.111), calls=%async_computation.5 | async-start | bytes 2097152 | tf_op jit(solution)/shard_map/all_to_all | solution.py:383
  181.0 7.3 %collective-permute-done.17.refs_3_ = bf16[3,2,256,128]{3,2,1,0:T(8,128)(2,1)} collective-permute-done((bf16[3,2,256,128]{3,2,1,0:T(8,128)(2,1)}, bf16[3,2,256,128]{3,2,1,0:T(8,128)(2,1)}, u32[]{:S(2)}, u32[]{:S(2)}) %collective-permute-start.17) | collective-permute-done | bytes 393248 | tf_op jit(solution)/shard_map/ppermute | solution.py:144
  188.3 2.8 %shard_map.114 = (bf16[256,1536]{1,0:T(8,128)(2,1)}, bf16[256,1536]{1,0:T(8,128)(2,1)}) custom-call(bf16[3,2,256,128]{3,2,1,0:T(8,128)(2,1)} %get-tuple-element.61.refs_0_, bf16[3,2,256,128]{3,2,1,0:T(8,128)(2,1)} %copy-done.3, bf16[3,2,256,128]{3,2,1,0:T(8,128)(2,1)} %copy-done.4, bf16[3,2,256,128]{3,2,1,0:T(8,128)(2,1)} %collective-permute-done.17.refs_3_), custom_call_target="tpu_custom_call" | custom-call | flops 99999997952 | bytes 1024 | tf_op jit(solution)/shard_map/pallas_call | solution.py:49
  191.0 3.3 %all-to-all-done.5.refs_1_ = bf16[4,4,256,128]{3,2,1,0:T(8,128)(2,1)} async-done(((bf16[4,4,256,128]{3,2,1,0:T(8,128)(2,1)}), bf16[4,4,256,128]{3,2,1,0:T(8,128)(2,1)}, u32[]{:S(2)}, u32[]{:S(2)}) %all-to-all-start.5) | async-done | bytes 1048608 | tf_op jit(solution)/shard_map/all_to_all | solution.py:383
  194.3 3.4 %shard_map.112 = (bf16[256,1536]{1,0:T(8,128)(2,1)}, bf16[256,1536]{1,0:T(8,128)(2,1)}, bf16[256,1536]{1,0:T(8,128)(2,1)}) custom-call(bf16[4,5,256,128]{3,2,1,0:T(8,128)(2,1)} %all-to-all-done.4.refs_3_.refs_0_, bf16[4,4,256,128]{3,2,1,0:T(8,128)(2,1)} %all-to-all-done.5.refs_1_), custom_call_target="tpu_custom_call" | custom-call | flops 100000000 | bytes 1024 | tf_op jit(solution)/shard_map/pallas_call | solution.py:49
  (46 shorter events, 12.1 us)
Async XLA Ops:
  3.5 25.4 %all-to-all-start.1 = ((bf16[4,3,2,256,128]{4,3,2,1,0:T(8,128)(2,1)}), bf16[4,3,2,256,128]{4,3,2,1,0:T(8,128)(2,1)}, u32[]{:S(2)}, u32[]{:S(2)}) async-start(bf16[4,3,2,256,128]{4,3,2,1,0:T(8,128)(2,1)} %shard_map.101.refs_3_), calls=%async_computation.1 | async-start | bytes 3145728 | tf_op jit(solution)/shard_map/all_to_all | solution.py:383
  11.2 29.5 %collective-permute-start.2 = (bf16[3,3,256,128]{3,2,1,0:T(8,128)(2,1)}, bf16[3,3,256,128]{3,2,1,0:T(8,128)(2,1)}, u32[]{:S(2)}, u32[]{:S(2)}) collective-permute-start(bf16[3,3,256,128]{3,2,1,0:T(8,128)(2,1)} %get-tuple-element.37), channel_id=1, source_target_pairs={{0,32},{32,0},{64,96},{96,64},{1,33},{33,1},{65,97},{97,65},{2,34}... | collective-permute-start | bytes 1769480 | tf_op jit(solution)/shard_map/ppermute | solution.py:144
  11.2 29.5 %collective-permute-start.3 = (bf16[3,3,256,128]{3,2,1,0:T(8,128)(2,1)}, bf16[3,3,256,128]{3,2,1,0:T(8,128)(2,1)}, u32[]{:S(2)}, u32[]{:S(2)}) collective-permute-start(bf16[3,3,256,128]{3,2,1,0:T(8,128)(2,1)} %get-tuple-element.38), channel_id=1, source_target_pairs={{0,64},{32,96},{64,0},{96,32},{1,65},{33,97},{65,1},{97,33},{2,66}... | collective-permute-start | bytes 1769480 | tf_op jit(solution)/shard_map/ppermute | solution.py:144
  13.5 27.5 %collective-permute-start.4 = (bf16[3,3,256,128]{3,2,1,0:T(8,128)(2,1)}, bf16[3,3,256,128]{3,2,1,0:T(8,128)(2,1)}, u32[]{:S(2)}, u32[]{:S(2)}) collective-permute-start(bf16[3,3,256,128]{3,2,1,0:T(8,128)(2,1)} %get-tuple-element.39), channel_id=1, source_target_pairs={{0,96},{32,64},{64,32},{96,0},{1,97},{33,65},{65,33},{97,1},{2,98}... | collective-permute-start | bytes 1769480 | tf_op jit(solution)/shard_map/ppermute | solution.py:144
  28.9 61.2 %collective-permute-start.1 = (bf16[4,3,2,256,128]{4,3,2,1,0:T(8,128)(2,1)}, bf16[4,3,2,256,128]{4,3,2,1,0:T(8,128)(2,1)}, u32[]{:S(2)}, u32[]{:S(2)}) collective-permute-start(bf16[4,3,2,256,128]{4,3,2,1,0:T(8,128)(2,1)} %all-to-all-done.1.refs_4_.own_ref), channel_id=1, source_target_pairs={{0,1},{1,0},{2,3},{3,2},{4,5},{5,4},{6,7},{7,6},{8,9},{9,8},{10,11... | collective-permute-start | bytes 4718600 | tf_op jit(solution)/shard_map/ppermute | solution.py:387
  30.8 59.3 %collective-permute-start = (bf16[4,3,2,256,128]{4,3,2,1,0:T(8,128)(2,1)}, bf16[4,3,2,256,128]{4,3,2,1,0:T(8,128)(2,1)}, u32[]{:S(2)}, u32[]{:S(2)}) collective-permute-start(bf16[4,3,2,256,128]{4,3,2,1,0:T(8,128)(2,1)} %all-to-all-done.1.refs_4_.own_ref), channel_id=1, source_target_pairs={{1,2},{3,4},{5,6},{2,1},{4,3},{6,5},{9,10},{11,12},{13,14},{10,9},... | collective-permute-start | bytes 4718600 | tf_op jit(solution)/shard_map/ppermute | solution.py:393
  37.2 48.1 %all-to-all-start = ((bf16[4,3,1,256,128]{4,3,2,1,0:T(8,128)(2,1)}), bf16[4,3,1,256,128]{4,3,2,1,0:T(8,128)(2,1)S(1)}, u32[]{:S(2)}, u32[]{:S(2)}) async-start(bf16[4,3,1,256,128]{4,3,2,1,0:T(8,128)(2,1)} %shard_map.103.refs_5_), calls=%async_computation | async-start | bytes 1572864 | tf_op jit(solution)/shard_map/all_to_all | solution.py:383
  47.5 3.6 %collective-permute-start.5 = (bf16[3,1,256,128]{3,2,1,0:T(8,128)(2,1)}, bf16[3,1,256,128]{3,2,1,0:T(8,128)(2,1)S(1)}, u32[]{:S(2)}, u32[]{:S(2)}) collective-permute-start(bf16[3,1,256,128]{3,2,1,0:T(8,128)(2,1)} %get-tuple-element.41), channel_id=1, source_target_pairs={{0,32},{32,0},{64,96},{96,64},{1,33},{33,1},{65,97},{97,65},{2,34}... | collective-permute-start | bytes 589832 | tf_op jit(solution)/shard_map/ppermute | solution.py:144
  48.2 31.6 %collective-permute-start.6 = (bf16[3,1,256,128]{3,2,1,0:T(8,128)(2,1)}, bf16[3,1,256,128]{3,2,1,0:T(8,128)(2,1)}, u32[]{:S(2)}, u32[]{:S(2)}) collective-permute-start(bf16[3,1,256,128]{3,2,1,0:T(8,128)(2,1)} %get-tuple-element.42), channel_id=1, source_target_pairs={{0,64},{32,96},{64,0},{96,32},{1,65},{33,97},{65,1},{97,33},{2,66}... | collective-permute-start | bytes 589832 | tf_op jit(solution)/shard_map/ppermute | solution.py:144
  50.5 32.7 %collective-permute-start.7 = (bf16[3,1,256,128]{3,2,1,0:T(8,128)(2,1)}, bf16[3,1,256,128]{3,2,1,0:T(8,128)(2,1)}, u32[]{:S(2)}, u32[]{:S(2)}) collective-permute-start(bf16[3,1,256,128]{3,2,1,0:T(8,128)(2,1)} %get-tuple-element.43), channel_id=1, source_target_pairs={{0,96},{32,64},{64,32},{96,0},{1,97},{33,65},{65,33},{97,1},{2,98}... | collective-permute-start | bytes 589832 | tf_op jit(solution)/shard_map/ppermute | solution.py:144
  51.1 32.1 %copy-start.2 = (bf16[3,1,256,128]{3,2,1,0:T(8,128)(2,1)}, bf16[3,1,256,128]{3,2,1,0:T(8,128)(2,1)S(1)}, u32[]{:S(2)}) copy-start(bf16[3,1,256,128]{3,2,1,0:T(8,128)(2,1)S(1)} %collective-permute-done.5.refs_1_) | copy-start | bytes 589828
  85.3 4.8 %copy-start.1 = (bf16[4,3,1,256,128]{4,3,2,1,0:T(8,128)(2,1)}, bf16[4,3,1,256,128]{4,3,2,1,0:T(8,128)(2,1)S(1)}, u32[]{:S(2)}) copy-start(bf16[4,3,1,256,128]{4,3,2,1,0:T(8,128)(2,1)S(1)} %all-to-all-done.q_ref) | copy-start | bytes 2359300
  85.3 17.5 %all-to-all-start.2 = ((bf16[4,3,1,256,128]{4,3,2,1,0:T(8,128)(2,1)}), bf16[4,3,1,256,128]{4,3,2,1,0:T(8,128)(2,1)}, u32[]{:S(2)}, u32[]{:S(2)}) async-start(bf16[4,3,1,256,128]{4,3,2,1,0:T(8,128)(2,1)} %shard_map.105._), calls=%async_computation.2 | async-start | bytes 1572864 | tf_op jit(solution)/shard_map/all_to_all | solution.py:383
  102.9 18.6 %all-to-all-start.3 = ((bf16[4,3,1,256,128]{4,3,2,1,0:T(8,128)(2,1)}), bf16[4,3,1,256,128]{4,3,2,1,0:T(8,128)(2,1)S(1)}, u32[]{:S(2)}, u32[]{:S(2)}) async-start(bf16[4,3,1,256,128]{4,3,2,1,0:T(8,128)(2,1)} %get-tuple-element.44.o_ref), calls=%async_computation.3 | async-start | bytes 1572864 | tf_op jit(solution)/shard_map/all_to_all | solution.py:383
  115.5 26.2 %collective-permute-start.8 = (bf16[4,1,2,256,128]{4,3,2,1,0:T(8,128)(2,1)}, bf16[4,1,2,256,128]{4,3,2,1,0:T(8,128)(2,1)}, u32[]{:S(2)}, u32[]{:S(2)}) collective-permute-start(bf16[4,1,2,256,128]{4,3,2,1,0:T(8,128)(2,1)} %get-tuple-element.48), channel_id=1, source_target_pairs={{1,2},{3,4},{5,6},{2,1},{4,3},{6,5},{9,10},{11,12},{13,14},{10,9},... | collective-permute-start | bytes 1572872 | tf_op jit(solution)/shard_map/ppermute | solution.py:393
  121.4 24.5 %collective-permute-start.9 = (bf16[4,1,2,256,128]{4,3,2,1,0:T(8,128)(2,1)}, bf16[4,1,2,256,128]{4,3,2,1,0:T(8,128)(2,1)}, u32[]{:S(2)}, u32[]{:S(2)}) collective-permute-start(bf16[4,1,2,256,128]{4,3,2,1,0:T(8,128)(2,1)} %get-tuple-element.49), channel_id=1, source_target_pairs={{0,1},{1,0},{2,3},{3,2},{4,5},{5,4},{6,7},{7,6},{8,9},{9,8},{10,11... | collective-permute-start | bytes 1572872 | tf_op jit(solution)/shard_map/ppermute | solution.py:387
  121.5 0.9 copy-start
  124.4 29.0 %collective-permute-start.12 = (bf16[3,1,256,128]{3,2,1,0:T(8,128)(2,1)}, bf16[3,1,256,128]{3,2,1,0:T(8,128)(2,1)S(1)}, u32[]{:S(2)}, u32[]{:S(2)}) collective-permute-start(bf16[3,1,256,128]{3,2,1,0:T(8,128)(2,1)} %get-tuple-element.58), channel_id=1, source_target_pairs={{0,32},{32,0},{64,96},{96,64},{1,33},{33,1},{65,97},{97,65},{2,34}... | collective-permute-start | bytes 589832 | tf_op jit(solution)/shard_map/ppermute | solution.py:144
  124.4 29.0 %collective-permute-start.13 = (bf16[3,1,256,128]{3,2,1,0:T(8,128)(2,1)}, bf16[3,1,256,128]{3,2,1,0:T(8,128)(2,1)S(1)}, u32[]{:S(2)}, u32[]{:S(2)}) collective-permute-start(bf16[3,1,256,128]{3,2,1,0:T(8,128)(2,1)} %get-tuple-element.59), channel_id=1, source_target_pairs={{0,64},{32,96},{64,0},{96,32},{1,65},{33,97},{65,1},{97,33},{2,66}... | collective-permute-start | bytes 589832 | tf_op jit(solution)/shard_map/ppermute | solution.py:144
  127.0 26.4 %collective-permute-start.14 = (bf16[3,1,256,128]{3,2,1,0:T(8,128)(2,1)}, bf16[3,1,256,128]{3,2,1,0:T(8,128)(2,1)S(1)}, u32[]{:S(2)}, u32[]{:S(2)}) collective-permute-start(bf16[3,1,256,128]{3,2,1,0:T(8,128)(2,1)} %get-tuple-element.60), channel_id=1, source_target_pairs={{0,96},{32,64},{64,32},{96,0},{1,97},{33,65},{65,33},{97,1},{2,98}... | collective-permute-start | bytes 589832 | tf_op jit(solution)/shard_map/ppermute | solution.py:144
  141.8 30.3 %collective-permute-start.10 = (bf16[4,2,2,256,128]{4,3,2,1,0:T(8,128)(2,1)}, bf16[4,2,2,256,128]{4,3,2,1,0:T(8,128)(2,1)}, u32[]{:S(2)}, u32[]{:S(2)}) collective-permute-start(bf16[4,2,2,256,128]{4,3,2,1,0:T(8,128)(2,1)} %get-tuple-element.53), channel_id=1, source_target_pairs={{1,2},{3,4},{5,6},{2,1},{4,3},{6,5},{9,10},{11,12},{13,14},{10,9},... | collective-permute-start | bytes 3145736 | tf_op jit(solution)/shard_map/ppermute | solution.py:393
  145.8 26.2 %collective-permute-start.11 = (bf16[4,2,2,256,128]{4,3,2,1,0:T(8,128)(2,1)}, bf16[4,2,2,256,128]{4,3,2,1,0:T(8,128)(2,1)}, u32[]{:S(2)}, u32[]{:S(2)}) collective-permute-start(bf16[4,2,2,256,128]{4,3,2,1,0:T(8,128)(2,1)} %get-tuple-element.54), channel_id=1, source_target_pairs={{0,1},{1,0},{2,3},{3,2},{4,5},{5,4},{6,7},{7,6},{8,9},{9,8},{10,11... | collective-permute-start | bytes 3145736 | tf_op jit(solution)/shard_map/ppermute | solution.py:387
  148.8 22.8 %all-to-all-start.4 = ((bf16[4,5,256,128]{3,2,1,0:T(8,128)(2,1)}), bf16[4,5,256,128]{3,2,1,0:T(8,128)(2,1)}, u32[]{:S(2)}, u32[]{:S(2)}) async-start(bf16[4,5,256,128]{3,2,1,0:T(8,128)(2,1)} %shard_map.110.refs_8_), calls=%async_computation.4 | async-start | bytes 2621440 | tf_op jit(solution)/shard_map/all_to_all | solution.py:383
  153.4 0.7 copy-start.5
  153.4 0.8 copy-start.6
  154.2 0.7 copy-start.7
  163.6 16.5 %collective-permute-start.15 = (bf16[3,2,256,128]{3,2,1,0:T(8,128)(2,1)}, bf16[3,2,256,128]{3,2,1,0:T(8,128)(2,1)S(1)}, u32[]{:S(2)}, u32[]{:S(2)}) collective-permute-start(bf16[3,2,256,128]{3,2,1,0:T(8,128)(2,1)} %get-tuple-element.62), channel_id=1, source_target_pairs={{0,32},{32,0},{64,96},{96,64},{1,33},{33,1},{65,97},{97,65},{2,34}... | collective-permute-start | bytes 1179656 | tf_op jit(solution)/shard_map/ppermute | solution.py:144
  163.7 17.3 %collective-permute-start.16 = (bf16[3,2,256,128]{3,2,1,0:T(8,128)(2,1)}, bf16[3,2,256,128]{3,2,1,0:T(8,128)(2,1)S(1)}, u32[]{:S(2)}, u32[]{:S(2)}) collective-permute-start(bf16[3,2,256,128]{3,2,1,0:T(8,128)(2,1)} %get-tuple-element.63), channel_id=1, source_target_pairs={{0,64},{32,96},{64,0},{96,32},{1,65},{33,97},{65,1},{97,33},{2,66}... | collective-permute-start | bytes 1179656 | tf_op jit(solution)/shard_map/ppermute | solution.py:144
  166.4 21.9 %collective-permute-start.17 = (bf16[3,2,256,128]{3,2,1,0:T(8,128)(2,1)}, bf16[3,2,256,128]{3,2,1,0:T(8,128)(2,1)}, u32[]{:S(2)}, u32[]{:S(2)}) collective-permute-start(bf16[3,2,256,128]{3,2,1,0:T(8,128)(2,1)} %get-tuple-element.64), channel_id=1, source_target_pairs={{0,96},{32,64},{64,32},{96,0},{1,97},{33,65},{65,33},{97,1},{2,98}... | collective-permute-start | bytes 1179656 | tf_op jit(solution)/shard_map/ppermute | solution.py:144
  175.3 19.0 %all-to-all-start.5 = ((bf16[4,4,256,128]{3,2,1,0:T(8,128)(2,1)}), bf16[4,4,256,128]{3,2,1,0:T(8,128)(2,1)}, u32[]{:S(2)}, u32[]{:S(2)}) async-start(bf16[4,4,256,128]{3,2,1,0:T(8,128)(2,1)} %shard_map.111), calls=%async_computation.5 | async-start | bytes 2097152 | tf_op jit(solution)/shard_map/all_to_all | solution.py:383
  180.1 8.2 %copy-start.3 = (bf16[3,2,256,128]{3,2,1,0:T(8,128)(2,1)}, bf16[3,2,256,128]{3,2,1,0:T(8,128)(2,1)S(1)}, u32[]{:S(2)}) copy-start(bf16[3,2,256,128]{3,2,1,0:T(8,128)(2,1)S(1)} %collective-permute-done.15.refs_1_) | copy-start | bytes 1179652
  181.0 7.3 %copy-start.4 = (bf16[3,2,256,128]{3,2,1,0:T(8,128)(2,1)}, bf16[3,2,256,128]{3,2,1,0:T(8,128)(2,1)S(1)}, u32[]{:S(2)}) copy-start(bf16[3,2,256,128]{3,2,1,0:T(8,128)(2,1)S(1)} %collective-permute-done.16.refs_2_) | copy-start | bytes 1179652

commit v6 on v5

--- a/solution.py
+++ b/solution.py
@@ -27,7 +27,7 @@
 
 
 def params():
-    return pltpu.CompilerParams(vmem_limit_bytes=63 * 1024 * 1024)
+    return pltpu.CompilerParams(vmem_limit_bytes=64 * 1024 * 1024)
 
 
 def cost(microseconds):

time: 199 us -> 198 us (level)
  local copies, waits for them, and re-layouts: 2.33 us -> 0 us
    unnamed x16 -> x0, local copies, waits for them, and re-layouts: 2.33 us -> none
  transfers between devices with their start and end apart: 24 -> 24, of which waited for: 10 -> 9; matrix products, arithmetic and copies ran while one was open for 0% -> 0% of each run, Pallas kernels for 35% -> 35%
where the time goes in v6:
time: 198 us; the launch traced here: 197 us
  Pallas kernels  74.6 us (38%)
  waiting for transfers between devices  64 us (32%)
  starting transfers between devices  57.3 us (29%)
    ppermute x12, waiting for transfers between devices, trade(): lax.ppermute(chunks[s], 'tm', [(i, i ^ s) for i in range(PARTS)])  40.3 us
    all_to_all x6, starting transfers between devices, swap(): return lax.all_to_all(x, axis, split_axis=0, concat_axis=0, tiled=True)  27.2 us
    all_to_all x6, waiting for transfers between devices, swap(): return lax.all_to_all(x, axis, split_axis=0, concat_axis=0, tiled=True)  23.4 us
    pallas_call x2, Pallas kernels, attend_backward(): pl.pallas_call(backward_kernel, grid=(heads,), in_specs=[pl.BlockSpec(mem...  21.8 us
    pallas_call x7, Pallas kernels, move(): pl.pallas_call(kernel, in_specs=[pl.BlockSpec(memory_space=pltpu.VMEM)] *...  18.8 us
    pallas_call x2, Pallas kernels, temporal_call(): pl.pallas_call(kernel, grid=(group, tokens // rows), in_specs=[spec(a.sha...  15.2 us
    ppermute x3, starting transfers between devices, trade_other(): return lax.ppermute(x, 'wa', pairs)  14.4 us
    ppermute x12, starting transfers between devices, trade(): lax.ppermute(chunks[s], 'tm', [(i, i ^ s) for i in range(PARTS)])  13.6 us
  transfers between devices with their start and end apart: 24, of which 9 were waited for; matrix products, arithmetic and copies ran while one was open for 0% of the time, Pallas kernels for 35%

profile of v6, /device:TPU:8, one launch (start us, length us, event | category | flops | bytes accessed | tf_op | source)
XLA Modules:
  0.0 196.7 jit_solution(14156863116621018259)
XLA Ops:
  0.6 2.8 %shard_map.101.refs_3_ = bf16[4,3,2,256,128]{4,3,2,1,0:T(8,128)(2,1)} custom-call(bf16[256,1536]{1,0:T(8,128)(2,1)} %bitcast.13, bf16[256,1536]{1,0:T(8,128)(2,1)} %bitcast.14), custom_call_target="tpu_custom_call" | custom-call | flops 100000000 | bytes 1024 | tf_op jit(solution)/shard_map/pallas_call | solution.py:49
  3.4 4.4 %all-to-all-start.1 = ((bf16[4,3,2,256,128]{4,3,2,1,0:T(8,128)(2,1)}), bf16[4,3,2,256,128]{4,3,2,1,0:T(8,128)(2,1)}, u32[]{:S(2)}, u32[]{:S(2)}) async-start(bf16[4,3,2,256,128]{4,3,2,1,0:T(8,128)(2,1)} %shard_map.101.refs_3_), calls=%async_computation.1 | async-start | bytes 3145728 | tf_op jit(solution)/shard_map/all_to_all | solution.py:383
  7.8 3.4 %shard_map.102 = (bf16[3,3,256,128]{3,2,1,0:T(8,128)(2,1)}, bf16[3,3,256,128]{3,2,1,0:T(8,128)(2,1)}, bf16[3,3,256,128]{3,2,1,0:T(8,128)(2,1)}, bf16[3,3,256,128]{3,2,1,0:T(8,128)(2,1)}) custom-call(bf16[256,1536]{1,0:T(8,128)(2,1)} %bitcast.15, bf16[256,1536]{1,0:T(8,128)(2,1)} %bitcast.16, bf16[256,1536]{1,0:T(8,128)(2,1)} %bitcast.17, ...), custom_call_target="tpu_custom_call" | custom-call | flops 100000000 | bytes 1024 | tf_op jit(solution)/shard_map/pallas_call | solution.py:49
  11.2 2.3 %collective-permute-start.3 = (bf16[3,3,256,128]{3,2,1,0:T(8,128)(2,1)}, bf16[3,3,256,128]{3,2,1,0:T(8,128)(2,1)}, u32[]{:S(2)}, u32[]{:S(2)}) collective-permute-start(bf16[3,3,256,128]{3,2,1,0:T(8,128)(2,1)} %get-tuple-element.38), channel_id=1, source_target_pairs={{0,64},{32,96},{64,0},{96,32},{1,65},{33,97},{65,1},{97,33},{2,66}... | collective-permute-start | bytes 1769480 | tf_op jit(solution)/shard_map/ppermute | solution.py:144
  14.6 14.3 %all-to-all-done.1.refs_4_.own_ref = bf16[4,3,2,256,128]{4,3,2,1,0:T(8,128)(2,1)} async-done(((bf16[4,3,2,256,128]{4,3,2,1,0:T(8,128)(2,1)}), bf16[4,3,2,256,128]{4,3,2,1,0:T(8,128)(2,1)}, u32[]{:S(2)}, u32[]{:S(2)}) %all-to-all-start.1) | async-done | bytes 1572896 | tf_op jit(solution)/shard_map/all_to_all | solution.py:383
  30.8 4.3 %collective-permute-start = (bf16[4,3,2,256,128]{4,3,2,1,0:T(8,128)(2,1)}, bf16[4,3,2,256,128]{4,3,2,1,0:T(8,128)(2,1)}, u32[]{:S(2)}, u32[]{:S(2)}) collective-permute-start(bf16[4,3,2,256,128]{4,3,2,1,0:T(8,128)(2,1)} %all-to-all-done.1.refs_4_.own_ref), channel_id=1, source_target_pairs={{1,2},{3,4},{5,6},{2,1},{4,3},{6,5},{9,10},{11,12},{13,14},{10,9},... | collective-permute-start | bytes 4718600 | tf_op jit(solution)/shard_map/ppermute | solution.py:393
  35.1 2.1 %shard_map.103.refs_5_ = bf16[4,3,1,256,128]{4,3,2,1,0:T(8,128)(2,1)} custom-call(bf16[256,1536]{1,0:T(8,128)(2,1)} %bitcast.12, bf16[3,3,256,128]{3,2,1,0:T(8,128)(2,1)} %get-tuple-element.36.refs_1_.refs_0_), custom_call_target="tpu_custom_call" | custom-call | flops 100000000 | bytes 1024 | tf_op jit(solution)/shard_map/pallas_call | solution.py:49
  37.2 4.2 %all-to-all-start = ((bf16[4,3,1,256,128]{4,3,2,1,0:T(8,128)(2,1)}), bf16[4,3,1,256,128]{4,3,2,1,0:T(8,128)(2,1)}, u32[]{:S(2)}, u32[]{:S(2)}) async-start(bf16[4,3,1,256,128]{4,3,2,1,0:T(8,128)(2,1)} %shard_map.103.refs_5_), calls=%async_computation | async-start | bytes 1572864 | tf_op jit(solution)/shard_map/all_to_all | solution.py:383
  41.5 6.5 %shard_map.104 = (bf16[3,1,256,128]{3,2,1,0:T(8,128)(2,1)}, bf16[3,1,256,128]{3,2,1,0:T(8,128)(2,1)}, bf16[3,1,256,128]{3,2,1,0:T(8,128)(2,1)}, bf16[3,1,256,128]{3,2,1,0:T(8,128)(2,1)}) custom-call(bf16[3,3,256,128]{3,2,1,0:T(8,128)(2,1)} %get-tuple-element.36.refs_1_.refs_0_, bf16[3,3,256,128]{3,2,1,0:T(8,128)(2,1)} %collective-permute-done.2.refs_1_, ...), custom_call_target="tpu_custom_call" | custom-call | flops 10000000000 | bytes 1024 | tf_op jit(solution)/shard_map/pallas_call | solution.py:370
  48.1 2.6 %collective-permute-start.6 = (bf16[3,1,256,128]{3,2,1,0:T(8,128)(2,1)}, bf16[3,1,256,128]{3,2,1,0:T(8,128)(2,1)}, u32[]{:S(2)}, u32[]{:S(2)}) collective-permute-start(bf16[3,1,256,128]{3,2,1,0:T(8,128)(2,1)} %get-tuple-element.42), channel_id=1, source_target_pairs={{0,64},{32,96},{64,0},{96,32},{1,65},{33,97},{65,1},{97,33},{2,66}... | collective-permute-start | bytes 589832 | tf_op jit(solution)/shard_map/ppermute | solution.py:144
  51.4 28.3 %collective-permute-done.6.refs_2_ = bf16[3,1,256,128]{3,2,1,0:T(8,128)(2,1)} collective-permute-done((bf16[3,1,256,128]{3,2,1,0:T(8,128)(2,1)}, bf16[3,1,256,128]{3,2,1,0:T(8,128)(2,1)}, u32[]{:S(2)}, u32[]{:S(2)}) %collective-permute-start.6) | collective-permute-done | bytes 196640 | tf_op jit(solution)/shard_map/ppermute | solution.py:144
  79.7 3.4 %collective-permute-done.7.refs_3_ = bf16[3,1,256,128]{3,2,1,0:T(8,128)(2,1)} collective-permute-done((bf16[3,1,256,128]{3,2,1,0:T(8,128)(2,1)}, bf16[3,1,256,128]{3,2,1,0:T(8,128)(2,1)}, u32[]{:S(2)}, u32[]{:S(2)}) %collective-permute-start.7) | collective-permute-done | bytes 196640 | tf_op jit(solution)/shard_map/ppermute | solution.py:144
  83.2 2.2 %shard_map.105._ = bf16[4,3,1,256,128]{4,3,2,1,0:T(8,128)(2,1)} custom-call(bf16[3,1,256,128]{3,2,1,0:T(8,128)(2,1)} %get-tuple-element.40.refs_0_, bf16[3,1,256,128]{3,2,1,0:T(8,128)(2,1)} %collective-permute-done.5.refs_1_, bf16[3,1,256,128]{3,2,1,0:T(8,128)(2,1)} %collective-permute-done.6.refs_2_, bf16[3,1,256,128]{3,2,1,0:T(8,128)(2,1)} %collective-permute-done.7.refs_3_), custom_call_target="tpu_custom_call" | custom-call | flops 100000000 | bytes 1024 | tf_op jit(solution)/shard_map/pallas_call | solution.py:49
  85.3 4.7 %all-to-all-start.2 = ((bf16[4,3,1,256,128]{4,3,2,1,0:T(8,128)(2,1)}), bf16[4,3,1,256,128]{4,3,2,1,0:T(8,128)(2,1)}, u32[]{:S(2)}, u32[]{:S(2)}) async-start(bf16[4,3,1,256,128]{4,3,2,1,0:T(8,128)(2,1)} %shard_map.105._), calls=%async_computation.2 | async-start | bytes 1572864 | tf_op jit(solution)/shard_map/all_to_all | solution.py:383
  90.1 12.7 %shard_map.106 = (bf16[4,3,1,256,128]{4,3,2,1,0:T(8,128)(2,1)}, f32[3,1,1024]{2,1,0:T(1,128)}) custom-call(f32[1]{0:T(128)} %bitcast.bad_ref, bf16[4,3,1,256,128]{4,3,2,1,0:T(8,128)(2,1)} %all-to-all-done.q_ref, bf16[4,3,2,256,128]{4,3,2,1,0:T(8,128)(2,1)} %collective-permute-done.other_ref, bf16[4,3,2,256,128]{4,3,2,1,0:T(8,128)(2,1)} %all-to-all-done.1.refs_4_.own_ref, ...), custom_call_target="tpu_custom_call" | custom-call | flops 99999997952 | bytes 1024 | tf_op jit(solution)/shard_map/pallas_call | solution.py:191
  102.8 4.7 %all-to-all-start.3 = ((bf16[4,3,1,256,128]{4,3,2,1,0:T(8,128)(2,1)}), bf16[4,3,1,256,128]{4,3,2,1,0:T(8,128)(2,1)}, u32[]{:S(2)}, u32[]{:S(2)}) async-start(bf16[4,3,1,256,128]{4,3,2,1,0:T(8,128)(2,1)} %get-tuple-element.44.o_ref), calls=%async_computation.3 | async-start | bytes 1572864 | tf_op jit(solution)/shard_map/all_to_all | solution.py:383
  107.6 7.9 %shard_map.107 = (bf16[4,1,1,256,128]{4,3,2,1,0:T(8,128)(2,1)}, bf16[4,1,2,256,128]{4,3,2,1,0:T(8,128)(2,1)}, bf16[4,1,2,256,128]{4,3,2,1,0:T(8,128)(2,1)}, bf16[4,1,2,256,128]{4,3,2,1,0:T(8,128)(2,1)}) custom-call(f32[1]{0:T(128)} %bitcast.bad_ref, bf16[4,3,1,256,128]{4,3,2,1,0:T(8,128)(2,1)} %all-to-all-done.q_ref, ...), custom_call_target="tpu_custom_call" | custom-call | flops 99999997952 | bytes 1024 | tf_op jit(solution)/shard_map/pallas_call | solution.py:252
  115.4 5.8 %collective-permute-start.8 = (bf16[4,1,2,256,128]{4,3,2,1,0:T(8,128)(2,1)}, bf16[4,1,2,256,128]{4,3,2,1,0:T(8,128)(2,1)}, u32[]{:S(2)}, u32[]{:S(2)}) collective-permute-start(bf16[4,1,2,256,128]{4,3,2,1,0:T(8,128)(2,1)} %get-tuple-element.48), channel_id=1, source_target_pairs={{1,2},{3,4},{5,6},{2,1},{4,3},{6,5},{9,10},{11,12},{13,14},{10,9},... | collective-permute-start | bytes 1572872 | tf_op jit(solution)/shard_map/ppermute | solution.py:393
  123.4 2.6 %collective-permute-start.13 = (bf16[3,1,256,128]{3,2,1,0:T(8,128)(2,1)}, bf16[3,1,256,128]{3,2,1,0:T(8,128)(2,1)}, u32[]{:S(2)}, u32[]{:S(2)}) collective-permute-start(bf16[3,1,256,128]{3,2,1,0:T(8,128)(2,1)} %get-tuple-element.59), channel_id=1, source_target_pairs={{0,64},{32,96},{64,0},{96,32},{1,65},{33,97},{65,1},{97,33},{2,66}... | collective-permute-start | bytes 589832 | tf_op jit(solution)/shard_map/ppermute | solution.py:144
  126.8 14.0 %shard_map.109 = (bf16[4,2,1,256,128]{4,3,2,1,0:T(8,128)(2,1)}, bf16[4,2,2,256,128]{4,3,2,1,0:T(8,128)(2,1)}, bf16[4,2,2,256,128]{4,3,2,1,0:T(8,128)(2,1)}, bf16[4,2,2,256,128]{4,3,2,1,0:T(8,128)(2,1)}) custom-call(f32[1]{0:T(128)} %bitcast.bad_ref, bf16[4,3,1,256,128]{4,3,2,1,0:T(8,128)(2,1)} %all-to-all-done.q_ref, ...), custom_call_target="tpu_custom_call" | custom-call | flops 99999997952 | bytes 1024 | tf_op jit(solution)/shard_map/pallas_call | solution.py:252
  140.8 4.3 %collective-permute-start.10 = (bf16[4,2,2,256,128]{4,3,2,1,0:T(8,128)(2,1)}, bf16[4,2,2,256,128]{4,3,2,1,0:T(8,128)(2,1)}, u32[]{:S(2)}, u32[]{:S(2)}) collective-permute-start(bf16[4,2,2,256,128]{4,3,2,1,0:T(8,128)(2,1)} %get-tuple-element.53), channel_id=1, source_target_pairs={{1,2},{3,4},{5,6},{2,1},{4,3},{6,5},{9,10},{11,12},{13,14},{10,9},... | collective-permute-start | bytes 3145736 | tf_op jit(solution)/shard_map/ppermute | solution.py:393
  145.2 2.9 %shard_map.110.refs_8_ = bf16[4,5,256,128]{3,2,1,0:T(8,128)(2,1)} custom-call(bf16[4,1,1,256,128]{4,3,2,1,0:T(8,128)(2,1)} %get-tuple-element.46.rest_1_.dq_ref, bf16[4,1,2,256,128]{4,3,2,1,0:T(8,128)(2,1)} %get-tuple-element.47.refs_0_, bf16[4,1,2,256,128]{4,3,2,1,0:T(8,128)(2,1)} %collective-permute-done.8.refs_1_, ...), custom_call_target="tpu_custom_call" | custom-call | flops 100000000 | bytes 1024 | tf_op jit(solution)/shard_map/pallas_call | solution.py:298
  148.1 4.4 %all-to-all-start.4 = ((bf16[4,5,256,128]{3,2,1,0:T(8,128)(2,1)}), bf16[4,5,256,128]{3,2,1,0:T(8,128)(2,1)}, u32[]{:S(2)}, u32[]{:S(2)}) async-start(bf16[4,5,256,128]{3,2,1,0:T(8,128)(2,1)} %shard_map.110.refs_8_), calls=%async_computation.4 | async-start | bytes 2621440 | tf_op jit(solution)/shard_map/all_to_all | solution.py:383
  152.5 8.7 %shard_map.113 = (bf16[3,2,256,128]{3,2,1,0:T(8,128)(2,1)}, bf16[3,2,256,128]{3,2,1,0:T(8,128)(2,1)}, bf16[3,2,256,128]{3,2,1,0:T(8,128)(2,1)}, bf16[3,2,256,128]{3,2,1,0:T(8,128)(2,1)}) custom-call(bf16[3,3,256,128]{3,2,1,0:T(8,128)(2,1)} %get-tuple-element.36.refs_1_.refs_0_, bf16[3,3,256,128]{3,2,1,0:T(8,128)(2,1)} %collective-permute-done.2.refs_1_, ...), custom_call_target="tpu_custom_call" | custom-call | flops 5000000000 | bytes 1024 | tf_op jit(solution)/shard_map/pallas_call | solution.py:370
  161.3 2.7 %collective-permute-start.16 = (bf16[3,2,256,128]{3,2,1,0:T(8,128)(2,1)}, bf16[3,2,256,128]{3,2,1,0:T(8,128)(2,1)}, u32[]{:S(2)}, u32[]{:S(2)}) collective-permute-start(bf16[3,2,256,128]{3,2,1,0:T(8,128)(2,1)} %get-tuple-element.63), channel_id=1, source_target_pairs={{0,64},{32,96},{64,0},{96,32},{1,65},{33,97},{65,1},{97,33},{2,66}... | collective-permute-start | bytes 1179656 | tf_op jit(solution)/shard_map/ppermute | solution.py:144
  164.7 6.1 %all-to-all-done.4.refs_3_.refs_0_ = bf16[4,5,256,128]{3,2,1,0:T(8,128)(2,1)} async-done(((bf16[4,5,256,128]{3,2,1,0:T(8,128)(2,1)}), bf16[4,5,256,128]{3,2,1,0:T(8,128)(2,1)}, u32[]{:S(2)}, u32[]{:S(2)}) %all-to-all-start.4) | async-done | bytes 1310752 | tf_op jit(solution)/shard_map/all_to_all | solution.py:383
  171.1 3.2 %shard_map.111 = bf16[4,4,256,128]{3,2,1,0:T(8,128)(2,1)} custom-call(bf16[4,2,2,256,128]{4,3,2,1,0:T(8,128)(2,1)} %get-tuple-element.52.refs_0_, bf16[4,2,2,256,128]{4,3,2,1,0:T(8,128)(2,1)} %collective-permute-done.10.refs_1_, bf16[4,2,2,256,128]{4,3,2,1,0:T(8,128)(2,1)} %collective-permute-done.11.refs_2_, ...), custom_call_target="tpu_custom_call" | custom-call | flops 100000000 | bytes 1024 | tf_op jit(solution)/shard_map/pallas_call | solution.py:298
  174.3 4.8 %all-to-all-start.5 = ((bf16[4,4,256,128]{3,2,1,0:T(8,128)(2,1)}), bf16[4,4,256,128]{3,2,1,0:T(8,128)(2,1)}, u32[]{:S(2)}, u32[]{:S(2)}) async-start(bf16[4,4,256,128]{3,2,1,0:T(8,128)(2,1)} %shard_map.111), calls=%async_computation.5 | async-start | bytes 2097152 | tf_op jit(solution)/shard_map/all_to_all | solution.py:383
  180.4 7.2 %collective-permute-done.17.refs_3_ = bf16[3,2,256,128]{3,2,1,0:T(8,128)(2,1)} collective-permute-done((bf16[3,2,256,128]{3,2,1,0:T(8,128)(2,1)}, bf16[3,2,256,128]{3,2,1,0:T(8,128)(2,1)}, u32[]{:S(2)}, u32[]{:S(2)}) %collective-permute-start.17) | collective-permute-done | bytes 393248 | tf_op jit(solution)/shard_map/ppermute | solution.py:144
  187.5 2.8 %shard_map.114 = (bf16[256,1536]{1,0:T(8,128)(2,1)}, bf16[256,1536]{1,0:T(8,128)(2,1)}) custom-call(bf16[3,2,256,128]{3,2,1,0:T(8,128)(2,1)} %get-tuple-element.61.refs_0_, bf16[3,2,256,128]{3,2,1,0:T(8,128)(2,1)} %collective-permute-done.15.refs_1_, bf16[3,2,256,128]{3,2,1,0:T(8,128)(2,1)} %collective-permute-done.16.refs_2_, ...), custom_call_target="tpu_custom_call" | custom-call | flops 99999997952 | bytes 1024 | tf_op jit(solution)/shard_map/pallas_call | solution.py:49
  190.3 3.0 %all-to-all-done.5.refs_1_ = bf16[4,4,256,128]{3,2,1,0:T(8,128)(2,1)} async-done(((bf16[4,4,256,128]{3,2,1,0:T(8,128)(2,1)}), bf16[4,4,256,128]{3,2,1,0:T(8,128)(2,1)}, u32[]{:S(2)}, u32[]{:S(2)}) %all-to-all-start.5) | async-done | bytes 1048608 | tf_op jit(solution)/shard_map/all_to_all | solution.py:383
  193.3 3.4 %shard_map.112 = (bf16[256,1536]{1,0:T(8,128)(2,1)}, bf16[256,1536]{1,0:T(8,128)(2,1)}, bf16[256,1536]{1,0:T(8,128)(2,1)}) custom-call(bf16[4,5,256,128]{3,2,1,0:T(8,128)(2,1)} %all-to-all-done.4.refs_3_.refs_0_, bf16[4,4,256,128]{3,2,1,0:T(8,128)(2,1)} %all-to-all-done.5.refs_1_), custom_call_target="tpu_custom_call" | custom-call | flops 100000000 | bytes 1024 | tf_op jit(solution)/shard_map/pallas_call | solution.py:49
  (30 shorter events, 9.3 us)
Async XLA Ops:
  3.4 25.4 %all-to-all-start.1 = ((bf16[4,3,2,256,128]{4,3,2,1,0:T(8,128)(2,1)}), bf16[4,3,2,256,128]{4,3,2,1,0:T(8,128)(2,1)}, u32[]{:S(2)}, u32[]{:S(2)}) async-start(bf16[4,3,2,256,128]{4,3,2,1,0:T(8,128)(2,1)} %shard_map.101.refs_3_), calls=%async_computation.1 | async-start | bytes 3145728 | tf_op jit(solution)/shard_map/all_to_all | solution.py:383
  11.2 30.2 %collective-permute-start.2 = (bf16[3,3,256,128]{3,2,1,0:T(8,128)(2,1)}, bf16[3,3,256,128]{3,2,1,0:T(8,128)(2,1)}, u32[]{:S(2)}, u32[]{:S(2)}) collective-permute-start(bf16[3,3,256,128]{3,2,1,0:T(8,128)(2,1)} %get-tuple-element.37), channel_id=1, source_target_pairs={{0,32},{32,0},{64,96},{96,64},{1,33},{33,1},{65,97},{97,65},{2,34}... | collective-permute-start | bytes 1769480 | tf_op jit(solution)/shard_map/ppermute | solution.py:144
  11.2 30.2 %collective-permute-start.3 = (bf16[3,3,256,128]{3,2,1,0:T(8,128)(2,1)}, bf16[3,3,256,128]{3,2,1,0:T(8,128)(2,1)}, u32[]{:S(2)}, u32[]{:S(2)}) collective-permute-start(bf16[3,3,256,128]{3,2,1,0:T(8,128)(2,1)} %get-tuple-element.38), channel_id=1, source_target_pairs={{0,64},{32,96},{64,0},{96,32},{1,65},{33,97},{65,1},{97,33},{2,66}... | collective-permute-start | bytes 1769480 | tf_op jit(solution)/shard_map/ppermute | solution.py:144
  13.5 28.0 %collective-permute-start.4 = (bf16[3,3,256,128]{3,2,1,0:T(8,128)(2,1)}, bf16[3,3,256,128]{3,2,1,0:T(8,128)(2,1)}, u32[]{:S(2)}, u32[]{:S(2)}) collective-permute-start(bf16[3,3,256,128]{3,2,1,0:T(8,128)(2,1)} %get-tuple-element.39), channel_id=1, source_target_pairs={{0,96},{32,64},{64,32},{96,0},{1,97},{33,65},{65,33},{97,1},{2,98}... | collective-permute-start | bytes 1769480 | tf_op jit(solution)/shard_map/ppermute | solution.py:144
  28.8 61.2 %collective-permute-start.1 = (bf16[4,3,2,256,128]{4,3,2,1,0:T(8,128)(2,1)}, bf16[4,3,2,256,128]{4,3,2,1,0:T(8,128)(2,1)}, u32[]{:S(2)}, u32[]{:S(2)}) collective-permute-start(bf16[4,3,2,256,128]{4,3,2,1,0:T(8,128)(2,1)} %all-to-all-done.1.refs_4_.own_ref), channel_id=1, source_target_pairs={{0,1},{1,0},{2,3},{3,2},{4,5},{5,4},{6,7},{7,6},{8,9},{9,8},{10,11... | collective-permute-start | bytes 4718600 | tf_op jit(solution)/shard_map/ppermute | solution.py:387
  30.8 59.3 %collective-permute-start = (bf16[4,3,2,256,128]{4,3,2,1,0:T(8,128)(2,1)}, bf16[4,3,2,256,128]{4,3,2,1,0:T(8,128)(2,1)}, u32[]{:S(2)}, u32[]{:S(2)}) collective-permute-start(bf16[4,3,2,256,128]{4,3,2,1,0:T(8,128)(2,1)} %all-to-all-done.1.refs_4_.own_ref), channel_id=1, source_target_pairs={{1,2},{3,4},{5,6},{2,1},{4,3},{6,5},{9,10},{11,12},{13,14},{10,9},... | collective-permute-start | bytes 4718600 | tf_op jit(solution)/shard_map/ppermute | solution.py:393
  37.2 48.1 %all-to-all-start = ((bf16[4,3,1,256,128]{4,3,2,1,0:T(8,128)(2,1)}), bf16[4,3,1,256,128]{4,3,2,1,0:T(8,128)(2,1)}, u32[]{:S(2)}, u32[]{:S(2)}) async-start(bf16[4,3,1,256,128]{4,3,2,1,0:T(8,128)(2,1)} %shard_map.103.refs_5_), calls=%async_computation | async-start | bytes 1572864 | tf_op jit(solution)/shard_map/all_to_all | solution.py:383
  48.0 3.4 %collective-permute-start.5 = (bf16[3,1,256,128]{3,2,1,0:T(8,128)(2,1)}, bf16[3,1,256,128]{3,2,1,0:T(8,128)(2,1)}, u32[]{:S(2)}, u32[]{:S(2)}) collective-permute-start(bf16[3,1,256,128]{3,2,1,0:T(8,128)(2,1)} %get-tuple-element.41), channel_id=1, source_target_pairs={{0,32},{32,0},{64,96},{96,64},{1,33},{33,1},{65,97},{97,65},{2,34}... | collective-permute-start | bytes 589832 | tf_op jit(solution)/shard_map/ppermute | solution.py:144
  48.1 31.6 %collective-permute-start.6 = (bf16[3,1,256,128]{3,2,1,0:T(8,128)(2,1)}, bf16[3,1,256,128]{3,2,1,0:T(8,128)(2,1)}, u32[]{:S(2)}, u32[]{:S(2)}) collective-permute-start(bf16[3,1,256,128]{3,2,1,0:T(8,128)(2,1)} %get-tuple-element.42), channel_id=1, source_target_pairs={{0,64},{32,96},{64,0},{96,32},{1,65},{33,97},{65,1},{97,33},{2,66}... | collective-permute-start | bytes 589832 | tf_op jit(solution)/shard_map/ppermute | solution.py:144
  50.7 32.5 %collective-permute-start.7 = (bf16[3,1,256,128]{3,2,1,0:T(8,128)(2,1)}, bf16[3,1,256,128]{3,2,1,0:T(8,128)(2,1)}, u32[]{:S(2)}, u32[]{:S(2)}) collective-permute-start(bf16[3,1,256,128]{3,2,1,0:T(8,128)(2,1)} %get-tuple-element.43), channel_id=1, source_target_pairs={{0,96},{32,64},{64,32},{96,0},{1,97},{33,65},{65,33},{97,1},{2,98}... | collective-permute-start | bytes 589832 | tf_op jit(solution)/shard_map/ppermute | solution.py:144
  85.3 17.5 %all-to-all-start.2 = ((bf16[4,3,1,256,128]{4,3,2,1,0:T(8,128)(2,1)}), bf16[4,3,1,256,128]{4,3,2,1,0:T(8,128)(2,1)}, u32[]{:S(2)}, u32[]{:S(2)}) async-start(bf16[4,3,1,256,128]{4,3,2,1,0:T(8,128)(2,1)} %shard_map.105._), calls=%async_computation.2 | async-start | bytes 1572864 | tf_op jit(solution)/shard_map/all_to_all | solution.py:383
  102.8 18.5 %all-to-all-start.3 = ((bf16[4,3,1,256,128]{4,3,2,1,0:T(8,128)(2,1)}), bf16[4,3,1,256,128]{4,3,2,1,0:T(8,128)(2,1)}, u32[]{:S(2)}, u32[]{:S(2)}) async-start(bf16[4,3,1,256,128]{4,3,2,1,0:T(8,128)(2,1)} %get-tuple-element.44.o_ref), calls=%async_computation.3 | async-start | bytes 1572864 | tf_op jit(solution)/shard_map/all_to_all | solution.py:383
  115.4 25.3 %collective-permute-start.8 = (bf16[4,1,2,256,128]{4,3,2,1,0:T(8,128)(2,1)}, bf16[4,1,2,256,128]{4,3,2,1,0:T(8,128)(2,1)}, u32[]{:S(2)}, u32[]{:S(2)}) collective-permute-start(bf16[4,1,2,256,128]{4,3,2,1,0:T(8,128)(2,1)} %get-tuple-element.48), channel_id=1, source_target_pairs={{1,2},{3,4},{5,6},{2,1},{4,3},{6,5},{9,10},{11,12},{13,14},{10,9},... | collective-permute-start | bytes 1572872 | tf_op jit(solution)/shard_map/ppermute | solution.py:393
  121.3 23.8 %collective-permute-start.9 = (bf16[4,1,2,256,128]{4,3,2,1,0:T(8,128)(2,1)}, bf16[4,1,2,256,128]{4,3,2,1,0:T(8,128)(2,1)}, u32[]{:S(2)}, u32[]{:S(2)}) collective-permute-start(bf16[4,1,2,256,128]{4,3,2,1,0:T(8,128)(2,1)} %get-tuple-element.49), channel_id=1, source_target_pairs={{0,1},{1,0},{2,3},{3,2},{4,5},{5,4},{6,7},{7,6},{8,9},{9,8},{10,11... | collective-permute-start | bytes 1572872 | tf_op jit(solution)/shard_map/ppermute | solution.py:387
  123.4 29.0 %collective-permute-start.12 = (bf16[3,1,256,128]{3,2,1,0:T(8,128)(2,1)}, bf16[3,1,256,128]{3,2,1,0:T(8,128)(2,1)}, u32[]{:S(2)}, u32[]{:S(2)}) collective-permute-start(bf16[3,1,256,128]{3,2,1,0:T(8,128)(2,1)} %get-tuple-element.58), channel_id=1, source_target_pairs={{0,32},{32,0},{64,96},{96,64},{1,33},{33,1},{65,97},{97,65},{2,34}... | collective-permute-start | bytes 589832 | tf_op jit(solution)/shard_map/ppermute | solution.py:144
  123.4 29.0 %collective-permute-start.13 = (bf16[3,1,256,128]{3,2,1,0:T(8,128)(2,1)}, bf16[3,1,256,128]{3,2,1,0:T(8,128)(2,1)}, u32[]{:S(2)}, u32[]{:S(2)}) collective-permute-start(bf16[3,1,256,128]{3,2,1,0:T(8,128)(2,1)} %get-tuple-element.59), channel_id=1, source_target_pairs={{0,64},{32,96},{64,0},{96,32},{1,65},{33,97},{65,1},{97,33},{2,66}... | collective-permute-start | bytes 589832 | tf_op jit(solution)/shard_map/ppermute | solution.py:144
  126.0 26.4 %collective-permute-start.14 = (bf16[3,1,256,128]{3,2,1,0:T(8,128)(2,1)}, bf16[3,1,256,128]{3,2,1,0:T(8,128)(2,1)}, u32[]{:S(2)}, u32[]{:S(2)}) collective-permute-start(bf16[3,1,256,128]{3,2,1,0:T(8,128)(2,1)} %get-tuple-element.60), channel_id=1, source_target_pairs={{0,96},{32,64},{64,32},{96,0},{1,97},{33,65},{65,33},{97,1},{2,98}... | collective-permute-start | bytes 589832 | tf_op jit(solution)/shard_map/ppermute | solution.py:144
  140.8 30.3 %collective-permute-start.10 = (bf16[4,2,2,256,128]{4,3,2,1,0:T(8,128)(2,1)}, bf16[4,2,2,256,128]{4,3,2,1,0:T(8,128)(2,1)}, u32[]{:S(2)}, u32[]{:S(2)}) collective-permute-start(bf16[4,2,2,256,128]{4,3,2,1,0:T(8,128)(2,1)} %get-tuple-element.53), channel_id=1, source_target_pairs={{1,2},{3,4},{5,6},{2,1},{4,3},{6,5},{9,10},{11,12},{13,14},{10,9},... | collective-permute-start | bytes 3145736 | tf_op jit(solution)/shard_map/ppermute | solution.py:393
  145.1 26.0 %collective-permute-start.11 = (bf16[4,2,2,256,128]{4,3,2,1,0:T(8,128)(2,1)}, bf16[4,2,2,256,128]{4,3,2,1,0:T(8,128)(2,1)}, u32[]{:S(2)}, u32[]{:S(2)}) collective-permute-start(bf16[4,2,2,256,128]{4,3,2,1,0:T(8,128)(2,1)} %get-tuple-element.54), channel_id=1, source_target_pairs={{0,1},{1,0},{2,3},{3,2},{4,5},{5,4},{6,7},{7,6},{8,9},{9,8},{10,11... | collective-permute-start | bytes 3145736 | tf_op jit(solution)/shard_map/ppermute | solution.py:387
  148.1 22.7 %all-to-all-start.4 = ((bf16[4,5,256,128]{3,2,1,0:T(8,128)(2,1)}), bf16[4,5,256,128]{3,2,1,0:T(8,128)(2,1)}, u32[]{:S(2)}, u32[]{:S(2)}) async-start(bf16[4,5,256,128]{3,2,1,0:T(8,128)(2,1)} %shard_map.110.refs_8_), calls=%async_computation.4 | async-start | bytes 2621440 | tf_op jit(solution)/shard_map/all_to_all | solution.py:383
  161.2 17.9 %collective-permute-start.15 = (bf16[3,2,256,128]{3,2,1,0:T(8,128)(2,1)}, bf16[3,2,256,128]{3,2,1,0:T(8,128)(2,1)}, u32[]{:S(2)}, u32[]{:S(2)}) collective-permute-start(bf16[3,2,256,128]{3,2,1,0:T(8,128)(2,1)} %get-tuple-element.62), channel_id=1, source_target_pairs={{0,32},{32,0},{64,96},{96,64},{1,33},{33,1},{65,97},{97,65},{2,34}... | collective-permute-start | bytes 1179656 | tf_op jit(solution)/shard_map/ppermute | solution.py:144
  161.3 19.1 %collective-permute-start.16 = (bf16[3,2,256,128]{3,2,1,0:T(8,128)(2,1)}, bf16[3,2,256,128]{3,2,1,0:T(8,128)(2,1)}, u32[]{:S(2)}, u32[]{:S(2)}) collective-permute-start(bf16[3,2,256,128]{3,2,1,0:T(8,128)(2,1)} %get-tuple-element.63), channel_id=1, source_target_pairs={{0,64},{32,96},{64,0},{96,32},{1,65},{33,97},{65,1},{97,33},{2,66}... | collective-permute-start | bytes 1179656 | tf_op jit(solution)/shard_map/ppermute | solution.py:144
  164.0 23.6 %collective-permute-start.17 = (bf16[3,2,256,128]{3,2,1,0:T(8,128)(2,1)}, bf16[3,2,256,128]{3,2,1,0:T(8,128)(2,1)}, u32[]{:S(2)}, u32[]{:S(2)}) collective-permute-start(bf16[3,2,256,128]{3,2,1,0:T(8,128)(2,1)} %get-tuple-element.64), channel_id=1, source_target_pairs={{0,96},{32,64},{64,32},{96,0},{1,97},{33,65},{65,33},{97,1},{2,98}... | collective-permute-start | bytes 1179656 | tf_op jit(solution)/shard_map/ppermute | solution.py:144
  174.3 19.0 %all-to-all-start.5 = ((bf16[4,4,256,128]{3,2,1,0:T(8,128)(2,1)}), bf16[4,4,256,128]{3,2,1,0:T(8,128)(2,1)}, u32[]{:S(2)}, u32[]{:S(2)}) async-start(bf16[4,4,256,128]{3,2,1,0:T(8,128)(2,1)} %shard_map.111), calls=%async_computation.5 | async-start | bytes 2097152 | tf_op jit(solution)/shard_map/all_to_all | solution.py:383

commit v7 on v6

--- a/solution.py
+++ b/solution.py
@@ -431,7 +431,7 @@
         temporal_backward_kernel, pau + mixed_parts, 2, 5, [early]
     )
     early = swap(early, "ha")
-    late = swap(totals(late_kernel, 2 * (GROUP - 1), two[1:], [early]), "ha")
+    late = swap(totals(late_kernel, 2 * (GROUP - 1), two[1:], times_sent[:1]), "ha")
     probe_grad, anchor_grad = unpack_partners(trade(times_sent), [])
     query_grad, key_grad, value_grad = unpack_heads(early, late)
     outs = (query_grad, key_grad, value_grad, probe_grad, anchor_grad)

time: 198 us -> 198 us (level)
    ppermute x3, waiting for transfers between devices: 0.29 us -> 6.43 us  [trade_other(): return lax.ppermute(x, 'wa', pairs)]
    all_to_all x6, waiting for transfers between devices: 23.4 us -> 17.3 us  [swap(): return lax.all_to_all(x, axis, split_axis=0, concat_axis=0, tiled=True)]
  transfers between devices with their start and end apart: 24 -> 24, of which waited for: 9 -> 8; matrix products, arithmetic and copies ran while one was open for 0% -> 0% of each run, Pallas kernels for 35% -> 35%
where the time goes in v7:
time: 198 us; the launch traced here: 197 us
  Pallas kernels  74.6 us (38%)
  waiting for transfers between devices  64 us (32%)
  starting transfers between devices  57.3 us (29%)
    ppermute x12, waiting for transfers between devices, trade(): lax.ppermute(chunks[s], 'tm', [(i, i ^ s) for i in range(PARTS)])  40.2 us
    all_to_all x6, starting transfers between devices, swap(): return lax.all_to_all(x, axis, split_axis=0, concat_axis=0, tiled=True)  27.2 us
    pallas_call x2, Pallas kernels, attend_backward(): pl.pallas_call(backward_kernel, grid=(heads,), in_specs=[pl.BlockSpec(mem...  21.8 us
    pallas_call x7, Pallas kernels, move(): pl.pallas_call(kernel, in_specs=[pl.BlockSpec(memory_space=pltpu.VMEM)] *...  18.8 us
    all_to_all x6, waiting for transfers between devices, swap(): return lax.all_to_all(x, axis, split_axis=0, concat_axis=0, tiled=True)  17.3 us
    pallas_call x2, Pallas kernels, temporal_call(): pl.pallas_call(kernel, grid=(group, tokens // rows), in_specs=[spec(a.sha...  15.2 us
    ppermute x3, starting transfers between devices, trade_other(): return lax.ppermute(x, 'wa', pairs)  14.4 us
    ppermute x12, starting transfers between devices, trade(): lax.ppermute(chunks[s], 'tm', [(i, i ^ s) for i in range(PARTS)])  13.6 us
  transfers between devices with their start and end apart: 24, of which 8 were waited for; matrix products, arithmetic and copies ran while one was open for 0% of the time, Pallas kernels for 35%

profile of v7, /device:TPU:8, one launch (start us, length us, event | category | flops | bytes accessed | tf_op | source)
XLA Modules:
  0.0 196.7 jit_solution(1739682672072462407)
XLA Ops:
  0.6 2.8 %shard_map.101.refs_3_ = bf16[4,3,2,256,128]{4,3,2,1,0:T(8,128)(2,1)} custom-call(bf16[256,1536]{1,0:T(8,128)(2,1)} %bitcast.13, bf16[256,1536]{1,0:T(8,128)(2,1)} %bitcast.14), custom_call_target="tpu_custom_call" | custom-call | flops 100000000 | bytes 1024 | tf_op jit(solution)/shard_map/pallas_call | solution.py:49
  3.4 4.4 %all-to-all-start.1 = ((bf16[4,3,2,256,128]{4,3,2,1,0:T(8,128)(2,1)}), bf16[4,3,2,256,128]{4,3,2,1,0:T(8,128)(2,1)}, u32[]{:S(2)}, u32[]{:S(2)}) async-start(bf16[4,3,2,256,128]{4,3,2,1,0:T(8,128)(2,1)} %shard_map.101.refs_3_), calls=%async_computation.1 | async-start | bytes 3145728 | tf_op jit(solution)/shard_map/all_to_all | solution.py:383
  7.8 3.4 %shard_map.102 = (bf16[3,3,256,128]{3,2,1,0:T(8,128)(2,1)}, bf16[3,3,256,128]{3,2,1,0:T(8,128)(2,1)}, bf16[3,3,256,128]{3,2,1,0:T(8,128)(2,1)}, bf16[3,3,256,128]{3,2,1,0:T(8,128)(2,1)}) custom-call(bf16[256,1536]{1,0:T(8,128)(2,1)} %bitcast.15, bf16[256,1536]{1,0:T(8,128)(2,1)} %bitcast.16, bf16[256,1536]{1,0:T(8,128)(2,1)} %bitcast.17, ...), custom_call_target="tpu_custom_call" | custom-call | flops 100000000 | bytes 1024 | tf_op jit(solution)/shard_map/pallas_call | solution.py:49
  11.2 2.3 %collective-permute-start.3 = (bf16[3,3,256,128]{3,2,1,0:T(8,128)(2,1)}, bf16[3,3,256,128]{3,2,1,0:T(8,128)(2,1)}, u32[]{:S(2)}, u32[]{:S(2)}) collective-permute-start(bf16[3,3,256,128]{3,2,1,0:T(8,128)(2,1)} %get-tuple-element.38), channel_id=1, source_target_pairs={{0,64},{32,96},{64,0},{96,32},{1,65},{33,97},{65,1},{97,33},{2,66}... | collective-permute-start | bytes 1769480 | tf_op jit(solution)/shard_map/ppermute | solution.py:144
  14.6 14.3 %all-to-all-done.1.refs_4_.own_ref = bf16[4,3,2,256,128]{4,3,2,1,0:T(8,128)(2,1)} async-done(((bf16[4,3,2,256,128]{4,3,2,1,0:T(8,128)(2,1)}), bf16[4,3,2,256,128]{4,3,2,1,0:T(8,128)(2,1)}, u32[]{:S(2)}, u32[]{:S(2)}) %all-to-all-start.1) | async-done | bytes 1572896 | tf_op jit(solution)/shard_map/all_to_all | solution.py:383
  30.8 4.3 %collective-permute-start = (bf16[4,3,2,256,128]{4,3,2,1,0:T(8,128)(2,1)}, bf16[4,3,2,256,128]{4,3,2,1,0:T(8,128)(2,1)}, u32[]{:S(2)}, u32[]{:S(2)}) collective-permute-start(bf16[4,3,2,256,128]{4,3,2,1,0:T(8,128)(2,1)} %all-to-all-done.1.refs_4_.own_ref), channel_id=1, source_target_pairs={{1,2},{3,4},{5,6},{2,1},{4,3},{6,5},{9,10},{11,12},{13,14},{10,9},... | collective-permute-start | bytes 4718600 | tf_op jit(solution)/shard_map/ppermute | solution.py:393
  35.1 2.1 %shard_map.103.refs_5_ = bf16[4,3,1,256,128]{4,3,2,1,0:T(8,128)(2,1)} custom-call(bf16[256,1536]{1,0:T(8,128)(2,1)} %bitcast.12, bf16[3,3,256,128]{3,2,1,0:T(8,128)(2,1)} %get-tuple-element.36.refs_1_.refs_0_), custom_call_target="tpu_custom_call" | custom-call | flops 100000000 | bytes 1024 | tf_op jit(solution)/shard_map/pallas_call | solution.py:49
  37.2 4.2 %all-to-all-start = ((bf16[4,3,1,256,128]{4,3,2,1,0:T(8,128)(2,1)}), bf16[4,3,1,256,128]{4,3,2,1,0:T(8,128)(2,1)}, u32[]{:S(2)}, u32[]{:S(2)}) async-start(bf16[4,3,1,256,128]{4,3,2,1,0:T(8,128)(2,1)} %shard_map.103.refs_5_), calls=%async_computation | async-start | bytes 1572864 | tf_op jit(solution)/shard_map/all_to_all | solution.py:383
  41.5 6.5 %shard_map.104 = (bf16[3,1,256,128]{3,2,1,0:T(8,128)(2,1)}, bf16[3,1,256,128]{3,2,1,0:T(8,128)(2,1)}, bf16[3,1,256,128]{3,2,1,0:T(8,128)(2,1)}, bf16[3,1,256,128]{3,2,1,0:T(8,128)(2,1)}) custom-call(bf16[3,3,256,128]{3,2,1,0:T(8,128)(2,1)} %get-tuple-element.36.refs_1_.refs_0_, bf16[3,3,256,128]{3,2,1,0:T(8,128)(2,1)} %collective-permute-done.2.refs_1_, ...), custom_call_target="tpu_custom_call" | custom-call | flops 10000000000 | bytes 1024 | tf_op jit(solution)/shard_map/pallas_call | solution.py:370
  48.1 2.6 %collective-permute-start.6 = (bf16[3,1,256,128]{3,2,1,0:T(8,128)(2,1)}, bf16[3,1,256,128]{3,2,1,0:T(8,128)(2,1)}, u32[]{:S(2)}, u32[]{:S(2)}) collective-permute-start(bf16[3,1,256,128]{3,2,1,0:T(8,128)(2,1)} %get-tuple-element.42), channel_id=1, source_target_pairs={{0,64},{32,96},{64,0},{96,32},{1,65},{33,97},{65,1},{97,33},{2,66}... | collective-permute-start | bytes 589832 | tf_op jit(solution)/shard_map/ppermute | solution.py:144
  51.4 28.3 %collective-permute-done.6.refs_2_ = bf16[3,1,256,128]{3,2,1,0:T(8,128)(2,1)} collective-permute-done((bf16[3,1,256,128]{3,2,1,0:T(8,128)(2,1)}, bf16[3,1,256,128]{3,2,1,0:T(8,128)(2,1)}, u32[]{:S(2)}, u32[]{:S(2)}) %collective-permute-start.6) | collective-permute-done | bytes 196640 | tf_op jit(solution)/shard_map/ppermute | solution.py:144
  79.7 3.4 %collective-permute-done.7.refs_3_ = bf16[3,1,256,128]{3,2,1,0:T(8,128)(2,1)} collective-permute-done((bf16[3,1,256,128]{3,2,1,0:T(8,128)(2,1)}, bf16[3,1,256,128]{3,2,1,0:T(8,128)(2,1)}, u32[]{:S(2)}, u32[]{:S(2)}) %collective-permute-start.7) | collective-permute-done | bytes 196640 | tf_op jit(solution)/shard_map/ppermute | solution.py:144
  83.2 2.2 %shard_map.105._ = bf16[4,3,1,256,128]{4,3,2,1,0:T(8,128)(2,1)} custom-call(bf16[3,1,256,128]{3,2,1,0:T(8,128)(2,1)} %get-tuple-element.40.refs_0_, bf16[3,1,256,128]{3,2,1,0:T(8,128)(2,1)} %collective-permute-done.5.refs_1_, bf16[3,1,256,128]{3,2,1,0:T(8,128)(2,1)} %collective-permute-done.6.refs_2_, bf16[3,1,256,128]{3,2,1,0:T(8,128)(2,1)} %collective-permute-done.7.refs_3_), custom_call_target="tpu_custom_call" | custom-call | flops 100000000 | bytes 1024 | tf_op jit(solution)/shard_map/pallas_call | solution.py:49
  85.3 4.7 %all-to-all-start.2 = ((bf16[4,3,1,256,128]{4,3,2,1,0:T(8,128)(2,1)}), bf16[4,3,1,256,128]{4,3,2,1,0:T(8,128)(2,1)}, u32[]{:S(2)}, u32[]{:S(2)}) async-start(bf16[4,3,1,256,128]{4,3,2,1,0:T(8,128)(2,1)} %shard_map.105._), calls=%async_computation.2 | async-start | bytes 1572864 | tf_op jit(solution)/shard_map/all_to_all | solution.py:383
  90.1 12.7 %shard_map.106 = (bf16[4,3,1,256,128]{4,3,2,1,0:T(8,128)(2,1)}, f32[3,1,1024]{2,1,0:T(1,128)}) custom-call(f32[1]{0:T(128)} %bitcast.bad_ref, bf16[4,3,1,256,128]{4,3,2,1,0:T(8,128)(2,1)} %all-to-all-done.q_ref, bf16[4,3,2,256,128]{4,3,2,1,0:T(8,128)(2,1)} %collective-permute-done.other_ref, bf16[4,3,2,256,128]{4,3,2,1,0:T(8,128)(2,1)} %all-to-all-done.1.refs_4_.own_ref, ...), custom_call_target="tpu_custom_call" | custom-call | flops 99999997952 | bytes 1024 | tf_op jit(solution)/shard_map/pallas_call | solution.py:191
  102.8 4.7 %all-to-all-start.3 = ((bf16[4,3,1,256,128]{4,3,2,1,0:T(8,128)(2,1)}), bf16[4,3,1,256,128]{4,3,2,1,0:T(8,128)(2,1)}, u32[]{:S(2)}, u32[]{:S(2)}) async-start(bf16[4,3,1,256,128]{4,3,2,1,0:T(8,128)(2,1)} %get-tuple-element.44.o_ref), calls=%async_computation.3 | async-start | bytes 1572864 | tf_op jit(solution)/shard_map/all_to_all | solution.py:383
  107.6 7.9 %shard_map.107 = (bf16[4,1,1,256,128]{4,3,2,1,0:T(8,128)(2,1)}, bf16[4,1,2,256,128]{4,3,2,1,0:T(8,128)(2,1)}, bf16[4,1,2,256,128]{4,3,2,1,0:T(8,128)(2,1)}, bf16[4,1,2,256,128]{4,3,2,1,0:T(8,128)(2,1)}) custom-call(f32[1]{0:T(128)} %bitcast.bad_ref, bf16[4,3,1,256,128]{4,3,2,1,0:T(8,128)(2,1)} %all-to-all-done.q_ref, ...), custom_call_target="tpu_custom_call" | custom-call | flops 99999997952 | bytes 1024 | tf_op jit(solution)/shard_map/pallas_call | solution.py:252
  115.4 5.8 %collective-permute-start.8 = (bf16[4,1,2,256,128]{4,3,2,1,0:T(8,128)(2,1)}, bf16[4,1,2,256,128]{4,3,2,1,0:T(8,128)(2,1)}, u32[]{:S(2)}, u32[]{:S(2)}) collective-permute-start(bf16[4,1,2,256,128]{4,3,2,1,0:T(8,128)(2,1)} %get-tuple-element.48), channel_id=1, source_target_pairs={{1,2},{3,4},{5,6},{2,1},{4,3},{6,5},{9,10},{11,12},{13,14},{10,9},... | collective-permute-start | bytes 1572872 | tf_op jit(solution)/shard_map/ppermute | solution.py:393
  123.4 2.6 %collective-permute-start.13 = (bf16[3,1,256,128]{3,2,1,0:T(8,128)(2,1)}, bf16[3,1,256,128]{3,2,1,0:T(8,128)(2,1)}, u32[]{:S(2)}, u32[]{:S(2)}) collective-permute-start(bf16[3,1,256,128]{3,2,1,0:T(8,128)(2,1)} %get-tuple-element.56), channel_id=1, source_target_pairs={{0,64},{32,96},{64,0},{96,32},{1,65},{33,97},{65,1},{97,33},{2,66}... | collective-permute-start | bytes 589832 | tf_op jit(solution)/shard_map/ppermute | solution.py:144
  126.8 14.0 %shard_map.109 = (bf16[4,2,1,256,128]{4,3,2,1,0:T(8,128)(2,1)}, bf16[4,2,2,256,128]{4,3,2,1,0:T(8,128)(2,1)}, bf16[4,2,2,256,128]{4,3,2,1,0:T(8,128)(2,1)}, bf16[4,2,2,256,128]{4,3,2,1,0:T(8,128)(2,1)}) custom-call(f32[1]{0:T(128)} %bitcast.bad_ref, bf16[4,3,1,256,128]{4,3,2,1,0:T(8,128)(2,1)} %all-to-all-done.q_ref, ...), custom_call_target="tpu_custom_call" | custom-call | flops 99999997952 | bytes 1024 | tf_op jit(solution)/shard_map/pallas_call | solution.py:252
  140.8 4.3 %collective-permute-start.10 = (bf16[4,2,2,256,128]{4,3,2,1,0:T(8,128)(2,1)}, bf16[4,2,2,256,128]{4,3,2,1,0:T(8,128)(2,1)}, u32[]{:S(2)}, u32[]{:S(2)}) collective-permute-start(bf16[4,2,2,256,128]{4,3,2,1,0:T(8,128)(2,1)} %get-tuple-element.53), channel_id=1, source_target_pairs={{1,2},{3,4},{5,6},{2,1},{4,3},{6,5},{9,10},{11,12},{13,14},{10,9},... | collective-permute-start | bytes 3145736 | tf_op jit(solution)/shard_map/ppermute | solution.py:393
  145.2 2.9 %shard_map.110.refs_8_ = bf16[4,5,256,128]{3,2,1,0:T(8,128)(2,1)} custom-call(bf16[4,1,1,256,128]{4,3,2,1,0:T(8,128)(2,1)} %get-tuple-element.46.rest_1_.dq_ref, bf16[4,1,2,256,128]{4,3,2,1,0:T(8,128)(2,1)} %get-tuple-element.47.refs_0_, bf16[4,1,2,256,128]{4,3,2,1,0:T(8,128)(2,1)} %collective-permute-done.8.refs_1_, ...), custom_call_target="tpu_custom_call" | custom-call | flops 100000000 | bytes 1024 | tf_op jit(solution)/shard_map/pallas_call | solution.py:298
  148.1 4.4 %all-to-all-start.4 = ((bf16[4,5,256,128]{3,2,1,0:T(8,128)(2,1)}), bf16[4,5,256,128]{3,2,1,0:T(8,128)(2,1)}, u32[]{:S(2)}, u32[]{:S(2)}) async-start(bf16[4,5,256,128]{3,2,1,0:T(8,128)(2,1)} %shard_map.110.refs_8_), calls=%async_computation.4 | async-start | bytes 2621440 | tf_op jit(solution)/shard_map/all_to_all | solution.py:383
  152.5 8.7 %shard_map.111 = (bf16[3,2,256,128]{3,2,1,0:T(8,128)(2,1)}, bf16[3,2,256,128]{3,2,1,0:T(8,128)(2,1)}, bf16[3,2,256,128]{3,2,1,0:T(8,128)(2,1)}, bf16[3,2,256,128]{3,2,1,0:T(8,128)(2,1)}) custom-call(bf16[3,3,256,128]{3,2,1,0:T(8,128)(2,1)} %get-tuple-element.36.refs_1_.refs_0_, bf16[3,3,256,128]{3,2,1,0:T(8,128)(2,1)} %collective-permute-done.2.refs_1_, ...), custom_call_target="tpu_custom_call" | custom-call | flops 5000000000 | bytes 1024 | tf_op jit(solution)/shard_map/pallas_call | solution.py:370
  161.3 2.7 %collective-permute-start.16 = (bf16[3,2,256,128]{3,2,1,0:T(8,128)(2,1)}, bf16[3,2,256,128]{3,2,1,0:T(8,128)(2,1)}, u32[]{:S(2)}, u32[]{:S(2)}) collective-permute-start(bf16[3,2,256,128]{3,2,1,0:T(8,128)(2,1)} %get-tuple-element.63), channel_id=1, source_target_pairs={{0,64},{32,96},{64,0},{96,32},{1,65},{33,97},{65,1},{97,33},{2,66}... | collective-permute-start | bytes 1179656 | tf_op jit(solution)/shard_map/ppermute | solution.py:144
  164.7 6.4 %collective-permute-done.10.refs_1_ = bf16[4,2,2,256,128]{4,3,2,1,0:T(8,128)(2,1)} collective-permute-done((bf16[4,2,2,256,128]{4,3,2,1,0:T(8,128)(2,1)}, bf16[4,2,2,256,128]{4,3,2,1,0:T(8,128)(2,1)}, u32[]{:S(2)}, u32[]{:S(2)}) %collective-permute-start.10) | collective-permute-done | bytes 1048608 | tf_op jit(solution)/shard_map/ppermute | solution.py:393
  171.1 3.2 %shard_map.112 = bf16[4,4,256,128]{3,2,1,0:T(8,128)(2,1)} custom-call(bf16[4,2,2,256,128]{4,3,2,1,0:T(8,128)(2,1)} %get-tuple-element.52.refs_0_, bf16[4,2,2,256,128]{4,3,2,1,0:T(8,128)(2,1)} %collective-permute-done.10.refs_1_, bf16[4,2,2,256,128]{4,3,2,1,0:T(8,128)(2,1)} %collective-permute-done.11.refs_2_, ...), custom_call_target="tpu_custom_call" | custom-call | flops 100000000 | bytes 1024 | tf_op jit(solution)/shard_map/pallas_call | solution.py:298
  174.3 4.8 %all-to-all-start.5 = ((bf16[4,4,256,128]{3,2,1,0:T(8,128)(2,1)}), bf16[4,4,256,128]{3,2,1,0:T(8,128)(2,1)}, u32[]{:S(2)}, u32[]{:S(2)}) async-start(bf16[4,4,256,128]{3,2,1,0:T(8,128)(2,1)} %shard_map.112), calls=%async_computation.5 | async-start | bytes 2097152 | tf_op jit(solution)/shard_map/all_to_all | solution.py:383
  180.4 7.2 %collective-permute-done.17.refs_3_ = bf16[3,2,256,128]{3,2,1,0:T(8,128)(2,1)} collective-permute-done((bf16[3,2,256,128]{3,2,1,0:T(8,128)(2,1)}, bf16[3,2,256,128]{3,2,1,0:T(8,128)(2,1)}, u32[]{:S(2)}, u32[]{:S(2)}) %collective-permute-start.17) | collective-permute-done | bytes 393248 | tf_op jit(solution)/shard_map/ppermute | solution.py:144
  187.5 2.8 %shard_map.114 = (bf16[256,1536]{1,0:T(8,128)(2,1)}, bf16[256,1536]{1,0:T(8,128)(2,1)}) custom-call(bf16[3,2,256,128]{3,2,1,0:T(8,128)(2,1)} %get-tuple-element.58.refs_3_.refs_0_, bf16[3,2,256,128]{3,2,1,0:T(8,128)(2,1)} %collective-permute-done.15.refs_1_, bf16[3,2,256,128]{3,2,1,0:T(8,128)(2,1)} %collective-permute-done.16.refs_2_, ...), custom_call_target="tpu_custom_call" | custom-call | flops 99999997952 | bytes 1024 | tf_op jit(solution)/shard_map/pallas_call | solution.py:49
  190.3 3.0 %all-to-all-done.5.refs_1_ = bf16[4,4,256,128]{3,2,1,0:T(8,128)(2,1)} async-done(((bf16[4,4,256,128]{3,2,1,0:T(8,128)(2,1)}), bf16[4,4,256,128]{3,2,1,0:T(8,128)(2,1)}, u32[]{:S(2)}, u32[]{:S(2)}) %all-to-all-start.5) | async-done | bytes 1048608 | tf_op jit(solution)/shard_map/all_to_all | solution.py:383
  193.3 3.4 %shard_map.113 = (bf16[256,1536]{1,0:T(8,128)(2,1)}, bf16[256,1536]{1,0:T(8,128)(2,1)}, bf16[256,1536]{1,0:T(8,128)(2,1)}) custom-call(bf16[4,5,256,128]{3,2,1,0:T(8,128)(2,1)} %all-to-all-done.4.refs_0_, bf16[4,4,256,128]{3,2,1,0:T(8,128)(2,1)} %all-to-all-done.5.refs_1_), custom_call_target="tpu_custom_call" | custom-call | flops 100000000 | bytes 1024 | tf_op jit(solution)/shard_map/pallas_call | solution.py:49
  (30 shorter events, 9.0 us)
Async XLA Ops:
  3.4 25.4 %all-to-all-start.1 = ((bf16[4,3,2,256,128]{4,3,2,1,0:T(8,128)(2,1)}), bf16[4,3,2,256,128]{4,3,2,1,0:T(8,128)(2,1)}, u32[]{:S(2)}, u32[]{:S(2)}) async-start(bf16[4,3,2,256,128]{4,3,2,1,0:T(8,128)(2,1)} %shard_map.101.refs_3_), calls=%async_computation.1 | async-start | bytes 3145728 | tf_op jit(solution)/shard_map/all_to_all | solution.py:383
  11.2 30.2 %collective-permute-start.2 = (bf16[3,3,256,128]{3,2,1,0:T(8,128)(2,1)}, bf16[3,3,256,128]{3,2,1,0:T(8,128)(2,1)}, u32[]{:S(2)}, u32[]{:S(2)}) collective-permute-start(bf16[3,3,256,128]{3,2,1,0:T(8,128)(2,1)} %get-tuple-element.37), channel_id=1, source_target_pairs={{0,32},{32,0},{64,96},{96,64},{1,33},{33,1},{65,97},{97,65},{2,34}... | collective-permute-start | bytes 1769480 | tf_op jit(solution)/shard_map/ppermute | solution.py:144
  11.2 30.2 %collective-permute-start.3 = (bf16[3,3,256,128]{3,2,1,0:T(8,128)(2,1)}, bf16[3,3,256,128]{3,2,1,0:T(8,128)(2,1)}, u32[]{:S(2)}, u32[]{:S(2)}) collective-permute-start(bf16[3,3,256,128]{3,2,1,0:T(8,128)(2,1)} %get-tuple-element.38), channel_id=1, source_target_pairs={{0,64},{32,96},{64,0},{96,32},{1,65},{33,97},{65,1},{97,33},{2,66}... | collective-permute-start | bytes 1769480 | tf_op jit(solution)/shard_map/ppermute | solution.py:144
  13.5 28.0 %collective-permute-start.4 = (bf16[3,3,256,128]{3,2,1,0:T(8,128)(2,1)}, bf16[3,3,256,128]{3,2,1,0:T(8,128)(2,1)}, u32[]{:S(2)}, u32[]{:S(2)}) collective-permute-start(bf16[3,3,256,128]{3,2,1,0:T(8,128)(2,1)} %get-tuple-element.39), channel_id=1, source_target_pairs={{0,96},{32,64},{64,32},{96,0},{1,97},{33,65},{65,33},{97,1},{2,98}... | collective-permute-start | bytes 1769480 | tf_op jit(solution)/shard_map/ppermute | solution.py:144
  28.8 61.2 %collective-permute-start.1 = (bf16[4,3,2,256,128]{4,3,2,1,0:T(8,128)(2,1)}, bf16[4,3,2,256,128]{4,3,2,1,0:T(8,128)(2,1)}, u32[]{:S(2)}, u32[]{:S(2)}) collective-permute-start(bf16[4,3,2,256,128]{4,3,2,1,0:T(8,128)(2,1)} %all-to-all-done.1.refs_4_.own_ref), channel_id=1, source_target_pairs={{0,1},{1,0},{2,3},{3,2},{4,5},{5,4},{6,7},{7,6},{8,9},{9,8},{10,11... | collective-permute-start | bytes 4718600 | tf_op jit(solution)/shard_map/ppermute | solution.py:387
  30.8 59.3 %collective-permute-start = (bf16[4,3,2,256,128]{4,3,2,1,0:T(8,128)(2,1)}, bf16[4,3,2,256,128]{4,3,2,1,0:T(8,128)(2,1)}, u32[]{:S(2)}, u32[]{:S(2)}) collective-permute-start(bf16[4,3,2,256,128]{4,3,2,1,0:T(8,128)(2,1)} %all-to-all-done.1.refs_4_.own_ref), channel_id=1, source_target_pairs={{1,2},{3,4},{5,6},{2,1},{4,3},{6,5},{9,10},{11,12},{13,14},{10,9},... | collective-permute-start | bytes 4718600 | tf_op jit(solution)/shard_map/ppermute | solution.py:393
  37.2 48.1 %all-to-all-start = ((bf16[4,3,1,256,128]{4,3,2,1,0:T(8,128)(2,1)}), bf16[4,3,1,256,128]{4,3,2,1,0:T(8,128)(2,1)}, u32[]{:S(2)}, u32[]{:S(2)}) async-start(bf16[4,3,1,256,128]{4,3,2,1,0:T(8,128)(2,1)} %shard_map.103.refs_5_), calls=%async_computation | async-start | bytes 1572864 | tf_op jit(solution)/shard_map/all_to_all | solution.py:383
  48.0 3.4 %collective-permute-start.5 = (bf16[3,1,256,128]{3,2,1,0:T(8,128)(2,1)}, bf16[3,1,256,128]{3,2,1,0:T(8,128)(2,1)}, u32[]{:S(2)}, u32[]{:S(2)}) collective-permute-start(bf16[3,1,256,128]{3,2,1,0:T(8,128)(2,1)} %get-tuple-element.41), channel_id=1, source_target_pairs={{0,32},{32,0},{64,96},{96,64},{1,33},{33,1},{65,97},{97,65},{2,34}... | collective-permute-start | bytes 589832 | tf_op jit(solution)/shard_map/ppermute | solution.py:144
  48.1 31.6 %collective-permute-start.6 = (bf16[3,1,256,128]{3,2,1,0:T(8,128)(2,1)}, bf16[3,1,256,128]{3,2,1,0:T(8,128)(2,1)}, u32[]{:S(2)}, u32[]{:S(2)}) collective-permute-start(bf16[3,1,256,128]{3,2,1,0:T(8,128)(2,1)} %get-tuple-element.42), channel_id=1, source_target_pairs={{0,64},{32,96},{64,0},{96,32},{1,65},{33,97},{65,1},{97,33},{2,66}... | collective-permute-start | bytes 589832 | tf_op jit(solution)/shard_map/ppermute | solution.py:144
  50.7 32.5 %collective-permute-start.7 = (bf16[3,1,256,128]{3,2,1,0:T(8,128)(2,1)}, bf16[3,1,256,128]{3,2,1,0:T(8,128)(2,1)}, u32[]{:S(2)}, u32[]{:S(2)}) collective-permute-start(bf16[3,1,256,128]{3,2,1,0:T(8,128)(2,1)} %get-tuple-element.43), channel_id=1, source_target_pairs={{0,96},{32,64},{64,32},{96,0},{1,97},{33,65},{65,33},{97,1},{2,98}... | collective-permute-start | bytes 589832 | tf_op jit(solution)/shard_map/ppermute | solution.py:144
  85.3 17.5 %all-to-all-start.2 = ((bf16[4,3,1,256,128]{4,3,2,1,0:T(8,128)(2,1)}), bf16[4,3,1,256,128]{4,3,2,1,0:T(8,128)(2,1)}, u32[]{:S(2)}, u32[]{:S(2)}) async-start(bf16[4,3,1,256,128]{4,3,2,1,0:T(8,128)(2,1)} %shard_map.105._), calls=%async_computation.2 | async-start | bytes 1572864 | tf_op jit(solution)/shard_map/all_to_all | solution.py:383
  102.8 18.5 %all-to-all-start.3 = ((bf16[4,3,1,256,128]{4,3,2,1,0:T(8,128)(2,1)}), bf16[4,3,1,256,128]{4,3,2,1,0:T(8,128)(2,1)}, u32[]{:S(2)}, u32[]{:S(2)}) async-start(bf16[4,3,1,256,128]{4,3,2,1,0:T(8,128)(2,1)} %get-tuple-element.44.o_ref), calls=%async_computation.3 | async-start | bytes 1572864 | tf_op jit(solution)/shard_map/all_to_all | solution.py:383
  115.4 25.3 %collective-permute-start.8 = (bf16[4,1,2,256,128]{4,3,2,1,0:T(8,128)(2,1)}, bf16[4,1,2,256,128]{4,3,2,1,0:T(8,128)(2,1)}, u32[]{:S(2)}, u32[]{:S(2)}) collective-permute-start(bf16[4,1,2,256,128]{4,3,2,1,0:T(8,128)(2,1)} %get-tuple-element.48), channel_id=1, source_target_pairs={{1,2},{3,4},{5,6},{2,1},{4,3},{6,5},{9,10},{11,12},{13,14},{10,9},... | collective-permute-start | bytes 1572872 | tf_op jit(solution)/shard_map/ppermute | solution.py:393
  121.3 23.8 %collective-permute-start.9 = (bf16[4,1,2,256,128]{4,3,2,1,0:T(8,128)(2,1)}, bf16[4,1,2,256,128]{4,3,2,1,0:T(8,128)(2,1)}, u32[]{:S(2)}, u32[]{:S(2)}) collective-permute-start(bf16[4,1,2,256,128]{4,3,2,1,0:T(8,128)(2,1)} %get-tuple-element.49), channel_id=1, source_target_pairs={{0,1},{1,0},{2,3},{3,2},{4,5},{5,4},{6,7},{7,6},{8,9},{9,8},{10,11... | collective-permute-start | bytes 1572872 | tf_op jit(solution)/shard_map/ppermute | solution.py:387
  123.4 29.0 %collective-permute-start.12 = (bf16[3,1,256,128]{3,2,1,0:T(8,128)(2,1)}, bf16[3,1,256,128]{3,2,1,0:T(8,128)(2,1)}, u32[]{:S(2)}, u32[]{:S(2)}) collective-permute-start(bf16[3,1,256,128]{3,2,1,0:T(8,128)(2,1)} %get-tuple-element.55), channel_id=1, source_target_pairs={{0,32},{32,0},{64,96},{96,64},{1,33},{33,1},{65,97},{97,65},{2,34}... | collective-permute-start | bytes 589832 | tf_op jit(solution)/shard_map/ppermute | solution.py:144
  123.4 29.0 %collective-permute-start.13 = (bf16[3,1,256,128]{3,2,1,0:T(8,128)(2,1)}, bf16[3,1,256,128]{3,2,1,0:T(8,128)(2,1)}, u32[]{:S(2)}, u32[]{:S(2)}) collective-permute-start(bf16[3,1,256,128]{3,2,1,0:T(8,128)(2,1)} %get-tuple-element.56), channel_id=1, source_target_pairs={{0,64},{32,96},{64,0},{96,32},{1,65},{33,97},{65,1},{97,33},{2,66}... | collective-permute-start | bytes 589832 | tf_op jit(solution)/shard_map/ppermute | solution.py:144
  126.0 26.4 %collective-permute-start.14 = (bf16[3,1,256,128]{3,2,1,0:T(8,128)(2,1)}, bf16[3,1,256,128]{3,2,1,0:T(8,128)(2,1)}, u32[]{:S(2)}, u32[]{:S(2)}) collective-permute-start(bf16[3,1,256,128]{3,2,1,0:T(8,128)(2,1)} %get-tuple-element.57), channel_id=1, source_target_pairs={{0,96},{32,64},{64,32},{96,0},{1,97},{33,65},{65,33},{97,1},{2,98}... | collective-permute-start | bytes 589832 | tf_op jit(solution)/shard_map/ppermute | solution.py:144
  140.8 30.3 %collective-permute-start.10 = (bf16[4,2,2,256,128]{4,3,2,1,0:T(8,128)(2,1)}, bf16[4,2,2,256,128]{4,3,2,1,0:T(8,128)(2,1)}, u32[]{:S(2)}, u32[]{:S(2)}) collective-permute-start(bf16[4,2,2,256,128]{4,3,2,1,0:T(8,128)(2,1)} %get-tuple-element.53), channel_id=1, source_target_pairs={{1,2},{3,4},{5,6},{2,1},{4,3},{6,5},{9,10},{11,12},{13,14},{10,9},... | collective-permute-start | bytes 3145736 | tf_op jit(solution)/shard_map/ppermute | solution.py:393
  145.1 26.0 %collective-permute-start.11 = (bf16[4,2,2,256,128]{4,3,2,1,0:T(8,128)(2,1)}, bf16[4,2,2,256,128]{4,3,2,1,0:T(8,128)(2,1)}, u32[]{:S(2)}, u32[]{:S(2)}) collective-permute-start(bf16[4,2,2,256,128]{4,3,2,1,0:T(8,128)(2,1)} %get-tuple-element.54), channel_id=1, source_target_pairs={{0,1},{1,0},{2,3},{3,2},{4,5},{5,4},{6,7},{7,6},{8,9},{9,8},{10,11... | collective-permute-start | bytes 3145736 | tf_op jit(solution)/shard_map/ppermute | solution.py:387
  148.1 26.2 %all-to-all-start.4 = ((bf16[4,5,256,128]{3,2,1,0:T(8,128)(2,1)}), bf16[4,5,256,128]{3,2,1,0:T(8,128)(2,1)}, u32[]{:S(2)}, u32[]{:S(2)}) async-start(bf16[4,5,256,128]{3,2,1,0:T(8,128)(2,1)} %shard_map.110.refs_8_), calls=%async_computation.4 | async-start | bytes 2621440 | tf_op jit(solution)/shard_map/all_to_all | solution.py:383
  161.2 17.9 %collective-permute-start.15 = (bf16[3,2,256,128]{3,2,1,0:T(8,128)(2,1)}, bf16[3,2,256,128]{3,2,1,0:T(8,128)(2,1)}, u32[]{:S(2)}, u32[]{:S(2)}) collective-permute-start(bf16[3,2,256,128]{3,2,1,0:T(8,128)(2,1)} %get-tuple-element.62), channel_id=1, source_target_pairs={{0,32},{32,0},{64,96},{96,64},{1,33},{33,1},{65,97},{97,65},{2,34}... | collective-permute-start | bytes 1179656 | tf_op jit(solution)/shard_map/ppermute | solution.py:144
  161.3 19.1 %collective-permute-start.16 = (bf16[3,2,256,128]{3,2,1,0:T(8,128)(2,1)}, bf16[3,2,256,128]{3,2,1,0:T(8,128)(2,1)}, u32[]{:S(2)}, u32[]{:S(2)}) collective-permute-start(bf16[3,2,256,128]{3,2,1,0:T(8,128)(2,1)} %get-tuple-element.63), channel_id=1, source_target_pairs={{0,64},{32,96},{64,0},{96,32},{1,65},{33,97},{65,1},{97,33},{2,66}... | collective-permute-start | bytes 1179656 | tf_op jit(solution)/shard_map/ppermute | solution.py:144
  164.0 23.6 %collective-permute-start.17 = (bf16[3,2,256,128]{3,2,1,0:T(8,128)(2,1)}, bf16[3,2,256,128]{3,2,1,0:T(8,128)(2,1)}, u32[]{:S(2)}, u32[]{:S(2)}) collective-permute-start(bf16[3,2,256,128]{3,2,1,0:T(8,128)(2,1)} %get-tuple-element.64), channel_id=1, source_target_pairs={{0,96},{32,64},{64,32},{96,0},{1,97},{33,65},{65,33},{97,1},{2,98}... | collective-permute-start | bytes 1179656 | tf_op jit(solution)/shard_map/ppermute | solution.py:144
  174.3 19.0 %all-to-all-start.5 = ((bf16[4,4,256,128]{3,2,1,0:T(8,128)(2,1)}), bf16[4,4,256,128]{3,2,1,0:T(8,128)(2,1)}, u32[]{:S(2)}, u32[]{:S(2)}) async-start(bf16[4,4,256,128]{3,2,1,0:T(8,128)(2,1)} %shard_map.112), calls=%async_computation.5 | async-start | bytes 2097152 | tf_op jit(solution)/shard_map/all_to_all | solution.py:383

commit v8 on v6

--- a/solution.py
+++ b/solution.py
@@ -362,7 +362,7 @@
 
 def temporal_call(kernel, arrays, count_out, told, after=()):
     group, _, tokens, _ = arrays[0].shape
-    rows = 128
+    rows = 256
 
     def spec(count):
         return pl.BlockSpec((1, count, rows, HEAD_DIM), lambda h, i: (h, 0, i, 0))

time: 198 us -> 198 us (level)
  transfers between devices with their start and end apart: 24 -> 24, of which waited for: 9 -> 9; matrix products, arithmetic and copies ran while one was open for 0% -> 0% of each run, Pallas kernels for 35% -> 34%
where the time goes in v8:
time: 198 us; the launch traced here: 197 us
  Pallas kernels  73.5 us (37%)
  waiting for transfers between devices  65.1 us (33%)
  starting transfers between devices  57.3 us (29%)
    ppermute x12, waiting for transfers between devices, trade(): lax.ppermute(chunks[s], 'tm', [(i, i ^ s) for i in range(PARTS)])  41.3 us
    all_to_all x6, starting transfers between devices, swap(): return lax.all_to_all(x, axis, split_axis=0, concat_axis=0, tiled=True)  27.2 us
    all_to_all x6, waiting for transfers between devices, swap(): return lax.all_to_all(x, axis, split_axis=0, concat_axis=0, tiled=True)  23.6 us
    pallas_call x2, Pallas kernels, attend_backward(): pl.pallas_call(backward_kernel, grid=(heads,), in_specs=[pl.BlockSpec(mem...  21.8 us
    pallas_call x7, Pallas kernels, move(): pl.pallas_call(kernel, in_specs=[pl.BlockSpec(memory_space=pltpu.VMEM)] *...  18.8 us
    ppermute x3, starting transfers between devices, trade_other(): return lax.ppermute(x, 'wa', pairs)  14.4 us
    pallas_call x2, Pallas kernels, temporal_call(): pl.pallas_call(kernel, grid=(group, tokens // rows), in_specs=[spec(a.sha...  14.1 us
    ppermute x12, starting transfers between devices, trade(): lax.ppermute(chunks[s], 'tm', [(i, i ^ s) for i in range(PARTS)])  13.6 us
  transfers between devices with their start and end apart: 24, of which 9 were waited for; matrix products, arithmetic and copies ran while one was open for 0% of the time, Pallas kernels for 34%

profile of v8, /device:TPU:8, one launch (start us, length us, event | category | flops | bytes accessed | tf_op | source)
XLA Modules:
  0.0 196.7 jit_solution(2806675289003355673)
XLA Ops:
  0.6 2.8 %shard_map.101.refs_3_ = bf16[4,3,2,256,128]{4,3,2,1,0:T(8,128)(2,1)} custom-call(bf16[256,1536]{1,0:T(8,128)(2,1)} %bitcast.13, bf16[256,1536]{1,0:T(8,128)(2,1)} %bitcast.14), custom_call_target="tpu_custom_call" | custom-call | flops 100000000 | bytes 1024 | tf_op jit(solution)/shard_map/pallas_call | solution.py:49
  3.4 4.4 %all-to-all-start.1 = ((bf16[4,3,2,256,128]{4,3,2,1,0:T(8,128)(2,1)}), bf16[4,3,2,256,128]{4,3,2,1,0:T(8,128)(2,1)}, u32[]{:S(2)}, u32[]{:S(2)}) async-start(bf16[4,3,2,256,128]{4,3,2,1,0:T(8,128)(2,1)} %shard_map.101.refs_3_), calls=%async_computation.1 | async-start | bytes 3145728 | tf_op jit(solution)/shard_map/all_to_all | solution.py:383
  7.8 3.4 %shard_map.102 = (bf16[3,3,256,128]{3,2,1,0:T(8,128)(2,1)}, bf16[3,3,256,128]{3,2,1,0:T(8,128)(2,1)}, bf16[3,3,256,128]{3,2,1,0:T(8,128)(2,1)}, bf16[3,3,256,128]{3,2,1,0:T(8,128)(2,1)}) custom-call(bf16[256,1536]{1,0:T(8,128)(2,1)} %bitcast.15, bf16[256,1536]{1,0:T(8,128)(2,1)} %bitcast.16, bf16[256,1536]{1,0:T(8,128)(2,1)} %bitcast.17, ...), custom_call_target="tpu_custom_call" | custom-call | flops 100000000 | bytes 1024 | tf_op jit(solution)/shard_map/pallas_call | solution.py:49
  11.2 2.3 %collective-permute-start.3 = (bf16[3,3,256,128]{3,2,1,0:T(8,128)(2,1)}, bf16[3,3,256,128]{3,2,1,0:T(8,128)(2,1)}, u32[]{:S(2)}, u32[]{:S(2)}) collective-permute-start(bf16[3,3,256,128]{3,2,1,0:T(8,128)(2,1)} %get-tuple-element.38), channel_id=1, source_target_pairs={{0,64},{32,96},{64,0},{96,32},{1,65},{33,97},{65,1},{97,33},{2,66}... | collective-permute-start | bytes 1769480 | tf_op jit(solution)/shard_map/ppermute | solution.py:144
  14.6 14.3 %all-to-all-done.1.refs_4_.own_ref = bf16[4,3,2,256,128]{4,3,2,1,0:T(8,128)(2,1)} async-done(((bf16[4,3,2,256,128]{4,3,2,1,0:T(8,128)(2,1)}), bf16[4,3,2,256,128]{4,3,2,1,0:T(8,128)(2,1)}, u32[]{:S(2)}, u32[]{:S(2)}) %all-to-all-start.1) | async-done | bytes 1572896 | tf_op jit(solution)/shard_map/all_to_all | solution.py:383
  30.8 4.3 %collective-permute-start = (bf16[4,3,2,256,128]{4,3,2,1,0:T(8,128)(2,1)}, bf16[4,3,2,256,128]{4,3,2,1,0:T(8,128)(2,1)}, u32[]{:S(2)}, u32[]{:S(2)}) collective-permute-start(bf16[4,3,2,256,128]{4,3,2,1,0:T(8,128)(2,1)} %all-to-all-done.1.refs_4_.own_ref), channel_id=1, source_target_pairs={{1,2},{3,4},{5,6},{2,1},{4,3},{6,5},{9,10},{11,12},{13,14},{10,9},... | collective-permute-start | bytes 4718600 | tf_op jit(solution)/shard_map/ppermute | solution.py:393
  35.1 2.1 %shard_map.103.refs_5_ = bf16[4,3,1,256,128]{4,3,2,1,0:T(8,128)(2,1)} custom-call(bf16[256,1536]{1,0:T(8,128)(2,1)} %bitcast.12, bf16[3,3,256,128]{3,2,1,0:T(8,128)(2,1)} %get-tuple-element.36.refs_1_.refs_0_), custom_call_target="tpu_custom_call" | custom-call | flops 100000000 | bytes 1024 | tf_op jit(solution)/shard_map/pallas_call | solution.py:49
  37.2 4.2 %all-to-all-start = ((bf16[4,3,1,256,128]{4,3,2,1,0:T(8,128)(2,1)}), bf16[4,3,1,256,128]{4,3,2,1,0:T(8,128)(2,1)}, u32[]{:S(2)}, u32[]{:S(2)}) async-start(bf16[4,3,1,256,128]{4,3,2,1,0:T(8,128)(2,1)} %shard_map.103.refs_5_), calls=%async_computation | async-start | bytes 1572864 | tf_op jit(solution)/shard_map/all_to_all | solution.py:383
  41.5 5.5 %shard_map.104 = (bf16[3,1,256,128]{3,2,1,0:T(8,128)(2,1)}, bf16[3,1,256,128]{3,2,1,0:T(8,128)(2,1)}, bf16[3,1,256,128]{3,2,1,0:T(8,128)(2,1)}, bf16[3,1,256,128]{3,2,1,0:T(8,128)(2,1)}) custom-call(bf16[3,3,256,128]{3,2,1,0:T(8,128)(2,1)} %get-tuple-element.36.refs_1_.refs_0_, bf16[3,3,256,128]{3,2,1,0:T(8,128)(2,1)} %collective-permute-done.2.refs_1_, ...), custom_call_target="tpu_custom_call" | custom-call | flops 10000000000 | bytes 1024 | tf_op jit(solution)/shard_map/pallas_call | solution.py:370
  47.1 2.6 %collective-permute-start.6 = (bf16[3,1,256,128]{3,2,1,0:T(8,128)(2,1)}, bf16[3,1,256,128]{3,2,1,0:T(8,128)(2,1)}, u32[]{:S(2)}, u32[]{:S(2)}) collective-permute-start(bf16[3,1,256,128]{3,2,1,0:T(8,128)(2,1)} %get-tuple-element.42), channel_id=1, source_target_pairs={{0,64},{32,96},{64,0},{96,32},{1,65},{33,97},{65,1},{97,33},{2,66}... | collective-permute-start | bytes 589832 | tf_op jit(solution)/shard_map/ppermute | solution.py:144
  50.4 29.3 %collective-permute-done.6.refs_2_ = bf16[3,1,256,128]{3,2,1,0:T(8,128)(2,1)} collective-permute-done((bf16[3,1,256,128]{3,2,1,0:T(8,128)(2,1)}, bf16[3,1,256,128]{3,2,1,0:T(8,128)(2,1)}, u32[]{:S(2)}, u32[]{:S(2)}) %collective-permute-start.6) | collective-permute-done | bytes 196640 | tf_op jit(solution)/shard_map/ppermute | solution.py:144
  79.7 3.4 %collective-permute-done.7.refs_3_ = bf16[3,1,256,128]{3,2,1,0:T(8,128)(2,1)} collective-permute-done((bf16[3,1,256,128]{3,2,1,0:T(8,128)(2,1)}, bf16[3,1,256,128]{3,2,1,0:T(8,128)(2,1)}, u32[]{:S(2)}, u32[]{:S(2)}) %collective-permute-start.7) | collective-permute-done | bytes 196640 | tf_op jit(solution)/shard_map/ppermute | solution.py:144
  83.2 2.2 %shard_map.105._ = bf16[4,3,1,256,128]{4,3,2,1,0:T(8,128)(2,1)} custom-call(bf16[3,1,256,128]{3,2,1,0:T(8,128)(2,1)} %get-tuple-element.40.refs_0_, bf16[3,1,256,128]{3,2,1,0:T(8,128)(2,1)} %collective-permute-done.5.refs_1_, bf16[3,1,256,128]{3,2,1,0:T(8,128)(2,1)} %collective-permute-done.6.refs_2_, bf16[3,1,256,128]{3,2,1,0:T(8,128)(2,1)} %collective-permute-done.7.refs_3_), custom_call_target="tpu_custom_call" | custom-call | flops 100000000 | bytes 1024 | tf_op jit(solution)/shard_map/pallas_call | solution.py:49
  85.3 4.7 %all-to-all-start.2 = ((bf16[4,3,1,256,128]{4,3,2,1,0:T(8,128)(2,1)}), bf16[4,3,1,256,128]{4,3,2,1,0:T(8,128)(2,1)}, u32[]{:S(2)}, u32[]{:S(2)}) async-start(bf16[4,3,1,256,128]{4,3,2,1,0:T(8,128)(2,1)} %shard_map.105._), calls=%async_computation.2 | async-start | bytes 1572864 | tf_op jit(solution)/shard_map/all_to_all | solution.py:383
  90.1 12.7 %shard_map.106 = (bf16[4,3,1,256,128]{4,3,2,1,0:T(8,128)(2,1)}, f32[3,1,1024]{2,1,0:T(1,128)}) custom-call(f32[1]{0:T(128)} %bitcast.bad_ref, bf16[4,3,1,256,128]{4,3,2,1,0:T(8,128)(2,1)} %all-to-all-done.q_ref, bf16[4,3,2,256,128]{4,3,2,1,0:T(8,128)(2,1)} %collective-permute-done.other_ref, bf16[4,3,2,256,128]{4,3,2,1,0:T(8,128)(2,1)} %all-to-all-done.1.refs_4_.own_ref, ...), custom_call_target="tpu_custom_call" | custom-call | flops 99999997952 | bytes 1024 | tf_op jit(solution)/shard_map/pallas_call | solution.py:191
  102.8 4.7 %all-to-all-start.3 = ((bf16[4,3,1,256,128]{4,3,2,1,0:T(8,128)(2,1)}), bf16[4,3,1,256,128]{4,3,2,1,0:T(8,128)(2,1)}, u32[]{:S(2)}, u32[]{:S(2)}) async-start(bf16[4,3,1,256,128]{4,3,2,1,0:T(8,128)(2,1)} %get-tuple-element.44.o_ref), calls=%async_computation.3 | async-start | bytes 1572864 | tf_op jit(solution)/shard_map/all_to_all | solution.py:383
  107.6 7.9 %shard_map.107 = (bf16[4,1,1,256,128]{4,3,2,1,0:T(8,128)(2,1)}, bf16[4,1,2,256,128]{4,3,2,1,0:T(8,128)(2,1)}, bf16[4,1,2,256,128]{4,3,2,1,0:T(8,128)(2,1)}, bf16[4,1,2,256,128]{4,3,2,1,0:T(8,128)(2,1)}) custom-call(f32[1]{0:T(128)} %bitcast.bad_ref, bf16[4,3,1,256,128]{4,3,2,1,0:T(8,128)(2,1)} %all-to-all-done.q_ref, ...), custom_call_target="tpu_custom_call" | custom-call | flops 99999997952 | bytes 1024 | tf_op jit(solution)/shard_map/pallas_call | solution.py:252
  115.4 5.8 %collective-permute-start.8 = (bf16[4,1,2,256,128]{4,3,2,1,0:T(8,128)(2,1)}, bf16[4,1,2,256,128]{4,3,2,1,0:T(8,128)(2,1)}, u32[]{:S(2)}, u32[]{:S(2)}) collective-permute-start(bf16[4,1,2,256,128]{4,3,2,1,0:T(8,128)(2,1)} %get-tuple-element.48), channel_id=1, source_target_pairs={{1,2},{3,4},{5,6},{2,1},{4,3},{6,5},{9,10},{11,12},{13,14},{10,9},... | collective-permute-start | bytes 1572872 | tf_op jit(solution)/shard_map/ppermute | solution.py:393
  123.4 2.6 %collective-permute-start.13 = (bf16[3,1,256,128]{3,2,1,0:T(8,128)(2,1)}, bf16[3,1,256,128]{3,2,1,0:T(8,128)(2,1)}, u32[]{:S(2)}, u32[]{:S(2)}) collective-permute-start(bf16[3,1,256,128]{3,2,1,0:T(8,128)(2,1)} %get-tuple-element.59), channel_id=1, source_target_pairs={{0,64},{32,96},{64,0},{96,32},{1,65},{33,97},{65,1},{97,33},{2,66}... | collective-permute-start | bytes 589832 | tf_op jit(solution)/shard_map/ppermute | solution.py:144
  126.8 14.0 %shard_map.109 = (bf16[4,2,1,256,128]{4,3,2,1,0:T(8,128)(2,1)}, bf16[4,2,2,256,128]{4,3,2,1,0:T(8,128)(2,1)}, bf16[4,2,2,256,128]{4,3,2,1,0:T(8,128)(2,1)}, bf16[4,2,2,256,128]{4,3,2,1,0:T(8,128)(2,1)}) custom-call(f32[1]{0:T(128)} %bitcast.bad_ref, bf16[4,3,1,256,128]{4,3,2,1,0:T(8,128)(2,1)} %all-to-all-done.q_ref, ...), custom_call_target="tpu_custom_call" | custom-call | flops 99999997952 | bytes 1024 | tf_op jit(solution)/shard_map/pallas_call | solution.py:252
  140.8 4.3 %collective-permute-start.10 = (bf16[4,2,2,256,128]{4,3,2,1,0:T(8,128)(2,1)}, bf16[4,2,2,256,128]{4,3,2,1,0:T(8,128)(2,1)}, u32[]{:S(2)}, u32[]{:S(2)}) collective-permute-start(bf16[4,2,2,256,128]{4,3,2,1,0:T(8,128)(2,1)} %get-tuple-element.53), channel_id=1, source_target_pairs={{1,2},{3,4},{5,6},{2,1},{4,3},{6,5},{9,10},{11,12},{13,14},{10,9},... | collective-permute-start | bytes 3145736 | tf_op jit(solution)/shard_map/ppermute | solution.py:393
  145.2 2.9 %shard_map.110.refs_8_ = bf16[4,5,256,128]{3,2,1,0:T(8,128)(2,1)} custom-call(bf16[4,1,1,256,128]{4,3,2,1,0:T(8,128)(2,1)} %get-tuple-element.46.rest_1_.dq_ref, bf16[4,1,2,256,128]{4,3,2,1,0:T(8,128)(2,1)} %get-tuple-element.47.refs_0_, bf16[4,1,2,256,128]{4,3,2,1,0:T(8,128)(2,1)} %collective-permute-done.8.refs_1_, ...), custom_call_target="tpu_custom_call" | custom-call | flops 100000000 | bytes 1024 | tf_op jit(solution)/shard_map/pallas_call | solution.py:298
  148.1 4.4 %all-to-all-start.4 = ((bf16[4,5,256,128]{3,2,1,0:T(8,128)(2,1)}), bf16[4,5,256,128]{3,2,1,0:T(8,128)(2,1)}, u32[]{:S(2)}, u32[]{:S(2)}) async-start(bf16[4,5,256,128]{3,2,1,0:T(8,128)(2,1)} %shard_map.110.refs_8_), calls=%async_computation.4 | async-start | bytes 2621440 | tf_op jit(solution)/shard_map/all_to_all | solution.py:383
  152.5 8.6 %shard_map.113 = (bf16[3,2,256,128]{3,2,1,0:T(8,128)(2,1)}, bf16[3,2,256,128]{3,2,1,0:T(8,128)(2,1)}, bf16[3,2,256,128]{3,2,1,0:T(8,128)(2,1)}, bf16[3,2,256,128]{3,2,1,0:T(8,128)(2,1)}) custom-call(bf16[3,3,256,128]{3,2,1,0:T(8,128)(2,1)} %get-tuple-element.36.refs_1_.refs_0_, bf16[3,3,256,128]{3,2,1,0:T(8,128)(2,1)} %collective-permute-done.2.refs_1_, ...), custom_call_target="tpu_custom_call" | custom-call | flops 5000000000 | bytes 1024 | tf_op jit(solution)/shard_map/pallas_call | solution.py:370
  161.2 2.7 %collective-permute-start.16 = (bf16[3,2,256,128]{3,2,1,0:T(8,128)(2,1)}, bf16[3,2,256,128]{3,2,1,0:T(8,128)(2,1)}, u32[]{:S(2)}, u32[]{:S(2)}) collective-permute-start(bf16[3,2,256,128]{3,2,1,0:T(8,128)(2,1)} %get-tuple-element.63), channel_id=1, source_target_pairs={{0,64},{32,96},{64,0},{96,32},{1,65},{33,97},{65,1},{97,33},{2,66}... | collective-permute-start | bytes 1179656 | tf_op jit(solution)/shard_map/ppermute | solution.py:144
  164.5 6.3 %all-to-all-done.4.refs_3_.refs_0_ = bf16[4,5,256,128]{3,2,1,0:T(8,128)(2,1)} async-done(((bf16[4,5,256,128]{3,2,1,0:T(8,128)(2,1)}), bf16[4,5,256,128]{3,2,1,0:T(8,128)(2,1)}, u32[]{:S(2)}, u32[]{:S(2)}) %all-to-all-start.4) | async-done | bytes 1310752 | tf_op jit(solution)/shard_map/all_to_all | solution.py:383
  171.1 3.2 %shard_map.111 = bf16[4,4,256,128]{3,2,1,0:T(8,128)(2,1)} custom-call(bf16[4,2,2,256,128]{4,3,2,1,0:T(8,128)(2,1)} %get-tuple-element.52.refs_0_, bf16[4,2,2,256,128]{4,3,2,1,0:T(8,128)(2,1)} %collective-permute-done.10.refs_1_, bf16[4,2,2,256,128]{4,3,2,1,0:T(8,128)(2,1)} %collective-permute-done.11.refs_2_, ...), custom_call_target="tpu_custom_call" | custom-call | flops 100000000 | bytes 1024 | tf_op jit(solution)/shard_map/pallas_call | solution.py:298
  174.3 4.8 %all-to-all-start.5 = ((bf16[4,4,256,128]{3,2,1,0:T(8,128)(2,1)}), bf16[4,4,256,128]{3,2,1,0:T(8,128)(2,1)}, u32[]{:S(2)}, u32[]{:S(2)}) async-start(bf16[4,4,256,128]{3,2,1,0:T(8,128)(2,1)} %shard_map.111), calls=%async_computation.5 | async-start | bytes 2097152 | tf_op jit(solution)/shard_map/all_to_all | solution.py:383
  180.4 7.2 %collective-permute-done.17.refs_3_ = bf16[3,2,256,128]{3,2,1,0:T(8,128)(2,1)} collective-permute-done((bf16[3,2,256,128]{3,2,1,0:T(8,128)(2,1)}, bf16[3,2,256,128]{3,2,1,0:T(8,128)(2,1)}, u32[]{:S(2)}, u32[]{:S(2)}) %collective-permute-start.17) | collective-permute-done | bytes 393248 | tf_op jit(solution)/shard_map/ppermute | solution.py:144
  187.5 2.8 %shard_map.114 = (bf16[256,1536]{1,0:T(8,128)(2,1)}, bf16[256,1536]{1,0:T(8,128)(2,1)}) custom-call(bf16[3,2,256,128]{3,2,1,0:T(8,128)(2,1)} %get-tuple-element.61.refs_0_, bf16[3,2,256,128]{3,2,1,0:T(8,128)(2,1)} %collective-permute-done.15.refs_1_, bf16[3,2,256,128]{3,2,1,0:T(8,128)(2,1)} %collective-permute-done.16.refs_2_, ...), custom_call_target="tpu_custom_call" | custom-call | flops 99999997952 | bytes 1024 | tf_op jit(solution)/shard_map/pallas_call | solution.py:49
  190.3 3.0 %all-to-all-done.5.refs_1_ = bf16[4,4,256,128]{3,2,1,0:T(8,128)(2,1)} async-done(((bf16[4,4,256,128]{3,2,1,0:T(8,128)(2,1)}), bf16[4,4,256,128]{3,2,1,0:T(8,128)(2,1)}, u32[]{:S(2)}, u32[]{:S(2)}) %all-to-all-start.5) | async-done | bytes 1048608 | tf_op jit(solution)/shard_map/all_to_all | solution.py:383
  193.3 3.4 %shard_map.112 = (bf16[256,1536]{1,0:T(8,128)(2,1)}, bf16[256,1536]{1,0:T(8,128)(2,1)}, bf16[256,1536]{1,0:T(8,128)(2,1)}) custom-call(bf16[4,5,256,128]{3,2,1,0:T(8,128)(2,1)} %all-to-all-done.4.refs_3_.refs_0_, bf16[4,4,256,128]{3,2,1,0:T(8,128)(2,1)} %all-to-all-done.5.refs_1_), custom_call_target="tpu_custom_call" | custom-call | flops 100000000 | bytes 1024 | tf_op jit(solution)/shard_map/pallas_call | solution.py:49
  (30 shorter events, 9.3 us)
Async XLA Ops:
  3.4 25.4 %all-to-all-start.1 = ((bf16[4,3,2,256,128]{4,3,2,1,0:T(8,128)(2,1)}), bf16[4,3,2,256,128]{4,3,2,1,0:T(8,128)(2,1)}, u32[]{:S(2)}, u32[]{:S(2)}) async-start(bf16[4,3,2,256,128]{4,3,2,1,0:T(8,128)(2,1)} %shard_map.101.refs_3_), calls=%async_computation.1 | async-start | bytes 3145728 | tf_op jit(solution)/shard_map/all_to_all | solution.py:383
  11.2 30.2 %collective-permute-start.2 = (bf16[3,3,256,128]{3,2,1,0:T(8,128)(2,1)}, bf16[3,3,256,128]{3,2,1,0:T(8,128)(2,1)}, u32[]{:S(2)}, u32[]{:S(2)}) collective-permute-start(bf16[3,3,256,128]{3,2,1,0:T(8,128)(2,1)} %get-tuple-element.37), channel_id=1, source_target_pairs={{0,32},{32,0},{64,96},{96,64},{1,33},{33,1},{65,97},{97,65},{2,34}... | collective-permute-start | bytes 1769480 | tf_op jit(solution)/shard_map/ppermute | solution.py:144
  11.2 30.2 %collective-permute-start.3 = (bf16[3,3,256,128]{3,2,1,0:T(8,128)(2,1)}, bf16[3,3,256,128]{3,2,1,0:T(8,128)(2,1)}, u32[]{:S(2)}, u32[]{:S(2)}) collective-permute-start(bf16[3,3,256,128]{3,2,1,0:T(8,128)(2,1)} %get-tuple-element.38), channel_id=1, source_target_pairs={{0,64},{32,96},{64,0},{96,32},{1,65},{33,97},{65,1},{97,33},{2,66}... | collective-permute-start | bytes 1769480 | tf_op jit(solution)/shard_map/ppermute | solution.py:144
  13.5 28.0 %collective-permute-start.4 = (bf16[3,3,256,128]{3,2,1,0:T(8,128)(2,1)}, bf16[3,3,256,128]{3,2,1,0:T(8,128)(2,1)}, u32[]{:S(2)}, u32[]{:S(2)}) collective-permute-start(bf16[3,3,256,128]{3,2,1,0:T(8,128)(2,1)} %get-tuple-element.39), channel_id=1, source_target_pairs={{0,96},{32,64},{64,32},{96,0},{1,97},{33,65},{65,33},{97,1},{2,98}... | collective-permute-start | bytes 1769480 | tf_op jit(solution)/shard_map/ppermute | solution.py:144
  28.8 61.2 %collective-permute-start.1 = (bf16[4,3,2,256,128]{4,3,2,1,0:T(8,128)(2,1)}, bf16[4,3,2,256,128]{4,3,2,1,0:T(8,128)(2,1)}, u32[]{:S(2)}, u32[]{:S(2)}) collective-permute-start(bf16[4,3,2,256,128]{4,3,2,1,0:T(8,128)(2,1)} %all-to-all-done.1.refs_4_.own_ref), channel_id=1, source_target_pairs={{0,1},{1,0},{2,3},{3,2},{4,5},{5,4},{6,7},{7,6},{8,9},{9,8},{10,11... | collective-permute-start | bytes 4718600 | tf_op jit(solution)/shard_map/ppermute | solution.py:387
  30.8 59.3 %collective-permute-start = (bf16[4,3,2,256,128]{4,3,2,1,0:T(8,128)(2,1)}, bf16[4,3,2,256,128]{4,3,2,1,0:T(8,128)(2,1)}, u32[]{:S(2)}, u32[]{:S(2)}) collective-permute-start(bf16[4,3,2,256,128]{4,3,2,1,0:T(8,128)(2,1)} %all-to-all-done.1.refs_4_.own_ref), channel_id=1, source_target_pairs={{1,2},{3,4},{5,6},{2,1},{4,3},{6,5},{9,10},{11,12},{13,14},{10,9},... | collective-permute-start | bytes 4718600 | tf_op jit(solution)/shard_map/ppermute | solution.py:393
  37.2 48.1 %all-to-all-start = ((bf16[4,3,1,256,128]{4,3,2,1,0:T(8,128)(2,1)}), bf16[4,3,1,256,128]{4,3,2,1,0:T(8,128)(2,1)}, u32[]{:S(2)}, u32[]{:S(2)}) async-start(bf16[4,3,1,256,128]{4,3,2,1,0:T(8,128)(2,1)} %shard_map.103.refs_5_), calls=%async_computation | async-start | bytes 1572864 | tf_op jit(solution)/shard_map/all_to_all | solution.py:383
  47.0 3.4 %collective-permute-start.5 = (bf16[3,1,256,128]{3,2,1,0:T(8,128)(2,1)}, bf16[3,1,256,128]{3,2,1,0:T(8,128)(2,1)}, u32[]{:S(2)}, u32[]{:S(2)}) collective-permute-start(bf16[3,1,256,128]{3,2,1,0:T(8,128)(2,1)} %get-tuple-element.41), channel_id=1, source_target_pairs={{0,32},{32,0},{64,96},{96,64},{1,33},{33,1},{65,97},{97,65},{2,34}... | collective-permute-start | bytes 589832 | tf_op jit(solution)/shard_map/ppermute | solution.py:144
  47.1 32.6 %collective-permute-start.6 = (bf16[3,1,256,128]{3,2,1,0:T(8,128)(2,1)}, bf16[3,1,256,128]{3,2,1,0:T(8,128)(2,1)}, u32[]{:S(2)}, u32[]{:S(2)}) collective-permute-start(bf16[3,1,256,128]{3,2,1,0:T(8,128)(2,1)} %get-tuple-element.42), channel_id=1, source_target_pairs={{0,64},{32,96},{64,0},{96,32},{1,65},{33,97},{65,1},{97,33},{2,66}... | collective-permute-start | bytes 589832 | tf_op jit(solution)/shard_map/ppermute | solution.py:144
  49.7 33.5 %collective-permute-start.7 = (bf16[3,1,256,128]{3,2,1,0:T(8,128)(2,1)}, bf16[3,1,256,128]{3,2,1,0:T(8,128)(2,1)}, u32[]{:S(2)}, u32[]{:S(2)}) collective-permute-start(bf16[3,1,256,128]{3,2,1,0:T(8,128)(2,1)} %get-tuple-element.43), channel_id=1, source_target_pairs={{0,96},{32,64},{64,32},{96,0},{1,97},{33,65},{65,33},{97,1},{2,98}... | collective-permute-start | bytes 589832 | tf_op jit(solution)/shard_map/ppermute | solution.py:144
  85.3 17.5 %all-to-all-start.2 = ((bf16[4,3,1,256,128]{4,3,2,1,0:T(8,128)(2,1)}), bf16[4,3,1,256,128]{4,3,2,1,0:T(8,128)(2,1)}, u32[]{:S(2)}, u32[]{:S(2)}) async-start(bf16[4,3,1,256,128]{4,3,2,1,0:T(8,128)(2,1)} %shard_map.105._), calls=%async_computation.2 | async-start | bytes 1572864 | tf_op jit(solution)/shard_map/all_to_all | solution.py:383
  102.8 18.5 %all-to-all-start.3 = ((bf16[4,3,1,256,128]{4,3,2,1,0:T(8,128)(2,1)}), bf16[4,3,1,256,128]{4,3,2,1,0:T(8,128)(2,1)}, u32[]{:S(2)}, u32[]{:S(2)}) async-start(bf16[4,3,1,256,128]{4,3,2,1,0:T(8,128)(2,1)} %get-tuple-element.44.o_ref), calls=%async_computation.3 | async-start | bytes 1572864 | tf_op jit(solution)/shard_map/all_to_all | solution.py:383
  115.4 25.3 %collective-permute-start.8 = (bf16[4,1,2,256,128]{4,3,2,1,0:T(8,128)(2,1)}, bf16[4,1,2,256,128]{4,3,2,1,0:T(8,128)(2,1)}, u32[]{:S(2)}, u32[]{:S(2)}) collective-permute-start(bf16[4,1,2,256,128]{4,3,2,1,0:T(8,128)(2,1)} %get-tuple-element.48), channel_id=1, source_target_pairs={{1,2},{3,4},{5,6},{2,1},{4,3},{6,5},{9,10},{11,12},{13,14},{10,9},... | collective-permute-start | bytes 1572872 | tf_op jit(solution)/shard_map/ppermute | solution.py:393
  121.3 23.8 %collective-permute-start.9 = (bf16[4,1,2,256,128]{4,3,2,1,0:T(8,128)(2,1)}, bf16[4,1,2,256,128]{4,3,2,1,0:T(8,128)(2,1)}, u32[]{:S(2)}, u32[]{:S(2)}) collective-permute-start(bf16[4,1,2,256,128]{4,3,2,1,0:T(8,128)(2,1)} %get-tuple-element.49), channel_id=1, source_target_pairs={{0,1},{1,0},{2,3},{3,2},{4,5},{5,4},{6,7},{7,6},{8,9},{9,8},{10,11... | collective-permute-start | bytes 1572872 | tf_op jit(solution)/shard_map/ppermute | solution.py:387
  123.4 29.0 %collective-permute-start.12 = (bf16[3,1,256,128]{3,2,1,0:T(8,128)(2,1)}, bf16[3,1,256,128]{3,2,1,0:T(8,128)(2,1)}, u32[]{:S(2)}, u32[]{:S(2)}) collective-permute-start(bf16[3,1,256,128]{3,2,1,0:T(8,128)(2,1)} %get-tuple-element.58), channel_id=1, source_target_pairs={{0,32},{32,0},{64,96},{96,64},{1,33},{33,1},{65,97},{97,65},{2,34}... | collective-permute-start | bytes 589832 | tf_op jit(solution)/shard_map/ppermute | solution.py:144
  123.4 29.0 %collective-permute-start.13 = (bf16[3,1,256,128]{3,2,1,0:T(8,128)(2,1)}, bf16[3,1,256,128]{3,2,1,0:T(8,128)(2,1)}, u32[]{:S(2)}, u32[]{:S(2)}) collective-permute-start(bf16[3,1,256,128]{3,2,1,0:T(8,128)(2,1)} %get-tuple-element.59), channel_id=1, source_target_pairs={{0,64},{32,96},{64,0},{96,32},{1,65},{33,97},{65,1},{97,33},{2,66}... | collective-permute-start | bytes 589832 | tf_op jit(solution)/shard_map/ppermute | solution.py:144
  126.0 26.4 %collective-permute-start.14 = (bf16[3,1,256,128]{3,2,1,0:T(8,128)(2,1)}, bf16[3,1,256,128]{3,2,1,0:T(8,128)(2,1)}, u32[]{:S(2)}, u32[]{:S(2)}) collective-permute-start(bf16[3,1,256,128]{3,2,1,0:T(8,128)(2,1)} %get-tuple-element.60), channel_id=1, source_target_pairs={{0,96},{32,64},{64,32},{96,0},{1,97},{33,65},{65,33},{97,1},{2,98}... | collective-permute-start | bytes 589832 | tf_op jit(solution)/shard_map/ppermute | solution.py:144
  140.8 30.3 %collective-permute-start.10 = (bf16[4,2,2,256,128]{4,3,2,1,0:T(8,128)(2,1)}, bf16[4,2,2,256,128]{4,3,2,1,0:T(8,128)(2,1)}, u32[]{:S(2)}, u32[]{:S(2)}) collective-permute-start(bf16[4,2,2,256,128]{4,3,2,1,0:T(8,128)(2,1)} %get-tuple-element.53), channel_id=1, source_target_pairs={{1,2},{3,4},{5,6},{2,1},{4,3},{6,5},{9,10},{11,12},{13,14},{10,9},... | collective-permute-start | bytes 3145736 | tf_op jit(solution)/shard_map/ppermute | solution.py:393
  145.1 26.0 %collective-permute-start.11 = (bf16[4,2,2,256,128]{4,3,2,1,0:T(8,128)(2,1)}, bf16[4,2,2,256,128]{4,3,2,1,0:T(8,128)(2,1)}, u32[]{:S(2)}, u32[]{:S(2)}) collective-permute-start(bf16[4,2,2,256,128]{4,3,2,1,0:T(8,128)(2,1)} %get-tuple-element.54), channel_id=1, source_target_pairs={{0,1},{1,0},{2,3},{3,2},{4,5},{5,4},{6,7},{7,6},{8,9},{9,8},{10,11... | collective-permute-start | bytes 3145736 | tf_op jit(solution)/shard_map/ppermute | solution.py:387
  148.1 22.7 %all-to-all-start.4 = ((bf16[4,5,256,128]{3,2,1,0:T(8,128)(2,1)}), bf16[4,5,256,128]{3,2,1,0:T(8,128)(2,1)}, u32[]{:S(2)}, u32[]{:S(2)}) async-start(bf16[4,5,256,128]{3,2,1,0:T(8,128)(2,1)} %shard_map.110.refs_8_), calls=%async_computation.4 | async-start | bytes 2621440 | tf_op jit(solution)/shard_map/all_to_all | solution.py:383
  161.1 18.0 %collective-permute-start.15 = (bf16[3,2,256,128]{3,2,1,0:T(8,128)(2,1)}, bf16[3,2,256,128]{3,2,1,0:T(8,128)(2,1)}, u32[]{:S(2)}, u32[]{:S(2)}) collective-permute-start(bf16[3,2,256,128]{3,2,1,0:T(8,128)(2,1)} %get-tuple-element.62), channel_id=1, source_target_pairs={{0,32},{32,0},{64,96},{96,64},{1,33},{33,1},{65,97},{97,65},{2,34}... | collective-permute-start | bytes 1179656 | tf_op jit(solution)/shard_map/ppermute | solution.py:144
  161.2 19.2 %collective-permute-start.16 = (bf16[3,2,256,128]{3,2,1,0:T(8,128)(2,1)}, bf16[3,2,256,128]{3,2,1,0:T(8,128)(2,1)}, u32[]{:S(2)}, u32[]{:S(2)}) collective-permute-start(bf16[3,2,256,128]{3,2,1,0:T(8,128)(2,1)} %get-tuple-element.63), channel_id=1, source_target_pairs={{0,64},{32,96},{64,0},{96,32},{1,65},{33,97},{65,1},{97,33},{2,66}... | collective-permute-start | bytes 1179656 | tf_op jit(solution)/shard_map/ppermute | solution.py:144
  163.8 23.7 %collective-permute-start.17 = (bf16[3,2,256,128]{3,2,1,0:T(8,128)(2,1)}, bf16[3,2,256,128]{3,2,1,0:T(8,128)(2,1)}, u32[]{:S(2)}, u32[]{:S(2)}) collective-permute-start(bf16[3,2,256,128]{3,2,1,0:T(8,128)(2,1)} %get-tuple-element.64), channel_id=1, source_target_pairs={{0,96},{32,64},{64,32},{96,0},{1,97},{33,65},{65,33},{97,1},{2,98}... | collective-permute-start | bytes 1179656 | tf_op jit(solution)/shard_map/ppermute | solution.py:144
  174.3 19.0 %all-to-all-start.5 = ((bf16[4,4,256,128]{3,2,1,0:T(8,128)(2,1)}), bf16[4,4,256,128]{3,2,1,0:T(8,128)(2,1)}, u32[]{:S(2)}, u32[]{:S(2)}) async-start(bf16[4,4,256,128]{3,2,1,0:T(8,128)(2,1)} %shard_map.111), calls=%async_computation.5 | async-start | bytes 2097152 | tf_op jit(solution)/shard_map/all_to_all | solution.py:383

commit v9 on v8

--- a/solution.py
+++ b/solution.py
@@ -123,18 +123,16 @@
     )
 
 
-def unpack_heads(early, late):
-    tokens = early.shape[2]
-    places = [[(0, 0), (0, 1), (0, 2)]]
-    for h in range(GROUP - 1):
-        places.append([(0, 3 + h), (1, 2 * h), (1, 2 * h + 1)])
-    cells = [(a, d, h) for h in range(GROUP) for d in range(PARTS) for a in range(3)]
-    return move(
-        [early, late],
-        [bf16(tokens, HEADS * HEAD_DIM)] * 3,
+def unpack_slots(blocks, places, told=0.1):
+    tokens = blocks[0].shape[2]
+    cells = [(a, d, h) for h in range(GROUP) for d in range(PARTS) for a in range(len(places))]
+    return move(
+        blocks,
+        [bf16(tokens, HEADS * HEAD_DIM)] * len(places),
         lambda me: [
-            (places[h][a][0], (d, places[h][a][1]), a, columns(d, h)) for a, d, h in cells
+            (places[a][h][0], (d, places[a][h][1]), a, columns(d, h)) for a, d, h in cells
         ],
+        told=told,
     )
 
 
@@ -432,8 +430,13 @@
     )
     early = swap(early, "ha")
     late = swap(totals(late_kernel, 2 * (GROUP - 1), two[1:], [early]), "ha")
-    probe_grad, anchor_grad = unpack_partners(trade(times_sent), [])
-    query_grad, key_grad, value_grad = unpack_heads(early, late)
+    late_heads = range(GROUP - 1)
+    (query_grad,) = unpack_slots([early], [[(0, 0)] + [(0, 3 + h) for h in late_heads]], 100)
+    probe_grad, anchor_grad = unpack_partners(trade(times_sent), [query_grad])
+    key_grad, value_grad = unpack_slots(
+        [early, late],
+        [[(0, 1 + t)] + [(1, 2 * h + t) for h in late_heads] for t in range(2)],
+    )
     outs = (query_grad, key_grad, value_grad, probe_grad, anchor_grad)
     return tuple(x.reshape(shape) for x in outs)
 

time: 198 us -> 210 us (1.061)
  waiting for transfers between devices: 65.1 us -> 73.6 us
    ppermute x3, waiting for transfers between devices: 0.29 us -> 10.3 us  [trade_other(): return lax.ppermute(x, 'wa', pairs)]
    all_to_all x6, waiting for transfers between devices: 23.6 us -> 19.9 us  [swap(): return lax.all_to_all(x, axis, split_axis=0, concat_axis=0, tiled=True)]
    ppermute x12, waiting for transfers between devices: 41.3 us -> 43.4 us  [trade(): lax.ppermute(chunks[s], 'tm', [(i, i ^ s) for i in range(PARTS)])]
    pallas_call x7 -> x8, Pallas kernels: 18.8 us -> 20.7 us  [move(): pl.pallas_call(kernel, in_specs=[pl.BlockSpec(memory_space=pltpu.VMEM)] *...]
  transfers between devices with their start and end apart: 24 -> 24, of which waited for: 9 -> 9; matrix products, arithmetic and copies ran while one was open for 0% -> 0% of each run, Pallas kernels for 34% -> 32%
where the time goes in v9:
time: 210 us; the launch traced here: 209 us
  Pallas kernels  75.4 us (36%)
  waiting for transfers between devices  73.6 us (35%)
  starting transfers between devices  58 us (28%)
    ppermute x12, waiting for transfers between devices, trade(): lax.ppermute(chunks[s], 'tm', [(i, i ^ s) for i in range(PARTS)])  43.4 us
    all_to_all x6, starting transfers between devices, swap(): return lax.all_to_all(x, axis, split_axis=0, concat_axis=0, tiled=True)  27.3 us
    pallas_call x2, Pallas kernels, attend_backward(): pl.pallas_call(backward_kernel, grid=(heads,), in_specs=[pl.BlockSpec(mem...  21.9 us
    pallas_call x8, Pallas kernels, move(): pl.pallas_call(kernel, in_specs=[pl.BlockSpec(memory_space=pltpu.VMEM)] *...  20.7 us
    all_to_all x6, waiting for transfers between devices, swap(): return lax.all_to_all(x, axis, split_axis=0, concat_axis=0, tiled=True)  19.9 us
    ppermute x3, starting transfers between devices, trade_other(): return lax.ppermute(x, 'wa', pairs)  14.3 us
    ppermute x12, starting transfers between devices, trade(): lax.ppermute(chunks[s], 'tm', [(i, i ^ s) for i in range(PARTS)])  14.2 us
    pallas_call x2, Pallas kernels, temporal_call(): pl.pallas_call(kernel, grid=(group, tokens // rows), in_specs=[spec(a.sha...  14.1 us
  transfers between devices with their start and end apart: 24, of which 9 were waited for; matrix products, arithmetic and copies ran while one was open for 0% of the time, Pallas kernels for 32%

profile of v9, /device:TPU:8, one launch (start us, length us, event | category | flops | bytes accessed | tf_op | source)
XLA Modules:
  0.0 208.5 jit_solution(15423921251663672478)
XLA Ops:
  0.6 2.8 %shard_map.101.refs_3_ = bf16[4,3,2,256,128]{4,3,2,1,0:T(8,128)(2,1)} custom-call(bf16[256,1536]{1,0:T(8,128)(2,1)} %bitcast.13, bf16[256,1536]{1,0:T(8,128)(2,1)} %bitcast.14), custom_call_target="tpu_custom_call" | custom-call | flops 100000000 | bytes 1024 | tf_op jit(solution)/shard_map/pallas_call | solution.py:49
  3.4 4.3 %all-to-all-start.1 = ((bf16[4,3,2,256,128]{4,3,2,1,0:T(8,128)(2,1)}), bf16[4,3,2,256,128]{4,3,2,1,0:T(8,128)(2,1)}, u32[]{:S(2)}, u32[]{:S(2)}) async-start(bf16[4,3,2,256,128]{4,3,2,1,0:T(8,128)(2,1)} %shard_map.101.refs_3_), calls=%async_computation.1 | async-start | bytes 3145728 | tf_op jit(solution)/shard_map/all_to_all | solution.py:381
  7.8 3.4 %shard_map.102 = (bf16[3,3,256,128]{3,2,1,0:T(8,128)(2,1)}, bf16[3,3,256,128]{3,2,1,0:T(8,128)(2,1)}, bf16[3,3,256,128]{3,2,1,0:T(8,128)(2,1)}, bf16[3,3,256,128]{3,2,1,0:T(8,128)(2,1)}) custom-call(bf16[256,1536]{1,0:T(8,128)(2,1)} %bitcast.15, bf16[256,1536]{1,0:T(8,128)(2,1)} %bitcast.16, bf16[256,1536]{1,0:T(8,128)(2,1)} %bitcast.17, ...), custom_call_target="tpu_custom_call" | custom-call | flops 100000000 | bytes 1024 | tf_op jit(solution)/shard_map/pallas_call | solution.py:49
  11.2 2.3 %collective-permute-start.3 = (bf16[3,3,256,128]{3,2,1,0:T(8,128)(2,1)}, bf16[3,3,256,128]{3,2,1,0:T(8,128)(2,1)}, u32[]{:S(2)}, u32[]{:S(2)}) collective-permute-start(bf16[3,3,256,128]{3,2,1,0:T(8,128)(2,1)} %get-tuple-element.37), channel_id=1, source_target_pairs={{0,64},{32,96},{64,0},{96,32},{1,65},{33,97},{65,1},{97,33},{2,66}... | collective-permute-start | bytes 1769480 | tf_op jit(solution)/shard_map/ppermute | solution.py:142
  14.6 14.3 %all-to-all-done.1.refs_4_.own_ref = bf16[4,3,2,256,128]{4,3,2,1,0:T(8,128)(2,1)} async-done(((bf16[4,3,2,256,128]{4,3,2,1,0:T(8,128)(2,1)}), bf16[4,3,2,256,128]{4,3,2,1,0:T(8,128)(2,1)}, u32[]{:S(2)}, u32[]{:S(2)}) %all-to-all-start.1) | async-done | bytes 1572896 | tf_op jit(solution)/shard_map/all_to_all | solution.py:381
  30.7 4.3 %collective-permute-start = (bf16[4,3,2,256,128]{4,3,2,1,0:T(8,128)(2,1)}, bf16[4,3,2,256,128]{4,3,2,1,0:T(8,128)(2,1)}, u32[]{:S(2)}, u32[]{:S(2)}) collective-permute-start(bf16[4,3,2,256,128]{4,3,2,1,0:T(8,128)(2,1)} %all-to-all-done.1.refs_4_.own_ref), channel_id=1, source_target_pairs={{1,2},{3,4},{5,6},{2,1},{4,3},{6,5},{9,10},{11,12},{13,14},{10,9},... | collective-permute-start | bytes 4718600 | tf_op jit(solution)/shard_map/ppermute | solution.py:391
  37.2 4.2 %all-to-all-start = ((bf16[4,3,1,256,128]{4,3,2,1,0:T(8,128)(2,1)}), bf16[4,3,1,256,128]{4,3,2,1,0:T(8,128)(2,1)}, u32[]{:S(2)}, u32[]{:S(2)}) async-start(bf16[4,3,1,256,128]{4,3,2,1,0:T(8,128)(2,1)} %shard_map.103.refs_5_), calls=%async_computation | async-start | bytes 1572864 | tf_op jit(solution)/shard_map/all_to_all | solution.py:381
  41.5 5.5 %shard_map.104 = (bf16[3,1,256,128]{3,2,1,0:T(8,128)(2,1)}, bf16[3,1,256,128]{3,2,1,0:T(8,128)(2,1)}, bf16[3,1,256,128]{3,2,1,0:T(8,128)(2,1)}, bf16[3,1,256,128]{3,2,1,0:T(8,128)(2,1)}) custom-call(bf16[3,3,256,128]{3,2,1,0:T(8,128)(2,1)} %get-tuple-element.35.refs_1_.refs_0_, bf16[3,3,256,128]{3,2,1,0:T(8,128)(2,1)} %collective-permute-done.2.refs_1_, ...), custom_call_target="tpu_custom_call" | custom-call | flops 10000000000 | bytes 1024 | tf_op jit(solution)/shard_map/pallas_call | solution.py:368
  47.1 2.6 %collective-permute-start.6 = (bf16[3,1,256,128]{3,2,1,0:T(8,128)(2,1)}, bf16[3,1,256,128]{3,2,1,0:T(8,128)(2,1)}, u32[]{:S(2)}, u32[]{:S(2)}) collective-permute-start(bf16[3,1,256,128]{3,2,1,0:T(8,128)(2,1)} %get-tuple-element.41), channel_id=1, source_target_pairs={{0,64},{32,96},{64,0},{96,32},{1,65},{33,97},{65,1},{97,33},{2,66}... | collective-permute-start | bytes 589832 | tf_op jit(solution)/shard_map/ppermute | solution.py:142
  50.4 29.3 %collective-permute-done.6.refs_2_ = bf16[3,1,256,128]{3,2,1,0:T(8,128)(2,1)} collective-permute-done((bf16[3,1,256,128]{3,2,1,0:T(8,128)(2,1)}, bf16[3,1,256,128]{3,2,1,0:T(8,128)(2,1)}, u32[]{:S(2)}, u32[]{:S(2)}) %collective-permute-start.6) | collective-permute-done | bytes 196640 | tf_op jit(solution)/shard_map/ppermute | solution.py:142
  79.7 3.4 %collective-permute-done.7.refs_3_ = bf16[3,1,256,128]{3,2,1,0:T(8,128)(2,1)} collective-permute-done((bf16[3,1,256,128]{3,2,1,0:T(8,128)(2,1)}, bf16[3,1,256,128]{3,2,1,0:T(8,128)(2,1)}, u32[]{:S(2)}, u32[]{:S(2)}) %collective-permute-start.7) | collective-permute-done | bytes 196640 | tf_op jit(solution)/shard_map/ppermute | solution.py:142
  85.3 4.7 %all-to-all-start.2 = ((bf16[4,3,1,256,128]{4,3,2,1,0:T(8,128)(2,1)}), bf16[4,3,1,256,128]{4,3,2,1,0:T(8,128)(2,1)}, u32[]{:S(2)}, u32[]{:S(2)}) async-start(bf16[4,3,1,256,128]{4,3,2,1,0:T(8,128)(2,1)} %shard_map.105._), calls=%async_computation.2 | async-start | bytes 1572864 | tf_op jit(solution)/shard_map/all_to_all | solution.py:381
  90.1 12.7 %shard_map.106 = (bf16[4,3,1,256,128]{4,3,2,1,0:T(8,128)(2,1)}, f32[3,1,1024]{2,1,0:T(1,128)}) custom-call(f32[1]{0:T(128)} %bitcast.bad_ref, bf16[4,3,1,256,128]{4,3,2,1,0:T(8,128)(2,1)} %all-to-all-done.q_ref, bf16[4,3,2,256,128]{4,3,2,1,0:T(8,128)(2,1)} %collective-permute-done.other_ref, bf16[4,3,2,256,128]{4,3,2,1,0:T(8,128)(2,1)} %all-to-all-done.1.refs_4_.own_ref, ...), custom_call_target="tpu_custom_call" | custom-call | flops 99999997952 | bytes 1024 | tf_op jit(solution)/shard_map/pallas_call | solution.py:189
  102.8 4.7 %all-to-all-start.3 = ((bf16[4,3,1,256,128]{4,3,2,1,0:T(8,128)(2,1)}), bf16[4,3,1,256,128]{4,3,2,1,0:T(8,128)(2,1)}, u32[]{:S(2)}, u32[]{:S(2)}) async-start(bf16[4,3,1,256,128]{4,3,2,1,0:T(8,128)(2,1)} %get-tuple-element.43.o_ref), calls=%async_computation.3 | async-start | bytes 1572864 | tf_op jit(solution)/shard_map/all_to_all | solution.py:381
  107.5 7.9 %shard_map.107 = (bf16[4,1,1,256,128]{4,3,2,1,0:T(8,128)(2,1)}, bf16[4,1,2,256,128]{4,3,2,1,0:T(8,128)(2,1)}, bf16[4,1,2,256,128]{4,3,2,1,0:T(8,128)(2,1)}, bf16[4,1,2,256,128]{4,3,2,1,0:T(8,128)(2,1)}) custom-call(f32[1]{0:T(128)} %bitcast.bad_ref, bf16[4,3,1,256,128]{4,3,2,1,0:T(8,128)(2,1)} %all-to-all-done.q_ref, ...), custom_call_target="tpu_custom_call" | custom-call | flops 99999997952 | bytes 1024 | tf_op jit(solution)/shard_map/pallas_call | solution.py:250
  115.4 5.8 %collective-permute-start.8 = (bf16[4,1,2,256,128]{4,3,2,1,0:T(8,128)(2,1)}, bf16[4,1,2,256,128]{4,3,2,1,0:T(8,128)(2,1)}, u32[]{:S(2)}, u32[]{:S(2)}) collective-permute-start(bf16[4,1,2,256,128]{4,3,2,1,0:T(8,128)(2,1)} %get-tuple-element.47), channel_id=1, source_target_pairs={{1,2},{3,4},{5,6},{2,1},{4,3},{6,5},{9,10},{11,12},{13,14},{10,9},... | collective-permute-start | bytes 1572872 | tf_op jit(solution)/shard_map/ppermute | solution.py:391
  123.4 14.0 %shard_map.109 = (bf16[4,2,1,256,128]{4,3,2,1,0:T(8,128)(2,1)}, bf16[4,2,2,256,128]{4,3,2,1,0:T(8,128)(2,1)}, bf16[4,2,2,256,128]{4,3,2,1,0:T(8,128)(2,1)}, bf16[4,2,2,256,128]{4,3,2,1,0:T(8,128)(2,1)}) custom-call(f32[1]{0:T(128)} %bitcast.bad_ref, bf16[4,3,1,256,128]{4,3,2,1,0:T(8,128)(2,1)} %all-to-all-done.q_ref, ...), custom_call_target="tpu_custom_call" | custom-call | flops 99999997952 | bytes 1024 | tf_op jit(solution)/shard_map/pallas_call | solution.py:250
  137.4 2.9 %shard_map.110.refs_8_ = bf16[4,5,256,128]{3,2,1,0:T(8,128)(2,1)} custom-call(bf16[4,1,1,256,128]{4,3,2,1,0:T(8,128)(2,1)} %get-tuple-element.45.rest_1_.dq_ref, bf16[4,1,2,256,128]{4,3,2,1,0:T(8,128)(2,1)} %get-tuple-element.46.refs_0_, bf16[4,1,2,256,128]{4,3,2,1,0:T(8,128)(2,1)} %collective-permute-done.8.refs_1_, ...), custom_call_target="tpu_custom_call" | custom-call | flops 100000000 | bytes 1024 | tf_op jit(solution)/shard_map/pallas_call | solution.py:296
  140.3 4.9 %all-to-all-start.4 = ((bf16[4,5,256,128]{3,2,1,0:T(8,128)(2,1)}), bf16[4,5,256,128]{3,2,1,0:T(8,128)(2,1)}, u32[]{:S(2)}, u32[]{:S(2)}) async-start(bf16[4,5,256,128]{3,2,1,0:T(8,128)(2,1)} %shard_map.110.refs_8_), calls=%async_computation.4 | async-start | bytes 2621440 | tf_op jit(solution)/shard_map/all_to_all | solution.py:381
  145.2 2.7 %collective-permute-start.13 = (bf16[3,1,256,128]{3,2,1,0:T(8,128)(2,1)S(1)}, bf16[3,1,256,128]{3,2,1,0:T(8,128)(2,1)S(1)}, u32[]{:S(2)}, u32[]{:S(2)}) collective-permute-start(bf16[3,1,256,128]{3,2,1,0:T(8,128)(2,1)S(1)} %copy-done.1), channel_id=1, source_target_pairs={{0,64},{32,96},{64,0},{96,32},{1,65},{33,97},{65,1},{97,33},{2,66}... | collective-permute-start | bytes 589832 | tf_op jit(solution)/shard_map/ppermute | solution.py:142
  148.6 4.2 %collective-permute-start.10 = (bf16[4,2,2,256,128]{4,3,2,1,0:T(8,128)(2,1)}, bf16[4,2,2,256,128]{4,3,2,1,0:T(8,128)(2,1)}, u32[]{:S(2)}, u32[]{:S(2)}) collective-permute-start(bf16[4,2,2,256,128]{4,3,2,1,0:T(8,128)(2,1)} %get-tuple-element.52), channel_id=1, source_target_pairs={{1,2},{3,4},{5,6},{2,1},{4,3},{6,5},{9,10},{11,12},{13,14},{10,9},... | collective-permute-start | bytes 3145736 | tf_op jit(solution)/shard_map/ppermute | solution.py:391
  155.2 2.7 %collective-permute-done.14.refs_7_ = bf16[3,1,256,128]{3,2,1,0:T(8,128)(2,1)} collective-permute-done((bf16[3,1,256,128]{3,2,1,0:T(8,128)(2,1)S(1)}, bf16[3,1,256,128]{3,2,1,0:T(8,128)(2,1)}, u32[]{:S(2)}, u32[]{:S(2)}) %collective-permute-start.14) | collective-permute-done | bytes 196640 | tf_op jit(solution)/shard_map/ppermute | solution.py:142
  157.9 8.6 %shard_map.114 = (bf16[3,2,256,128]{3,2,1,0:T(8,128)(2,1)}, bf16[3,2,256,128]{3,2,1,0:T(8,128)(2,1)}, bf16[3,2,256,128]{3,2,1,0:T(8,128)(2,1)}, bf16[3,2,256,128]{3,2,1,0:T(8,128)(2,1)}) custom-call(bf16[3,3,256,128]{3,2,1,0:T(8,128)(2,1)} %get-tuple-element.35.refs_1_.refs_0_, bf16[3,3,256,128]{3,2,1,0:T(8,128)(2,1)} %collective-permute-done.2.refs_1_, ...), custom_call_target="tpu_custom_call" | custom-call | flops 5000000000 | bytes 1024 | tf_op jit(solution)/shard_map/pallas_call | solution.py:368
  167.6 2.6 %collective-permute-start.16 = (bf16[3,2,256,128]{3,2,1,0:T(8,128)(2,1)}, bf16[3,2,256,128]{3,2,1,0:T(8,128)(2,1)}, u32[]{:S(2)}, u32[]{:S(2)}) collective-permute-start(bf16[3,2,256,128]{3,2,1,0:T(8,128)(2,1)} %get-tuple-element.61), channel_id=1, source_target_pairs={{0,64},{32,96},{64,0},{96,32},{1,65},{33,97},{65,1},{97,33},{2,66}... | collective-permute-start | bytes 1179656 | tf_op jit(solution)/shard_map/ppermute | solution.py:142
  170.6 2.3 %shard_map.111.refs_4_ = bf16[256,1536]{1,0:T(8,128)(2,1)} custom-call(bf16[4,5,256,128]{3,2,1,0:T(8,128)(2,1)} %all-to-all-done.4.refs_0_.refs_3_), custom_call_target="tpu_custom_call" | custom-call | flops 99999997952 | bytes 1024 | tf_op jit(solution)/shard_map/pallas_call | solution.py:49
  172.9 10.3 %collective-permute-done.10.refs_1_ = bf16[4,2,2,256,128]{4,3,2,1,0:T(8,128)(2,1)} collective-permute-done((bf16[4,2,2,256,128]{4,3,2,1,0:T(8,128)(2,1)}, bf16[4,2,2,256,128]{4,3,2,1,0:T(8,128)(2,1)}, u32[]{:S(2)}, u32[]{:S(2)}) %collective-permute-start.10) | collective-permute-done | bytes 1048608 | tf_op jit(solution)/shard_map/ppermute | solution.py:391
  183.2 3.2 %shard_map.112 = bf16[4,4,256,128]{3,2,1,0:T(8,128)(2,1)} custom-call(bf16[4,2,2,256,128]{4,3,2,1,0:T(8,128)(2,1)} %get-tuple-element.51.refs_0_, bf16[4,2,2,256,128]{4,3,2,1,0:T(8,128)(2,1)} %collective-permute-done.10.refs_1_, bf16[4,2,2,256,128]{4,3,2,1,0:T(8,128)(2,1)} %collective-permute-done.11.refs_2_, ...), custom_call_target="tpu_custom_call" | custom-call | flops 100000000 | bytes 1024 | tf_op jit(solution)/shard_map/pallas_call | solution.py:296
  186.5 4.4 %all-to-all-start.5 = ((bf16[4,4,256,128]{3,2,1,0:T(8,128)(2,1)}), bf16[4,4,256,128]{3,2,1,0:T(8,128)(2,1)}, u32[]{:S(2)}, u32[]{:S(2)}) async-start(bf16[4,4,256,128]{3,2,1,0:T(8,128)(2,1)} %shard_map.112), calls=%async_computation.5 | async-start | bytes 2097152 | tf_op jit(solution)/shard_map/all_to_all | solution.py:381
  190.9 6.3 %collective-permute-done.17.refs_3_ = bf16[3,2,256,128]{3,2,1,0:T(8,128)(2,1)} collective-permute-done((bf16[3,2,256,128]{3,2,1,0:T(8,128)(2,1)}, bf16[3,2,256,128]{3,2,1,0:T(8,128)(2,1)}, u32[]{:S(2)}, u32[]{:S(2)}) %collective-permute-start.17) | collective-permute-done | bytes 393248 | tf_op jit(solution)/shard_map/ppermute | solution.py:142
  197.2 2.8 %shard_map.115 = (bf16[256,1536]{1,0:T(8,128)(2,1)}, bf16[256,1536]{1,0:T(8,128)(2,1)}) custom-call(bf16[3,2,256,128]{3,2,1,0:T(8,128)(2,1)} %get-tuple-element.59.refs_0_, bf16[3,2,256,128]{3,2,1,0:T(8,128)(2,1)} %collective-permute-done.15.refs_1_, bf16[3,2,256,128]{3,2,1,0:T(8,128)(2,1)} %collective-permute-done.16.refs_2_, ...), custom_call_target="tpu_custom_call" | custom-call | flops 99999997952 | bytes 1024 | tf_op jit(solution)/shard_map/pallas_call | solution.py:49
  200.0 5.5 %all-to-all-done.5.refs_1_ = bf16[4,4,256,128]{3,2,1,0:T(8,128)(2,1)} async-done(((bf16[4,4,256,128]{3,2,1,0:T(8,128)(2,1)}), bf16[4,4,256,128]{3,2,1,0:T(8,128)(2,1)}, u32[]{:S(2)}, u32[]{:S(2)}) %all-to-all-start.5) | async-done | bytes 1048608 | tf_op jit(solution)/shard_map/all_to_all | solution.py:381
  205.5 3.0 %shard_map.113 = (bf16[256,1536]{1,0:T(8,128)(2,1)}, bf16[256,1536]{1,0:T(8,128)(2,1)}) custom-call(bf16[4,5,256,128]{3,2,1,0:T(8,128)(2,1)} %all-to-all-done.4.refs_0_.refs_3_, bf16[4,4,256,128]{3,2,1,0:T(8,128)(2,1)} %all-to-all-done.5.refs_1_), custom_call_target="tpu_custom_call" | custom-call | flops 100000000 | bytes 1024 | tf_op jit(solution)/shard_map/pallas_call | solution.py:49
  (41 shorter events, 15.0 us)
Async XLA Ops:
  3.4 25.4 %all-to-all-start.1 = ((bf16[4,3,2,256,128]{4,3,2,1,0:T(8,128)(2,1)}), bf16[4,3,2,256,128]{4,3,2,1,0:T(8,128)(2,1)}, u32[]{:S(2)}, u32[]{:S(2)}) async-start(bf16[4,3,2,256,128]{4,3,2,1,0:T(8,128)(2,1)} %shard_map.101.refs_3_), calls=%async_computation.1 | async-start | bytes 3145728 | tf_op jit(solution)/shard_map/all_to_all | solution.py:381
  11.2 30.2 %collective-permute-start.2 = (bf16[3,3,256,128]{3,2,1,0:T(8,128)(2,1)}, bf16[3,3,256,128]{3,2,1,0:T(8,128)(2,1)}, u32[]{:S(2)}, u32[]{:S(2)}) collective-permute-start(bf16[3,3,256,128]{3,2,1,0:T(8,128)(2,1)} %get-tuple-element.36), channel_id=1, source_target_pairs={{0,32},{32,0},{64,96},{96,64},{1,33},{33,1},{65,97},{97,65},{2,34}... | collective-permute-start | bytes 1769480 | tf_op jit(solution)/shard_map/ppermute | solution.py:142
  11.2 30.2 %collective-permute-start.3 = (bf16[3,3,256,128]{3,2,1,0:T(8,128)(2,1)}, bf16[3,3,256,128]{3,2,1,0:T(8,128)(2,1)}, u32[]{:S(2)}, u32[]{:S(2)}) collective-permute-start(bf16[3,3,256,128]{3,2,1,0:T(8,128)(2,1)} %get-tuple-element.37), channel_id=1, source_target_pairs={{0,64},{32,96},{64,0},{96,32},{1,65},{33,97},{65,1},{97,33},{2,66}... | collective-permute-start | bytes 1769480 | tf_op jit(solution)/shard_map/ppermute | solution.py:142
  13.5 28.0 %collective-permute-start.4 = (bf16[3,3,256,128]{3,2,1,0:T(8,128)(2,1)}, bf16[3,3,256,128]{3,2,1,0:T(8,128)(2,1)}, u32[]{:S(2)}, u32[]{:S(2)}) collective-permute-start(bf16[3,3,256,128]{3,2,1,0:T(8,128)(2,1)} %get-tuple-element.38), channel_id=1, source_target_pairs={{0,96},{32,64},{64,32},{96,0},{1,97},{33,65},{65,33},{97,1},{2,98}... | collective-permute-start | bytes 1769480 | tf_op jit(solution)/shard_map/ppermute | solution.py:142
  28.8 61.2 %collective-permute-start.1 = (bf16[4,3,2,256,128]{4,3,2,1,0:T(8,128)(2,1)}, bf16[4,3,2,256,128]{4,3,2,1,0:T(8,128)(2,1)}, u32[]{:S(2)}, u32[]{:S(2)}) collective-permute-start(bf16[4,3,2,256,128]{4,3,2,1,0:T(8,128)(2,1)} %all-to-all-done.1.refs_4_.own_ref), channel_id=1, source_target_pairs={{0,1},{1,0},{2,3},{3,2},{4,5},{5,4},{6,7},{7,6},{8,9},{9,8},{10,11... | collective-permute-start | bytes 4718600 | tf_op jit(solution)/shard_map/ppermute | solution.py:385
  30.7 59.3 %collective-permute-start = (bf16[4,3,2,256,128]{4,3,2,1,0:T(8,128)(2,1)}, bf16[4,3,2,256,128]{4,3,2,1,0:T(8,128)(2,1)}, u32[]{:S(2)}, u32[]{:S(2)}) collective-permute-start(bf16[4,3,2,256,128]{4,3,2,1,0:T(8,128)(2,1)} %all-to-all-done.1.refs_4_.own_ref), channel_id=1, source_target_pairs={{1,2},{3,4},{5,6},{2,1},{4,3},{6,5},{9,10},{11,12},{13,14},{10,9},... | collective-permute-start | bytes 4718600 | tf_op jit(solution)/shard_map/ppermute | solution.py:391
  37.2 48.1 %all-to-all-start = ((bf16[4,3,1,256,128]{4,3,2,1,0:T(8,128)(2,1)}), bf16[4,3,1,256,128]{4,3,2,1,0:T(8,128)(2,1)}, u32[]{:S(2)}, u32[]{:S(2)}) async-start(bf16[4,3,1,256,128]{4,3,2,1,0:T(8,128)(2,1)} %shard_map.103.refs_5_), calls=%async_computation | async-start | bytes 1572864 | tf_op jit(solution)/shard_map/all_to_all | solution.py:381
  47.0 3.4 %collective-permute-start.5 = (bf16[3,1,256,128]{3,2,1,0:T(8,128)(2,1)}, bf16[3,1,256,128]{3,2,1,0:T(8,128)(2,1)}, u32[]{:S(2)}, u32[]{:S(2)}) collective-permute-start(bf16[3,1,256,128]{3,2,1,0:T(8,128)(2,1)} %get-tuple-element.40), channel_id=1, source_target_pairs={{0,32},{32,0},{64,96},{96,64},{1,33},{33,1},{65,97},{97,65},{2,34}... | collective-permute-start | bytes 589832 | tf_op jit(solution)/shard_map/ppermute | solution.py:142
  47.1 32.6 %collective-permute-start.6 = (bf16[3,1,256,128]{3,2,1,0:T(8,128)(2,1)}, bf16[3,1,256,128]{3,2,1,0:T(8,128)(2,1)}, u32[]{:S(2)}, u32[]{:S(2)}) collective-permute-start(bf16[3,1,256,128]{3,2,1,0:T(8,128)(2,1)} %get-tuple-element.41), channel_id=1, source_target_pairs={{0,64},{32,96},{64,0},{96,32},{1,65},{33,97},{65,1},{97,33},{2,66}... | collective-permute-start | bytes 589832 | tf_op jit(solution)/shard_map/ppermute | solution.py:142
  49.7 33.5 %collective-permute-start.7 = (bf16[3,1,256,128]{3,2,1,0:T(8,128)(2,1)}, bf16[3,1,256,128]{3,2,1,0:T(8,128)(2,1)}, u32[]{:S(2)}, u32[]{:S(2)}) collective-permute-start(bf16[3,1,256,128]{3,2,1,0:T(8,128)(2,1)} %get-tuple-element.42), channel_id=1, source_target_pairs={{0,96},{32,64},{64,32},{96,0},{1,97},{33,65},{65,33},{97,1},{2,98}... | collective-permute-start | bytes 589832 | tf_op jit(solution)/shard_map/ppermute | solution.py:142
  85.3 17.5 %all-to-all-start.2 = ((bf16[4,3,1,256,128]{4,3,2,1,0:T(8,128)(2,1)}), bf16[4,3,1,256,128]{4,3,2,1,0:T(8,128)(2,1)}, u32[]{:S(2)}, u32[]{:S(2)}) async-start(bf16[4,3,1,256,128]{4,3,2,1,0:T(8,128)(2,1)} %shard_map.105._), calls=%async_computation.2 | async-start | bytes 1572864 | tf_op jit(solution)/shard_map/all_to_all | solution.py:381
  102.8 18.5 %all-to-all-start.3 = ((bf16[4,3,1,256,128]{4,3,2,1,0:T(8,128)(2,1)}), bf16[4,3,1,256,128]{4,3,2,1,0:T(8,128)(2,1)}, u32[]{:S(2)}, u32[]{:S(2)}) async-start(bf16[4,3,1,256,128]{4,3,2,1,0:T(8,128)(2,1)} %get-tuple-element.43.o_ref), calls=%async_computation.3 | async-start | bytes 1572864 | tf_op jit(solution)/shard_map/all_to_all | solution.py:381
  115.4 22.0 %collective-permute-start.8 = (bf16[4,1,2,256,128]{4,3,2,1,0:T(8,128)(2,1)}, bf16[4,1,2,256,128]{4,3,2,1,0:T(8,128)(2,1)}, u32[]{:S(2)}, u32[]{:S(2)}) collective-permute-start(bf16[4,1,2,256,128]{4,3,2,1,0:T(8,128)(2,1)} %get-tuple-element.47), channel_id=1, source_target_pairs={{1,2},{3,4},{5,6},{2,1},{4,3},{6,5},{9,10},{11,12},{13,14},{10,9},... | collective-permute-start | bytes 1572872 | tf_op jit(solution)/shard_map/ppermute | solution.py:391
  121.3 16.1 %collective-permute-start.9 = (bf16[4,1,2,256,128]{4,3,2,1,0:T(8,128)(2,1)}, bf16[4,1,2,256,128]{4,3,2,1,0:T(8,128)(2,1)}, u32[]{:S(2)}, u32[]{:S(2)}) collective-permute-start(bf16[4,1,2,256,128]{4,3,2,1,0:T(8,128)(2,1)} %get-tuple-element.48), channel_id=1, source_target_pairs={{0,1},{1,0},{2,3},{3,2},{4,5},{5,4},{6,7},{7,6},{8,9},{9,8},{10,11... | collective-permute-start | bytes 1572872 | tf_op jit(solution)/shard_map/ppermute | solution.py:385
  140.3 4.9 %copy-start.2 = (bf16[3,1,256,128]{3,2,1,0:T(8,128)(2,1)S(1)}, bf16[3,1,256,128]{3,2,1,0:T(8,128)(2,1)}, u32[]{:S(2)}) copy-start(bf16[3,1,256,128]{3,2,1,0:T(8,128)(2,1)} %get-tuple-element.56) | copy-start | bytes 589828
  140.3 4.9 %copy-start.1 = (bf16[3,1,256,128]{3,2,1,0:T(8,128)(2,1)S(1)}, bf16[3,1,256,128]{3,2,1,0:T(8,128)(2,1)}, u32[]{:S(2)}) copy-start(bf16[3,1,256,128]{3,2,1,0:T(8,128)(2,1)} %get-tuple-element.57) | copy-start | bytes 589828
  140.3 7.6 %copy-start = (bf16[3,1,256,128]{3,2,1,0:T(8,128)(2,1)S(1)}, bf16[3,1,256,128]{3,2,1,0:T(8,128)(2,1)}, u32[]{:S(2)}) copy-start(bf16[3,1,256,128]{3,2,1,0:T(8,128)(2,1)} %get-tuple-element.58) | copy-start | bytes 589828
  140.3 30.3 %all-to-all-start.4 = ((bf16[4,5,256,128]{3,2,1,0:T(8,128)(2,1)}), bf16[4,5,256,128]{3,2,1,0:T(8,128)(2,1)}, u32[]{:S(2)}, u32[]{:S(2)}) async-start(bf16[4,5,256,128]{3,2,1,0:T(8,128)(2,1)} %shard_map.110.refs_8_), calls=%async_computation.4 | async-start | bytes 2621440 | tf_op jit(solution)/shard_map/all_to_all | solution.py:381
  145.2 7.6 %collective-permute-start.12 = (bf16[3,1,256,128]{3,2,1,0:T(8,128)(2,1)S(1)}, bf16[3,1,256,128]{3,2,1,0:T(8,128)(2,1)S(1)}, u32[]{:S(2)}, u32[]{:S(2)}) collective-permute-start(bf16[3,1,256,128]{3,2,1,0:T(8,128)(2,1)S(1)} %copy-done.2), channel_id=1, source_target_pairs={{0,32},{32,0},{64,96},{96,64},{1,33},{33,1},{65,97},{97,65},{2,34}... | collective-permute-start | bytes 589832 | tf_op jit(solution)/shard_map/ppermute | solution.py:142
  145.2 9.3 %collective-permute-start.13 = (bf16[3,1,256,128]{3,2,1,0:T(8,128)(2,1)S(1)}, bf16[3,1,256,128]{3,2,1,0:T(8,128)(2,1)S(1)}, u32[]{:S(2)}, u32[]{:S(2)}) collective-permute-start(bf16[3,1,256,128]{3,2,1,0:T(8,128)(2,1)S(1)} %copy-done.1), channel_id=1, source_target_pairs={{0,64},{32,96},{64,0},{96,32},{1,65},{33,97},{65,1},{97,33},{2,66}... | collective-permute-start | bytes 589832 | tf_op jit(solution)/shard_map/ppermute | solution.py:142
  147.9 10.0 %collective-permute-start.14 = (bf16[3,1,256,128]{3,2,1,0:T(8,128)(2,1)S(1)}, bf16[3,1,256,128]{3,2,1,0:T(8,128)(2,1)}, u32[]{:S(2)}, u32[]{:S(2)}) collective-permute-start(bf16[3,1,256,128]{3,2,1,0:T(8,128)(2,1)S(1)} %copy-done), channel_id=1, source_target_pairs={{0,96},{32,64},{64,32},{96,0},{1,97},{33,65},{65,33},{97,1},{2,98}... | collective-permute-start | bytes 589832 | tf_op jit(solution)/shard_map/ppermute | solution.py:142
  148.6 34.6 %collective-permute-start.10 = (bf16[4,2,2,256,128]{4,3,2,1,0:T(8,128)(2,1)}, bf16[4,2,2,256,128]{4,3,2,1,0:T(8,128)(2,1)}, u32[]{:S(2)}, u32[]{:S(2)}) collective-permute-start(bf16[4,2,2,256,128]{4,3,2,1,0:T(8,128)(2,1)} %get-tuple-element.52), channel_id=1, source_target_pairs={{1,2},{3,4},{5,6},{2,1},{4,3},{6,5},{9,10},{11,12},{13,14},{10,9},... | collective-permute-start | bytes 3145736 | tf_op jit(solution)/shard_map/ppermute | solution.py:391
  152.8 30.5 %collective-permute-start.11 = (bf16[4,2,2,256,128]{4,3,2,1,0:T(8,128)(2,1)}, bf16[4,2,2,256,128]{4,3,2,1,0:T(8,128)(2,1)}, u32[]{:S(2)}, u32[]{:S(2)}) collective-permute-start(bf16[4,2,2,256,128]{4,3,2,1,0:T(8,128)(2,1)} %get-tuple-element.53), channel_id=1, source_target_pairs={{0,1},{1,0},{2,3},{3,2},{4,5},{5,4},{6,7},{7,6},{8,9},{9,8},{10,11... | collective-permute-start | bytes 3145736 | tf_op jit(solution)/shard_map/ppermute | solution.py:385
  152.9 1.7 copy-start.3
  154.5 0.7 copy-start.4
  166.5 24.4 %collective-permute-start.15 = (bf16[3,2,256,128]{3,2,1,0:T(8,128)(2,1)}, bf16[3,2,256,128]{3,2,1,0:T(8,128)(2,1)}, u32[]{:S(2)}, u32[]{:S(2)}) collective-permute-start(bf16[3,2,256,128]{3,2,1,0:T(8,128)(2,1)} %get-tuple-element.60), channel_id=1, source_target_pairs={{0,32},{32,0},{64,96},{96,64},{1,33},{33,1},{65,97},{97,65},{2,34}... | collective-permute-start | bytes 1179656 | tf_op jit(solution)/shard_map/ppermute | solution.py:142
  167.6 23.3 %collective-permute-start.16 = (bf16[3,2,256,128]{3,2,1,0:T(8,128)(2,1)}, bf16[3,2,256,128]{3,2,1,0:T(8,128)(2,1)}, u32[]{:S(2)}, u32[]{:S(2)}) collective-permute-start(bf16[3,2,256,128]{3,2,1,0:T(8,128)(2,1)} %get-tuple-element.61), channel_id=1, source_target_pairs={{0,64},{32,96},{64,0},{96,32},{1,65},{33,97},{65,1},{97,33},{2,66}... | collective-permute-start | bytes 1179656 | tf_op jit(solution)/shard_map/ppermute | solution.py:142
  170.2 27.0 %collective-permute-start.17 = (bf16[3,2,256,128]{3,2,1,0:T(8,128)(2,1)}, bf16[3,2,256,128]{3,2,1,0:T(8,128)(2,1)}, u32[]{:S(2)}, u32[]{:S(2)}) collective-permute-start(bf16[3,2,256,128]{3,2,1,0:T(8,128)(2,1)} %get-tuple-element.62), channel_id=1, source_target_pairs={{0,96},{32,64},{64,32},{96,0},{1,97},{33,65},{65,33},{97,1},{2,98}... | collective-permute-start | bytes 1179656 | tf_op jit(solution)/shard_map/ppermute | solution.py:142
  186.5 19.0 %all-to-all-start.5 = ((bf16[4,4,256,128]{3,2,1,0:T(8,128)(2,1)}), bf16[4,4,256,128]{3,2,1,0:T(8,128)(2,1)}, u32[]{:S(2)}, u32[]{:S(2)}) async-start(bf16[4,4,256,128]{3,2,1,0:T(8,128)(2,1)} %shard_map.112), calls=%async_computation.5 | async-start | bytes 2097152 | tf_op jit(solution)/shard_map/all_to_all | solution.py:381
